TPU v7x, 32 devices: a whole 2x2x4 slice. The times are simulated.
32 devices in a mesh: seq: 8 (over z, x), mlp: 4 (over y, core).
Axes of the slice: x: 2, y: 2, z: 4, core: 2. Of those that a mesh axis runs over, the one named last changes fastest.
Arguments:
- inputs: bfloat16 [4096, 512], P('seq', 'mlp'), may hold values from -6 to 6
- lengths: int32 [9], replicated, may hold values from 16 to 3584, as said below
- valid: int32 [4096], P('seq'), may hold values 0 or 1
- norm_attn: float32 [2, 512], P(None, 'mlp'), may hold values from 0.4 to 1.6
- w_qkv: bfloat16 [2, 3, 512, 512], P(None, None, None, 'mlp'), may hold values from -0.25 to 0.25
- blend: float32 [2, 3, 8], P(None, None, 'mlp'), may hold values from 0.5 to 1.5
- w_out: bfloat16 [2, 512, 512], P(None, 'mlp'), may hold values from -0.25 to 0.25
- norm_ffn: float32 [2, 512], P(None, 'mlp'), may hold values from 0.4 to 1.6
- w_up: bfloat16 [2, 512, 2048], P(None, None, 'mlp'), may hold values from -0.25 to 0.25
- w_down: bfloat16 [2, 2048, 512], P(None, 'mlp'), may hold values from -0.125 to 0.125
- grad_out: bfloat16 [4096, 512], P('seq', 'mlp'), may hold values from -6 to 6
Outputs:
- output: bfloat16 [4096, 512], P('seq', 'mlp')
- d_inputs: bfloat16 [4096, 512], P('seq', 'mlp')
- d_norm_attn: float32 [2, 512], P(None, 'mlp')
- d_w_qkv: float32 [2, 3, 512, 512], P(None, None, None, 'mlp')
- d_blend: float32 [2, 3, 8], P(None, None, 'mlp')
- d_w_out: float32 [2, 512, 512], P(None, 'mlp')
- d_norm_ffn: float32 [2, 512], P(None, 'mlp')
- d_w_up: float32 [2, 512, 2048], P(None, None, 'mlp')
- d_w_down: float32 [2, 2048, 512], P(None, 'mlp')
Inputs may be any that keep to these rules, and one draw needn't show every extreme that they name: The item lengths sum to 4096. Item number 4 (counting from 0) has 3584 tokens and begins within the first 512 tokens; the other items together hold 512 tokens.
All inputs are finite; a program needn't handle non-finite values. No bound on the sum of `valid` on one device may be relied on, other than what follows from the above.
Results may differ from a plain program's by a relative error of at most 0.018.
Values may be sent and summed in bfloat16 or wider, within the bound.
No kernel may reach another device: no remote copies, remote signals or barrier semaphores. Data moves between devices by JAX's collectives and lax.ppermute only.
A program may use at most 128 MiB of HBM per device.

v0:
```python
import math

import jax
import jax.numpy as jnp
from jax import lax
from jax.sharding import PartitionSpec as P

HD = 64
D = 512
BAND = 30
LAYERS = 2


epsilon = 1e-05
masked_score = -1e30


def from_behind(value, axis, steps):
    count = lax.axis_size(axis)
    leading, last = (max(0, -steps), min(count, count - steps))
    return lax.ppermute(value, axis, [(source, source + steps) for source in range(leading, last)])


def prefix(value, axis, combine, identity):
    peers, mine = (lax.axis_size(axis), lax.axis_index(axis))
    everything = jax.tree.map(
        lambda part, kind: lax.all_gather(part.astype(kind), axis),
        value,
        (jnp.bfloat16, jnp.bfloat16, jnp.bfloat16, jnp.bfloat16),
    )
    start = jax.tree.map(
        lambda part, zero: jnp.broadcast_to(jnp.asarray(zero, part.dtype), part.shape),
        value,
        identity,
    )

    def prefix_lap(k, before):
        reached = k < mine
        new = combine(
            before, jax.tree.map(lambda part, own: part[k].astype(own.dtype), everything, value)
        )
        return jax.tree.map(lambda a, b: jnp.where(reached, a, b), new, before)

    return lax.fori_loop(0, peers, prefix_lap, start)


def carried_in(value, axis, combine, identity):
    peers, mine = (lax.axis_size(axis), lax.axis_index(axis))
    everything = jax.tree.map(
        lambda part, kind: lax.all_gather(part.astype(kind), axis),
        value,
        jax.tree.map(lambda a: jnp.bfloat16 if a.dtype == jnp.float32 else a.dtype, value),
    )
    start = jax.tree.map(
        lambda part, zero: jnp.broadcast_to(jnp.asarray(zero, part.dtype), part.shape),
        value,
        identity,
    )

    def carried_lap(k, before):
        at = peers - 1 - k
        reached = at > mine
        new = combine(
            before, jax.tree.map(lambda part, own: part[at].astype(own.dtype), everything, value)
        )
        return jax.tree.map(lambda a, b: jnp.where(reached, a, b), new, before)

    return lax.fori_loop(0, peers, carried_lap, start)


def item_start(lengths, positions):
    ends_cum = jnp.cumsum(lengths)
    picked = jnp.where(ends_cum[None, :] <= positions[:, None], lengths[None, :], 0)
    return jnp.sum(picked, axis=1)


def kernel_maps(values):
    return (jax.nn.elu(values) + 1.0, jnp.tanh(values))


def chain_states(earlier, later):
    return (
        later[0] + later[3] * earlier[0],
        later[1] + later[3] * earlier[1],
        later[2] + later[3] * earlier[2],
        earlier[3] * later[3],
    )


def state_identity(head_count):
    square = jnp.zeros((head_count, HD, HD), jnp.float32)
    return (square, square, jnp.zeros((head_count, HD), jnp.float32), jnp.ones((), jnp.float32))


def norm_rows(hidden_part, gain_part):
    square_sums = lax.psum(jnp.sum(hidden_part * hidden_part, axis=1), "mlp")
    row_scale = lax.rsqrt(square_sums / D + epsilon)
    return (row_scale, (hidden_part * row_scale[:, None] * gain_part[None, :]).astype(jnp.bfloat16))


def norm_back(hidden_part, row_scale, gain_part, grad_part):
    gained = grad_part * gain_part[None, :]
    inner_sums = lax.psum(jnp.sum(gained * hidden_part, axis=1), "mlp")
    returned = (
        row_scale[:, None] * gained
        - hidden_part * (row_scale * row_scale * row_scale * inner_sums / D)[:, None]
    )
    return (returned, jnp.sum(grad_part * hidden_part * row_scale[:, None], axis=0))


def gather_rows(normed_part):
    return lax.all_gather(normed_part, "mlp", axis=1, tiled=True)


def spread_sums(partial_rows):
    return lax.psum_scatter(
        partial_rows.astype(jnp.bfloat16), "mlp", scatter_dimension=1, tiled=True
    ).astype(jnp.float32)


def gather_grads(grad_part):
    return lax.all_gather(grad_part, "mlp", axis=1, tiled=True)


def spread_grads(partial_rows):
    return lax.psum_scatter(
        partial_rows.astype(jnp.bfloat16), "mlp", scatter_dimension=1, tiled=True
    ).astype(jnp.float32)


def band_mask(layout, lower_row, ext_valid):
    row_count, block_rows, first_row, positions, starts, halo_starts, valid = layout
    key_pos = first_row - BAND + lower_row + jnp.arange(block_rows + BAND, dtype=jnp.int32)
    ext_starts = jnp.concatenate([halo_starts, starts])
    gap_rows = positions[:, None] - key_pos[None, :]
    same_item = starts[:, None] == ext_starts[None, :]
    usable = ext_valid[None, :] | (gap_rows == 0)
    return (gap_rows >= 0) & (gap_rows <= BAND) & same_item & usable


def far_masks(layout, lower_row):
    row_count, block_rows, first_row, positions, starts, halo_starts, valid = layout
    block_valid = valid == 1
    order = jnp.arange(block_rows, dtype=jnp.int32)
    causal = (
        (order[None, :] <= order[:, None])
        & (starts[None, :] == starts[:, None])
        & block_valid[None, :]
    ).astype(jnp.float32)
    carried = (starts < first_row + lower_row).astype(jnp.float32)
    tail_rows = ((starts == starts[block_rows - 1]) & block_valid).astype(jnp.float32)
    keep_flag = (starts[block_rows - 1] < first_row + lower_row).astype(jnp.float32)
    return (causal, carried, tail_rows, keep_flag)


def project(gathered, weight_qkv):
    return jnp.einsum(
        "nd,cde->cne", gathered, weight_qkv, preferred_element_type=jnp.float32
    ).astype(jnp.bfloat16)


def attend(qkv, blend_layer, layout):
    row_count, block_rows, first_row, positions, starts, halo_starts, valid = layout
    head_count = qkv.shape[2] // HD
    precise = lax.Precision.HIGHEST
    score_scale = 1.0 / math.sqrt(HD)
    valid_words = valid.astype(jnp.bfloat16)
    edge_row = row_count - BAND
    halo_keys, halo_values, halo_valid = from_behind(
        (qkv[1, edge_row:], qkv[2, edge_row:], valid_words[edge_row:]), "seq", 1
    )
    ext_keys = jnp.concatenate([halo_keys, qkv[1]]).reshape(BAND + row_count, head_count, HD)
    ext_values = jnp.concatenate([halo_values, qkv[2]]).reshape(BAND + row_count, head_count, HD)
    ext_valid = jnp.concatenate([halo_valid, valid_words]) > 0.5
    queries = qkv[0].reshape(row_count, head_count, HD)
    query_float = queries.astype(jnp.float32)
    key_float = ext_keys[BAND:].astype(jnp.float32)
    values_low = ext_values[BAND:]
    maps_rounded = tuple(
        (
            member.astype(jnp.bfloat16)
            for member in kernel_maps(query_float) + kernel_maps(key_float)
        )
    )
    query_one, query_two, key_one, key_two = maps_rounded
    zero_square = jnp.zeros((head_count, HD, HD), jnp.float32)
    state_one, state_two = (zero_square, zero_square)
    key_total = jnp.zeros((head_count, HD), jnp.float32)
    near_list, first_list, second_list, zeta_list, carry_list = ([], [], [], [], [])
    allowed = band_mask(layout, 0, ext_valid)
    scores = (
        jnp.einsum("qhe,khe->hqk", queries, ext_keys, preferred_element_type=jnp.float32)
        * score_scale
    )
    band_weights = jax.nn.softmax(jnp.where(allowed[None], scores, masked_score), axis=-1).astype(
        jnp.bfloat16
    )
    near_list.append(
        jnp.einsum("hqk,khe->qhe", band_weights, ext_values, preferred_element_type=jnp.float32)
    )
    causal, carried, tail_rows, keep_flag = far_masks(layout, 0)
    carry_list.append((state_one, state_two, key_total))
    attn_one = (
        jnp.einsum("qhd,khd->hqk", query_one, key_one, preferred_element_type=jnp.float32)
        * causal[None]
    )
    attn_two = (
        jnp.einsum("qhd,khd->hqk", query_two, key_two, preferred_element_type=jnp.float32)
        * causal[None]
    )
    carried_rows = carried[:, None, None]
    first_list.append(
        carried_rows * jnp.einsum("qhd,hde->qhe", query_one, state_one, precision=precise)
        + jnp.einsum("hqk,khe->qhe", attn_one, values_low, precision=precise)
    )
    second_list.append(
        carried_rows * jnp.einsum("qhd,hde->qhe", query_two, state_two, precision=precise)
        + jnp.einsum("hqk,khe->qhe", attn_two, values_low, precision=precise)
    )
    zeta_list.append(
        carried[:, None] * jnp.einsum("qhd,hd->qh", query_one, key_total, precision=precise)
        + jnp.sum(attn_one, axis=2).T
    )
    tail_keys = tail_rows.astype(jnp.bfloat16)[:, None, None]
    state_one = keep_flag * state_one + jnp.einsum(
        "khd,khe->hde", key_one * tail_keys, values_low, preferred_element_type=jnp.float32
    )
    state_two = keep_flag * state_two + jnp.einsum(
        "khd,khe->hde", key_two * tail_keys, values_low, preferred_element_type=jnp.float32
    )
    key_total = keep_flag * key_total + jnp.sum(key_one * tail_keys, axis=0, dtype=jnp.float32)
    device_keep = (starts[row_count - 1] < first_row).astype(jnp.float32)
    device_one, device_two, device_total, unused_flag = prefix(
        (state_one, state_two, key_total, device_keep),
        "seq",
        chain_states,
        state_identity(head_count),
    )
    device_rows = (starts < first_row).astype(jnp.float32)
    num_one = first_list[0] + device_rows[:, None, None] * jnp.einsum(
        "qhd,hde->qhe", query_one, device_one, precision=precise
    )
    num_two = second_list[0] + device_rows[:, None, None] * jnp.einsum(
        "qhd,hde->qhe", query_two, device_two, precision=precise
    )
    zeta_sum = zeta_list[0] + device_rows[:, None] * jnp.einsum(
        "qhd,hd->qh", query_one, device_total, precision=precise
    )
    root_norm = jnp.sqrt(zeta_sum + 1.0)
    far_one = num_one / (math.sqrt(HD) * root_norm[:, :, None])
    far_two = num_two / root_norm[:, :, None]
    near_field = near_list[0]
    mixed_heads = (
        blend_layer[0][None, :, None] * near_field
        + blend_layer[1][None, :, None] * far_one
        + blend_layer[2][None, :, None] * far_two
    )
    mixed_heads = mixed_heads.reshape(row_count, head_count * HD).astype(jnp.bfloat16)
    attention_kept = (
        ext_keys,
        ext_values,
        ext_valid,
        queries,
        maps_rounded,
        values_low,
        query_float,
        key_float,
        near_field,
        far_one,
        far_two,
        root_norm,
        carry_list,
        (device_one, device_two, device_total),
    )
    return (mixed_heads, attention_kept)


def attend_back(d_mixed, blend_layer, attention_kept, layout):
    row_count, block_rows, first_row, positions, starts, halo_starts, valid = layout
    (
        ext_keys,
        ext_values,
        ext_valid,
        queries,
        maps_rounded,
        values_low,
        query_float,
        key_float,
        near_field,
        far_one,
        far_two,
        root_norm,
        carry_list,
        device_states,
    ) = attention_kept
    query_one, query_two, key_one, key_two = maps_rounded
    device_one, device_two, device_total = device_states
    head_count = queries.shape[1]
    precise = lax.Precision.HIGHEST
    score_scale = 1.0 / math.sqrt(HD)
    d_heads = d_mixed.reshape(row_count, head_count, HD)
    d_float = d_heads.astype(jnp.float32)
    dot_one = jnp.sum(d_float * far_one, axis=2)
    dot_two = jnp.sum(d_float * far_two, axis=2)
    d_blend = jnp.stack(
        [
            jnp.sum(d_float * near_field, axis=(0, 2)),
            jnp.sum(dot_one, axis=0),
            jnp.sum(dot_two, axis=0),
        ]
    )
    d_num_one = d_float * (blend_layer[1][None, :, None] / (math.sqrt(HD) * root_norm[:, :, None]))
    d_num_two = d_float * (blend_layer[2][None, :, None] / root_norm[:, :, None])
    d_zeta = -(blend_layer[1][None, :] * dot_one + blend_layer[2][None, :] * dot_two) / (
        2.0 * root_norm * root_norm
    )
    device_rows = (starts < first_row).astype(jnp.float32)
    device_keep = (starts[row_count - 1] < first_row).astype(jnp.float32)
    send_one = jnp.einsum(
        "qhd,qhe->hde", query_one * device_rows[:, None, None], d_num_one, precision=precise
    )
    send_two = jnp.einsum(
        "qhd,qhe->hde", query_two * device_rows[:, None, None], d_num_two, precision=precise
    )
    send_total = jnp.einsum(
        "qh,qhd->hd", d_zeta * device_rows[:, None], query_one, precision=precise
    )
    later_one, later_two, later_total, unused_flag = carried_in(
        (send_one, send_two, send_total, device_keep),
        "seq",
        chain_states,
        state_identity(head_count),
    )
    device_tail = ((starts == starts[row_count - 1]) & (valid == 1)).astype(jnp.float32)[
        :, None, None
    ]
    d_query_one = device_rows[:, None, None] * (
        jnp.einsum("qhe,hde->qhd", d_num_one, device_one, precision=precise)
        + d_zeta[:, :, None] * device_total[None]
    )
    d_query_two = device_rows[:, None, None] * jnp.einsum(
        "qhe,hde->qhd", d_num_two, device_two, precision=precise
    )
    d_key_one = device_tail * (
        jnp.einsum("hde,khe->khd", later_one, values_low, precision=precise) + later_total[None]
    )
    d_key_two = device_tail * jnp.einsum("hde,khe->khd", later_two, values_low, precision=precise)
    d_values = device_tail * (
        jnp.einsum("hde,khd->khe", later_one, key_one, precision=precise)
        + jnp.einsum("hde,khd->khe", later_two, key_two, precision=precise)
    )
    near_keys = jnp.zeros((BAND + row_count, head_count, HD), jnp.float32)
    near_values = jnp.zeros((BAND + row_count, head_count, HD), jnp.float32)
    zero_square = jnp.zeros((head_count, HD, HD), jnp.float32)
    back_one, back_two = (zero_square, zero_square)
    back_total = jnp.zeros((head_count, HD), jnp.float32)
    pieces = []
    for block_index in reversed(range(row_count // block_rows)):
        lower_row = block_index * block_rows
        upper_row = lower_row + block_rows
        causal, carried, tail_rows, keep_flag = far_masks(layout, lower_row)
        state_one, state_two, key_total = carry_list[block_index]
        carried_rows = carried[:, None, None]
        tail_keys = tail_rows[:, None, None]
        grad_one = (
            jnp.einsum("qhe,khe->hqk", d_num_one, values_low, precision=precise) * causal[None]
        )
        grad_two = (
            jnp.einsum("qhe,khe->hqk", d_num_two, values_low, precision=precise) * causal[None]
        )
        attn_one = (
            jnp.einsum("qhd,khd->hqk", query_one, key_one, preferred_element_type=jnp.float32)
            * causal[None]
        )
        attn_two = (
            jnp.einsum("qhd,khd->hqk", query_two, key_two, preferred_element_type=jnp.float32)
            * causal[None]
        )
        prefix_keys = carried_rows * key_total[None] + jnp.einsum(
            "qk,khd->qhd", causal, key_one, precision=precise
        )
        block_dq_one = (
            jnp.einsum("hqk,khd->qhd", grad_one, key_one, precision=precise)
            + carried_rows * jnp.einsum("qhe,hde->qhd", d_num_one, state_one, precision=precise)
            + d_zeta[:, :, None] * prefix_keys
        )
        block_dq_two = jnp.einsum(
            "hqk,khd->qhd", grad_two, key_two, precision=precise
        ) + carried_rows * jnp.einsum("qhe,hde->qhd", d_num_two, state_two, precision=precise)
        block_dk_one = (
            jnp.einsum("hqk,qhd->khd", grad_one, query_one, precision=precise)
            + jnp.einsum("qk,qhd->khd", causal, d_zeta[:, :, None] * query_one, precision=precise)
            + tail_keys * jnp.einsum("hde,khe->khd", back_one, values_low, precision=precise)
        )
        block_dk_two = jnp.einsum(
            "hqk,qhd->khd", grad_two, query_two, precision=precise
        ) + tail_keys * jnp.einsum("hde,khe->khd", back_two, values_low, precision=precise)
        block_dv = (
            jnp.einsum("hqk,qhe->khe", attn_one, d_num_one, precision=precise)
            + jnp.einsum("hqk,qhe->khe", attn_two, d_num_two, precision=precise)
            + tail_keys
            * (
                jnp.einsum("hde,khd->khe", back_one, key_one, precision=precise)
                + jnp.einsum("hde,khd->khe", back_two, key_two, precision=precise)
            )
        )
        back_one = keep_flag * back_one + jnp.einsum(
            "qhd,qhe->hde", query_one * carried_rows, d_num_one, precision=precise
        )
        back_two = keep_flag * back_two + jnp.einsum(
            "qhd,qhe->hde", query_two * carried_rows, d_num_two, precision=precise
        )
        back_total = keep_flag * back_total + jnp.einsum(
            "qh,qhd->hd", d_zeta * carried[:, None], query_one, precision=precise
        )
        allowed = band_mask(layout, lower_row, ext_valid)
        scores = (
            jnp.einsum("qhe,khe->hqk", queries, ext_keys, preferred_element_type=jnp.float32)
            * score_scale
        )
        band_probs = jax.nn.softmax(jnp.where(allowed[None], scores, masked_score), axis=-1)
        d_probs = blend_layer[0][:, None, None] * jnp.einsum(
            "qhe,khe->hqk", d_heads, ext_values, preferred_element_type=jnp.float32
        )
        d_scores = (
            band_probs * (d_probs - jnp.sum(band_probs * d_probs, axis=2, keepdims=True))
        ).astype(jnp.bfloat16)
        block_dq_near = score_scale * jnp.einsum(
            "hqk,khe->qhe", d_scores, ext_keys, preferred_element_type=jnp.float32
        )
        near_keys = near_keys.at[lower_row : upper_row + BAND].add(
            score_scale
            * jnp.einsum("hqk,qhe->khe", d_scores, queries, preferred_element_type=jnp.float32)
        )
        near_values = near_values.at[lower_row : upper_row + BAND].add(
            blend_layer[0][None, :, None]
            * jnp.einsum(
                "hqk,qhe->khe",
                band_probs.astype(jnp.bfloat16),
                d_heads,
                preferred_element_type=jnp.float32,
            )
        )
        pieces.insert(
            0, (block_dq_one, block_dq_two, block_dk_one, block_dk_two, block_dv, block_dq_near)
        )
    d_query_one = d_query_one + jnp.concatenate([member[0] for member in pieces])
    d_query_two = d_query_two + jnp.concatenate([member[1] for member in pieces])
    d_key_one = d_key_one + jnp.concatenate([member[2] for member in pieces])
    d_key_two = d_key_two + jnp.concatenate([member[3] for member in pieces])
    d_values = d_values + jnp.concatenate([member[4] for member in pieces]) + near_values[BAND:]
    d_queries = jax.vjp(kernel_maps, query_float)[1]((d_query_one, d_query_two))[
        0
    ] + jnp.concatenate([member[5] for member in pieces])
    d_keys = jax.vjp(kernel_maps, key_float)[1]((d_key_one, d_key_two))[0] + near_keys[BAND:]
    returned_keys, returned_values = from_behind((near_keys[:BAND], near_values[:BAND]), "seq", -1)
    edge_row = row_count - BAND
    d_keys = d_keys.at[edge_row:].add(returned_keys)
    d_values = d_values.at[edge_row:].add(returned_values)
    d_qkv_rows = (
        jnp.stack([d_queries, d_keys, d_values])
        .reshape(3, row_count, head_count * HD)
        .astype(jnp.bfloat16)
    )
    return (d_qkv_rows, d_blend)


def per_device(
    inputs, lengths, valid, norm_attn, w_qkv, blend, w_out, norm_ffn, w_up, w_down, grad_out
):
    row_count = inputs.shape[0]
    block_rows = min(512, row_count)
    first_row = lax.axis_index("seq") * row_count
    positions = first_row + jnp.arange(row_count, dtype=jnp.int32)
    starts = item_start(lengths, positions)
    halo_starts = item_start(lengths, first_row - BAND + jnp.arange(BAND, dtype=jnp.int32))
    layout = (row_count, block_rows, first_row, positions, starts, halo_starts, valid)
    hidden = inputs.astype(jnp.float32)
    saved_layers = []
    for layer_index in range(LAYERS):
        scale_attn, normed_attn = norm_rows(hidden, norm_attn[layer_index])
        gathered = gather_rows(normed_attn)
        qkv = project(gathered, w_qkv[layer_index])
        mixed_heads, attention_kept = attend(qkv, blend[layer_index], layout)
        middle = hidden + spread_sums(
            jnp.dot(mixed_heads, w_out[layer_index], preferred_element_type=jnp.float32)
        )
        scale_ffn, normed_ffn = norm_rows(middle, norm_ffn[layer_index])
        gathered_ffn = gather_rows(normed_ffn)
        up_proj = jnp.dot(gathered_ffn, w_up[layer_index], preferred_element_type=jnp.float32)
        activated = jax.nn.gelu(up_proj).astype(jnp.bfloat16)
        after_layer = middle + spread_sums(
            jnp.dot(activated, w_down[layer_index], preferred_element_type=jnp.float32)
        )
        rows_kept = (gathered, gathered_ffn)
        saved_layers.append(
            (
                hidden,
                scale_attn,
                rows_kept,
                qkv,
                mixed_heads,
                attention_kept,
                middle,
                scale_ffn,
                up_proj,
                activated,
            )
        )
        hidden = after_layer
    output = hidden.astype(jnp.bfloat16)
    residual_grad = grad_out.astype(jnp.float32)
    layer_terms = []
    for layer_index in reversed(range(LAYERS)):
        (
            hidden,
            scale_attn,
            rows_kept,
            qkv,
            mixed_heads,
            attention_kept,
            middle,
            scale_ffn,
            up_proj,
            activated,
        ) = saved_layers[layer_index]
        gathered, gathered_ffn = rows_kept
        grad_rows = gather_grads(residual_grad.astype(jnp.bfloat16))
        d_down = jnp.einsum("nf,nd->fd", activated, grad_rows, preferred_element_type=jnp.float32)
        d_act = jnp.einsum(
            "nd,fd->nf", grad_rows, w_down[layer_index], preferred_element_type=jnp.float32
        )
        d_up_rows = jax.vjp(jax.nn.gelu, up_proj)[1](d_act)[0].astype(jnp.bfloat16)
        d_up = jnp.einsum("nd,nf->df", gathered_ffn, d_up_rows, preferred_element_type=jnp.float32)
        grad_normed = spread_grads(
            jnp.einsum(
                "nf,df->nd", d_up_rows, w_up[layer_index], preferred_element_type=jnp.float32
            )
        )
        norm_part, d_gain_ffn = norm_back(middle, scale_ffn, norm_ffn[layer_index], grad_normed)
        residual_grad = residual_grad + norm_part
        grad_rows = gather_grads(residual_grad.astype(jnp.bfloat16))
        d_outw = jnp.einsum("ne,nd->ed", mixed_heads, grad_rows, preferred_element_type=jnp.float32)
        d_mixed = jnp.einsum(
            "nd,ed->ne", grad_rows, w_out[layer_index], preferred_element_type=jnp.float32
        ).astype(jnp.bfloat16)
        d_qkv_rows, d_blend_layer = attend_back(d_mixed, blend[layer_index], attention_kept, layout)
        d_qkvw = jnp.einsum("nd,cne->cde", gathered, d_qkv_rows, preferred_element_type=jnp.float32)
        grad_normed = spread_grads(
            jnp.einsum(
                "cne,cde->nd", d_qkv_rows, w_qkv[layer_index], preferred_element_type=jnp.float32
            )
        )
        norm_part, d_gain_attn = norm_back(hidden, scale_attn, norm_attn[layer_index], grad_normed)
        residual_grad = residual_grad + norm_part
        weight_terms = (d_gain_attn, d_qkvw, d_blend_layer, d_outw, d_gain_ffn, d_up, d_down)
        weight_terms = lax.psum(
            (
                weight_terms[0],
                weight_terms[1],
                weight_terms[2],
                weight_terms[3],
                weight_terms[4],
                weight_terms[5],
                weight_terms[6],
            ),
            "seq",
        )
        layer_terms.insert(0, weight_terms)
    stacked = tuple(
        (jnp.stack([member[position] for member in layer_terms]) for position in range(7))
    )
    return (
        output,
        residual_grad.astype(jnp.bfloat16),
        stacked[0],
        stacked[1],
        stacked[2],
        stacked[3],
        stacked[4],
        stacked[5],
        stacked[6],
    )


def solution(mesh):
    placed = (
        P("seq", "mlp"),
        P(),
        P("seq"),
        P(None, "mlp"),
        P(None, None, None, "mlp"),
        P(None, None, "mlp"),
        P(None, "mlp", None),
        P(None, "mlp"),
        P(None, None, "mlp"),
        P(None, "mlp", None),
        P("seq", "mlp"),
    )
    return jax.shard_map(
        per_device,
        mesh=mesh,
        in_specs=placed,
        out_specs=(
            P("seq", "mlp"),
            P("seq", "mlp"),
            P(None, "mlp"),
            P(None, None, None, "mlp"),
            P(None, None, "mlp"),
            P(None, "mlp", None),
            P(None, "mlp"),
            P(None, None, "mlp"),
            P(None, "mlp", None),
        ),
        check_vma=False,
    )
```

profile of v0, /device:TPU:0, one launch (start us, length us, event | category | flops | bytes accessed | tf_op | source)
XLA Modules:
  0.0 1232.2 jit_solution(9047248170779676175)
XLA Ops:
  9.6 8.4 psum.154
  47.7 30.9 %all-gather = bf16[16,64,64]{2,1,0:T(8,128)(2,1)S(1)} all-gather(bf16[2,64,64]{2,1,0:T(8,128)(2,1)S(1)} %convolution_convert_fusion.11), channel_id=2, replica_groups=mesh['seq'=8,'mlp'=4] {'seq'}, dimensions={0}, use_global_device_ids=true | all-gather | bytes 147456 | tf_op jit(solution)/shard_map/all_gather | solution.py:27
  79.9 18.0 %all-reduce = bf16[8]{0:T(256)(128)(2,1)S(1)} all-reduce(bf16[8]{0:T(256)(128)(2,1)S(1)} %dynamic-update-slice.24), channel_id=1, replica_groups=mesh['seq'=8,'mlp'=4] {'seq'}, use_global_device_ids=true, to_apply=%add | all-reduce | flops 8 | bytes 32
  97.9 30.7 %all-gather.1 = bf16[16,64,64]{2,1,0:T(8,128)(2,1)S(1)} all-gather(bf16[2,64,64]{2,1,0:T(8,128)(2,1)S(1)} %convolution_convert_fusion.10), channel_id=3, replica_groups=mesh['seq'=8,'mlp'=4] {'seq'}, dimensions={0}, use_global_device_ids=true | all-gather | bytes 147456 | tf_op jit(solution)/shard_map/all_gather | solution.py:27
  128.7 17.3 %all_gather.111 = bf16[8,2,64]{2,1,0:T(2,128)(2,1)S(1)} all-gather(bf16[1,2,64]{2,1,0:T(2,128)(2,1)S(1)} %convert_element_type.536), channel_id=1, replica_groups=mesh['seq'=8,'mlp'=4] {'seq'}, dimensions={0}, use_global_device_ids=true | all-gather | bytes 2304 | tf_op jit(solution)/shard_map/all_gather | solution.py:27
  146.0 10.7 while.88
  182.9 18.4 %reduce-scatter.25.cloned.1.call-done = bf16[128,512]{1,0:T(8,128)(2,1)} async-done(((bf16[512,512]{1,0:T(8,128)(2,1)}), bf16[128,512]{1,0:T(8,128)(2,1)}) %reduce-scatter.25.cloned.1.call-update) | async-done | bytes 131088
  209.6 7.6 all_gather.112
  225.9 20.1 %reduce-scatter.27.cloned.1.call-done = bf16[128,512]{1,0:T(8,128)(2,1)} async-done(((bf16[512,512]{1,0:T(8,128)(2,1)}), bf16[128,512]{1,0:T(8,128)(2,1)}) %reduce-scatter.27.cloned.1.call-update) | async-done | bytes 131088
  256.6 7.4 all_gather.113
  274.2 32.8 %all-gather.2 = bf16[16,64,64]{2,1,0:T(8,128)(2,1)} all-gather(bf16[2,64,64]{2,1,0:T(8,128)(2,1)S(1)} %convolution_convert_fusion.9), channel_id=4, replica_groups=mesh['seq'=8,'mlp'=4] {'seq'}, dimensions={0}, use_global_device_ids=true | all-gather | bytes 147456 | tf_op jit(solution)/shard_map/all_gather | solution.py:27
  307.0 32.8 %all-gather.3 = bf16[16,64,64]{2,1,0:T(8,128)(2,1)} all-gather(bf16[2,64,64]{2,1,0:T(8,128)(2,1)S(1)} %convolution_convert_fusion.8), channel_id=5, replica_groups=mesh['seq'=8,'mlp'=4] {'seq'}, dimensions={0}, use_global_device_ids=true | all-gather | bytes 147456 | tf_op jit(solution)/shard_map/all_gather | solution.py:27
  341.0 21.3 %all_gather.118 = bf16[8,2,64]{2,1,0:T(2,128)(2,1)} all-gather(bf16[1,2,64]{2,1,0:T(2,128)(2,1)} %convert_element_type.560), channel_id=1, replica_groups=mesh['seq'=8,'mlp'=4] {'seq'}, dimensions={0}, use_global_device_ids=true | all-gather | bytes 2304 | tf_op jit(solution)/shard_map/all_gather | solution.py:27
  362.3 32.3 %while.89 = (s32[]{:T(128)}, f32[2,64,64]{2,1,0:T(8,128)}, f32[2,64,64]{2,1,0:T(8,128)}, f32[2,64]{1,0:T(2,128)S(1)}, s32[]{:T(128)}, /*index=5*/bf16[8,2,64,64]...) while((s32[]{:T(128)}, f32[2,64,64]{2,1,0:T(8,128)}, ...), condition=%wide.region_21.22_spmd.clone, body=%wide.region_20.21_spmd.clone.sunk | while | flops 82565 | bytes 165289 | solution.py:44
  422.6 7.6 all_gather.120
  431.3 10.6 reduce-scatter.29.cloned.1.call-done
  453.4 18.1 %all_gather.119 = bf16[512,512]{1,0:T(8,128)(2,1)S(1)} all-gather(bf16[512,128]{1,0:T(8,128)(2,1)S(1)} %multiply_convert_fusion.4), channel_id=1, replica_groups=mesh['seq'=8,'mlp'=4] {'mlp'}, dimensions={1}, use_global_device_ids=true | all-gather | bytes 655360 | tf_op jit(solution)/shard_map/all_gather | solution.py:112
  487.5 13.6 %reduce-scatter.33.cloned.1.call-done = bf16[128,512]{1,0:T(8,128)(2,1)} async-done(((bf16[512,512]{1,0:T(8,128)(2,1)}), bf16[128,512]{1,0:T(8,128)(2,1)}) %reduce-scatter.33.cloned.1.call-update) | async-done | bytes 131088
  547.2 32.8 %all-gather.4 = bf16[16,64,64]{2,1,0:T(8,128)(2,1)} all-gather(bf16[2,64,64]{2,1,0:T(8,128)(2,1)S(1)} %convolution_convert_fusion.15), channel_id=6, replica_groups=mesh['seq'=8,'mlp'=4] {'seq'}, dimensions={0}, use_global_device_ids=true | all-gather | bytes 147456 | tf_op jit(solution)/shard_map/all_gather | solution.py:50
  580.0 32.8 %all-gather.5 = bf16[16,64,64]{2,1,0:T(8,128)(2,1)} all-gather(bf16[2,64,64]{2,1,0:T(8,128)(2,1)S(1)} %copy-done.148), channel_id=7, replica_groups=mesh['seq'=8,'mlp'=4] {'seq'}, dimensions={0}, use_global_device_ids=true | all-gather | bytes 147456 | tf_op jit(solution)/shard_map/all_gather | solution.py:50
  613.1 21.3 %all-gather.10 = bf16[8,2,64]{2,1,0:T(2,128)(2,1)} all-gather(bf16[1,2,64]{2,1,0:T(2,128)(2,1)S(1)} %convert_bitcast_fusion.3), channel_id=8, replica_groups=mesh['seq'=8,'mlp'=4] {'seq'}, dimensions={0}, use_global_device_ids=true | all-gather | bytes 2304 | tf_op jit(solution)/shard_map/all_gather | solution.py:50
  634.4 37.1 %while.90 = (s32[]{:T(128)}, f32[2,64,64]{2,1,0:T(8,128)}, f32[2,64,64]{2,1,0:T(8,128)}, f32[2,64]{1,0:T(2,128)}, s32[]{:T(128)}, /*index=5*/bf16[8,2,64,64]{3,2...) while((s32[]{:T(128)}, f32[2,64,64]{2,1,0:T(8,128)}, ...), condition=%wide.region_34.35_spmd.clone, body=%wide.region_33.34_spmd.clone.sunk | while | flops 82569 | bytes 165351 | solution.py:68
  710.8 19.8 %reduce-scatter.35.cloned.1.call-done = bf16[128,512]{1,0:T(8,128)(2,1)} async-done(((bf16[512,512]{1,0:T(8,128)(2,1)}), bf16[128,512]{1,0:T(8,128)(2,1)}) %reduce-scatter.35.cloned.1.call-update) | async-done | bytes 131088
  762.5 15.6 %reduce-scatter.37.cloned.1.call-done = bf16[128,512]{1,0:T(8,128)(2,1)} async-done(((bf16[512,512]{1,0:T(8,128)(2,1)}), bf16[128,512]{1,0:T(8,128)(2,1)}) %reduce-scatter.37.cloned.1.call-update) | async-done | bytes 131088
  790.1 7.4 all_gather.129
  821.9 32.8 %all-gather.7 = bf16[16,64,64]{2,1,0:T(8,128)(2,1)} all-gather(bf16[2,64,64]{2,1,0:T(8,128)(2,1)S(1)} %convolution_convert_fusion.13), channel_id=9, replica_groups=mesh['seq'=8,'mlp'=4] {'seq'}, dimensions={0}, use_global_device_ids=true | all-gather | bytes 147456 | tf_op jit(solution)/shard_map/all_gather | solution.py:50
  854.7 32.7 %all-gather.8 = bf16[16,64,64]{2,1,0:T(8,128)(2,1)} all-gather(bf16[2,64,64]{2,1,0:T(8,128)(2,1)S(1)} %copy-done.147), channel_id=10, replica_groups=mesh['seq'=8,'mlp'=4] {'seq'}, dimensions={0}, use_global_device_ids=true | all-gather | bytes 147456 | tf_op jit(solution)/shard_map/all_gather | solution.py:50
  887.7 20.6 %all-gather.11 = bf16[8,2,64]{2,1,0:T(2,128)(2,1)S(1)} all-gather(bf16[1,2,64]{2,1,0:T(2,128)(2,1)S(1)} %convert_bitcast_fusion.2), channel_id=11, replica_groups=mesh['seq'=8,'mlp'=4] {'seq'}, dimensions={0}, use_global_device_ids=true | all-gather | bytes 2304 | tf_op jit(solution)/shard_map/all_gather | solution.py:50
  908.3 36.7 %while.91 = (s32[]{:T(128)}, f32[2,64,64]{2,1,0:T(8,128)}, f32[2,64,64]{2,1,0:T(8,128)}, f32[2,64]{1,0:T(2,128)}, s32[]{:T(128)}, /*index=5*/bf16[8,2,64,64]{3,2...) while((s32[]{:T(128)}, f32[2,64,64]{2,1,0:T(8,128)}, ...), condition=%wide.region_45.46_spmd.clone, body=%wide.region_44.45_spmd.clone.sunk | while | flops 82569 | bytes 165351 | solution.py:68
  980.7 12.6 %reduce-scatter.39.cloned.1.call-done = bf16[128,512]{1,0:T(8,128)(2,1)} async-done(((bf16[512,512]{1,0:T(8,128)(2,1)}), bf16[128,512]{1,0:T(8,128)(2,1)}) %reduce-scatter.39.cloned.1.call-update) | async-done | bytes 131088
  994.6 21.7 %all-reduce.1 = (f32[1,128]{1,0:T(1,128)S(1)}, f32[1,128]{1,0:T(1,128)S(1)}, f32[1,3,2]{1,2,0:T(2,128)S(1)}, f32[1,3,2]{1,2,0:T(2,128)S(1)}, f32[1,128]{1,0:T(1,128)S(1)}, /*index=5*/f32[1,128]{1,0:T(1,128)S(1)}) all-reduce(f32[1,128]{1,0:T(1,128)S(1)} %bitcast.750, ...), channel_id=1, replica_groups=mesh['seq'=8,'mlp'=4] {'seq'}, use_global_device_ids=true, to_apply=%region_52.53 | all-reduce | flops 524 | bytes 4192 | tf_op jit(solution)/shard_map/psum | solution.py:557
  1024.6 192.5 %all-reduce.5.cloned.1.call-done = (f32[1,3,512,128]{2,3,1,0:T(8,128)}, f32[1,3,512,128]{2,3,1,0:T(8,128)}, f32[1,128,512]{2,1,0:T(8,128)}, f32[1,128,512]{2,1,0...) async-done(((f32[1,3,512,128]{2,3,1,0:T(8,128)}, f32[1,3,512,128]{2,3,1,0:T(8,128)}, ...) | async-done | bytes 6291472 | tf_op jit(solution)/shard_map/psum | solution.py:557
  (790 shorter events, 455.8 us)
Async XLA Ops:
  7.2 194.1 %reduce-scatter.25.cloned.1.call-start = ((), (), s32[]{:S(2)}) async-start(), calls=%async_computation.8 | async-start | bytes 655360
  29.6 142.7 %collective-permute-start = (bf16[30,128]{0,1:T(8,128)(2,1)}, bf16[30,128]{0,1:T(8,128)(2,1)}, u32[]{:S(2)}, u32[]{:S(2)}) collective-permute-start(bf16[30,128]{0,1:T(8,128)(2,1)} %get-tuple-element.1198), channel_id=1, source_target_pairs={{0,4},{4,8},{8,12},{12,16},{16,20},{20,24},{24,28},{1,5},{5,9},{9,... | collective-permute-start | bytes 23048 | tf_op jit(solution)/shard_map/ppermute | solution.py:21
  34.2 132.0 %collective-permute-start.1 = (bf16[30]{0:T(256)(128)(2,1)}, bf16[30]{0:T(256)(128)(2,1)}, u32[]{:S(2)}, u32[]{:S(2)}) collective-permute-start(bf16[30]{0:T(256)(128)(2,1)} %slice.355), channel_id=1, source_target_pairs={{0,4},{4,8},{8,12},{12,16},{16,20},{20,24},{24,28},{1,5},{5,9},{9,... | collective-permute-start | bytes 188 | tf_op jit(solution)/shard_map/ppermute | solution.py:21
  37.7 130.6 %collective-permute-start.2 = (bf16[30,128]{0,1:T(8,128)(2,1)}, bf16[30,128]{0,1:T(8,128)(2,1)}, u32[]{:S(2)}, u32[]{:S(2)}) collective-permute-start(bf16[30,128]{0,1:T(8,128)(2,1)} %get-tuple-element.1197), channel_id=1, source_target_pairs={{0,4},{4,8},{8,12},{12,16},{16,20},{20,24},{24,28},{1,5},{5,9},{9,... | collective-permute-start | bytes 23048 | tf_op jit(solution)/shard_map/ppermute | solution.py:21
  41.1 131.2 %copy-start.7 = (bf16[1,512,128]{1,2,0:T(8,128)(2,1)}, bf16[1,512,128]{1,2,0:T(8,128)(2,1)S(1)}, u32[]{:S(2)}) copy-start(bf16[1,512,128]{1,2,0:T(8,128)(2,1)S(1)} %get-tuple-element.1199) | copy-start | bytes 393220
  41.1 131.2 %copy-start.12 = (bf16[1,512,128]{1,2,0:T(8,128)(2,1)}, bf16[1,512,128]{1,2,0:T(8,128)(2,1)S(1)}, u32[]{:S(2)}) copy-start(bf16[1,512,128]{1,2,0:T(8,128)(2,1)S(1)} %get-tuple-element.1200) | copy-start | bytes 393220
  41.2 134.3 %copy-start.21 = (bf16[1,512,128]{1,2,0:T(8,128)(2,1)}, bf16[1,512,128]{1,2,0:T(8,128)(2,1)S(1)}, u32[]{:S(2)}) copy-start(bf16[1,512,128]{1,2,0:T(8,128)(2,1)S(1)} %get-tuple-element.1201) | copy-start | bytes 393220
  41.5 125.5 %copy-start.123 = (s32[512]{0:T(512)}, s32[512]{0:T(512)S(1)}, u32[]{:S(2)}) copy-start(s32[512]{0:T(512)S(1)} %select_reduce_fusion) | copy-start | bytes 6148
  42.7 115.1 %copy-start.186 = (pred[512]{0:T(512)(128)(4,1)}, pred[512]{0:T(512)(128)(4,1)S(1)}, u32[]{:S(2)}) copy-start(pred[512]{0:T(512)(128)(4,1)S(1)} %get-tuple-element.1180) | copy-start | bytes 1540
  182.2 63.8 %reduce-scatter.27.cloned.1.call-start = ((), (), s32[]{:S(2)}) async-start(), calls=%async_computation.9 | async-start | bytes 655360
  223.9 218.0 %reduce-scatter.29.cloned.1.call-start = ((), (), s32[]{:S(2)}) async-start(), calls=%async_computation.10 | async-start | bytes 655360
  265.7 146.0 %copy-start.9 = (bf16[1,512,128]{1,2,0:T(8,128)(2,1)}, bf16[1,512,128]{1,2,0:T(8,128)(2,1)S(1)}, u32[]{:S(2)}) copy-start(bf16[1,512,128]{1,2,0:T(8,128)(2,1)S(1)} %get-tuple-element.1194) | copy-start | bytes 393220
  396.8 133.6 %copy-start.120 = (f32[512,2]{0,1:T(2,128)}, f32[512,2]{0,1:T(2,128)S(1)}, u32[]{:S(2)}) copy-start(f32[512,2]{0,1:T(2,128)S(1)} %get-tuple-element.1174) | copy-start | bytes 12292
  397.4 10.1 collective-permute-start.4
  405.4 6.3 collective-permute-start.3
  422.5 78.6 %reduce-scatter.33.cloned.1.call-start = ((), (), s32[]{:S(2)}) async-start(), calls=%async_computation.12 | async-start | bytes 655360
  479.0 230.1 %reduce-scatter.31.cloned.1.call-start = ((), (), s32[]{:S(2)}) async-start(), calls=%async_computation.11 | async-start | bytes 655360
  487.5 243.1 %reduce-scatter.35.cloned.1.call-start = ((), (), s32[]{:S(2)}) async-start(), calls=%async_computation.13 | async-start | bytes 655360
  676.7 16.4 %collective-permute-start.6 = (f32[30,2,64]{0,2,1:T(8,128)}, f32[30,2,64]{0,2,1:T(8,128)}, u32[]{:S(2)}, u32[]{:S(2)}) collective-permute-start(f32[30,2,64]{0,2,1:T(8,128)} %slice.407), channel_id=1, source_target_pairs={{4,0},{8,4},{12,8},{16,12},{20,16},{24,20},{28,24},{5,1},{9,5},{13... | collective-permute-start | bytes 46088 | tf_op jit(solution)/shard_map/ppermute | solution.py:21
  681.4 16.1 %collective-permute-start.5 = (f32[30,2,64]{0,2,1:T(8,128)}, f32[30,2,64]{0,2,1:T(8,128)}, u32[]{:S(2)}, u32[]{:S(2)}) collective-permute-start(f32[30,2,64]{0,2,1:T(8,128)} %slice.404), channel_id=1, source_target_pairs={{4,0},{8,4},{12,8},{16,12},{20,16},{24,20},{28,24},{5,1},{9,5},{13... | collective-permute-start | bytes 46088 | tf_op jit(solution)/shard_map/ppermute | solution.py:21
  708.0 70.1 %reduce-scatter.37.cloned.1.call-start = ((), (), s32[]{:S(2)}) async-start(), calls=%async_computation.14 | async-start | bytes 655360
  756.0 237.3 %reduce-scatter.39.cloned.1.call-start = ((), (), s32[]{:S(2)}) async-start(), calls=%async_computation.15 | async-start | bytes 655360
  908.3 44.4 %copy-start.125 = (s32[512]{0:T(512)S(1)}, s32[512]{0:T(512)}, u32[]{:S(2)}) copy-start(s32[512]{0:T(512)} %copy-done.123) | copy-start | bytes 6148
  950.2 15.2 %collective-permute-start.8 = (f32[30,2,64]{0,2,1:T(8,128)}, f32[30,2,64]{0,2,1:T(8,128)}, u32[]{:S(2)}, u32[]{:S(2)}) collective-permute-start(f32[30,2,64]{0,2,1:T(8,128)} %slice.413), channel_id=1, source_target_pairs={{4,0},{8,4},{12,8},{16,12},{20,16},{24,20},{28,24},{5,1},{9,5},{13... | collective-permute-start | bytes 46088 | tf_op jit(solution)/shard_map/ppermute | solution.py:21
  954.8 12.5 %collective-permute-start.7 = (f32[30,2,64]{0,2,1:T(8,128)}, f32[30,2,64]{0,2,1:T(8,128)}, u32[]{:S(2)}, u32[]{:S(2)}) collective-permute-start(f32[30,2,64]{0,2,1:T(8,128)} %slice.410), channel_id=1, source_target_pairs={{4,0},{8,4},{12,8},{16,12},{20,16},{24,20},{28,24},{5,1},{9,5},{13... | collective-permute-start | bytes 46088 | tf_op jit(solution)/shard_map/ppermute | solution.py:21
  970.7 246.4 %all-reduce.5.cloned.1.call-start = ((), (), s32[]{:S(2)}) async-start(), calls=%async_computation.16 | async-start | bytes 12582912 | tf_op jit(solution)/shard_map/psum | solution.py:557
  979.9 43.6 %copy-start.28 = (bf16[512,128]{1,0:T(8,128)(2,1)S(1)}, bf16[512,128]{1,0:T(8,128)(2,1)}, u32[]{:S(2)}) copy-start(bf16[512,128]{1,0:T(8,128)(2,1)} %copy-done.27) | copy-start | bytes 393220
  979.9 43.6 %copy-start.53 = (f32[512,128]{1,0:T(8,128)S(1)}, f32[512,128]{1,0:T(8,128)}, u32[]{:S(2)}) copy-start(f32[512,128]{1,0:T(8,128)} %get-tuple-element.1171) | copy-start | bytes 786436
  979.9 43.6 %copy-start.56 = (bf16[512,128]{1,0:T(8,128)(2,1)S(1)}, bf16[512,128]{1,0:T(8,128)(2,1)}, u32[]{:S(2)}) copy-start(bf16[512,128]{1,0:T(8,128)(2,1)} %copy.240) | copy-start | bytes 393220
  980.0 43.6 %copy-start.137 = (f32[512]{0:T(512)S(1)}, f32[512]{0:T(512)}, u32[]{:S(2)}) copy-start(f32[512]{0:T(512)} %copy-done.135) | copy-start | bytes 6148
  980.0 43.6 %copy-start.150 = (f32[512]{0:T(512)S(1)}, f32[512]{0:T(512)}, u32[]{:S(2)}) copy-start(f32[512]{0:T(512)} %copy-done.149) | copy-start | bytes 6148
  980.0 43.6 %copy-start.160 = (f32[128]{0:T(128)S(1)}, f32[128]{0:T(128)}, u32[]{:S(2)}) copy-start(f32[128]{0:T(128)} %get-tuple-element.1207) | copy-start | bytes 1540
  (188 other events, 1122.1 us)
Sparse Core Ops, SparseCore 0:
  182.3 18.8 reduce-scatter.24
  224.0 21.9 reduce-scatter.26
  422.6 19.1 reduce-scatter.28
  479.2 21.9 reduce-scatter.32
  503.5 21.6 reduce-scatter.30
  708.1 22.3 reduce-scatter.34
  756.1 21.9 reduce-scatter.36
  970.8 22.3 reduce-scatter.38
  999.7 217.3 all-reduce.4
where the time goes:
time: 1240 us; the launch traced here: 1230 us
  blocking collectives  500 us (40%)
  waiting for transfers between devices  303 us (24%)
  matrix products  158 us (13%)
  other arithmetic  112 us (9%)
  local copies, waits for them, and re-layouts  100 us (8%)
  starting transfers between devices  21.3 us (2%)
  loops' own time  21.3 us (2%)
  between operations  17 us (1%)
    psum x1, waiting for transfers between devices, per_device(): lax.psum((weight_terms[0], weight_terms[1], weight_terms[2], weight_terms...  193 us
    all_gather x6, blocking collectives, carried_in(): lax.all_gather(part.astype(kind), axis)  173 us
    all_gather x6, blocking collectives, prefix(): lax.all_gather(part.astype(kind), axis)  166 us
    unnamed x17, waiting for transfers between devices  111 us
    select_n x32, other arithmetic, carried_lap(): return jax.tree.map(lambda a, b: jnp.where(reached, a, b), new, before)  44.2 us
    unnamed x426, local copies, waits for them, and re-layouts  44.2 us
    all_gather x4, blocking collectives, gather_rows(): return lax.all_gather(normed_part, 'mlp', axis=1, tiled=True)  39.6 us
    all_gather x4, blocking collectives, gather_grads(): return lax.all_gather(grad_part, 'mlp', axis=1, tiled=True)  29.6 us
  transfers between devices with their start and end apart: 18, of which 8 were waited for; matrix products, arithmetic and copies ran while one was open for 15% of the time, Pallas kernels for 0%

commit v1 on v0

v1 whole, which is shorter than its diff:
```python
import functools
import math

import jax
import jax.numpy as jnp
from jax import lax
from jax.experimental import pallas as pl
from jax.experimental.pallas import tpu as pltpu
from jax.sharding import PartitionSpec as P

HD = 64
D = 512
BAND = 30
LAYERS = 2
HALO = 32
TILE = 64
LANES = 128
STATE = 144
AXES = ("seq", "mlp")

epsilon = 1e-05
masked_score = -1e30
score_scale = 1.0 / math.sqrt(HD)
far_scale = 1.0 / math.sqrt(HD)
f32 = jnp.float32
bf16 = jnp.bfloat16

VM = pl.BlockSpec(memory_space=pltpu.VMEM)
SM = pl.BlockSpec(memory_space=pltpu.SMEM)


def dot(x, y):
    return jnp.dot(x, y, preferred_element_type=f32)


def dot_nt(x, y):
    return lax.dot_general(x, y, (((1,), (1,)), ((), ())), preferred_element_type=f32)


def dot_tn(x, y):
    return lax.dot_general(x, y, (((0,), (0,)), ((), ())), preferred_element_type=f32)


def low_lanes(rows):
    return lax.broadcasted_iota(jnp.int32, (rows, LANES), 1) < HD


def split_heads(x):
    low = low_lanes(x.shape[0])
    zero = jnp.zeros_like(x)
    return jnp.concatenate([jnp.where(low, x, zero), jnp.where(low, zero, x)], axis=0)


def merge_heads(y):
    rows = y.shape[0] // 2
    return jnp.where(low_lanes(rows), y[:rows], y[rows:])


def head_sum(x):
    row = lax.broadcasted_iota(jnp.int32, (LANES, LANES), 0) < HD
    ones = jnp.where(row == low_lanes(LANES), 1.0, 0.0).astype(bf16)
    high = x.astype(bf16)
    rest = (x - high.astype(f32)).astype(bf16)
    return dot(high, ones) + dot(rest, ones)


def kernel_maps(x):
    return (
        jnp.where(x > 0, x + 1.0, jnp.exp(jnp.minimum(x, 0.0))).astype(bf16),
        jnp.tanh(x).astype(bf16),
    )


def maps_back(x, d_one, d_two):
    tanh = jnp.tanh(x)
    return jnp.where(x > 0, 1.0, jnp.exp(jnp.minimum(x, 0.0))) * d_one + (1.0 - tanh * tanh) * d_two


def put_state(ref, quarter, one, two, total):
    row = lax.broadcasted_iota(jnp.int32, (STATE - 2 * HD, LANES), 0)
    low = low_lanes(HD)
    ref[quarter, 0:HD, :] = jnp.where(low, one[:HD], one[HD:]).astype(bf16)
    ref[quarter, HD : 2 * HD, :] = jnp.where(low, two[:HD], two[HD:]).astype(bf16)
    ref[quarter, 2 * HD : STATE, :] = jnp.where(row == 0, total, 0.0).astype(bf16)


def get_state(ref, quarter):
    one = split_heads(ref[quarter, 0:HD, :])
    two = split_heads(ref[quarter, HD : 2 * HD, :])
    total = ref[quarter, 2 * HD : STATE, :].astype(f32)[0:1]
    return one, two, total


def norm_scale(hidden):
    return lax.rsqrt(jnp.sum(hidden * hidden, axis=1, keepdims=True) * (1.0 / D) + epsilon)


def norm_back(hidden, gain, grad):
    scale = norm_scale(hidden)
    gained = grad * gain
    inner = jnp.sum(gained * hidden, axis=1, keepdims=True) * (1.0 / D)
    back = scale * gained - hidden * (scale * scale * scale * inner)
    return back, jnp.sum(grad * hidden * scale, axis=0, keepdims=True)


def extend(halo, rows):
    return jnp.concatenate([halo, rows, jnp.zeros((HALO, LANES), bf16)], axis=0)


def qkv_kernel(first, place, *refs):
    if first:
        inputs, gain, own, other, tail, hidden_out, normed_out, qkv_out, state_out, halo_out = refs
        hidden = inputs[...].astype(f32)
    else:
        base, part_a, part_b, gain, own, other, tail, hidden_out, normed_out, qkv_out, state_out, halo_out = refs
        hidden = base[...] + (part_a[...].astype(f32) + part_b[...].astype(f32))
    hidden_out[...] = hidden
    normed = (hidden * norm_scale(hidden) * gain[...]).astype(bf16)
    normed_out[...] = normed
    rows = hidden.shape[0]
    found = []
    for kind in range(3):
        weight = jnp.concatenate([own[kind], other[kind]], axis=1)
        found.append(dot(normed, weight).astype(bf16))
        qkv_out[kind] = found[kind]
    for pair in range(2):
        quarter = place[0] if pair == 0 else 1 - place[0]
        lanes = slice(pair * LANES, (pair + 1) * LANES)
        keys, values = found[1][:, lanes], found[2][:, lanes]
        one, two = kernel_maps(keys.astype(f32))
        one, two = one * tail[...], two * tail[...]
        put_state(
            state_out,
            quarter,
            dot_tn(one, values),
            dot_tn(two, values),
            jnp.sum(one.astype(f32), axis=0, keepdims=True),
        )
        halo_out[quarter, 0] = keys[rows - HALO :]
        halo_out[quarter, 1] = values[rows - HALO :]


def local_kernel(place, qkv, halo, causal, band, near_out, one_out, two_out, sums_out):
    rows = qkv.shape[1]
    masks = jnp.concatenate([causal[...], causal[...]], axis=0)
    for pair in range(2):
        quarter = place[0] if pair == 0 else 1 - place[0]
        lanes = slice(pair * LANES, (pair + 1) * LANES)
        queries, keys, values = qkv[0, :, lanes], qkv[1, :, lanes], qkv[2, :, lanes]
        maps_q, maps_k = kernel_maps(queries.astype(f32)), kernel_maps(keys.astype(f32))
        for query, key, out in ((maps_q[0], maps_k[0], one_out), (maps_q[1], maps_k[1], two_out)):
            attn = dot_nt(split_heads(query), key).astype(bf16) * masks
            out[:, lanes] = merge_heads(dot(attn, values))
        sums_out[:, lanes] = dot(causal[...], maps_k[0])
        ext_keys = extend(halo[quarter, 0], keys)
        ext_values = extend(halo[quarter, 1], values)
        for tile in range(rows // TILE):
            at = slice(tile * TILE, (tile + 1) * TILE)
            window = slice(tile * TILE, tile * TILE + LANES)
            allowed = jnp.concatenate([band[at], band[at]], axis=0)
            scores = dot_nt(split_heads(queries[at]), ext_keys[window]) * score_scale + allowed
            weights = jnp.exp(scores - jnp.max(scores, axis=1, keepdims=True))
            weights = weights / jnp.sum(weights, axis=1, keepdims=True)
            near_out[at, lanes] = merge_heads(dot(weights.astype(bf16), ext_values[window]))


def mix_kernel(
    place, qkv, near, one, two, sums, carried, state, blend, own, other,
    mixed_out, far_one_out, far_two_out, root_out, prefix_out, part_out,
):
    mixed = []
    for pair in range(2):
        quarter = place[0] if pair == 0 else 1 - place[0]
        lanes = slice(pair * LANES, (pair + 1) * LANES)
        query_one, query_two = kernel_maps(qkv[0, :, lanes].astype(f32))
        state_one, state_two, total = get_state(state, quarter)
        num_one = one[:, lanes] + carried[...] * dot(query_one, state_one)
        num_two = two[:, lanes] + carried[...] * dot(query_two, state_two)
        prefix = sums[:, lanes] + carried[...] * total
        zeta = head_sum(query_one.astype(f32) * prefix)
        root = lax.rsqrt(zeta + 1.0)
        far_one = num_one * root * far_scale
        far_two = num_two * root
        far_one_out[:, lanes] = far_one
        far_two_out[:, lanes] = far_two
        root_out[:, lanes] = root
        prefix_out[:, lanes] = prefix
        mixed.append(
            (
                blend[0:1, lanes] * near[:, lanes]
                + blend[1:2, lanes] * far_one
                + blend[2:3, lanes] * far_two
            ).astype(bf16)
        )
        mixed_out[:, lanes] = mixed[pair]
    weight = jnp.concatenate([own[...], other[...]], axis=0)
    part_out[...] = dot(jnp.concatenate(mixed, axis=1), weight).astype(bf16)


def ffn_kernel(
    base, part_a, part_b, gain, up_own, up_other, down_own, down_other,
    middle_out, normed_out, pre_own_out, pre_other_out, act_own_out, act_other_out, part_out,
):
    middle = base[...] + (part_a[...].astype(f32) + part_b[...].astype(f32))
    middle_out[...] = middle
    normed = (middle * norm_scale(middle) * gain[...]).astype(bf16)
    normed_out[...] = normed
    total = None
    for up, down, pre_out, act_out in (
        (up_own, down_own, pre_own_out, act_own_out),
        (up_other, down_other, pre_other_out, act_other_out),
    ):
        pre = dot(normed, up[...])
        pre_out[...] = pre
        inner = jnp.tanh(math.sqrt(2.0 / math.pi) * (pre + 0.044715 * pre * pre * pre))
        act = (0.5 * pre * (1.0 + inner)).astype(bf16)
        act_out[...] = act
        product = dot(act, down[...])
        total = product if total is None else total + product
    part_out[...] = total.astype(bf16)


def gelu_slope(pre):
    c = math.sqrt(2.0 / math.pi)
    inner = jnp.tanh(c * (pre + 0.044715 * pre * pre * pre))
    return 0.5 * (1.0 + inner) + 0.5 * pre * (1.0 - inner * inner) * (c * (1.0 + 3 * 0.044715 * pre * pre))


def ffn_back_kernel(first, *refs):
    if first:
        grad_in, up_own, up_other, down_own, down_other, pre_own, pre_other = refs[:7]
        resid_out, rows_out, d_up_own_out, d_up_other_out, part_out = refs[7:]
        resid = grad_in[...].astype(f32)
    else:
        (base, part_a, part_b, hidden, gain, up_own, up_other, down_own, down_other, pre_own, pre_other) = refs[:11]
        resid_out, rows_out, d_up_own_out, d_up_other_out, part_out, gain_out = refs[11:]
        back, gain_out[...] = norm_back(
            hidden[...], gain[...], part_a[...].astype(f32) + part_b[...].astype(f32)
        )
        resid = base[...] + back
    resid_out[...] = resid
    rows = resid.astype(bf16)
    rows_out[...] = rows
    total = None
    for up, down, pre, out in (
        (up_own, down_own, pre_own, d_up_own_out),
        (up_other, down_other, pre_other, d_up_other_out),
    ):
        d_up = (gelu_slope(pre[...]) * dot_nt(rows, down[...])).astype(bf16)
        out[...] = d_up
        product = dot_nt(d_up, up[...])
        total = product if total is None else total + product
    part_out[...] = total.astype(bf16)


def mix_back_kernel(
    place, base, part_a, part_b, middle, gain, own, other, qkv, far_one, far_two, root, carried, blend,
    resid_out, rows_out, mixed_out, gain_out, num_one_out, num_two_out, zeta_out, state_out, blend_out,
):
    back, gain_out[...] = norm_back(
        middle[...], gain[...], part_a[...].astype(f32) + part_b[...].astype(f32)
    )
    resid = base[...] + back
    resid_out[...] = resid
    rows = resid.astype(bf16)
    rows_out[...] = rows
    weight = jnp.concatenate([own[...], other[...]], axis=0)
    d_mixed = dot_nt(rows, weight).astype(bf16)
    mixed_out[...] = d_mixed
    for pair in range(2):
        quarter = place[0] if pair == 0 else 1 - place[0]
        lanes = slice(pair * LANES, (pair + 1) * LANES)
        grad = d_mixed[:, lanes].astype(f32)
        scale = root[:, lanes]
        dot_one = grad * far_one[:, lanes]
        dot_two = grad * far_two[:, lanes]
        blend_one, blend_two = blend[1:2, lanes], blend[2:3, lanes]
        blend_out[0:1, lanes] = jnp.sum(dot_one, axis=0, keepdims=True)
        blend_out[1:2, lanes] = jnp.sum(dot_two, axis=0, keepdims=True)
        num_one = (grad * (blend_one * far_scale) * scale).astype(bf16)
        num_two = (grad * blend_two * scale).astype(bf16)
        d_zeta = head_sum(blend_one * dot_one + blend_two * dot_two) * (-0.5 * scale * scale)
        num_one_out[:, lanes] = num_one
        num_two_out[:, lanes] = num_two
        zeta_out[:, lanes] = d_zeta
        query_one, query_two = kernel_maps(qkv[0, :, lanes].astype(f32))
        reach = carried[...].astype(bf16)
        put_state(
            state_out,
            quarter,
            dot_tn(query_one * reach, num_one),
            dot_tn(query_two * reach, num_two),
            jnp.sum(carried[...] * d_zeta * query_one.astype(f32), axis=0, keepdims=True),
        )


def local_back_kernel(
    place, qkv, halo, causal, causal_t, band, carried, state, prefix, d_mixed, num_one, num_two, d_zeta, blend,
    dq_out, dk_one_out, dk_two_out, dk_near_out, dv_out, halo_out, blend_out, near_k, near_v,
):
    rows = qkv.shape[1]
    masks = jnp.concatenate([causal[...], causal[...]], axis=0)
    masks_t = jnp.concatenate([causal_t[...], causal_t[...]], axis=1)
    row_low = lax.broadcasted_iota(jnp.int32, (2 * TILE, 1), 0) < TILE
    for pair in range(2):
        quarter = place[0] if pair == 0 else 1 - place[0]
        lanes = slice(pair * LANES, (pair + 1) * LANES)
        queries, keys, values = qkv[0, :, lanes], qkv[1, :, lanes], qkv[2, :, lanes]
        grads = d_mixed[:, lanes]
        state_one, state_two, unused_total = get_state(state, quarter)
        query_one, query_two = kernel_maps(queries.astype(f32))
        key_one, key_two = kernel_maps(keys.astype(f32))
        d_values = None
        d_queries = []
        for query, key, num, square, out in (
            (query_one, key_one, num_one[:, lanes], state_one, dk_one_out),
            (query_two, key_two, num_two[:, lanes], state_two, dk_two_out),
        ):
            query_split, num_split = split_heads(query), split_heads(num)
            attn_t = dot_nt(key, query_split).astype(bf16) * masks_t
            grad = dot_nt(num_split, values).astype(bf16) * masks
            grad_t = dot_nt(values, num_split).astype(bf16) * masks_t
            product = dot(attn_t, num_split)
            d_values = product if d_values is None else d_values + product
            d_queries.append(merge_heads(dot(grad, key)) + carried[...] * dot_nt(num, square))
            out[:, lanes] = dot(grad_t, query_split)
        zeta = d_zeta[:, lanes]
        d_queries[0] += zeta * prefix[:, lanes]
        dk_one_out[:, lanes] += dot(causal_t[...], (zeta * query_one.astype(f32)).astype(bf16))

        ext_keys = extend(halo[quarter, 0], keys)
        ext_values = extend(halo[quarter, 1], values)
        near_k[...] = jnp.zeros_like(near_k)
        near_v[...] = jnp.zeros_like(near_v)
        blend_low, blend_high = blend[0:1, pair * LANES : pair * LANES + 1], blend[0:1, pair * LANES + HD : pair * LANES + HD + 1]
        blend_rows = jnp.where(row_low, blend_low, blend_high)
        sums = None
        dq_near = []
        for tile in range(rows // TILE):
            at = slice(tile * TILE, (tile + 1) * TILE)
            window = slice(tile * TILE, tile * TILE + LANES)
            allowed = jnp.concatenate([band[at], band[at]], axis=0)
            query_split, grad_split = split_heads(queries[at]), split_heads(grads[at])
            scores = dot_nt(query_split, ext_keys[window]) * score_scale + allowed
            probs = jnp.exp(scores - jnp.max(scores, axis=1, keepdims=True))
            probs = probs / jnp.sum(probs, axis=1, keepdims=True)
            d_probs = dot_nt(grad_split, ext_values[window])
            inner = jnp.sum(probs * d_probs, axis=1, keepdims=True)
            sums = inner if sums is None else sums + inner
            d_scores = (probs * (d_probs - inner) * blend_rows).astype(bf16)
            dq_near.append(merge_heads(dot(d_scores, ext_keys[window])))
            near_k[window] += dot_tn(d_scores, query_split)
            near_v[window] += dot_tn(probs.astype(bf16), grad_split)
        sum_low = jnp.sum(sums[:TILE], axis=0, keepdims=True)
        sum_high = jnp.sum(sums[TILE:], axis=0, keepdims=True)
        blend_out[0:1, lanes] = jnp.where(low_lanes(1), sum_low, sum_high) * (1.0 / HD)
        back = maps_back(queries.astype(f32), d_queries[0], d_queries[1])
        dq_out[:, lanes] = (back + score_scale * jnp.concatenate(dq_near, axis=0)).astype(bf16)
        dk_near_out[:, lanes] = score_scale * near_k[HALO : HALO + rows]
        dv_out[:, lanes] = d_values + blend[0:1, lanes] * near_v[HALO : HALO + rows]
        halo_out[quarter, 0] = (score_scale * near_k[0:HALO]).astype(bf16)
        halo_out[quarter, 1] = (blend[0:1, lanes] * near_v[0:HALO]).astype(bf16)


def qkv_back_kernel(
    place, qkv, dq, dk_one, dk_two, dk_near, dv, tail, state, halo, own, other, d_qkv_out, part_out
):
    rows = qkv.shape[1]
    empty = jnp.zeros((rows - HALO, LANES), f32)
    for pair in range(2):
        quarter = place[0] if pair == 0 else 1 - place[0]
        lanes = slice(pair * LANES, (pair + 1) * LANES)
        keys, values = qkv[1, :, lanes], qkv[2, :, lanes]
        key_one, key_two = kernel_maps(keys.astype(f32))
        state_one, state_two, total = get_state(state, quarter)
        weight = tail[...].astype(f32)
        d_one = dk_one[:, lanes] + weight * (dot_nt(values, state_one) + total)
        d_two = dk_two[:, lanes] + weight * dot_nt(values, state_two)
        halo_k = jnp.concatenate([empty, halo[quarter, 0].astype(f32)], axis=0)
        halo_v = jnp.concatenate([empty, halo[quarter, 1].astype(f32)], axis=0)
        d_qkv_out[1, :, lanes] = (
            maps_back(keys.astype(f32), d_one, d_two) + dk_near[:, lanes] + halo_k
        ).astype(bf16)
        d_qkv_out[2, :, lanes] = (
            dv[:, lanes] + weight * (dot(key_one, state_one) + dot(key_two, state_two)) + halo_v
        ).astype(bf16)
    d_qkv_out[0] = dq[...]
    total = None
    for kind in range(3):
        weight = jnp.concatenate([own[kind], other[kind]], axis=1)
        product = dot_nt(d_qkv_out[kind], weight)
        total = product if total is None else total + product
    part_out[...] = total.astype(bf16)


def end_kernel(base, part_a, part_b, hidden, gain, out, gain_out):
    back, gain_out[...] = norm_back(
        hidden[...], gain[...], part_a[...].astype(f32) + part_b[...].astype(f32)
    )
    out[...] = (base[...] + back).astype(bf16)


def call(body, outs, operands, scalars=0, scratch=(), flops=0):
    return pl.pallas_call(
        body,
        out_shape=tuple(jax.ShapeDtypeStruct(shape, kind) for shape, kind in outs),
        in_specs=[SM] * scalars + [VM] * (len(operands) - scalars),
        out_specs=tuple(VM for _ in outs),
        scratch_shapes=scratch,
        compiler_params=pltpu.CompilerParams(vmem_limit_bytes=24 * 2**20),
    )(*operands)


def core_swap(value):
    count = lax.axis_size("mlp")
    return lax.ppermute(value, "mlp", [(i, i ^ 1) for i in range(count)])


def far_swap(value):
    count = lax.axis_size("mlp")
    return lax.ppermute(value, "mlp", [(i, i ^ 2) for i in range(count)])


def chunk_move(value, target):
    shards, parts = lax.axis_size("seq"), lax.axis_size("mlp")
    pairs = []
    for chunk in range(2 * shards):
        goal = target(chunk)
        if goal is None or not 0 <= goal < 2 * shards:
            continue
        for core in range(2):
            pairs.append(
                ((chunk // 2) * parts + (chunk % 2) * 2 + core, (goal // 2) * parts + (goal % 2) * 2 + core)
            )
    return lax.ppermute(value, AXES, pairs)


def item_start(lengths, positions):
    count = lengths.shape[0]
    order = jnp.arange(count)
    ends = jnp.sum(jnp.where(order[None, :] <= order[:, None], lengths[None, :], 0), axis=1)
    picked = jnp.where(ends[None, :] <= positions[:, None], lengths[None, :], 0)
    return jnp.sum(picked, axis=1)


def scan_plan(chunks):
    stages, size = [], 1
    while size < chunks:
        ways = min(4, chunks // size)
        stages.append((size, ways, size * ways >= chunks))
        size *= ways
    return stages


def scan_weights(lengths, chunk, chunks, rows, reverse):
    def inner(index):
        return index * rows + (0 if reverse else rows - 1)

    first, second = [], []
    for size, ways, last in scan_plan(chunks):
        member = (chunk // size) % ways
        base = chunk - member * size - chunk % size
        end = base + (0 if reverse else ways * size - 1)
        for step in range(ways):
            if last:
                other = member + step if reverse else member - step
            else:
                other = member ^ step
            block = base + other * size + (0 if reverse else size - 1)
            before = (other > member) if reverse else (other < member)
            before = before & (other >= 0) & (other < ways)
            edge = chunk * rows + (rows - 1 if reverse else 0)
            first.append((jnp.where(before, inner(block), -1), edge, before))
            second.append((inner(block), inner(end), jnp.bool_(True)))
    wanted = first + second
    left = item_start(lengths, jnp.stack([jnp.int32(w[0]) for w in wanted]))
    right = item_start(lengths, jnp.stack([jnp.int32(w[1]) for w in wanted]))
    flags = (left == right) & jnp.stack([w[2] for w in wanted])
    flags = flags.astype(f32)
    return flags[: len(first)], flags[len(first) :]


def scan(value, weights, chunks, reverse):
    to_mine, to_total = weights
    found, at = 0.0, 0
    for size, ways, last in scan_plan(chunks):
        got = [value]
        for step in range(1, ways):
            if last:

                def target(chunk, step=step):
                    member = (chunk // size) % ways + (-step if reverse else step)
                    return chunk + (-step if reverse else step) * size if 0 <= member < ways else None

            else:

                def target(chunk, step=step):
                    member = (chunk // size) % ways
                    return chunk + ((member ^ step) - member) * size

            got.append(chunk_move(value, target))
        for step in range(1, ways):
            found = found + to_mine[at + step] * got[step].astype(f32)
        if not last:
            value = sum(to_total[at + step] * got[step].astype(f32) for step in range(ways)).astype(bf16)
        at += ways
    return found.astype(bf16)


def three_parts(value):
    high = value.astype(bf16)
    rest = value - high.astype(f32)
    middle = rest.astype(bf16)
    return jnp.concatenate([high, middle, (rest - middle.astype(f32)).astype(bf16)], axis=0)


def by_place(flag, mine, other):
    return jnp.where(flag == 0, mine, other), jnp.where(flag == 0, other, mine)


def take_rows(value, half, core, more):
    rows = value.shape[0] // 2
    mine = lax.dynamic_slice_in_dim(value, half * rows, rows, 0)
    theirs = lax.dynamic_slice_in_dim(value, (1 - half) * rows, rows, 0)
    if more is not None:
        mine, theirs = jnp.concatenate([mine, more]), jnp.concatenate([theirs, more])
    got = far_swap(theirs)
    pair = jnp.stack(by_place(half, mine, got))
    even, odd = by_place(core, pair, core_swap(pair))
    whole = jnp.concatenate([even[0], odd[0], even[1], odd[1]], axis=1)
    return whole[:rows], whole[rows:], got[rows:]


def give_rows(whole, half, core):
    mine = lax.dynamic_slice_in_dim(whole, (2 * half + core) * LANES, LANES, 1)
    theirs = lax.dynamic_slice_in_dim(whole, (2 * (1 - half) + core) * LANES, LANES, 1)
    return jnp.concatenate(by_place(half, mine, far_swap(theirs)))


def per_device(inputs, lengths, valid, norm_attn, w_qkv, blend, w_out, norm_ffn, w_up, w_down, grad_out):
    shards, parts = lax.axis_size("seq"), lax.axis_size("mlp")
    shard, part = lax.axis_index("seq"), lax.axis_index("mlp")
    half, core = part // 2, part % 2
    rows = inputs.shape[0] // 2
    chunks = 2 * shards
    chunk = shard * 2 + half
    first_row = chunk * rows
    width = inputs.shape[1]
    place = jnp.reshape(half, (1,)).astype(jnp.int32)

    blend_lanes = jnp.repeat(blend, HD, axis=2).reshape(LAYERS * 3, width)
    small = jnp.concatenate([norm_attn, norm_ffn, blend_lanes], axis=0)
    small = jnp.concatenate([small, jnp.zeros((16 - small.shape[0], width), f32)], axis=0)
    whole, gains, far_small = take_rows(inputs, half, core, three_parts(small))

    def joined(value):
        count = value.shape[0] // 3
        value = value.astype(f32)
        return value[:count] + value[count : 2 * count] + value[2 * count :]

    gains, far_small = joined(gains), joined(far_small)
    others = []
    for layer in range(LAYERS):
        others.append(tuple(far_swap(w[layer]) for w in (w_qkv, w_out, w_up, w_down)))
    grad_whole, unused_a, unused_b = take_rows(grad_out, half, core, None)
    gain_attn = [gains[layer : layer + 1] for layer in range(LAYERS)]
    gain_ffn = [gains[LAYERS + layer : LAYERS + layer + 1] for layer in range(LAYERS)]
    blends = [
        jnp.concatenate(
            [blend_lanes[3 * layer : 3 * layer + 3], far_small[2 * LAYERS + 3 * layer : 2 * LAYERS + 3 * layer + 3]],
            axis=1,
        )
        for layer in range(LAYERS)
    ]

    halo_words = lax.ppermute(
        valid[2 * rows - HALO :], "seq", [(source, source + 1) for source in range(shards - 1)]
    )
    halo_words = jnp.where(half == 0, halo_words, valid[rows - HALO : rows])
    own_words = lax.dynamic_slice_in_dim(valid, half * rows, rows, 0)
    starts = item_start(lengths, first_row + jnp.arange(rows, dtype=jnp.int32))
    halo_starts = item_start(lengths, first_row - HALO + jnp.arange(HALO, dtype=jnp.int32))
    ext_starts = jnp.concatenate([halo_starts, starts, jnp.full((HALO,), -1, jnp.int32)])
    ext_valid = jnp.concatenate([halo_words, own_words, jnp.zeros((HALO,), jnp.int32)])
    order = jnp.arange(rows, dtype=jnp.int32)
    same = starts[:, None] == starts[None, :]
    causal = ((order[None, :] <= order[:, None]) & same & (own_words[None, :] == 1)).astype(bf16)
    causal_t = ((order[:, None] <= order[None, :]) & same & (own_words[:, None] == 1)).astype(bf16)
    tiles = rows // TILE
    window_starts = jnp.stack([ext_starts[t * TILE : t * TILE + LANES] for t in range(tiles)])
    window_valid = jnp.stack([ext_valid[t * TILE : t * TILE + LANES] for t in range(tiles)])
    gap = jnp.arange(TILE)[:, None] + HALO - jnp.arange(LANES)[None, :]
    allowed = (
        ((gap >= 0) & (gap <= BAND))[None]
        & (starts.reshape(tiles, TILE, 1) == window_starts[:, None, :])
        & ((window_valid[:, None, :] == 1) | (gap == 0)[None])
    )
    band = jnp.where(allowed, 0.0, masked_score).astype(f32).reshape(rows, LANES)
    carried = jnp.broadcast_to((starts < first_row).astype(f32)[:, None], (rows, LANES))
    tail = jnp.broadcast_to(
        ((starts == starts[rows - 1]) & (own_words == 1)).astype(bf16)[:, None], (rows, LANES)
    )
    ahead = scan_weights(lengths, chunk, chunks, rows, False)
    behind = scan_weights(lengths, chunk, chunks, rows, True)

    wide = 2 * LANES
    hidden_like = ((rows, D), f32)
    low_like = ((rows, D), bf16)
    heads_like = ((rows, wide), f32)
    heads_low = ((rows, wide), bf16)
    qkv_like = ((3, rows, wide), bf16)
    state_like = ((2, STATE, LANES), bf16)
    halo_like = ((2, 2, HALO, LANES), bf16)
    units = w_up.shape[2]
    ffn_like = ((rows, units), f32)
    ffn_low = ((rows, units), bf16)

    saved = []
    base, pieces = whole, ()
    for layer in range(LAYERS):
        far_qkv, far_out, far_up, far_down = others[layer]
        hidden, normed, qkv, state, halo = call(
            functools.partial(qkv_kernel, layer == 0),
            (hidden_like, low_like, qkv_like, state_like, halo_like),
            (place, base, *pieces, gain_attn[layer], w_qkv[layer], far_qkv, tail),
            1,
        )
        halo = chunk_move(halo, lambda c: c + 1)
        near, one, two, sums = call(
            local_kernel, (heads_like,) * 4, (place, qkv, halo, causal, band), 1
        )
        state = scan(state, ahead, chunks, False)
        mixed, far_one, far_two, root, prefix, piece = call(
            mix_kernel,
            (heads_low, heads_like, heads_like, heads_like, heads_like, low_like),
            (place, qkv, near, one, two, sums, carried, state, blends[layer], w_out[layer], far_out),
            1,
        )
        middle, normed_ffn, pre_own, pre_far, act_own, act_far, piece_ffn = call(
            ffn_kernel,
            (hidden_like, low_like, ffn_like, ffn_like, ffn_low, ffn_low, low_like),
            (hidden, piece, core_swap(piece), gain_ffn[layer], w_up[layer], far_up, w_down[layer], far_down),
        )
        saved.append(
            (hidden, normed, qkv, state, halo, mixed, far_one, far_two, root, prefix, middle, normed_ffn,
             pre_own, pre_far, act_own, act_far)
        )
        base, pieces = middle, (piece_ffn, core_swap(piece_ffn))
    result = (base + (pieces[0].astype(f32) + pieces[1].astype(f32))).astype(bf16)
    output = give_rows(result, half, core)

    def weight_grads(left, rights):
        return [
            lax.dot_general(left, right, (((0,), (0,)), ((), ())), preferred_element_type=f32)
            for right in rights
        ]

    def over_chips(own, other):
        got = far_swap(other.astype(bf16))
        return (own + got.astype(f32)).astype(bf16)

    base, pieces = None, None
    d_gain_attn, d_gain_ffn, d_blends = [None] * LAYERS, [None] * LAYERS, [None] * LAYERS
    grads = [None] * LAYERS
    for layer in reversed(range(LAYERS)):
        far_qkv, far_out, far_up, far_down = others[layer]
        (hidden, normed, qkv, state, halo, mixed, far_one, far_two, root, prefix, middle, normed_ffn,
         pre_own, pre_far, act_own, act_far) = saved[layer]
        weights = (w_up[layer], far_up, w_down[layer], far_down, pre_own, pre_far)
        outs = (hidden_like, low_like, ffn_low, ffn_low, low_like)
        if base is None:
            resid, grad_rows, d_up_own, d_up_far, piece = call(
                functools.partial(ffn_back_kernel, True), outs, (grad_whole, *weights)
            )
        else:
            resid, grad_rows, d_up_own, d_up_far, piece, d_gain_attn[layer + 1] = call(
                functools.partial(ffn_back_kernel, False),
                outs + (((1, D), f32),),
                (base, *pieces, saved[layer + 1][0], gain_attn[layer + 1], *weights),
            )
        swapped = core_swap(piece)
        d_down_own, d_down_far = [weight_grads(x, [grad_rows])[0] for x in (act_own, act_far)]
        d_up_own_w, d_up_far_w = weight_grads(normed_ffn, [d_up_own, d_up_far])
        (resid, grad_rows, d_mixed, d_gain_ffn[layer], num_one, num_two, d_zeta, state_back, blend_far) = call(
            mix_back_kernel,
            (hidden_like, low_like, heads_low, ((1, D), f32), heads_low, heads_low, heads_like, state_like,
             ((2, wide), f32)),
            (place, resid, piece, swapped, middle, gain_ffn[layer], w_out[layer], far_out, qkv, far_one, far_two,
             root, carried, blends[layer]),
            1,
        )
        d_out_own, d_out_far = [
            weight_grads(x, [grad_rows])[0] for x in (mixed[:, :LANES], mixed[:, LANES:])
        ]
        ext = HALO + rows + HALO
        dq, dk_one, dk_two, dk_near, dv, halo_back, blend_near = call(
            local_back_kernel,
            (heads_low, heads_like, heads_like, heads_like, heads_like, halo_like, ((1, wide), f32)),
            (place, qkv, halo, causal, causal_t, band, carried, state, prefix, d_mixed, num_one, num_two, d_zeta,
             blends[layer]),
            1,
            scratch=(pltpu.VMEM((ext, LANES), f32), pltpu.VMEM((ext, LANES), f32)),
        )
        state_back = scan(state_back, behind, chunks, True)
        halo_back = chunk_move(halo_back, lambda c: c - 1)
        d_qkv, piece = call(
            qkv_back_kernel,
            (qkv_like, low_like),
            (place, qkv, dq, dk_one, dk_two, dk_near, dv, tail, state_back, halo_back, w_qkv[layer], far_qkv),
            1,
        )
        base, pieces = resid, (piece, core_swap(piece))
        d_qkv_w = lax.dot_general(normed, d_qkv, (((0,), (1,)), ((), ())), preferred_element_type=f32)
        d_qkv_w = jnp.transpose(d_qkv_w, (1, 0, 2))
        d_blends[layer] = jnp.concatenate([blend_near, blend_far], axis=0)
        ready = [over_chips(d_up_own_w, d_up_far_w), over_chips(d_down_own, d_down_far), over_chips(d_out_own, d_out_far)]
        if layer > 0:
            ready.append(over_chips(d_qkv_w[:, :, :LANES], d_qkv_w[:, :, LANES:]))
        grads[layer] = lax.psum(tuple(ready), "seq")
    d_inputs, d_gain_attn[0] = call(
        end_kernel, (low_like, ((1, D), f32)), (base, *pieces, saved[0][0], gain_attn[0])
    )
    d_inputs = give_rows(d_inputs, half, core)

    gains_back = jnp.concatenate(d_gain_attn + d_gain_ffn, axis=0)
    blends_back = jnp.concatenate(d_blends, axis=0)
    blends_back = by_place(half, blends_back[:, :LANES], blends_back[:, LANES:])
    count = 2 * LAYERS + 3 * LAYERS
    extra = []
    for to in range(2):
        features = lax.dynamic_slice_in_dim(gains_back, (2 * to + core) * LANES, LANES, 1)
        extra.append(
            jnp.concatenate([features, blends_back[to], jnp.zeros((16 - count, LANES), f32)], axis=0)
        )
    flat = by_place(
        half,
        d_qkv_w[:, :, :LANES].reshape(shards, -1, LANES),
        d_qkv_w[:, :, LANES:].reshape(shards, -1, LANES),
    )
    block = flat[0].shape[1]
    send = jnp.stack(
        [
            jnp.concatenate([flat[to], jnp.broadcast_to(extra[to][None], (shards, 16, LANES))], axis=1)
            for to in range(2)
        ],
        axis=1,
    ).astype(bf16)
    groups = [
        [s * parts + h * 2 + c for s in range(shards) for h in range(2)] for c in range(2)
    ]
    got = lax.all_to_all(
        send.reshape(2 * shards, block + 16, LANES), AXES, 0, 0, axis_index_groups=groups, tiled=True
    )
    got = jnp.sum(got.astype(f32), axis=0)
    mine = jnp.broadcast_to(got[:block].astype(bf16)[None], (shards, block, LANES))
    qkv_last = lax.all_to_all(mine, "seq", 0, 0, tiled=True).reshape(3, D, LANES)
    rest = got[block:]

    d_norm_attn = rest[:LAYERS]
    d_norm_ffn = rest[LAYERS : 2 * LAYERS]
    d_blend = jnp.sum(rest[2 * LAYERS : count].reshape(LAYERS, 3, 2, HD), axis=3)
    up, down, out, qkv = [
        jnp.stack(pair).astype(f32)
        for pair in (
            (grads[0][0], grads[1][0]),
            (grads[0][1], grads[1][1]),
            (grads[0][2], grads[1][2]),
            (qkv_last, grads[1][3]),
        )
    ]
    return (output, d_inputs, d_norm_attn, qkv, d_blend, out, d_norm_ffn, up, down)


def solution(mesh):
    placed = (
        P("seq", "mlp"),
        P(),
        P("seq"),
        P(None, "mlp"),
        P(None, None, None, "mlp"),
        P(None, None, "mlp"),
        P(None, "mlp", None),
        P(None, "mlp"),
        P(None, None, "mlp"),
        P(None, "mlp", None),
        P("seq", "mlp"),
    )
    return jax.shard_map(
        per_device,
        mesh=mesh,
        in_specs=placed,
        out_specs=(
            P("seq", "mlp"),
            P("seq", "mlp"),
            P(None, "mlp"),
            P(None, None, None, "mlp"),
            P(None, None, "mlp"),
            P(None, "mlp", None),
            P(None, "mlp"),
            P(None, None, "mlp"),
            P(None, "mlp", None),
        ),
        check_vma=False,
    )
```

time: 1240 us -> 415 us (0.33)
  blocking collectives: 500 us -> 0 us
  matrix products: 158 us -> 8.73 us
  waiting for transfers between devices: 303 us -> 172 us
  starting transfers between devices: 21.3 us -> 93.5 us
  local copies, waits for them, and re-layouts: 100 us -> 38.2 us
  other arithmetic: 112 us -> 52.9 us
  Pallas kernels: 0 us -> 32.6 us
  loops' own time: 21.3 us -> 0 us
    all_gather x20 -> x0, blocking collectives: 408 us -> none  [the longest x6 173 us: carried_in(): lax.all_gather(part.astype(kind), axis)]
    dot_general x100 -> x14, matrix products: 141 us -> 8.73 us  [the longest x12 7.92 us: weight_grads(): lax.dot_general(left, right, (((0,), (0,)), ((), ())), preferred_element_...]
    psum x1, waiting for transfers between devices: 193 us -> 68.5 us  [per_device(): grads[layer] = lax.psum(tuple(ready), 'seq')]
    unnamed x17 -> x1, waiting for transfers between devices: 111 us -> 0.02 us
    psum x9 -> x0, blocking collectives: 73.6 us -> none  [the longest x4 26.4 us: norm_rows(): square_sums = lax.psum(jnp.sum(hidden_part * hidden_part, axis=1), 'mlp')]
    ppermute x9 -> x58, waiting for transfers between devices: 0.02 us -> 67.8 us  [the longest x28 41 us: chunk_move(): return lax.ppermute(value, AXES, pairs)]
    select_n x64 -> x7, other arithmetic: 62.4 us -> 1.7 us  [the longest x1 0.82 us: per_device(): jnp.where(allowed, 0.0, masked_score).astype(f32).reshape(rows, LANES)]
    ppermute x9 -> x58, starting transfers between devices: 20.9 us -> 74.8 us  [the longest x28 46.2 us: chunk_move(): return lax.ppermute(value, AXES, pairs)]
  transfers between devices with their start and end apart: 18 -> 61, of which waited for: 8 -> 20; matrix products, arithmetic and copies ran while one was open for 15% -> 19% of each run, Pallas kernels for 0% -> 7%
where the time goes in v1:
time: 415 us; the launch traced here: 414 us
  waiting for transfers between devices  172 us (41%)
  starting transfers between devices  93.5 us (23%)
  other arithmetic  52.9 us (13%)
  local copies, waits for them, and re-layouts  38.2 us (9%)
  Pallas kernels  32.6 us (8%)
  between operations  15.4 us (4%)
  matrix products  8.73 us (2%)
    psum x1, waiting for transfers between devices, per_device(): grads[layer] = lax.psum(tuple(ready), 'seq')  68.5 us
    ppermute x28, starting transfers between devices, chunk_move(): return lax.ppermute(value, AXES, pairs)  46.2 us
    ppermute x28, waiting for transfers between devices, chunk_move(): return lax.ppermute(value, AXES, pairs)  41 us
    pallas_call x17, Pallas kernels, call(): pl.pallas_call(body, out_shape=tuple((jax.ShapeDtypeStruct(shape, kind) f...  32.6 us
    all_to_all x1, waiting for transfers between devices, per_device(): lax.all_to_all(send.reshape(2 * shards, block + 16, LANES), AXES, 0, 0, a...  27.3 us
    ppermute x19, waiting for transfers between devices, far_swap(): return lax.ppermute(value, 'mlp', [(i, i ^ 2) for i in range(count)])  24.1 us
    ppermute x19, starting transfers between devices, far_swap(): return lax.ppermute(value, 'mlp', [(i, i ^ 2) for i in range(count)])  23.1 us
    convert_element_type x4, other arithmetic, scan(): return found.astype(bf16)  15.2 us
  transfers between devices with their start and end apart: 61, of which 20 were waited for; matrix products, arithmetic and copies ran while one was open for 19% of the time, Pallas kernels for 7%

profile of v1, /device:TPU:0, one launch (start us, length us, event | category | flops | bytes accessed | tf_op | source)
XLA Modules:
  0.0 413.5 jit_solution(4176142834694968066)
XLA Ops:
  11.4 3.0 collective-permute-start
  16.4 4.4 %collective-permute-start.4 = (s32[32]{0:T(128)}, s32[32]{0:T(128)}, u32[]{:S(2)}, u32[]{:S(2)}) collective-permute-start(s32[32]{0:T(128)} %slice.328), channel_id=1, source_target_pairs={{0,4},{4,8},{8,12},{12,16},{16,20},{20,24},{24,28},{1,5},{5,9},{9,... | collective-permute-start | bytes 392 | tf_op jit(solution)/shard_map/ppermute | solution.py:576
  62.0 3.4 collective-permute-start.3
  65.5 2.6 fusion.29
  68.1 5.1 %collective-permute-start.10 = (bf16[2,144,128]{2,1,0:T(8,128)(2,1)S(1)}, bf16[2,144,128]{2,1,0:T(8,128)(2,1)S(1)}, u32[]{:S(2)}, u32[]{:S(2)}) collective-permute-start(bf16[2,144,128]{2,1,0:T(8,128)(2,1)S(1)} %fusion.29), channel_id=1, source_target_pairs={{0,24},{1,25},{2,26},{3,27},{4,28},{5,29},{6,30},{7,31}} | collective-permute-start | bytes 221192 | tf_op jit(solution)/shard_map/ppermute | solution.py:435
  74.5 2.5 collective-permute-start.8
  77.1 2.9 shard_map.179
  80.9 3.8 fusion.25.state
  110.9 2.8 collective-permute-start.17
  113.7 2.6 fusion.39
  120.1 2.7 collective-permute-start.21
  124.2 2.9 shard_map.183
  127.9 3.8 fusion.35.state
  132.4 5.3 %collective-permute-done.26.up_other.refs_2_ = bf16[512,512]{1,0:T(8,128)(2,1)S(1)} collective-permute-done((bf16[512,512]{1,0:T(8,128)(2,1)S(1)}, bf16[512,512]{1,0:T(8,128)(2,1)S(1)}, u32[]{:S(2)}, u32[]{:S(2)}) %collective-permute-start.26) | collective-permute-done | bytes 524320 | tf_op jit(solution)/shard_map/ppermute | solution.py:421
  137.7 9.0 %collective-permute-done.27.down_other.refs_4_ = bf16[512,512]{1,0:T(8,128)(2,1)S(1)} collective-permute-done((bf16[512,512]{1,0:T(8,128)(2,1)S(1)}, bf16[512,512]{1,0:T(8,128)(2,1)S(1)}, u32[]{:S(2)}, u32[]{:S(2)}) %collective-permute-start.27) | collective-permute-done | bytes 524320 | tf_op jit(solution)/shard_map/ppermute | solution.py:421
  157.2 5.5 %shard_map.188 = (bf16[256,256]{1,0:T(8,128)(2,1)S(1)}, f32[256,256]{1,0:T(8,128)S(1)}, f32[256,256]{1,0:T(8,128)S(1)}, f32[256,256]{1,0:T(8,128)S(1)}, f32[256,...) custom-call(s32[1]{0:T(128)} %bitcast.place, ...), custom_call_target="tpu_custom_call" | custom-call | tf_op jit(solution)/shard_map/pallas_call | solution.py:404
  162.7 16.1 %collective-permute-done.33 = bf16[2,144,128]{2,1,0:T(8,128)(2,1)S(1)} collective-permute-done((bf16[2,144,128]{2,1,0:T(8,128)(2,1)S(1)}, bf16[2,144,128]{2,1,0:T(8,128)(2,1)S(1)}, u32[]{:S(2)}, u32[]{:S(2)}) %collective-permute-start.33) | collective-permute-done | bytes 73760 | tf_op jit(solution)/shard_map/ppermute | solution.py:435
  180.3 2.6 fusion.49
  187.6 3.9 collective-permute-done.38
  194.0 3.8 fusion.45.state
  204.2 2.6 shard_map.190
  218.4 5.5 %shard_map.192 = (bf16[256,256]{1,0:T(8,128)(2,1)S(1)}, f32[256,256]{1,0:T(8,128)S(1)}, f32[256,256]{1,0:T(8,128)S(1)}, f32[256,256]{1,0:T(8,128)S(1)}, f32[256,...) custom-call(s32[1]{0:T(128)} %bitcast.place, ...), custom_call_target="tpu_custom_call" | custom-call | tf_op jit(solution)/shard_map/pallas_call | solution.py:404
  223.9 13.4 %collective-permute-done.42 = bf16[2,144,128]{2,1,0:T(8,128)(2,1)S(1)} collective-permute-done((bf16[2,144,128]{2,1,0:T(8,128)(2,1)S(1)}, bf16[2,144,128]{2,1,0:T(8,128)(2,1)S(1)}, u32[]{:S(2)}, u32[]{:S(2)}) %collective-permute-start.42) | collective-permute-done | bytes 73760 | tf_op jit(solution)/shard_map/ppermute | solution.py:435
  239.1 2.6 fusion.59
  246.6 3.9 collective-permute-done.47
  253.0 3.8 fusion.55.state
  263.9 4.5 %all-to-all-start = ((bf16[16,208,128]{2,1,0:T(8,128)(2,1)}), bf16[16,208,128]{2,1,0:T(8,128)(2,1)S(1)}, u32[]{:S(2)}, u32[]{:S(2)}) async-start(bf16[16,208,128]{2,1,0:T(8,128)(2,1)} %bitcast.105), calls=%async_computation | async-start | bytes 1703936 | tf_op jit(solution)/shard_map/all_to_all | solution.py:751
  274.6 27.3 %all-to-all-done = bf16[16,208,128]{2,1,0:T(8,128)(2,1)S(1)} async-done(((bf16[16,208,128]{2,1,0:T(8,128)(2,1)}), bf16[16,208,128]{2,1,0:T(8,128)(2,1)S(1)}, u32[]{:S(2)}, u32[]{:S(2)}) %all-to-all-start) | async-done | bytes 852000 | tf_op jit(solution)/shard_map/all_to_all | solution.py:751
  302.8 14.2 %all-to-all-start.1 = ((bf16[8,192,128]{2,1,0:T(8,128)(2,1)}), bf16[8,192,128]{2,1,0:T(8,128)(2,1)S(1)}, u32[]{:S(2)}, u32[]{:S(2)}) async-start(bf16[8,192,128]{2,1,0:T(8,128)(2,1)} %broadcast_in_dim.200), calls=%async_computation.1 | async-start | bytes 786432 | tf_op jit(solution)/shard_map/all_to_all | solution.py:756
  318.1 3.2 collective-permute-done.50
  323.4 8.6 %all-to-all-done.1 = bf16[8,192,128]{2,1,0:T(8,128)(2,1)S(1)} async-done(((bf16[8,192,128]{2,1,0:T(8,128)(2,1)}), bf16[8,192,128]{2,1,0:T(8,128)(2,1)S(1)}, u32[]{:S(2)}, u32[]{:S(2)}) %all-to-all-start.1) | async-done | bytes 393248 | tf_op jit(solution)/shard_map/all_to_all | solution.py:756
  332.0 68.5 %all-reduce.5.cloned.1.call-done = (bf16[1,3,512,128]{3,2,1,0:T(8,128)(2,1)}, bf16[1,128,512]{2,1,0:T(8,128)(2,1)}, bf16[1,128,512]{2,1,0:T(8,128)(2,1)}, bf16[1...) async-done(((bf16[1,3,512,128]{3,2,1,0:T(8,128)(2,1)}, bf16[1,128,512]{2,1,0:T(8,128)(2,1)}, ...) | async-done | bytes 2752528 | tf_op jit(solution)/shard_map/psum | solution.py:719
  (381 shorter events, 151.3 us)
Async XLA Ops:
  7.2 393.3 %all-reduce.5.cloned.1.call-start = ((), (), s32[]{:S(2)}) async-start(), calls=%async_computation.2 | async-start | bytes 5505024 | tf_op jit(solution)/shard_map/psum | solution.py:719
  11.4 39.7 %collective-permute-start = (bf16[304,128]{1,0:T(8,128)(2,1)}, bf16[304,128]{1,0:T(8,128)(2,1)S(1)}, u32[]{:S(2)}, u32[]{:S(2)}) collective-permute-start(bf16[304,128]{1,0:T(8,128)(2,1)} %pad_maximum_fusion.7), channel_id=1, source_target_pairs={{0,2},{1,3},{2,0},{3,1},{4,6},{5,7},{6,4},{7,5},{8,10},{9,11},{10,... | collective-permute-start | bytes 233480 | tf_op jit(solution)/shard_map/ppermute | solution.py:421
  15.6 38.6 %collective-permute-start.2 = (bf16[3,512,128]{2,1,0:T(8,128)(2,1)S(1)}, bf16[3,512,128]{2,1,0:T(8,128)(2,1)S(1)}, u32[]{:S(2)}, u32[]{:S(2)}) collective-permute-start(bf16[3,512,128]{2,1,0:T(8,128)(2,1)S(1)} %get-tuple-element.234.refs_2_.own), channel_id=1, source_target_pairs={{0,2},{1,3},{2,0},{3,1},{4,6},{5,7},{6,4},{7,5},{8,10},{9,11},{10,... | collective-permute-start | bytes 1179656 | tf_op jit(solution)/shard_map/ppermute | solution.py:421
  16.4 31.0 %collective-permute-start.4 = (s32[32]{0:T(128)}, s32[32]{0:T(128)}, u32[]{:S(2)}, u32[]{:S(2)}) collective-permute-start(s32[32]{0:T(128)} %slice.328), channel_id=1, source_target_pairs={{0,4},{4,8},{8,12},{12,16},{16,20},{20,24},{24,28},{1,5},{5,9},{9,... | collective-permute-start | bytes 392 | tf_op jit(solution)/shard_map/ppermute | solution.py:576
  20.9 76.4 %collective-permute-start.13 = (bf16[512,512]{1,0:T(8,128)(2,1)S(1)}, bf16[512,512]{1,0:T(8,128)(2,1)}, u32[]{:S(2)}, u32[]{:S(2)}) collective-permute-start(bf16[512,512]{1,0:T(8,128)(2,1)S(1)} %get-tuple-element.230.up_own.refs_5_), channel_id=1, source_target_pairs={{0,2},{1,3},{2,0},{3,1},{4,6},{5,7},{6,4},{7,5},{8,10},{9,11},{10,... | collective-permute-start | bytes 1572872 | tf_op jit(solution)/shard_map/ppermute | solution.py:421
  22.6 75.6 %collective-permute-start.14 = (bf16[512,512]{1,0:T(8,128)(2,1)S(1)}, bf16[512,512]{1,0:T(8,128)(2,1)}, u32[]{:S(2)}, u32[]{:S(2)}) collective-permute-start(bf16[512,512]{1,0:T(8,128)(2,1)S(1)} %get-tuple-element.228.down_own.refs_7_), channel_id=1, source_target_pairs={{0,2},{1,3},{2,0},{3,1},{4,6},{5,7},{6,4},{7,5},{8,10},{9,11},{10,... | collective-permute-start | bytes 1572872 | tf_op jit(solution)/shard_map/ppermute | solution.py:421
  62.0 12.5 %collective-permute-start.3 = (bf16[2,2,32,128]{3,2,1,0:T(8,128)(2,1)S(1)}, bf16[2,2,32,128]{3,2,1,0:T(8,128)(2,1)S(1)}, u32[]{:S(2)}, u32[]{:S(2)}) collective-permute-start(bf16[2,2,32,128]{3,2,1,0:T(8,128)(2,1)S(1)} %get-tuple-element.104), channel_id=1, source_target_pairs={{0,2},{1,3},{2,4},{3,5},{4,6},{5,7},{6,8},{7,9},{8,10},{9,11},{10,... | collective-permute-start | bytes 98312 | tf_op jit(solution)/shard_map/ppermute | solution.py:435
  68.1 11.9 %collective-permute-start.10 = (bf16[2,144,128]{2,1,0:T(8,128)(2,1)S(1)}, bf16[2,144,128]{2,1,0:T(8,128)(2,1)S(1)}, u32[]{:S(2)}, u32[]{:S(2)}) collective-permute-start(bf16[2,144,128]{2,1,0:T(8,128)(2,1)S(1)} %fusion.29), channel_id=1, source_target_pairs={{0,24},{1,25},{2,26},{3,27},{4,28},{5,29},{6,30},{7,31}} | collective-permute-start | bytes 221192 | tf_op jit(solution)/shard_map/ppermute | solution.py:435
  89.9 14.5 %collective-permute-start.16 = (bf16[3,512,128]{2,1,0:T(8,128)(2,1)S(1)}, bf16[3,512,128]{2,1,0:T(8,128)(2,1)}, u32[]{:S(2)}, u32[]{:S(2)}) collective-permute-start(bf16[3,512,128]{2,1,0:T(8,128)(2,1)S(1)} %get-tuple-element.233.refs_4_.own), channel_id=1, source_target_pairs={{0,2},{1,3},{2,0},{3,1},{4,6},{5,7},{6,4},{7,5},{8,10},{9,11},{10,... | collective-permute-start | bytes 1179656 | tf_op jit(solution)/shard_map/ppermute | solution.py:421
  91.5 11.9 %collective-permute-start.30 = (bf16[256,128]{1,0:T(8,128)(2,1)}, bf16[256,128]{1,0:T(8,128)(2,1)}, u32[]{:S(2)}, u32[]{:S(2)}) collective-permute-start(bf16[256,128]{1,0:T(8,128)(2,1)} %constant_dynamic-slice_fusion.3), channel_id=1, source_target_pairs={{0,2},{1,3},{2,0},{3,1},{4,6},{5,7},{6,4},{7,5},{8,10},{9,11},{10,... | collective-permute-start | bytes 196616 | tf_op jit(solution)/shard_map/ppermute | solution.py:421
  97.3 34.4 %collective-permute-start.24 = (bf16[128,512]{1,0:T(8,128)(2,1)}, bf16[128,512]{1,0:T(8,128)(2,1)S(1)}, u32[]{:S(2)}, u32[]{:S(2)}) collective-permute-start(bf16[128,512]{1,0:T(8,128)(2,1)} %get-tuple-element.243.own), channel_id=1, source_target_pairs={{0,2},{1,3},{2,0},{3,1},{4,6},{5,7},{6,4},{7,5},{8,10},{9,11},{10,... | collective-permute-start | bytes 393224 | tf_op jit(solution)/shard_map/ppermute | solution.py:421
  104.3 15.8 %collective-permute-start.31 = (bf16[2,256,128]{2,1,0:T(8,128)(2,1)S(1)}, bf16[2,256,128]{2,1,0:T(8,128)(2,1)S(1)}, u32[]{:S(2)}, u32[]{:S(2)}) collective-permute-start(bf16[2,256,128]{2,1,0:T(8,128)(2,1)S(1)} %pad_maximum_fusion.5), channel_id=1, source_target_pairs={{0,1},{1,0},{2,3},{3,2},{4,5},{5,4},{6,7},{7,6},{8,9},{9,8},{10,11... | collective-permute-start | bytes 393224 | tf_op jit(solution)/shard_map/ppermute | solution.py:416
  110.9 11.8 %collective-permute-start.17 = (bf16[2,2,32,128]{3,2,1,0:T(8,128)(2,1)S(1)}, bf16[2,2,32,128]{3,2,1,0:T(8,128)(2,1)S(1)}, u32[]{:S(2)}, u32[]{:S(2)}) collective-permute-start(bf16[2,2,32,128]{3,2,1,0:T(8,128)(2,1)S(1)} %get-tuple-element.115), channel_id=1, source_target_pairs={{0,2},{1,3},{2,4},{3,5},{4,6},{5,7},{6,8},{7,9},{8,10},{9,11},{10,... | collective-permute-start | bytes 98312 | tf_op jit(solution)/shard_map/ppermute | solution.py:435
  116.3 10.8 %collective-permute-start.23 = (bf16[2,144,128]{2,1,0:T(8,128)(2,1)S(1)}, bf16[2,144,128]{2,1,0:T(8,128)(2,1)S(1)}, u32[]{:S(2)}, u32[]{:S(2)}) collective-permute-start(bf16[2,144,128]{2,1,0:T(8,128)(2,1)S(1)} %fusion.39), channel_id=1, source_target_pairs={{0,24},{1,25},{2,26},{3,27},{4,28},{5,29},{6,30},{7,31}} | collective-permute-start | bytes 221192 | tf_op jit(solution)/shard_map/ppermute | solution.py:435
  122.8 14.9 %collective-permute-start.26 = (bf16[512,512]{1,0:T(8,128)(2,1)S(1)}, bf16[512,512]{1,0:T(8,128)(2,1)S(1)}, u32[]{:S(2)}, u32[]{:S(2)}) collective-permute-start(bf16[512,512]{1,0:T(8,128)(2,1)S(1)} %get-tuple-element.229.up_own.refs_1_), channel_id=1, source_target_pairs={{0,2},{1,3},{2,0},{3,1},{4,6},{5,7},{6,4},{7,5},{8,10},{9,11},{10,... | collective-permute-start | bytes 1572872 | tf_op jit(solution)/shard_map/ppermute | solution.py:421
  127.2 19.5 %collective-permute-start.27 = (bf16[512,512]{1,0:T(8,128)(2,1)S(1)}, bf16[512,512]{1,0:T(8,128)(2,1)S(1)}, u32[]{:S(2)}, u32[]{:S(2)}) collective-permute-start(bf16[512,512]{1,0:T(8,128)(2,1)S(1)} %get-tuple-element.227.down_own.refs_3_), channel_id=1, source_target_pairs={{0,2},{1,3},{2,0},{3,1},{4,6},{5,7},{6,4},{7,5},{8,10},{9,11},{10,... | collective-permute-start | bytes 1572872 | tf_op jit(solution)/shard_map/ppermute | solution.py:421
  132.2 14.5 %collective-permute-start.25 = (bf16[256,512]{1,0:T(8,128)(2,1)S(1)}, bf16[256,512]{1,0:T(8,128)(2,1)S(1)}, u32[]{:S(2)}, u32[]{:S(2)}) collective-permute-start(bf16[256,512]{1,0:T(8,128)(2,1)S(1)} %get-tuple-element.121.part_a), channel_id=1, source_target_pairs={{0,1},{1,0},{2,3},{3,2},{4,5},{5,4},{6,7},{7,6},{8,9},{9,8},{10,11... | collective-permute-start | bytes 786440 | tf_op jit(solution)/shard_map/ppermute | solution.py:416
  150.0 51.9 %collective-permute-start.55 = (bf16[512,512]{1,0:T(8,128)(2,1)S(1)}, bf16[512,512]{1,0:T(8,128)(2,1)S(1)}, u32[]{:S(2)}, u32[]{:S(2)}) collective-permute-start(bf16[512,512]{1,0:T(8,128)(2,1)S(1)} %convolution_convert_fusion.2), channel_id=1, source_target_pairs={{0,2},{1,3},{2,0},{3,1},{4,6},{5,7},{6,4},{7,5},{8,10},{9,11},{10,... | collective-permute-start | bytes 1572872 | tf_op jit(solution)/shard_map/ppermute | solution.py:421
  151.9 51.2 %collective-permute-start.57 = (bf16[512,512]{1,0:T(8,128)(2,1)S(1)}, bf16[512,512]{1,0:T(8,128)(2,1)S(1)}, u32[]{:S(2)}, u32[]{:S(2)}) collective-permute-start(bf16[512,512]{1,0:T(8,128)(2,1)S(1)} %convolution_convert_fusion), channel_id=1, source_target_pairs={{0,2},{1,3},{2,0},{3,1},{4,6},{5,7},{6,4},{7,5},{8,10},{9,11},{10,... | collective-permute-start | bytes 1572872 | tf_op jit(solution)/shard_map/ppermute | solution.py:421
  153.4 25.4 %collective-permute-start.33 = (bf16[2,144,128]{2,1,0:T(8,128)(2,1)S(1)}, bf16[2,144,128]{2,1,0:T(8,128)(2,1)S(1)}, u32[]{:S(2)}, u32[]{:S(2)}) collective-permute-start(bf16[2,144,128]{2,1,0:T(8,128)(2,1)S(1)} %get-tuple-element.142), channel_id=1, source_target_pairs={{0,2},{1,3},{2,0},{3,1},{4,6},{5,7},{6,4},{7,5},{8,10},{9,11},{10,... | collective-permute-start | bytes 221192 | tf_op jit(solution)/shard_map/ppermute | solution.py:435
  154.9 25.4 %collective-permute-start.34 = (bf16[2,144,128]{2,1,0:T(8,128)(2,1)S(1)}, bf16[2,144,128]{2,1,0:T(8,128)(2,1)S(1)}, u32[]{:S(2)}, u32[]{:S(2)}) collective-permute-start(bf16[2,144,128]{2,1,0:T(8,128)(2,1)S(1)} %get-tuple-element.142), channel_id=1, source_target_pairs={{0,4},{1,5},{2,6},{3,7},{4,0},{5,1},{6,2},{7,3},{8,12},{9,13},{10,... | collective-permute-start | bytes 221192 | tf_op jit(solution)/shard_map/ppermute | solution.py:435
  154.9 25.4 %collective-permute-start.35 = (bf16[2,144,128]{2,1,0:T(8,128)(2,1)S(1)}, bf16[2,144,128]{2,1,0:T(8,128)(2,1)S(1)}, u32[]{:S(2)}, u32[]{:S(2)}) collective-permute-start(bf16[2,144,128]{2,1,0:T(8,128)(2,1)S(1)} %get-tuple-element.142), channel_id=1, source_target_pairs={{0,6},{1,7},{2,4},{3,5},{4,2},{5,3},{6,0},{7,1},{8,14},{9,15},{10,... | collective-permute-start | bytes 221192 | tf_op jit(solution)/shard_map/ppermute | solution.py:435
  184.2 9.8 %collective-permute-start.37 = (bf16[2,144,128]{2,1,0:T(8,128)(2,1)S(1)}, bf16[2,144,128]{2,1,0:T(8,128)(2,1)S(1)}, u32[]{:S(2)}, u32[]{:S(2)}) collective-permute-start(bf16[2,144,128]{2,1,0:T(8,128)(2,1)S(1)} %fusion.49), channel_id=1, source_target_pairs={{16,0},{17,1},{18,2},{19,3},{20,4},{21,5},{22,6},{23,7},{24,8},{25... | collective-permute-start | bytes 221192 | tf_op jit(solution)/shard_map/ppermute | solution.py:435
  200.1 12.0 %collective-permute-start.51 = (bf16[3,512,128]{2,1,0:T(8,128)(2,1)S(1)}, bf16[3,512,128]{2,1,0:T(8,128)(2,1)S(1)}, u32[]{:S(2)}, u32[]{:S(2)}) collective-permute-start(bf16[3,512,128]{2,1,0:T(8,128)(2,1)S(1)} %slice.489), channel_id=1, source_target_pairs={{0,2},{1,3},{2,0},{3,1},{4,6},{5,7},{6,4},{7,5},{8,10},{9,11},{10,... | collective-permute-start | bytes 1179656 | tf_op jit(solution)/shard_map/ppermute | solution.py:421
  207.5 51.4 %collective-permute-start.54 = (bf16[512,512]{1,0:T(8,128)(2,1)S(1)}, bf16[512,512]{1,0:T(8,128)(2,1)S(1)}, u32[]{:S(2)}, u32[]{:S(2)}) collective-permute-start(bf16[512,512]{1,0:T(8,128)(2,1)S(1)} %convolution_convert_fusion.3), channel_id=1, source_target_pairs={{0,2},{1,3},{2,0},{3,1},{4,6},{5,7},{6,4},{7,5},{8,10},{9,11},{10,... | collective-permute-start | bytes 1572872 | tf_op jit(solution)/shard_map/ppermute | solution.py:421
  208.2 51.8 %collective-permute-start.56 = (bf16[512,512]{1,0:T(8,128)(2,1)S(1)}, bf16[512,512]{1,0:T(8,128)(2,1)S(1)}, u32[]{:S(2)}, u32[]{:S(2)}) collective-permute-start(bf16[512,512]{1,0:T(8,128)(2,1)S(1)} %convolution_convert_fusion.1), channel_id=1, source_target_pairs={{0,2},{1,3},{2,0},{3,1},{4,6},{5,7},{6,4},{7,5},{8,10},{9,11},{10,... | collective-permute-start | bytes 1572872 | tf_op jit(solution)/shard_map/ppermute | solution.py:421
  214.7 22.7 %collective-permute-start.42 = (bf16[2,144,128]{2,1,0:T(8,128)(2,1)S(1)}, bf16[2,144,128]{2,1,0:T(8,128)(2,1)S(1)}, u32[]{:S(2)}, u32[]{:S(2)}) collective-permute-start(bf16[2,144,128]{2,1,0:T(8,128)(2,1)S(1)} %get-tuple-element.163), channel_id=1, source_target_pairs={{0,2},{1,3},{2,0},{3,1},{4,6},{5,7},{6,4},{7,5},{8,10},{9,11},{10,... | collective-permute-start | bytes 221192 | tf_op jit(solution)/shard_map/ppermute | solution.py:435
  216.4 22.6 %collective-permute-start.43 = (bf16[2,144,128]{2,1,0:T(8,128)(2,1)S(1)}, bf16[2,144,128]{2,1,0:T(8,128)(2,1)S(1)}, u32[]{:S(2)}, u32[]{:S(2)}) collective-permute-start(bf16[2,144,128]{2,1,0:T(8,128)(2,1)S(1)} %get-tuple-element.163), channel_id=1, source_target_pairs={{0,4},{1,5},{2,6},{3,7},{4,0},{5,1},{6,2},{7,3},{8,12},{9,13},{10,... | collective-permute-start | bytes 221192 | tf_op jit(solution)/shard_map/ppermute | solution.py:435
  217.4 21.7 %collective-permute-start.44 = (bf16[2,144,128]{2,1,0:T(8,128)(2,1)S(1)}, bf16[2,144,128]{2,1,0:T(8,128)(2,1)S(1)}, u32[]{:S(2)}, u32[]{:S(2)}) collective-permute-start(bf16[2,144,128]{2,1,0:T(8,128)(2,1)S(1)} %get-tuple-element.163), channel_id=1, source_target_pairs={{0,6},{1,7},{2,4},{3,5},{4,2},{5,3},{6,0},{7,1},{8,14},{9,15},{10,... | collective-permute-start | bytes 221192 | tf_op jit(solution)/shard_map/ppermute | solution.py:435
  243.1 9.8 %collective-permute-start.46 = (bf16[2,144,128]{2,1,0:T(8,128)(2,1)S(1)}, bf16[2,144,128]{2,1,0:T(8,128)(2,1)S(1)}, u32[]{:S(2)}, u32[]{:S(2)}) collective-permute-start(bf16[2,144,128]{2,1,0:T(8,128)(2,1)S(1)} %fusion.59), channel_id=1, source_target_pairs={{16,0},{17,1},{18,2},{19,3},{20,4},{21,5},{22,6},{23,7},{24,8},{25... | collective-permute-start | bytes 221192 | tf_op jit(solution)/shard_map/ppermute | solution.py:435
  263.9 37.9 %all-to-all-start = ((bf16[16,208,128]{2,1,0:T(8,128)(2,1)}), bf16[16,208,128]{2,1,0:T(8,128)(2,1)S(1)}, u32[]{:S(2)}, u32[]{:S(2)}) async-start(bf16[16,208,128]{2,1,0:T(8,128)(2,1)} %bitcast.105), calls=%async_computation | async-start | bytes 1703936 | tf_op jit(solution)/shard_map/all_to_all | solution.py:751
  302.8 29.2 %all-to-all-start.1 = ((bf16[8,192,128]{2,1,0:T(8,128)(2,1)}), bf16[8,192,128]{2,1,0:T(8,128)(2,1)S(1)}, u32[]{:S(2)}, u32[]{:S(2)}) async-start(bf16[8,192,128]{2,1,0:T(8,128)(2,1)} %broadcast_in_dim.200), calls=%async_computation.1 | async-start | bytes 786432 | tf_op jit(solution)/shard_map/all_to_all | solution.py:756
  (101 other events, 750.6 us)
Sparse Core Ops, SparseCore 0:
  261.3 139.1 all-reduce.4

commit v2 on v1

v2 whole, which is shorter than its diff:
```python
import functools
import math

import jax
import jax.numpy as jnp
from jax import lax
from jax.experimental import pallas as pl
from jax.experimental.pallas import tpu as pltpu
from jax.sharding import PartitionSpec as P

HD = 64
D = 512
BAND = 30
LAYERS = 2
HALO = 32
TILE = 64
LANES = 128
STATE = 144
SMALL = 16
AXES = ("seq", "mlp")

epsilon = 1e-05
masked_score = -1e30
score_scale = 1.0 / math.sqrt(HD)
far_scale = 1.0 / math.sqrt(HD)
f32 = jnp.float32
bf16 = jnp.bfloat16

VM = pl.BlockSpec(memory_space=pltpu.VMEM)
SM = pl.BlockSpec(memory_space=pltpu.SMEM)


def dot(x, y):
    return jnp.dot(x, y, preferred_element_type=f32)


def dot_nt(x, y):
    return lax.dot_general(x, y, (((1,), (1,)), ((), ())), preferred_element_type=f32)


def dot_tn(x, y):
    return lax.dot_general(x, y, (((0,), (0,)), ((), ())), preferred_element_type=f32)


def low_lanes(rows):
    return lax.broadcasted_iota(jnp.int32, (rows, LANES), 1) < HD


def split_heads(x):
    low = low_lanes(x.shape[0])
    zero = jnp.zeros_like(x)
    return jnp.concatenate([jnp.where(low, x, zero), jnp.where(low, zero, x)], axis=0)


def merge_heads(y):
    rows = y.shape[0] // 2
    return jnp.where(low_lanes(rows), y[:rows], y[rows:])


def head_sum(x):
    row = lax.broadcasted_iota(jnp.int32, (LANES, LANES), 0) < HD
    ones = jnp.where(row == low_lanes(LANES), 1.0, 0.0).astype(bf16)
    high = x.astype(bf16)
    rest = (x - high.astype(f32)).astype(bf16)
    return dot(high, ones) + dot(rest, ones)


def kernel_maps(x):
    return (
        jnp.where(x > 0, x + 1.0, jnp.exp(jnp.minimum(x, 0.0))).astype(bf16),
        jnp.tanh(x).astype(bf16),
    )


def maps_back(x, d_one, d_two):
    tanh = jnp.tanh(x)
    return jnp.where(x > 0, 1.0, jnp.exp(jnp.minimum(x, 0.0))) * d_one + (1.0 - tanh * tanh) * d_two


def put_state(ref, quarter, one, two, total):
    row = lax.broadcasted_iota(jnp.int32, (STATE - 2 * HD, LANES), 0)
    low = low_lanes(HD)
    ref[quarter, 0:HD, :] = jnp.where(low, one[:HD], one[HD:]).astype(bf16)
    ref[quarter, HD : 2 * HD, :] = jnp.where(low, two[:HD], two[HD:]).astype(bf16)
    ref[quarter, 2 * HD : STATE, :] = jnp.where(row == 0, total, 0.0).astype(bf16)


def get_state(ref, quarter):
    one = split_heads(ref[quarter, 0:HD, :])
    two = split_heads(ref[quarter, HD : 2 * HD, :])
    total = ref[quarter, 2 * HD : STATE, :].astype(f32)[0:1]
    return one, two, total


def norm_scale(hidden):
    return lax.rsqrt(jnp.sum(hidden * hidden, axis=1, keepdims=True) * (1.0 / D) + epsilon)


def norm_back(hidden, gain, grad):
    scale = norm_scale(hidden)
    gained = grad * gain
    inner = jnp.sum(gained * hidden, axis=1, keepdims=True) * (1.0 / D)
    back = scale * gained - hidden * (scale * scale * scale * inner)
    return back, jnp.sum(grad * hidden * scale, axis=0, keepdims=True)


def extend(halo, rows):
    return jnp.concatenate([halo, rows, jnp.zeros((HALO, LANES), bf16)], axis=0)


def three_parts(value):
    high = value.astype(bf16)
    rest = value - high.astype(f32)
    middle = rest.astype(bf16)
    low = (rest - middle.astype(f32)).astype(bf16)
    return jnp.concatenate([high, middle, low], axis=0)


def pack_kernel(place, blend, inputs, norm_attn, norm_ffn, mine_out, theirs_out):
    rows = inputs.shape[0] // 2
    low = low_lanes(1)
    small = [norm_attn[...], norm_ffn[...]]
    for layer in range(LAYERS):
        for kind in range(3):
            small.append(jnp.where(low, blend[layer, kind, 0], blend[layer, kind, 1]))
    small.append(jnp.zeros((SMALL - 5 * LAYERS, LANES), f32))
    small = three_parts(jnp.concatenate(small, axis=0))
    first, second = inputs[:rows], inputs[rows:]
    mine_out[:rows] = jnp.where(place[0] == 0, first, second)
    theirs_out[:rows] = jnp.where(place[0] == 0, second, first)
    mine_out[rows:] = small
    theirs_out[rows:] = small


def pack_grad_kernel(place, grads, mine_out, theirs_out):
    rows = grads.shape[0] // 2
    first, second = grads[:rows], grads[rows:]
    mine_out[...] = jnp.where(place[0] == 0, first, second)
    theirs_out[...] = jnp.where(place[0] == 0, second, first)


def quarters(place):
    half, core = place[0], place[1]
    return 2 * half + core, 2 * (1 - half) + core, 2 * half + 1 - core, 2 * (1 - half) + 1 - core


def quarter_lanes(quarter):
    return pl.ds(pl.multiple_of(quarter * LANES, LANES), LANES)


def item_ends(lengths):
    ends = []
    for k in range(lengths.shape[0]):
        ends.append(lengths[k] if k == 0 else ends[-1] + lengths[k])
    return ends


def item_start(lengths, ends, positions):
    start = jnp.zeros_like(positions)
    for k, end in enumerate(ends):
        start = start + jnp.where(end <= positions, lengths[k], 0)
    return start


def scan_plan(chunks):
    stages, size = [], 1
    while size < chunks:
        ways = min(4, chunks // size)
        stages.append((size, ways, size * ways >= chunks))
        size *= ways
    return stages


def flag_places(chunks):
    at, places = 0, {}
    for reverse in (False, True):
        for stage, (_, ways, _) in enumerate(scan_plan(chunks)):
            places[reverse, stage] = at
            at += 2 * ways
    return places, at


def setup_kernel(chunks, place, lengths, valid, before, causal_out, causal_t_out, band_out, carried_out, tail_out, flags_out):
    rows = causal_out.shape[0]
    chunk = place[2] * 2 + place[0]
    first_row = chunk * rows
    ends = item_ends(lengths)

    def start_of(positions):
        return item_start(lengths, ends, positions)

    lane = lax.broadcasted_iota(jnp.int32, (1, rows), 1)
    starts_row = start_of(first_row + lane)
    starts = start_of(first_row + lax.broadcasted_iota(jnp.int32, (rows, LANES), 0))
    both = jnp.concatenate([starts, starts], axis=1)
    words = valid[...]
    own_words = jnp.where(place[0] == 0, words[:, :rows], words[:, rows:])
    last_words = jnp.where(place[0] == 0, before[...], words[:, rows - LANES : rows])
    row_at = lax.broadcasted_iota(jnp.int32, (rows, rows), 0)
    lane_at = lax.broadcasted_iota(jnp.int32, (rows, rows), 1)
    own_column = jnp.sum(jnp.where(row_at == lane_at, own_words, 0), axis=1, keepdims=True)
    same = both == starts_row
    causal_out[...] = jnp.where((lane_at <= row_at) & same & (own_words == 1), 1.0, 0.0).astype(bf16)
    causal_t_out[...] = jnp.where((row_at <= lane_at) & same & (own_column == 1), 1.0, 0.0).astype(bf16)
    carried_out[...] = jnp.where(starts < first_row, 1.0, 0.0)
    last_start = start_of(first_row + rows - 1)
    tail_out[...] = jnp.where((starts == last_start) & (own_column == 1), 1.0, 0.0).astype(bf16)
    all_words = jnp.concatenate([last_words, own_words, jnp.zeros((1, LANES), jnp.int32)], axis=1)
    tile_row = lax.broadcasted_iota(jnp.int32, (TILE, LANES), 0)
    tile_lane = lax.broadcasted_iota(jnp.int32, (TILE, LANES), 1)
    gap = tile_row + HALO - tile_lane
    for tile in range(rows // TILE):
        key_starts = start_of(first_row + tile * TILE - HALO + lax.broadcasted_iota(jnp.int32, (1, LANES), 1))
        offset = LANES - HALO + tile * TILE
        key_words = all_words[:, offset : offset + LANES]
        at = slice(tile * TILE, (tile + 1) * TILE)
        allowed = (gap >= 0) & (gap <= BAND) & (starts[at] == key_starts) & ((key_words == 1) | (gap == 0))
        band_out[at] = jnp.where(allowed, 0.0, masked_score)

    places, _ = flag_places(chunks)
    for reverse in (False, True):
        edge = start_of(first_row + (rows - 1 if reverse else 0))
        for stage, (size, ways, last) in enumerate(scan_plan(chunks)):
            member = lax.rem(lax.div(chunk, size), ways)
            base = chunk - member * size - lax.rem(chunk, size)
            group = base if reverse else base + ways * size - 1
            group = start_of(group * rows + (0 if reverse else rows - 1))
            for step in range(ways):
                if last:
                    other = member + step if reverse else member - step
                else:
                    other = jnp.bitwise_xor(member, step)
                block = base + other * size + (0 if reverse else size - 1)
                start = start_of(block * rows + (0 if reverse else rows - 1))
                ahead = (other > member) if reverse else (other < member)
                ahead = ahead & (other >= 0) & (other < ways)
                at = places[reverse, stage] + 2 * step
                flags_out[at] = jnp.where(ahead & (start == edge), 1.0, 0.0)
                flags_out[at + 1] = jnp.where(start == group, 1.0, 0.0)


def combine_kernel(at, ways, has_found, flags, *refs):
    got, refs = refs[:ways], refs[ways:]
    total = sum(flags[at + 2 * step + 1] * got[step][...].astype(f32) for step in range(ways))
    refs[-2][...] = total.astype(bf16)
    found = sum(flags[at + 2 * step] * got[step][...].astype(f32) for step in range(1, ways))
    refs[-1][...] = found + refs[0][...] if has_found else found


def last_combine(at, flags, found, got, out):
    value = found[...]
    for step, part in enumerate(got):
        value = value + flags[at + 2 * (step + 1)] * part[...].astype(f32)
    out[...] = value.astype(bf16)


def qkv_kernel(first, layer, place, *refs):
    if first:
        refs, outs = refs[:7], refs[7:]
        pieces, (own, other, tail) = refs[:4], refs[4:]
        hidden_out, normed_out, qkv_out, state_out, halo_out, gains, blends_out = outs
        rows = hidden_out.shape[0]
        for index, (piece, quarter) in enumerate(zip(pieces, quarters(place))):
            hidden_out[:, quarter_lanes(quarter)] = piece[:rows].astype(f32)
            parts = piece[rows:].astype(f32)
            small = parts[:SMALL] + parts[SMALL : 2 * SMALL] + parts[2 * SMALL :]
            gains[:, quarter_lanes(quarter)] = small
            if index < 2:
                blends_out[:, index * LANES : (index + 1) * LANES] = small
        hidden = hidden_out[...]
    else:
        base, part_a, part_b, gains, own, other, tail, hidden_out, normed_out, qkv_out, state_out, halo_out = refs
        hidden = base[...] + (part_a[...].astype(f32) + part_b[...].astype(f32))
        hidden_out[...] = hidden
    rows = hidden.shape[0]
    normed = (hidden * norm_scale(hidden) * gains[layer : layer + 1]).astype(bf16)
    normed_out[...] = normed
    found = []
    for kind in range(3):
        weight = jnp.concatenate([own[layer, kind], other[kind]], axis=1)
        found.append(dot(normed, weight).astype(bf16))
        qkv_out[kind] = found[kind]
    for pair in range(2):
        quarter = place[0] if pair == 0 else 1 - place[0]
        lanes = slice(pair * LANES, (pair + 1) * LANES)
        keys, values = found[1][:, lanes], found[2][:, lanes]
        one, two = kernel_maps(keys.astype(f32))
        one, two = one * tail[...], two * tail[...]
        put_state(
            state_out,
            quarter,
            dot_tn(one, values),
            dot_tn(two, values),
            jnp.sum(one.astype(f32), axis=0, keepdims=True),
        )
        halo_out[quarter, 0] = keys[rows - HALO :]
        halo_out[quarter, 1] = values[rows - HALO :]


def local_kernel(place, qkv, halo, causal, band, near_out, one_out, two_out, sums_out):
    rows = qkv.shape[1]
    masks = jnp.concatenate([causal[...], causal[...]], axis=0)
    for pair in range(2):
        quarter = place[0] if pair == 0 else 1 - place[0]
        lanes = slice(pair * LANES, (pair + 1) * LANES)
        queries, keys, values = qkv[0, :, lanes], qkv[1, :, lanes], qkv[2, :, lanes]
        maps_q, maps_k = kernel_maps(queries.astype(f32)), kernel_maps(keys.astype(f32))
        for query, key, out in ((maps_q[0], maps_k[0], one_out), (maps_q[1], maps_k[1], two_out)):
            attn = dot_nt(split_heads(query), key).astype(bf16) * masks
            out[:, lanes] = merge_heads(dot(attn, values))
        sums_out[:, lanes] = dot(causal[...], maps_k[0])
        ext_keys = extend(halo[quarter, 0], keys)
        ext_values = extend(halo[quarter, 1], values)
        for tile in range(rows // TILE):
            at = slice(tile * TILE, (tile + 1) * TILE)
            window = slice(tile * TILE, tile * TILE + LANES)
            allowed = jnp.concatenate([band[at], band[at]], axis=0)
            scores = dot_nt(split_heads(queries[at]), ext_keys[window]) * score_scale + allowed
            weights = jnp.exp(scores - jnp.max(scores, axis=1, keepdims=True))
            weights = weights / jnp.sum(weights, axis=1, keepdims=True)
            near_out[at, lanes] = merge_heads(dot(weights.astype(bf16), ext_values[window]))


def mix_kernel(layer, at, count, place, flags, qkv, near, one, two, sums, carried, blends, own, other, found, *refs):
    got = refs[:count]
    mixed_out, far_one_out, far_two_out, root_out, prefix_out, state, part_out = refs[count:]
    last_combine(at, flags, found, got, state)
    mixed = []
    row = 2 * LAYERS + 3 * layer
    for pair in range(2):
        quarter = place[0] if pair == 0 else 1 - place[0]
        lanes = slice(pair * LANES, (pair + 1) * LANES)
        query_one, query_two = kernel_maps(qkv[0, :, lanes].astype(f32))
        state_one, state_two, total = get_state(state, quarter)
        num_one = one[:, lanes] + carried[...] * dot(query_one, state_one)
        num_two = two[:, lanes] + carried[...] * dot(query_two, state_two)
        prefix = sums[:, lanes] + carried[...] * total
        zeta = head_sum(query_one.astype(f32) * prefix)
        root = lax.rsqrt(zeta + 1.0)
        far_one = num_one * root * far_scale
        far_two = num_two * root
        far_one_out[:, lanes] = far_one
        far_two_out[:, lanes] = far_two
        root_out[:, lanes] = root
        prefix_out[:, lanes] = prefix
        mixed.append(
            (
                blends[row : row + 1, lanes] * near[:, lanes]
                + blends[row + 1 : row + 2, lanes] * far_one
                + blends[row + 2 : row + 3, lanes] * far_two
            ).astype(bf16)
        )
        mixed_out[:, lanes] = mixed[pair]
    weight = jnp.concatenate([own[layer], other[...]], axis=0)
    part_out[...] = dot(jnp.concatenate(mixed, axis=1), weight).astype(bf16)


def ffn_kernel(
    layer, base, part_a, part_b, gains, up_own, down_own, up_a, down_a, up_b, down_b,
    middle_out, normed_out, pre_own_out, pre_far_out, act_own_out, act_far_out, part_out,
):
    middle = base[...] + (part_a[...].astype(f32) + part_b[...].astype(f32))
    middle_out[...] = middle
    gain = gains[LAYERS + layer : LAYERS + layer + 1]
    normed = (middle * norm_scale(middle) * gain).astype(bf16)
    normed_out[...] = normed
    weights = (
        (up_own[layer], down_own[layer], pre_own_out, act_own_out),
        (
            jnp.concatenate([up_a[...], up_b[...]], axis=1),
            jnp.concatenate([down_a[...], down_b[...]], axis=0),
            pre_far_out,
            act_far_out,
        ),
    )
    total = None
    for up, down, pre_out, act_out in weights:
        pre = dot(normed, up)
        pre_out[...] = pre
        inner = jnp.tanh(math.sqrt(2.0 / math.pi) * (pre + 0.044715 * pre * pre * pre))
        act = (0.5 * pre * (1.0 + inner)).astype(bf16)
        act_out[...] = act
        product = dot(act, down)
        total = product if total is None else total + product
    part_out[...] = total.astype(bf16)


def shard_rows(whole, place, mine_out, theirs_out):
    first = [whole[:, m * LANES : (m + 1) * LANES] for m in range(4)]
    even, odd = [jnp.where(place[1] == 0, first[2 * h], first[2 * h + 1]) for h in range(2)]
    mine_out[...] = jnp.where(place[0] == 0, even, odd)
    theirs_out[...] = jnp.where(place[0] == 0, odd, even)


def output_kernel(place, base, part_a, part_b, mine_out, theirs_out):
    whole = base[...] + (part_a[...].astype(f32) + part_b[...].astype(f32))
    shard_rows(whole.astype(bf16), place, mine_out, theirs_out)


def gelu_slope(pre):
    c = math.sqrt(2.0 / math.pi)
    inner = jnp.tanh(c * (pre + 0.044715 * pre * pre * pre))
    return 0.5 * (1.0 + inner) + 0.5 * pre * (1.0 - inner * inner) * (c * (1.0 + 3 * 0.044715 * pre * pre))


def ffn_back_kernel(first, layer, *refs):
    if first:
        place, *refs = refs
        pieces, refs = refs[:4], refs[4:]
        weights, outs = refs[:8], refs[8:]
        resid_out, rows_out, d_up_own_out, d_up_far_out, part_out = outs
        for piece, quarter in zip(pieces, quarters(place)):
            resid_out[:, quarter_lanes(quarter)] = piece[...].astype(f32)
        resid = resid_out[...]
    else:
        base, part_a, part_b, hidden, gains, *refs = refs
        weights, outs = refs[:8], refs[8:]
        resid_out, rows_out, d_up_own_out, d_up_far_out, part_out, gain_out = outs
        back, gain_out[...] = norm_back(
            hidden[...], gains[layer + 1 : layer + 2], part_a[...].astype(f32) + part_b[...].astype(f32)
        )
        resid = base[...] + back
        resid_out[...] = resid
    up_own, down_own, up_a, down_a, up_b, down_b, pre_own, pre_far = weights
    rows = resid.astype(bf16)
    rows_out[...] = rows
    total = None
    for up, down, pre, out in (
        (up_own[layer], down_own[layer], pre_own, d_up_own_out),
        (
            jnp.concatenate([up_a[...], up_b[...]], axis=1),
            jnp.concatenate([down_a[...], down_b[...]], axis=0),
            pre_far,
            d_up_far_out,
        ),
    ):
        d_up = (gelu_slope(pre[...]) * dot_nt(rows, down)).astype(bf16)
        out[...] = d_up
        product = dot_nt(d_up, up)
        total = product if total is None else total + product
    part_out[...] = total.astype(bf16)


def mix_back_kernel(
    layer, place, base, part_a, part_b, middle, gains, own, other, qkv, far_one, far_two, root, carried, blends,
    resid_out, rows_out, mixed_out, gain_out, num_one_out, num_two_out, zeta_out, state_out, blend_out,
):
    back, gain_out[...] = norm_back(
        middle[...],
        gains[LAYERS + layer : LAYERS + layer + 1],
        part_a[...].astype(f32) + part_b[...].astype(f32),
    )
    resid = base[...] + back
    resid_out[...] = resid
    blend = blends[2 * LAYERS + 3 * layer : 2 * LAYERS + 3 * layer + 3]
    rows = resid.astype(bf16)
    rows_out[...] = rows
    weight = jnp.concatenate([own[layer], other[...]], axis=0)
    d_mixed = dot_nt(rows, weight).astype(bf16)
    mixed_out[...] = d_mixed
    for pair in range(2):
        quarter = place[0] if pair == 0 else 1 - place[0]
        lanes = slice(pair * LANES, (pair + 1) * LANES)
        grad = d_mixed[:, lanes].astype(f32)
        scale = root[:, lanes]
        dot_one = grad * far_one[:, lanes]
        dot_two = grad * far_two[:, lanes]
        blend_one, blend_two = blend[1:2, lanes], blend[2:3, lanes]
        blend_out[0:1, lanes] = jnp.sum(dot_one, axis=0, keepdims=True)
        blend_out[1:2, lanes] = jnp.sum(dot_two, axis=0, keepdims=True)
        num_one = (grad * (blend_one * far_scale) * scale).astype(bf16)
        num_two = (grad * blend_two * scale).astype(bf16)
        d_zeta = head_sum(blend_one * dot_one + blend_two * dot_two) * (-0.5 * scale * scale)
        num_one_out[:, lanes] = num_one
        num_two_out[:, lanes] = num_two
        zeta_out[:, lanes] = d_zeta
        query_one, query_two = kernel_maps(qkv[0, :, lanes].astype(f32))
        reach = carried[...].astype(bf16)
        put_state(
            state_out,
            quarter,
            dot_tn(query_one * reach, num_one),
            dot_tn(query_two * reach, num_two),
            jnp.sum(carried[...] * d_zeta * query_one.astype(f32), axis=0, keepdims=True),
        )


def local_back_kernel(
    layer, place, qkv, halo, causal, causal_t, band, carried, state, prefix, d_mixed, num_one, num_two, d_zeta, blends,
    dq_out, dk_one_out, dk_two_out, dk_near_out, dv_out, halo_out, blend_out, near_k, near_v,
):
    rows = qkv.shape[1]
    masks = jnp.concatenate([causal[...], causal[...]], axis=0)
    masks_t = jnp.concatenate([causal_t[...], causal_t[...]], axis=1)
    row_low = lax.broadcasted_iota(jnp.int32, (2 * TILE, 1), 0) < TILE
    blend = blends[2 * LAYERS + 3 * layer : 2 * LAYERS + 3 * layer + 3]
    for pair in range(2):
        quarter = place[0] if pair == 0 else 1 - place[0]
        lanes = slice(pair * LANES, (pair + 1) * LANES)
        queries, keys, values = qkv[0, :, lanes], qkv[1, :, lanes], qkv[2, :, lanes]
        grads = d_mixed[:, lanes]
        state_one, state_two, unused_total = get_state(state, quarter)
        query_one, query_two = kernel_maps(queries.astype(f32))
        key_one, key_two = kernel_maps(keys.astype(f32))
        d_values = None
        d_queries = []
        for query, key, num, square, out in (
            (query_one, key_one, num_one[:, lanes], state_one, dk_one_out),
            (query_two, key_two, num_two[:, lanes], state_two, dk_two_out),
        ):
            query_split, num_split = split_heads(query), split_heads(num)
            attn_t = dot_nt(key, query_split).astype(bf16) * masks_t
            grad = dot_nt(num_split, values).astype(bf16) * masks
            grad_t = dot_nt(values, num_split).astype(bf16) * masks_t
            product = dot(attn_t, num_split)
            d_values = product if d_values is None else d_values + product
            d_queries.append(merge_heads(dot(grad, key)) + carried[...] * dot_nt(num, square))
            out[:, lanes] = dot(grad_t, query_split)
        zeta = d_zeta[:, lanes]
        d_queries[0] += zeta * prefix[:, lanes]
        dk_one_out[:, lanes] += dot(causal_t[...], (zeta * query_one.astype(f32)).astype(bf16))

        ext_keys = extend(halo[quarter, 0], keys)
        ext_values = extend(halo[quarter, 1], values)
        near_k[...] = jnp.zeros_like(near_k)
        near_v[...] = jnp.zeros_like(near_v)
        blend_low, blend_high = blend[0:1, pair * LANES : pair * LANES + 1], blend[0:1, pair * LANES + HD : pair * LANES + HD + 1]
        blend_rows = jnp.where(row_low, blend_low, blend_high)
        sums = None
        dq_near = []
        for tile in range(rows // TILE):
            at = slice(tile * TILE, (tile + 1) * TILE)
            window = slice(tile * TILE, tile * TILE + LANES)
            allowed = jnp.concatenate([band[at], band[at]], axis=0)
            query_split, grad_split = split_heads(queries[at]), split_heads(grads[at])
            scores = dot_nt(query_split, ext_keys[window]) * score_scale + allowed
            probs = jnp.exp(scores - jnp.max(scores, axis=1, keepdims=True))
            probs = probs / jnp.sum(probs, axis=1, keepdims=True)
            d_probs = dot_nt(grad_split, ext_values[window])
            inner = jnp.sum(probs * d_probs, axis=1, keepdims=True)
            sums = inner if sums is None else sums + inner
            d_scores = (probs * (d_probs - inner) * blend_rows).astype(bf16)
            dq_near.append(merge_heads(dot(d_scores, ext_keys[window])))
            near_k[window] += dot_tn(d_scores, query_split)
            near_v[window] += dot_tn(probs.astype(bf16), grad_split)
        sum_low = jnp.sum(sums[:TILE], axis=0, keepdims=True)
        sum_high = jnp.sum(sums[TILE:], axis=0, keepdims=True)
        blend_out[0:1, lanes] = jnp.where(low_lanes(1), sum_low, sum_high) * (1.0 / HD)
        back = maps_back(queries.astype(f32), d_queries[0], d_queries[1])
        dq_out[:, lanes] = (back + score_scale * jnp.concatenate(dq_near, axis=0)).astype(bf16)
        dk_near_out[:, lanes] = score_scale * near_k[HALO : HALO + rows]
        dv_out[:, lanes] = d_values + blend[0:1, lanes] * near_v[HALO : HALO + rows]
        halo_out[quarter, 0] = (score_scale * near_k[0:HALO]).astype(bf16)
        halo_out[quarter, 1] = (blend[0:1, lanes] * near_v[0:HALO]).astype(bf16)


def qkv_back_kernel(
    layer, at, count, place, flags, qkv, dq, dk_one, dk_two, dk_near, dv, tail, halo, own, other, found, *refs
):
    got = refs[:count]
    d_qkv_out, part_out, state = refs[count:]
    last_combine(at, flags, found, got, state)
    rows = qkv.shape[1]
    empty = jnp.zeros((rows - HALO, LANES), f32)
    for pair in range(2):
        quarter = place[0] if pair == 0 else 1 - place[0]
        lanes = slice(pair * LANES, (pair + 1) * LANES)
        keys, values = qkv[1, :, lanes], qkv[2, :, lanes]
        key_one, key_two = kernel_maps(keys.astype(f32))
        state_one, state_two, total = get_state(state, quarter)
        weight = tail[...].astype(f32)
        d_one = dk_one[:, lanes] + weight * (dot_nt(values, state_one) + total)
        d_two = dk_two[:, lanes] + weight * dot_nt(values, state_two)
        halo_k = jnp.concatenate([empty, halo[quarter, 0].astype(f32)], axis=0)
        halo_v = jnp.concatenate([empty, halo[quarter, 1].astype(f32)], axis=0)
        d_qkv_out[1, :, lanes] = (
            maps_back(keys.astype(f32), d_one, d_two) + dk_near[:, lanes] + halo_k
        ).astype(bf16)
        d_qkv_out[2, :, lanes] = (
            dv[:, lanes] + weight * (dot(key_one, state_one) + dot(key_two, state_two)) + halo_v
        ).astype(bf16)
    d_qkv_out[0] = dq[...]
    total = None
    for kind in range(3):
        weight = jnp.concatenate([own[layer, kind], other[kind]], axis=1)
        product = dot_nt(d_qkv_out[kind], weight)
        total = product if total is None else total + product
    part_out[...] = total.astype(bf16)


def wide_grads_kernel(with_qkv, place, normed, act_own, act_far, d_up_own, d_up_far, grad_rows, mixed, out_rows, *refs):
    if with_qkv:
        above, d_qkv, own, far = refs
    else:
        own, far = refs
    units = act_own.shape[1]
    piece = units // 2
    side = lax.rem(place[2], 2)
    own[:D] = dot_tn(normed[...], d_up_own[...]).astype(bf16)
    own[D : D + units] = dot_tn(act_own[...], grad_rows[...]).astype(bf16)
    d_up = dot_tn(normed[...], d_up_far[...]).astype(bf16)
    d_down = dot_tn(act_far[...], grad_rows[...]).astype(bf16)
    far[:D] = jnp.where(side == 0, d_up, jnp.concatenate([d_up[:, piece:], d_up[:, :piece]], axis=1))
    far[D : D + units] = jnp.where(side == 0, d_down, jnp.concatenate([d_down[piece:], d_down[:piece]], axis=0))
    d_out = dot_tn(mixed[...], out_rows[...]).astype(bf16)
    at = D + units
    own[at : at + LANES] = d_out[:LANES]
    far[at : at + LANES] = d_out[LANES:]
    if with_qkv:
        at += LANES
        for kind in range(3):
            found = dot_tn(above[...], d_qkv[kind]).astype(bf16)
            for block in range(D // LANES):
                rows = slice(at + kind * LANES, at + (kind + 1) * LANES)
                lanes = slice(block * LANES, (block + 1) * LANES)
                own[rows, lanes] = found[lanes, :LANES]
                far[rows, lanes] = found[lanes, LANES:]


def halve_kernel(place, own, got, keep_out, send_out):
    rows = own.shape[0] // 2
    total = own[...].astype(f32) + got[...].astype(f32)
    side = lax.rem(place[2], 2)
    keep_out[...] = jnp.where(side == 0, total[:rows], total[rows:])
    send_out[...] = jnp.where(side == 0, total[rows:], total[:rows]).astype(bf16)


def add_kernel(keep, got, out):
    out[...] = (keep[...] + got[...].astype(f32)).astype(bf16)


def fold_kernel(ways, got, out):
    rows = got.shape[0] // ways
    whole = got[...].astype(f32)
    total = sum(whole[k * rows : (k + 1) * rows] for k in range(ways)).astype(bf16)
    for k in range(ways):
        out[k * rows : (k + 1) * rows] = total


def last_qkv_kernel(normed, d_qkv, own_out, far_out):
    for kind in range(3):
        found = dot_tn(normed[...], d_qkv[kind])
        own_out[kind * D : (kind + 1) * D] = found[:, :LANES]
        far_out[kind * D : (kind + 1) * D] = found[:, LANES:]


def end_kernel(
    shards, place, base, part_a, part_b, hidden, gains, own, far, *refs
):
    smalls, (mine_out, theirs_out, send_out) = refs[: 4 * LAYERS - 1], refs[4 * LAYERS - 1 :]
    gain_refs, blend_refs = smalls[: 2 * LAYERS - 1], smalls[2 * LAYERS - 1 :]
    back, gain = norm_back(hidden[...], gains[0:1], part_a[...].astype(f32) + part_b[...].astype(f32))
    shard_rows((base[...] + back).astype(bf16), place, mine_out, theirs_out)
    block = own.shape[0] // shards
    gain_rows = jnp.concatenate([gain] + [ref[...] for ref in gain_refs], axis=0)
    blend_rows = jnp.concatenate([ref[...] for ref in blend_refs], axis=0)
    for to in range(2):
        features = jnp.where(
            place[1] == 0,
            gain_rows[:, 2 * to * LANES : (2 * to + 1) * LANES],
            gain_rows[:, (2 * to + 1) * LANES : (2 * to + 2) * LANES],
        )
        blends = jnp.where(place[0] == to, blend_rows[:, :LANES], blend_rows[:, LANES:])
        empty = jnp.zeros((SMALL - 5 * LAYERS, LANES), f32)
        extra = jnp.concatenate([features, blends, empty], axis=0).astype(bf16)
        rows = jnp.where(place[0] == to, own[...], far[...])
        for shard in range(shards):
            send_out[2 * shard + to, :SMALL] = extra
            send_out[2 * shard + to, SMALL:] = rows[shard * block : (shard + 1) * block].astype(bf16)


def collect_kernel(shards, got, out, rest_out):
    total = jnp.sum(got[...].astype(f32), axis=0)
    rest_out[...] = total[:SMALL]
    mine = total[SMALL:].astype(bf16)
    for shard in range(shards):
        out[shard] = mine


def in_order(place, mine, other):
    side = lax.rem(place[2], 2)
    return jnp.where(side == 0, mine[...], other[...]), jnp.where(side == 0, other[...], mine[...])


def finish_wide_kernel(place, low_mine, low_other, high_mine, high_other, up_out, down_out, out_out, above_out):
    units = up_out.shape[2]
    for layer, pair in ((0, (low_mine, low_other)), (1, (high_mine, high_other))):
        whole = jnp.concatenate(in_order(place, *pair), axis=0)
        up_out[layer] = whole[:D].astype(f32)
        down_out[layer] = whole[D : D + units].astype(f32)
        out_out[layer] = whole[D + units : D + units + LANES].astype(f32)
        if layer == 0:
            above_out[...] = whole[D + units + LANES :]


def finish_qkv_kernel(last, above, out):
    for kind in range(3):
        out[0, kind] = last[kind * D : (kind + 1) * D].astype(f32)
        for block in range(D // LANES):
            lanes = slice(block * LANES, (block + 1) * LANES)
            out[1, kind, lanes] = above[kind * LANES : (kind + 1) * LANES, lanes].astype(f32)


def call(body, outs, operands, scalars=0, scratch=(), scalar_outs=0):
    return pl.pallas_call(
        body,
        out_shape=tuple(jax.ShapeDtypeStruct(shape, kind) for shape, kind in outs),
        in_specs=[SM] * scalars + [VM] * (len(operands) - scalars),
        out_specs=tuple([VM] * (len(outs) - scalar_outs) + [SM] * scalar_outs),
        scratch_shapes=scratch,
        compiler_params=pltpu.CompilerParams(vmem_limit_bytes=24 * 2**20),
    )(*operands)


def after(value, *others):
    return lax.optimization_barrier((value, *others))[0]


def core_swap(value):
    count = lax.axis_size("mlp")
    return lax.ppermute(value, "mlp", [(i, i ^ 1) for i in range(count)])


def far_swap(value):
    count = lax.axis_size("mlp")
    return lax.ppermute(value, "mlp", [(i, i ^ 2) for i in range(count)])


def side_swap(value):
    count = lax.axis_size("seq")
    return lax.ppermute(value, "seq", [(i, i ^ 1) for i in range(count)])


def chunk_move(value, target):
    shards, parts = lax.axis_size("seq"), lax.axis_size("mlp")
    pairs = []
    for chunk in range(2 * shards):
        goal = target(chunk)
        if goal is None or not 0 <= goal < 2 * shards:
            continue
        for core in range(2):
            pairs.append(
                ((chunk // 2) * parts + (chunk % 2) * 2 + core, (goal // 2) * parts + (goal % 2) * 2 + core)
            )
    return lax.ppermute(value, AXES, pairs)


def scan(value, flags, chunks, reverse):
    places, _ = flag_places(chunks)
    found, arrived = None, None
    for stage, (size, ways, last) in enumerate(scan_plan(chunks)):
        got = []
        for step in range(1, ways):
            if last:

                def target(chunk, step=step):
                    move = -step if reverse else step
                    return chunk + move * size if 0 <= (chunk // size) % ways + move < ways else None

            else:

                def target(chunk, step=step):
                    member = (chunk // size) % ways
                    return chunk + ((member ^ step) - member) * size

            got.append(chunk_move(value, target))
        at = places[reverse, stage]
        if last:
            return (found, tuple(got), at), arrived
        arrived = arrived or tuple(got)
        operands = (flags, value, *got) + (() if found is None else (found,))
        value, found = call(
            functools.partial(combine_kernel, at, ways, found is not None),
            ((value.shape, bf16), (value.shape, f32)),
            operands,
            1,
        )


def line_exchange(value):
    shards, parts = lax.axis_size("seq"), lax.axis_size("mlp")
    groups = [
        [shard * parts + part for shard in range(side, shards, 2)] for side in range(2) for part in range(parts)
    ]
    return lax.all_to_all(value, AXES, 0, 0, axis_index_groups=groups, tiled=True)


def by_place(flag, mine, other):
    return jnp.where(flag == 0, mine, other), jnp.where(flag == 0, other, mine)


def per_device(inputs, lengths, valid, norm_attn, w_qkv, blend, w_out, norm_ffn, w_up, w_down, grad_out):
    shards, parts = lax.axis_size("seq"), lax.axis_size("mlp")
    shard, part = lax.axis_index("seq"), lax.axis_index("mlp")
    half, core = part // 2, part % 2
    side = shard % 2
    rows = inputs.shape[0] // 2
    chunks = 2 * shards
    units = w_up.shape[2]
    place = jnp.stack([half, core, shard]).astype(jnp.int32)

    wide = 2 * LANES
    hidden_like = ((rows, D), f32)
    low_like = ((rows, D), bf16)
    heads_like = ((rows, wide), f32)
    heads_low = ((rows, wide), bf16)
    qkv_like = ((3, rows, wide), bf16)
    state_like = ((2, STATE, LANES), bf16)
    halo_like = ((2, 2, HALO, LANES), bf16)
    ffn_like = ((rows, units), f32)
    ffn_low = ((rows, units), bf16)
    shard_like = ((rows, LANES), bf16)
    gain_like = ((1, D), f32)

    piece_like = ((rows + 3 * SMALL, LANES), bf16)
    mine, theirs = call(pack_kernel, (piece_like, piece_like), (place, blend, inputs, norm_attn, norm_ffn), 2)
    got = far_swap(theirs)
    pieces = (mine, got, core_swap(mine), core_swap(got))
    far_qkv = [far_swap(after(w_qkv[0], theirs)), None]
    far_out = [far_swap(after(w_out[0], theirs)), None]

    def up_piece(layer):
        return lax.dynamic_slice_in_dim(w_up[layer], side * (units // 2), units // 2, 1)

    def down_piece(layer):
        return lax.dynamic_slice_in_dim(w_down[layer], side * (units // 2), units // 2, 0)

    up_a, up_b, down_a, down_b = ([None] * LAYERS for _ in range(4))
    up_a[0] = far_swap(after(up_piece(0), theirs))

    before = lax.ppermute(
        valid[2 * rows - LANES :].reshape(1, LANES), "seq", [(source, source + 1) for source in range(shards - 1)]
    )
    _, flag_count = flag_places(chunks)
    causal, causal_t, band, carried, tail, flags = call(
        functools.partial(setup_kernel, chunks),
        (
            ((rows, rows), bf16),
            ((rows, rows), bf16),
            ((rows, LANES), f32),
            ((rows, LANES), f32),
            ((rows, LANES), bf16),
            ((flag_count,), f32),
        ),
        (place, lengths, valid.reshape(1, 2 * rows), before),
        2,
        scalar_outs=1,
    )

    saved = []
    base, adds = None, None
    for layer in range(LAYERS):
        outs = (hidden_like, low_like, qkv_like, state_like, halo_like)
        if layer == 0:
            hidden, normed, qkv, state, halo, gains, blends = call(
                functools.partial(qkv_kernel, True, layer),
                outs + (((SMALL, D), f32), ((SMALL, wide), f32)),
                (place, *pieces, w_qkv, far_qkv[layer], tail),
                1,
            )
        else:
            hidden, normed, qkv, state, halo = call(
                functools.partial(qkv_kernel, False, layer),
                outs,
                (place, base, *adds, gains, w_qkv, far_qkv[layer], tail),
                1,
            )
        halo = chunk_move(halo, lambda c: c + 1)
        (found, parts_got, at), arrived = scan(state, flags, chunks, False)
        if layer == 0:
            down_a[0] = far_swap(after(down_piece(0), *arrived))
            up_b[0] = side_swap(after(up_a[0], *arrived))
            far_qkv[1] = far_swap(after(w_qkv[1], *arrived))
            down_b[0] = side_swap(down_a[0])
            far_out[1] = far_swap(after(w_out[1], *arrived))
            up_a[1] = far_swap(after(up_piece(1), *arrived))
            down_a[1] = far_swap(after(down_piece(1), *arrived))
            up_b[1] = side_swap(after(up_a[1], *arrived))
            down_b[1] = side_swap(after(down_a[1], *arrived))
        near, one, two, sums = call(
            local_kernel, (heads_like,) * 4, (place, qkv, halo, causal, band), 1
        )
        mixed, far_one, far_two, root, prefix, state, piece = call(
            functools.partial(mix_kernel, layer, at, len(parts_got)),
            (heads_low, heads_like, heads_like, heads_like, heads_like, state_like, low_like),
            (place, flags, qkv, near, one, two, sums, carried, blends, w_out, far_out[layer], found, *parts_got),
            2,
        )
        weights = (w_up, w_down, up_a[layer], down_a[layer], up_b[layer], down_b[layer])
        middle, normed_ffn, pre_own, pre_far, act_own, act_far, piece_ffn = call(
            functools.partial(ffn_kernel, layer),
            (hidden_like, low_like, ffn_like, ffn_like, ffn_low, ffn_low, low_like),
            (hidden, piece, core_swap(piece), gains, *weights),
        )
        saved.append(
            (hidden, normed, qkv, state, halo, mixed, far_one, far_two, root, prefix, middle, normed_ffn,
             weights, pre_own, pre_far, act_own, act_far)
        )
        base, adds = middle, (piece_ffn, core_swap(piece_ffn))
    out_mine, out_theirs = call(output_kernel, (shard_like, shard_like), (place, base, *adds), 1)
    output = jnp.concatenate(by_place(half, out_mine, far_swap(out_theirs)))

    mine, theirs = call(pack_grad_kernel, (shard_like, shard_like), (place, after(grad_out, saved[0][2])), 1)
    got = far_swap(theirs)
    grad_pieces = (mine, got, core_swap(mine), core_swap(got))

    base, adds = None, None
    d_gain_attn, d_gain_ffn, d_blends = [None] * LAYERS, [None] * LAYERS, [None] * LAYERS
    wide_sums = [None] * LAYERS
    d_qkvs = [None] * LAYERS
    arrived = None
    for layer in reversed(range(LAYERS)):
        (hidden, normed, qkv, state, halo, mixed, far_one, far_two, root, prefix, middle, normed_ffn,
         weights, pre_own, pre_far, act_own, act_far) = saved[layer]
        outs = (hidden_like, low_like, ffn_low, ffn_low, low_like)
        if base is None:
            resid, grad_rows, d_up_own, d_up_far, piece = call(
                functools.partial(ffn_back_kernel, True, layer),
                outs,
                (place, *grad_pieces, *weights, pre_own, pre_far),
                1,
            )
        else:
            resid, grad_rows, d_up_own, d_up_far, piece, d_gain_attn[layer + 1] = call(
                functools.partial(ffn_back_kernel, False, layer),
                outs + (gain_like,),
                (base, *adds, saved[layer + 1][0], gains, *weights, pre_own, pre_far),
            )
        (resid, out_rows, d_mixed, d_gain_ffn[layer], num_one, num_two, d_zeta, state_back, blend_far) = call(
            functools.partial(mix_back_kernel, layer),
            (hidden_like, low_like, heads_low, gain_like, heads_low, heads_low, heads_like, state_like,
             ((2, wide), f32)),
            (place, resid, piece, core_swap(piece), middle, gains, w_out, far_out[layer], qkv, far_one, far_two,
             root, carried, blends),
            1,
        )
        (found, parts_got, at), arrived = scan(state_back, flags, chunks, True)
        ext = HALO + rows + HALO
        dq, dk_one, dk_two, dk_near, dv, halo_back, blend_near = call(
            functools.partial(local_back_kernel, layer),
            (heads_low, heads_like, heads_like, heads_like, heads_like, halo_like, ((1, wide), f32)),
            (place, qkv, halo, causal, causal_t, band, carried, state, prefix, d_mixed, num_one, num_two, d_zeta,
             blends),
            1,
            scratch=(pltpu.VMEM((ext, LANES), f32), pltpu.VMEM((ext, LANES), f32)),
        )
        halo_back = chunk_move(halo_back, lambda c: c - 1)
        with_qkv = layer + 1 < LAYERS
        height = D + units + LANES + (3 * LANES if with_qkv else 0)
        own, far = call(
            functools.partial(wide_grads_kernel, with_qkv),
            (((height, D), bf16), ((height, D), bf16)),
            (place, normed_ffn, act_own, act_far, d_up_own, d_up_far, grad_rows, mixed, out_rows)
            + ((saved[layer + 1][1], d_qkvs[layer + 1]) if with_qkv else ()),
            1,
        )
        keep, send = call(
            halve_kernel,
            (((height // 2, D), f32), ((height // 2, D), bf16)),
            (place, own, far_swap(after(far, *arrived))),
            1,
        )
        (folded,) = call(add_kernel, (((height // 2, D), bf16),), (keep, side_swap(send)))
        (folded,) = call(
            functools.partial(fold_kernel, shards // 2), (((height // 2, D), bf16),), (line_exchange(folded),)
        )
        folded = line_exchange(folded)
        wide_sums[layer] = (folded, side_swap(folded))
        d_qkvs[layer], piece = call(
            functools.partial(qkv_back_kernel, layer, at, len(parts_got)),
            (qkv_like, low_like),
            (place, flags, qkv, dq, dk_one, dk_two, dk_near, dv, tail, halo_back, w_qkv, far_qkv[layer], found,
             *parts_got),
            2,
            scratch=(pltpu.VMEM((2, STATE, LANES), bf16),),
        )
        base, adds = resid, (piece, core_swap(piece))
        d_blends[layer] = (blend_near, blend_far)

    last_like = ((3 * D, LANES), f32)
    own, far = call(last_qkv_kernel, (last_like, last_like), (saved[0][1], d_qkvs[0]))
    block = 3 * D // shards
    smalls = d_gain_attn[1:] + d_gain_ffn + [ref for pair in d_blends for ref in pair]
    mine, theirs, send = call(
        functools.partial(end_kernel, shards),
        (shard_like, shard_like, ((chunks, SMALL + block, LANES), bf16)),
        (place, base, *adds, saved[0][0], gains, own, far, *smalls),
        1,
    )
    groups = [[s * parts + h * 2 + c for s in range(shards) for h in range(2)] for c in range(2)]
    got = lax.all_to_all(send, AXES, 0, 0, axis_index_groups=groups, tiled=True)
    spread, rest = call(
        functools.partial(collect_kernel, shards),
        (((shards, block, LANES), bf16), ((SMALL, LANES), f32)),
        (got,),
    )
    last = lax.all_to_all(spread, "seq", 0, 0, tiled=True).reshape(3 * D, LANES)
    d_inputs = jnp.concatenate(by_place(half, mine, far_swap(theirs)))

    count = 2 * LAYERS + 3 * LAYERS
    d_norm_attn = rest[:LAYERS]
    d_norm_ffn = rest[LAYERS : 2 * LAYERS]
    d_blend = jnp.sum(rest[2 * LAYERS : count].reshape(LAYERS, 3, 2, HD), axis=3)
    d_up, d_down, d_out, above = call(
        finish_wide_kernel,
        (((LAYERS, D, units), f32), ((LAYERS, units, D), f32), ((LAYERS, LANES, D), f32), ((3 * LANES, D), bf16)),
        (place, *wide_sums[0], *wide_sums[1]),
        1,
    )
    (d_qkv,) = call(finish_qkv_kernel, (((LAYERS, 3, D, LANES), f32),), (last, above))
    return (output, d_inputs, d_norm_attn, d_qkv, d_blend, d_out, d_norm_ffn, d_up, d_down)


def solution(mesh):
    placed = (
        P("seq", "mlp"),
        P(),
        P("seq"),
        P(None, "mlp"),
        P(None, None, None, "mlp"),
        P(None, None, "mlp"),
        P(None, "mlp", None),
        P(None, "mlp"),
        P(None, None, "mlp"),
        P(None, "mlp", None),
        P("seq", "mlp"),
    )
    return jax.shard_map(
        per_device,
        mesh=mesh,
        in_specs=placed,
        out_specs=(
            P("seq", "mlp"),
            P("seq", "mlp"),
            P(None, "mlp"),
            P(None, None, None, "mlp"),
            P(None, None, "mlp"),
            P(None, "mlp", None),
            P(None, "mlp"),
            P(None, None, "mlp"),
            P(None, "mlp", None),
        ),
        check_vma=False,
    )
```

time: 415 us -> 358 us (0.86)
  other arithmetic: 52.9 us -> 1.53 us
  Pallas kernels: 32.6 us -> 63.3 us
  local copies, waits for them, and re-layouts: 38.2 us -> 15.7 us
  between operations: 15.4 us -> 1.57 us
  starting transfers between devices: 93.5 us -> 106 us
  matrix products: 8.73 us -> 0 us
    psum x1 -> x0, waiting for transfers between devices: 68.5 us -> none  [per_device(): grads[layer] = lax.psum(tuple(ready), 'seq')]
    ppermute x1 -> x9, waiting for transfers between devices: 0.01 us -> 54.8 us  [the longest x8 54.8 us: side_swap(): return lax.ppermute(value, 'seq', [(i, i ^ 1) for i in range(count)])]
    convert_element_type x20 -> x0, other arithmetic: 36.7 us -> none  [the longest x4 15.2 us: scan(): return found.astype(bf16)]
    pallas_call x17 -> x37, Pallas kernels: 32.6 us -> 63.3 us  [call(): pl.pallas_call(body, out_shape=tuple((jax.ShapeDtypeStruct(shape, kind) f...]
    ppermute x1 -> x9, starting transfers between devices: 4.45 us -> 14.6 us  [the longest x8 10.7 us: side_swap(): return lax.ppermute(value, 'seq', [(i, i ^ 1) for i in range(count)])]
    ppermute x19 -> x14, waiting for transfers between devices: 24.1 us -> 14.5 us  [far_swap(): return lax.ppermute(value, 'mlp', [(i, i ^ 2) for i in range(count)])]
    dot_general x14 -> x0, matrix products: 8.73 us -> none  [the longest x12 7.92 us: weight_grads(): lax.dot_general(left, right, (((0,), (0,)), ((), ())), preferred_element_...]
    all_to_all x2 -> x6, starting transfers between devices: 18.6 us -> 26.9 us  [the longest x4 16.2 us: line_exchange(): lax.all_to_all(value, AXES, 0, 0, axis_index_groups=groups, tiled=True)]
  transfers between devices with their start and end apart: 61 -> 69, of which waited for: 20 -> 27; matrix products, arithmetic and copies ran while one was open for 19% -> 2% of each run, Pallas kernels for 7% -> 15%
where the time goes in v2:
time: 358 us; the launch traced here: 356 us
  waiting for transfers between devices  168 us (47%)
  starting transfers between devices  106 us (30%)
  Pallas kernels  63.3 us (18%)
  local copies, waits for them, and re-layouts  15.7 us (4%)
    pallas_call x37, Pallas kernels, call(): pl.pallas_call(body, out_shape=tuple((jax.ShapeDtypeStruct(shape, kind) f...  63.3 us
    ppermute x8, waiting for transfers between devices, side_swap(): return lax.ppermute(value, 'seq', [(i, i ^ 1) for i in range(count)])  54.8 us
    ppermute x28, waiting for transfers between devices, chunk_move(): return lax.ppermute(value, AXES, pairs)  48 us
    ppermute x28, starting transfers between devices, chunk_move(): return lax.ppermute(value, AXES, pairs)  47.5 us
    all_to_all x4, waiting for transfers between devices, line_exchange(): lax.all_to_all(value, AXES, 0, 0, axis_index_groups=groups, tiled=True)  43.7 us
    all_to_all x4, starting transfers between devices, line_exchange(): lax.all_to_all(value, AXES, 0, 0, axis_index_groups=groups, tiled=True)  16.2 us
    ppermute x14, starting transfers between devices, far_swap(): return lax.ppermute(value, 'mlp', [(i, i ^ 2) for i in range(count)])  16.1 us
    ppermute x14, waiting for transfers between devices, far_swap(): return lax.ppermute(value, 'mlp', [(i, i ^ 2) for i in range(count)])  14.5 us
  transfers between devices with their start and end apart: 69, of which 27 were waited for; matrix products, arithmetic and copies ran while one was open for 2% of the time, Pallas kernels for 15%

profile of v2, /device:TPU:0, one launch (start us, length us, event | category | flops | bytes accessed | tf_op | source)
XLA Modules:
  0.0 356.4 jit_solution(12177268217290233779)
XLA Ops:
  5.1 3.0 collective-permute-start
  10.2 3.9 %collective-permute-start.4 = (s32[1,128]{1,0:T(1,128)S(1)}, s32[1,128]{1,0:T(1,128)S(1)}, u32[]{:S(2)}, u32[]{:S(2)}) collective-permute-start(s32[1,128]{1,0:T(1,128)S(1)} %slice_bitcast_fusion.4), channel_id=1, source_target_pairs={{0,4},{4,8},{8,12},{12,16},{16,20},{20,24},{24,28},{1,5},{5,9},{9,... | collective-permute-start | bytes 1544 | tf_op jit(solution)/shard_map/ppermute | solution.py:831
  33.5 3.4 collective-permute-start.5
  37.6 3.6 %collective-permute-start.10 = (bf16[2,144,128]{2,1,0:T(8,128)(2,1)S(1)}, bf16[2,144,128]{2,1,0:T(8,128)(2,1)S(1)}, u32[]{:S(2)}, u32[]{:S(2)}) collective-permute-start(bf16[2,144,128]{2,1,0:T(8,128)(2,1)S(1)} %get-tuple-element.176), channel_id=1, source_target_pairs={{0,8},{1,9},{2,10},{3,11},{4,12},{5,13},{6,14},{7,15},{8,16},{9,17... | collective-permute-start | bytes 221192 | tf_op jit(solution)/shard_map/ppermute | solution.py:745
  41.2 4.5 %collective-permute-start.11 = (bf16[2,144,128]{2,1,0:T(8,128)(2,1)S(1)}, bf16[2,144,128]{2,1,0:T(8,128)(2,1)S(1)}, u32[]{:S(2)}, u32[]{:S(2)}) collective-permute-start(bf16[2,144,128]{2,1,0:T(8,128)(2,1)S(1)} %get-tuple-element.176), channel_id=1, source_target_pairs={{0,16},{1,17},{2,18},{3,19},{4,20},{5,21},{6,22},{7,23},{8,24},{9,... | collective-permute-start | bytes 221192 | tf_op jit(solution)/shard_map/ppermute | solution.py:745
  47.1 3.5 shard_map.181
  55.2 3.2 collective-permute-done.16.up_b.refs_9_
  58.4 4.2 %collective-permute-done.17.down_b.refs_10_ = bf16[256,512]{1,0:T(8,128)(2,1)S(1)} collective-permute-done((bf16[256,512]{1,0:T(8,128)(2,1)S(1)}, bf16[256,512]{1,0:T(8,128)(2,1)S(1)}, u32[]{:S(2)}, u32[]{:S(2)}) %collective-permute-start.17) | collective-permute-done | bytes 262176 | tf_op jit(solution)/shard_map/ppermute | solution.py:731
  70.7 10.5 %collective-permute-done.22.refs_1_ = bf16[2,144,128]{2,1,0:T(8,128)(2,1)S(1)} collective-permute-done((bf16[2,144,128]{2,1,0:T(8,128)(2,1)S(1)}, bf16[2,144,128]{2,1,0:T(8,128)(2,1)S(1)}, u32[]{:S(2)}, u32[]{:S(2)}) %collective-permute-start.22) | collective-permute-done | bytes 73760 | tf_op jit(solution)/shard_map/ppermute | solution.py:745
  84.6 3.6 %collective-permute-start.26 = (bf16[2,144,128]{2,1,0:T(8,128)(2,1)S(1)}, bf16[2,144,128]{2,1,0:T(8,128)(2,1)S(1)}, u32[]{:S(2)}, u32[]{:S(2)}) collective-permute-start(bf16[2,144,128]{2,1,0:T(8,128)(2,1)S(1)} %get-tuple-element.195), channel_id=1, source_target_pairs={{0,16},{1,17},{2,18},{3,19},{4,20},{5,21},{6,22},{7,23},{8,24},{9,... | collective-permute-start | bytes 221192 | tf_op jit(solution)/shard_map/ppermute | solution.py:745
  89.6 2.9 collective-permute-start.20
  93.8 3.3 collective-permute-start.31
  97.1 3.5 shard_map.186
  103.8 3.3 collective-permute-done.35.refs_2_
  127.3 6.1 %shard_map.194 = (bf16[256,256]{1,0:T(8,128)(2,1)S(1)}, f32[256,256]{1,0:T(8,128)S(1)}, f32[256,256]{1,0:T(8,128)S(1)}, f32[256,256]{1,0:T(8,128)S(1)}, f32[256,...) custom-call(s32[3]{0:T(128)S(1)} %pad_add_fusion.place.refs_0_, ...), custom_call_target="tpu_custom_call" | custom-call | tf_op jit(solution)/shard_map/pallas_call | solution.py:705
  135.0 4.3 %collective-permute-done.39.halo = bf16[2,2,32,128]{3,2,1,0:T(8,128)(2,1)S(1)} collective-permute-done((bf16[2,2,32,128]{3,2,1,0:T(8,128)(2,1)S(1)}, bf16[2,2,32,128]{3,2,1,0:T(8,128)(2,1)S(1)}, u32[]{:S(2)}, u32[]{:S(2)}) %collective-permute-start.39) | collective-permute-done | bytes 32800 | tf_op jit(solution)/shard_map/ppermute | solution.py:745
  161.4 6.1 %shard_map.199 = (bf16[256,256]{1,0:T(8,128)(2,1)S(1)}, f32[256,256]{1,0:T(8,128)S(1)}, f32[256,256]{1,0:T(8,128)S(1)}, f32[256,256]{1,0:T(8,128)S(1)}, f32[256,...) custom-call(s32[3]{0:T(128)S(1)} %pad_add_fusion.place.refs_0_, ...), custom_call_target="tpu_custom_call" | custom-call | tf_op jit(solution)/shard_map/pallas_call | solution.py:705
  168.8 22.9 %collective-permute-done.48.halo = bf16[2,2,32,128]{3,2,1,0:T(8,128)(2,1)S(1)} collective-permute-done((bf16[2,2,32,128]{3,2,1,0:T(8,128)(2,1)S(1)}, bf16[2,2,32,128]{3,2,1,0:T(8,128)(2,1)S(1)}, u32[]{:S(2)}, u32[]{:S(2)}) %collective-permute-start.48) | collective-permute-done | bytes 32800 | tf_op jit(solution)/shard_map/ppermute | solution.py:745
  197.9 7.2 %all-to-all-start = ((bf16[16,208,128]{2,1,0:T(8,128)(2,1)}), bf16[16,208,128]{2,1,0:T(8,128)(2,1)S(1)}, u32[]{:S(2)}, u32[]{:S(2)}) async-start(bf16[16,208,128]{2,1,0:T(8,128)(2,1)} %get-tuple-element.270), calls=%async_computation | async-start | bytes 1703936 | tf_op jit(solution)/shard_map/all_to_all | solution.py:991
  215.5 18.2 %collective-permute-done.58.got = bf16[768,512]{1,0:T(8,128)(2,1)S(1)} collective-permute-done((bf16[768,512]{1,0:T(8,128)(2,1)S(1)}, bf16[768,512]{1,0:T(8,128)(2,1)S(1)}, u32[]{:S(2)}, u32[]{:S(2)}) %collective-permute-start.58) | collective-permute-done | bytes 786464 | tf_op jit(solution)/shard_map/ppermute | solution.py:731
  234.8 4.6 %all-to-all-start.2 = ((bf16[4,192,512]{2,1,0:T(8,128)(2,1)}), bf16[4,192,512]{2,1,0:T(8,128)(2,1)S(1)}, u32[]{:S(2)}, u32[]{:S(2)}) async-start(bf16[4,192,512]{2,1,0:T(8,128)(2,1)} %bitcast.14), calls=%async_computation.2 | async-start | bytes 1572864 | tf_op jit(solution)/shard_map/all_to_all | solution.py:785
  239.4 7.3 %collective-permute-done.60.got = bf16[1152,512]{1,0:T(8,128)(2,1)} collective-permute-done((bf16[1152,512]{1,0:T(8,128)(2,1)}, bf16[1152,512]{1,0:T(8,128)(2,1)}, u32[]{:S(2)}, u32[]{:S(2)}) %collective-permute-start.60) | collective-permute-done | bytes 1179680 | tf_op jit(solution)/shard_map/ppermute | solution.py:726
  249.7 14.0 %collective-permute-done.61.got = bf16[576,512]{1,0:T(8,128)(2,1)S(1)} collective-permute-done((bf16[576,512]{1,0:T(8,128)(2,1)S(1)}, bf16[576,512]{1,0:T(8,128)(2,1)S(1)}, u32[]{:S(2)}, u32[]{:S(2)}) %collective-permute-start.61) | collective-permute-done | bytes 589856 | tf_op jit(solution)/shard_map/ppermute | solution.py:731
  264.7 4.6 %all-to-all-start.4 = ((bf16[4,144,512]{2,1,0:T(8,128)(2,1)}), bf16[4,144,512]{2,1,0:T(8,128)(2,1)S(1)}, u32[]{:S(2)}, u32[]{:S(2)}) async-start(bf16[4,144,512]{2,1,0:T(8,128)(2,1)} %bitcast.18), calls=%async_computation.4 | async-start | bytes 1179648 | tf_op jit(solution)/shard_map/all_to_all | solution.py:785
  270.3 14.2 %all-to-all-done.4 = bf16[4,144,512]{2,1,0:T(8,128)(2,1)S(1)} async-done(((bf16[4,144,512]{2,1,0:T(8,128)(2,1)}), bf16[4,144,512]{2,1,0:T(8,128)(2,1)S(1)}, u32[]{:S(2)}, u32[]{:S(2)}) %all-to-all-start.4) | async-done | bytes 589856 | tf_op jit(solution)/shard_map/all_to_all | solution.py:785
  284.4 3.5 all-to-all-start.3
  288.8 18.7 %all-to-all-done.3 = bf16[4,192,512]{2,1,0:T(8,128)(2,1)S(1)} async-done(((bf16[4,192,512]{2,1,0:T(8,128)(2,1)}), bf16[4,192,512]{2,1,0:T(8,128)(2,1)S(1)}, u32[]{:S(2)}, u32[]{:S(2)}) %all-to-all-start.3) | async-done | bytes 786464 | tf_op jit(solution)/shard_map/all_to_all | solution.py:785
  307.5 3.5 all-to-all-start.5
  315.4 10.9 %all-to-all-done.5 = bf16[4,144,512]{2,1,0:T(8,128)(2,1)S(1)} async-done(((bf16[4,144,512]{2,1,0:T(8,128)(2,1)}), bf16[4,144,512]{2,1,0:T(8,128)(2,1)S(1)}, u32[]{:S(2)}, u32[]{:S(2)}) %all-to-all-start.5) | async-done | bytes 589856 | tf_op jit(solution)/shard_map/all_to_all | solution.py:785
  326.3 3.5 all-to-all-start.1
  336.5 15.2 %collective-permute-done.62.high_other = bf16[576,512]{1,0:T(8,128)(2,1)} collective-permute-done((bf16[576,512]{1,0:T(8,128)(2,1)S(1)}, bf16[576,512]{1,0:T(8,128)(2,1)}, u32[]{:S(2)}, u32[]{:S(2)}) %collective-permute-start.62) | collective-permute-done | bytes 589856 | tf_op jit(solution)/shard_map/ppermute | solution.py:731
  351.7 3.4 shard_map.213
  (236 shorter events, 130.4 us)
Async XLA Ops:
  16.2 25.1 %collective-permute-start.14 = (bf16[512,256]{1,0:T(8,128)(2,1)S(1)}, bf16[512,256]{1,0:T(8,128)(2,1)S(1)}, u32[]{:S(2)}, u32[]{:S(2)}) collective-permute-start(bf16[512,256]{1,0:T(8,128)(2,1)S(1)} %dynamic-slice_bitcast_fusion.3), channel_id=1, source_target_pairs={{0,2},{1,3},{2,0},{3,1},{4,6},{5,7},{6,4},{7,5},{8,10},{9,11},{10,... | collective-permute-start | bytes 786440 | tf_op jit(solution)/shard_map/ppermute | solution.py:726
  31.4 21.0 %collective-permute-start.15 = (bf16[256,512]{1,0:T(8,128)(2,1)S(1)}, bf16[256,512]{1,0:T(8,128)(2,1)S(1)}, u32[]{:S(2)}, u32[]{:S(2)}) collective-permute-start(bf16[256,512]{1,0:T(8,128)(2,1)S(1)} %get-tuple-element.180), channel_id=1, source_target_pairs={{0,2},{1,3},{2,0},{3,1},{4,6},{5,7},{6,4},{7,5},{8,10},{9,11},{10,... | collective-permute-start | bytes 786440 | tf_op jit(solution)/shard_map/ppermute | solution.py:726
  33.0 17.6 %collective-permute-start.6 = (bf16[128,512]{1,0:T(8,128)(2,1)S(1)}, bf16[128,512]{1,0:T(8,128)(2,1)S(1)}, u32[]{:S(2)}, u32[]{:S(2)}) collective-permute-start(bf16[128,512]{1,0:T(8,128)(2,1)S(1)} %get-tuple-element.173), channel_id=1, source_target_pairs={{0,2},{1,3},{2,0},{3,1},{4,6},{5,7},{6,4},{7,5},{8,10},{9,11},{10,... | collective-permute-start | bytes 393224 | tf_op jit(solution)/shard_map/ppermute | solution.py:726
  37.6 13.5 %collective-permute-start.10 = (bf16[2,144,128]{2,1,0:T(8,128)(2,1)S(1)}, bf16[2,144,128]{2,1,0:T(8,128)(2,1)S(1)}, u32[]{:S(2)}, u32[]{:S(2)}) collective-permute-start(bf16[2,144,128]{2,1,0:T(8,128)(2,1)S(1)} %get-tuple-element.176), channel_id=1, source_target_pairs={{0,8},{1,9},{2,10},{3,11},{4,12},{5,13},{6,14},{7,15},{8,16},{9,17... | collective-permute-start | bytes 221192 | tf_op jit(solution)/shard_map/ppermute | solution.py:745
  63.7 24.5 %collective-permute-start.29 = (bf16[512,256]{1,0:T(8,128)(2,1)S(1)}, bf16[512,256]{1,0:T(8,128)(2,1)S(1)}, u32[]{:S(2)}, u32[]{:S(2)}) collective-permute-start(bf16[512,256]{1,0:T(8,128)(2,1)S(1)} %dynamic-slice_bitcast_fusion.1), channel_id=1, source_target_pairs={{0,2},{1,3},{2,0},{3,1},{4,6},{5,7},{6,4},{7,5},{8,10},{9,11},{10,... | collective-permute-start | bytes 786440 | tf_op jit(solution)/shard_map/ppermute | solution.py:726
  65.0 24.5 %collective-permute-start.30 = (bf16[256,512]{1,0:T(8,128)(2,1)S(1)}, bf16[256,512]{1,0:T(8,128)(2,1)S(1)}, u32[]{:S(2)}, u32[]{:S(2)}) collective-permute-start(bf16[256,512]{1,0:T(8,128)(2,1)S(1)} %get-tuple-element.198), channel_id=1, source_target_pairs={{0,2},{1,3},{2,0},{3,1},{4,6},{5,7},{6,4},{7,5},{8,10},{9,11},{10,... | collective-permute-start | bytes 786440 | tf_op jit(solution)/shard_map/ppermute | solution.py:726
  67.2 14.1 %collective-permute-start.22 = (bf16[2,144,128]{2,1,0:T(8,128)(2,1)S(1)}, bf16[2,144,128]{2,1,0:T(8,128)(2,1)S(1)}, u32[]{:S(2)}, u32[]{:S(2)}) collective-permute-start(bf16[2,144,128]{2,1,0:T(8,128)(2,1)S(1)} %get-tuple-element.193.refs_0_), channel_id=1, source_target_pairs={{0,2},{1,3},{2,0},{3,1},{4,6},{5,7},{6,4},{7,5},{8,10},{9,11},{10,... | collective-permute-start | bytes 221192 | tf_op jit(solution)/shard_map/ppermute | solution.py:745
  68.5 14.0 %collective-permute-start.23 = (bf16[2,144,128]{2,1,0:T(8,128)(2,1)S(1)}, bf16[2,144,128]{2,1,0:T(8,128)(2,1)S(1)}, u32[]{:S(2)}, u32[]{:S(2)}) collective-permute-start(bf16[2,144,128]{2,1,0:T(8,128)(2,1)S(1)} %get-tuple-element.193.refs_0_), channel_id=1, source_target_pairs={{0,4},{1,5},{2,6},{3,7},{4,0},{5,1},{6,2},{7,3},{8,12},{9,13},{10,... | collective-permute-start | bytes 221192 | tf_op jit(solution)/shard_map/ppermute | solution.py:745
  69.0 13.5 %collective-permute-start.24 = (bf16[2,144,128]{2,1,0:T(8,128)(2,1)S(1)}, bf16[2,144,128]{2,1,0:T(8,128)(2,1)S(1)}, u32[]{:S(2)}, u32[]{:S(2)}) collective-permute-start(bf16[2,144,128]{2,1,0:T(8,128)(2,1)S(1)} %get-tuple-element.193.refs_0_), channel_id=1, source_target_pairs={{0,6},{1,7},{2,4},{3,5},{4,2},{5,3},{6,0},{7,1},{8,14},{9,15},{10,... | collective-permute-start | bytes 221192 | tf_op jit(solution)/shard_map/ppermute | solution.py:745
  81.2 19.4 %collective-permute-start.21 = (bf16[128,512]{1,0:T(8,128)(2,1)S(1)}, bf16[128,512]{1,0:T(8,128)(2,1)S(1)}, u32[]{:S(2)}, u32[]{:S(2)}) collective-permute-start(bf16[128,512]{1,0:T(8,128)(2,1)S(1)} %get-tuple-element.192), channel_id=1, source_target_pairs={{0,2},{1,3},{2,0},{3,1},{4,6},{5,7},{6,4},{7,5},{8,10},{9,11},{10,... | collective-permute-start | bytes 393224 | tf_op jit(solution)/shard_map/ppermute | solution.py:726
  83.2 17.5 %collective-permute-start.25 = (bf16[2,144,128]{2,1,0:T(8,128)(2,1)S(1)}, bf16[2,144,128]{2,1,0:T(8,128)(2,1)S(1)}, u32[]{:S(2)}, u32[]{:S(2)}) collective-permute-start(bf16[2,144,128]{2,1,0:T(8,128)(2,1)S(1)} %get-tuple-element.195), channel_id=1, source_target_pairs={{0,8},{1,9},{2,10},{3,11},{4,12},{5,13},{6,14},{7,15},{8,16},{9,17... | collective-permute-start | bytes 221192 | tf_op jit(solution)/shard_map/ppermute | solution.py:745
  84.6 16.1 %collective-permute-start.26 = (bf16[2,144,128]{2,1,0:T(8,128)(2,1)S(1)}, bf16[2,144,128]{2,1,0:T(8,128)(2,1)S(1)}, u32[]{:S(2)}, u32[]{:S(2)}) collective-permute-start(bf16[2,144,128]{2,1,0:T(8,128)(2,1)S(1)} %get-tuple-element.195), channel_id=1, source_target_pairs={{0,16},{1,17},{2,18},{3,19},{4,20},{5,21},{6,22},{7,23},{8,24},{9,... | collective-permute-start | bytes 221192 | tf_op jit(solution)/shard_map/ppermute | solution.py:745
  93.8 13.2 %collective-permute-start.31 = (bf16[512,256]{1,0:T(8,128)(2,1)S(1)}, bf16[512,256]{1,0:T(8,128)(2,1)S(1)}, u32[]{:S(2)}, u32[]{:S(2)}) collective-permute-start(bf16[512,256]{1,0:T(8,128)(2,1)S(1)} %collective-permute-done.29.up_a.refs_7_), channel_id=1, source_target_pairs={{0,4},{4,0},{8,12},{12,8},{16,20},{20,16},{24,28},{28,24},{1,5},{5... | collective-permute-start | bytes 786440 | tf_op jit(solution)/shard_map/ppermute | solution.py:731
  123.4 15.8 %collective-permute-start.43 = (bf16[2,144,128]{2,1,0:T(8,128)(2,1)S(1)}, bf16[2,144,128]{2,1,0:T(8,128)(2,1)S(1)}, u32[]{:S(2)}, u32[]{:S(2)}) collective-permute-start(bf16[2,144,128]{2,1,0:T(8,128)(2,1)S(1)} %get-tuple-element.231), channel_id=1, source_target_pairs={{8,0},{9,1},{10,2},{11,3},{12,4},{13,5},{14,6},{15,7},{16,8},{17,9... | collective-permute-start | bytes 221192 | tf_op jit(solution)/shard_map/ppermute | solution.py:745
  124.7 14.5 %collective-permute-start.44 = (bf16[2,144,128]{2,1,0:T(8,128)(2,1)S(1)}, bf16[2,144,128]{2,1,0:T(8,128)(2,1)S(1)}, u32[]{:S(2)}, u32[]{:S(2)}) collective-permute-start(bf16[2,144,128]{2,1,0:T(8,128)(2,1)S(1)} %get-tuple-element.231), channel_id=1, source_target_pairs={{16,0},{17,1},{18,2},{19,3},{20,4},{21,5},{22,6},{23,7},{24,8},{25... | collective-permute-start | bytes 221192 | tf_op jit(solution)/shard_map/ppermute | solution.py:745
  155.9 49.2 %collective-permute-start.57 = (bf16[1536,512]{1,0:T(8,128)(2,1)}, bf16[1536,512]{1,0:T(8,128)(2,1)}, u32[]{:S(2)}, u32[]{:S(2)}) collective-permute-start(bf16[1536,512]{1,0:T(8,128)(2,1)} %get-tuple-element.285), channel_id=1, source_target_pairs={{0,2},{1,3},{2,0},{3,1},{4,6},{5,7},{6,4},{7,5},{8,10},{9,11},{10,... | collective-permute-start | bytes 4718600 | tf_op jit(solution)/shard_map/ppermute | solution.py:726
  157.5 34.2 %collective-permute-start.52 = (bf16[2,144,128]{2,1,0:T(8,128)(2,1)S(1)}, bf16[2,144,128]{2,1,0:T(8,128)(2,1)S(1)}, u32[]{:S(2)}, u32[]{:S(2)}) collective-permute-start(bf16[2,144,128]{2,1,0:T(8,128)(2,1)S(1)} %get-tuple-element.255), channel_id=1, source_target_pairs={{8,0},{9,1},{10,2},{11,3},{12,4},{13,5},{14,6},{15,7},{16,8},{17,9... | collective-permute-start | bytes 221192 | tf_op jit(solution)/shard_map/ppermute | solution.py:745
  158.8 32.9 %collective-permute-start.53 = (bf16[2,144,128]{2,1,0:T(8,128)(2,1)S(1)}, bf16[2,144,128]{2,1,0:T(8,128)(2,1)S(1)}, u32[]{:S(2)}, u32[]{:S(2)}) collective-permute-start(bf16[2,144,128]{2,1,0:T(8,128)(2,1)S(1)} %get-tuple-element.255), channel_id=1, source_target_pairs={{16,0},{17,1},{18,2},{19,3},{20,4},{21,5},{22,6},{23,7},{24,8},{25... | collective-permute-start | bytes 221192 | tf_op jit(solution)/shard_map/ppermute | solution.py:745
  160.1 31.6 %collective-permute-start.54 = (bf16[2,144,128]{2,1,0:T(8,128)(2,1)S(1)}, bf16[2,144,128]{2,1,0:T(8,128)(2,1)S(1)}, u32[]{:S(2)}, u32[]{:S(2)}) collective-permute-start(bf16[2,144,128]{2,1,0:T(8,128)(2,1)S(1)} %get-tuple-element.255), channel_id=1, source_target_pairs={{24,0},{25,1},{26,2},{27,3},{28,4},{29,5},{30,6},{31,7}} | collective-permute-start | bytes 221192 | tf_op jit(solution)/shard_map/ppermute | solution.py:745
  167.5 24.2 %collective-permute-start.48 = (bf16[2,2,32,128]{3,2,1,0:T(8,128)(2,1)S(1)}, bf16[2,2,32,128]{3,2,1,0:T(8,128)(2,1)S(1)}, u32[]{:S(2)}, u32[]{:S(2)}) collective-permute-start(bf16[2,2,32,128]{3,2,1,0:T(8,128)(2,1)S(1)} %get-tuple-element.252), channel_id=1, source_target_pairs={{2,0},{3,1},{4,2},{5,3},{6,4},{7,5},{8,6},{9,7},{10,8},{11,9},{12,... | collective-permute-start | bytes 98312 | tf_op jit(solution)/shard_map/ppermute | solution.py:745
  197.9 36.9 %all-to-all-start = ((bf16[16,208,128]{2,1,0:T(8,128)(2,1)}), bf16[16,208,128]{2,1,0:T(8,128)(2,1)S(1)}, u32[]{:S(2)}, u32[]{:S(2)}) async-start(bf16[16,208,128]{2,1,0:T(8,128)(2,1)} %get-tuple-element.270), calls=%async_computation | async-start | bytes 1703936 | tf_op jit(solution)/shard_map/all_to_all | solution.py:991
  208.6 25.1 %collective-permute-start.58 = (bf16[768,512]{1,0:T(8,128)(2,1)S(1)}, bf16[768,512]{1,0:T(8,128)(2,1)S(1)}, u32[]{:S(2)}, u32[]{:S(2)}) collective-permute-start(bf16[768,512]{1,0:T(8,128)(2,1)S(1)} %get-tuple-element.287), channel_id=1, source_target_pairs={{0,4},{4,0},{8,12},{12,8},{16,20},{20,16},{24,28},{28,24},{1,5},{5... | collective-permute-start | bytes 2359304 | tf_op jit(solution)/shard_map/ppermute | solution.py:731
  214.1 32.7 %collective-permute-start.60 = (bf16[1152,512]{1,0:T(8,128)(2,1)}, bf16[1152,512]{1,0:T(8,128)(2,1)}, u32[]{:S(2)}, u32[]{:S(2)}) collective-permute-start(bf16[1152,512]{1,0:T(8,128)(2,1)} %get-tuple-element.298), channel_id=1, source_target_pairs={{0,2},{1,3},{2,0},{3,1},{4,6},{5,7},{6,4},{7,5},{8,10},{9,11},{10,... | collective-permute-start | bytes 3538952 | tf_op jit(solution)/shard_map/ppermute | solution.py:726
  234.8 29.9 %all-to-all-start.2 = ((bf16[4,192,512]{2,1,0:T(8,128)(2,1)}), bf16[4,192,512]{2,1,0:T(8,128)(2,1)S(1)}, u32[]{:S(2)}, u32[]{:S(2)}) async-start(bf16[4,192,512]{2,1,0:T(8,128)(2,1)} %bitcast.14), calls=%async_computation.2 | async-start | bytes 1572864 | tf_op jit(solution)/shard_map/all_to_all | solution.py:785
  248.4 15.3 %collective-permute-start.61 = (bf16[576,512]{1,0:T(8,128)(2,1)S(1)}, bf16[576,512]{1,0:T(8,128)(2,1)S(1)}, u32[]{:S(2)}, u32[]{:S(2)}) collective-permute-start(bf16[576,512]{1,0:T(8,128)(2,1)S(1)} %get-tuple-element.300), channel_id=1, source_target_pairs={{0,4},{4,0},{8,12},{12,8},{16,20},{20,16},{24,28},{28,24},{1,5},{5... | collective-permute-start | bytes 1769480 | tf_op jit(solution)/shard_map/ppermute | solution.py:731
  264.7 19.8 %all-to-all-start.4 = ((bf16[4,144,512]{2,1,0:T(8,128)(2,1)}), bf16[4,144,512]{2,1,0:T(8,128)(2,1)S(1)}, u32[]{:S(2)}, u32[]{:S(2)}) async-start(bf16[4,144,512]{2,1,0:T(8,128)(2,1)} %bitcast.18), calls=%async_computation.4 | async-start | bytes 1179648 | tf_op jit(solution)/shard_map/all_to_all | solution.py:785
  284.4 23.1 %all-to-all-start.3 = ((bf16[4,192,512]{2,1,0:T(8,128)(2,1)}), bf16[4,192,512]{2,1,0:T(8,128)(2,1)S(1)}, u32[]{:S(2)}, u32[]{:S(2)}) async-start(bf16[4,192,512]{2,1,0:T(8,128)(2,1)} %bitcast.16), calls=%async_computation.3 | async-start | bytes 1572864 | tf_op jit(solution)/shard_map/all_to_all | solution.py:785
  307.5 18.8 %all-to-all-start.5 = ((bf16[4,144,512]{2,1,0:T(8,128)(2,1)}), bf16[4,144,512]{2,1,0:T(8,128)(2,1)S(1)}, u32[]{:S(2)}, u32[]{:S(2)}) async-start(bf16[4,144,512]{2,1,0:T(8,128)(2,1)} %bitcast.20), calls=%async_computation.5 | async-start | bytes 1179648 | tf_op jit(solution)/shard_map/all_to_all | solution.py:785
  313.9 15.9 %collective-permute-start.34 = (bf16[256,128]{1,0:T(8,128)(2,1)}, bf16[256,128]{1,0:T(8,128)(2,1)S(1)}, u32[]{:S(2)}, u32[]{:S(2)}) collective-permute-start(bf16[256,128]{1,0:T(8,128)(2,1)} %get-tuple-element.204), channel_id=1, source_target_pairs={{0,2},{1,3},{2,0},{3,1},{4,6},{5,7},{6,4},{7,5},{8,10},{9,11},{10,... | collective-permute-start | bytes 196616 | tf_op jit(solution)/shard_map/ppermute | solution.py:726
  315.4 36.3 %collective-permute-start.59 = (bf16[768,512]{1,0:T(8,128)(2,1)S(1)}, bf16[768,512]{1,0:T(8,128)(2,1)S(1)}, u32[]{:S(2)}, u32[]{:S(2)}) collective-permute-start(bf16[768,512]{1,0:T(8,128)(2,1)S(1)} %bitcast.32), channel_id=1, source_target_pairs={{0,4},{4,0},{8,12},{12,8},{16,20},{20,16},{24,28},{28,24},{1,5},{5... | collective-permute-start | bytes 2359304 | tf_op jit(solution)/shard_map/ppermute | solution.py:731
  326.3 28.8 %all-to-all-start.1 = ((bf16[8,192,128]{2,1,0:T(8,128)(2,1)}), bf16[8,192,128]{2,1,0:T(8,128)(2,1)S(1)}, u32[]{:S(2)}, u32[]{:S(2)}) async-start(bf16[8,192,128]{2,1,0:T(8,128)(2,1)} %get-tuple-element.272), calls=%async_computation.1 | async-start | bytes 786432 | tf_op jit(solution)/shard_map/all_to_all | solution.py:997
  330.6 21.1 %collective-permute-start.62 = (bf16[576,512]{1,0:T(8,128)(2,1)S(1)}, bf16[576,512]{1,0:T(8,128)(2,1)}, u32[]{:S(2)}, u32[]{:S(2)}) collective-permute-start(bf16[576,512]{1,0:T(8,128)(2,1)S(1)} %bitcast.35), channel_id=1, source_target_pairs={{0,4},{4,0},{8,12},{12,8},{16,20},{20,16},{24,28},{28,24},{1,5},{5... | collective-permute-start | bytes 1769480 | tf_op jit(solution)/shard_map/ppermute | solution.py:731
  (74 other events, 501.8 us)

commit v3 on v2

--- a/solution.py
+++ b/solution.py
@@ -297,11 +297,9 @@
         halo_out[quarter, 1] = values[rows - HALO :]
 
 
-def local_kernel(place, qkv, halo, causal, band, near_out, one_out, two_out, sums_out):
-    rows = qkv.shape[1]
+def far_kernel(qkv, causal, one_out, two_out, sums_out):
     masks = jnp.concatenate([causal[...], causal[...]], axis=0)
     for pair in range(2):
-        quarter = place[0] if pair == 0 else 1 - place[0]
         lanes = slice(pair * LANES, (pair + 1) * LANES)
         queries, keys, values = qkv[0, :, lanes], qkv[1, :, lanes], qkv[2, :, lanes]
         maps_q, maps_k = kernel_maps(queries.astype(f32)), kernel_maps(keys.astype(f32))
@@ -309,6 +307,14 @@
             attn = dot_nt(split_heads(query), key).astype(bf16) * masks
             out[:, lanes] = merge_heads(dot(attn, values))
         sums_out[:, lanes] = dot(causal[...], maps_k[0])
+
+
+def near_kernel(place, qkv, halo, band, near_out):
+    rows = qkv.shape[1]
+    for pair in range(2):
+        quarter = place[0] if pair == 0 else 1 - place[0]
+        lanes = slice(pair * LANES, (pair + 1) * LANES)
+        queries, keys, values = qkv[0, :, lanes], qkv[1, :, lanes], qkv[2, :, lanes]
         ext_keys = extend(halo[quarter, 0], keys)
         ext_values = extend(halo[quarter, 1], values)
         for tile in range(rows // TILE):
@@ -485,49 +491,24 @@
         )
 
 
-def local_back_kernel(
-    layer, place, qkv, halo, causal, causal_t, band, carried, state, prefix, d_mixed, num_one, num_two, d_zeta, blends,
-    dq_out, dk_one_out, dk_two_out, dk_near_out, dv_out, halo_out, blend_out, near_k, near_v,
+def near_back_kernel(
+    layer, place, qkv, halo, band, d_mixed, blends, dq_out, dk_out, dv_out, halo_out, blend_out, near_k, near_v
 ):
     rows = qkv.shape[1]
-    masks = jnp.concatenate([causal[...], causal[...]], axis=0)
-    masks_t = jnp.concatenate([causal_t[...], causal_t[...]], axis=1)
     row_low = lax.broadcasted_iota(jnp.int32, (2 * TILE, 1), 0) < TILE
-    blend = blends[2 * LAYERS + 3 * layer : 2 * LAYERS + 3 * layer + 3]
+    row = 2 * LAYERS + 3 * layer
     for pair in range(2):
         quarter = place[0] if pair == 0 else 1 - place[0]
         lanes = slice(pair * LANES, (pair + 1) * LANES)
         queries, keys, values = qkv[0, :, lanes], qkv[1, :, lanes], qkv[2, :, lanes]
         grads = d_mixed[:, lanes]
-        state_one, state_two, unused_total = get_state(state, quarter)
-        query_one, query_two = kernel_maps(queries.astype(f32))
-        key_one, key_two = kernel_maps(keys.astype(f32))
-        d_values = None
-        d_queries = []
-        for query, key, num, square, out in (
-            (query_one, key_one, num_one[:, lanes], state_one, dk_one_out),
-            (query_two, key_two, num_two[:, lanes], state_two, dk_two_out),
-        ):
-            query_split, num_split = split_heads(query), split_heads(num)
-            attn_t = dot_nt(key, query_split).astype(bf16) * masks_t
-            grad = dot_nt(num_split, values).astype(bf16) * masks
-            grad_t = dot_nt(values, num_split).astype(bf16) * masks_t
-            product = dot(attn_t, num_split)
-            d_values = product if d_values is None else d_values + product
-            d_queries.append(merge_heads(dot(grad, key)) + carried[...] * dot_nt(num, square))
-            out[:, lanes] = dot(grad_t, query_split)
-        zeta = d_zeta[:, lanes]
-        d_queries[0] += zeta * prefix[:, lanes]
-        dk_one_out[:, lanes] += dot(causal_t[...], (zeta * query_one.astype(f32)).astype(bf16))
-
+        blend = blends[row : row + 1, lanes]
         ext_keys = extend(halo[quarter, 0], keys)
         ext_values = extend(halo[quarter, 1], values)
         near_k[...] = jnp.zeros_like(near_k)
         near_v[...] = jnp.zeros_like(near_v)
-        blend_low, blend_high = blend[0:1, pair * LANES : pair * LANES + 1], blend[0:1, pair * LANES + HD : pair * LANES + HD + 1]
-        blend_rows = jnp.where(row_low, blend_low, blend_high)
+        blend_rows = jnp.where(row_low, blend[:, :1], blend[:, HD : HD + 1])
         sums = None
-        dq_near = []
         for tile in range(rows // TILE):
             at = slice(tile * TILE, (tile + 1) * TILE)
             window = slice(tile * TILE, tile * TILE + LANES)
@@ -540,18 +521,50 @@
             inner = jnp.sum(probs * d_probs, axis=1, keepdims=True)
             sums = inner if sums is None else sums + inner
             d_scores = (probs * (d_probs - inner) * blend_rows).astype(bf16)
-            dq_near.append(merge_heads(dot(d_scores, ext_keys[window])))
+            dq_out[at, lanes] = score_scale * merge_heads(dot(d_scores, ext_keys[window]))
             near_k[window] += dot_tn(d_scores, query_split)
             near_v[window] += dot_tn(probs.astype(bf16), grad_split)
         sum_low = jnp.sum(sums[:TILE], axis=0, keepdims=True)
         sum_high = jnp.sum(sums[TILE:], axis=0, keepdims=True)
         blend_out[0:1, lanes] = jnp.where(low_lanes(1), sum_low, sum_high) * (1.0 / HD)
+        dk_out[:, lanes] = score_scale * near_k[HALO : HALO + rows]
+        dv_out[:, lanes] = blend * near_v[HALO : HALO + rows]
+        halo_out[quarter, 0] = (score_scale * near_k[0:HALO]).astype(bf16)
+        halo_out[quarter, 1] = (blend * near_v[0:HALO]).astype(bf16)
+
+
+def far_back_kernel(
+    place, qkv, causal, causal_t, carried, state, prefix, num_one, num_two, d_zeta, dq_near, dv_near,
+    dq_out, dk_one_out, dk_two_out, dv_out,
+):
+    masks = jnp.concatenate([causal[...], causal[...]], axis=0)
+    masks_t = jnp.concatenate([causal_t[...], causal_t[...]], axis=1)
+    for pair in range(2):
+        quarter = place[0] if pair == 0 else 1 - place[0]
+        lanes = slice(pair * LANES, (pair + 1) * LANES)
+        queries, keys, values = qkv[0, :, lanes], qkv[1, :, lanes], qkv[2, :, lanes]
+        state_one, state_two, unused_total = get_state(state, quarter)
+        query_one, query_two = kernel_maps(queries.astype(f32))
+        key_one, key_two = kernel_maps(keys.astype(f32))
+        d_values = dv_near[:, lanes]
+        d_queries = []
+        for query, key, num, square, out in (
+            (query_one, key_one, num_one[:, lanes], state_one, dk_one_out),
+            (query_two, key_two, num_two[:, lanes], state_two, dk_two_out),
+        ):
+            query_split, num_split = split_heads(query), split_heads(num)
+            attn_t = dot_nt(key, query_split).astype(bf16) * masks_t
+            grad = dot_nt(num_split, values).astype(bf16) * masks
+            grad_t = dot_nt(values, num_split).astype(bf16) * masks_t
+            d_values = d_values + dot(attn_t, num_split)
+            d_queries.append(merge_heads(dot(grad, key)) + carried[...] * dot_nt(num, square))
+            out[:, lanes] = dot(grad_t, query_split)
+        zeta = d_zeta[:, lanes]
+        d_queries[0] += zeta * prefix[:, lanes]
+        dk_one_out[:, lanes] += dot(causal_t[...], (zeta * query_one.astype(f32)).astype(bf16))
         back = maps_back(queries.astype(f32), d_queries[0], d_queries[1])
-        dq_out[:, lanes] = (back + score_scale * jnp.concatenate(dq_near, axis=0)).astype(bf16)
-        dk_near_out[:, lanes] = score_scale * near_k[HALO : HALO + rows]
-        dv_out[:, lanes] = d_values + blend[0:1, lanes] * near_v[HALO : HALO + rows]
-        halo_out[quarter, 0] = (score_scale * near_k[0:HALO]).astype(bf16)
-        halo_out[quarter, 1] = (blend[0:1, lanes] * near_v[0:HALO]).astype(bf16)
+        dq_out[:, lanes] = (back + dq_near[:, lanes]).astype(bf16)
+        dv_out[:, lanes] = d_values
 
 
 def qkv_back_kernel(
@@ -588,53 +601,101 @@
     part_out[...] = total.astype(bf16)
 
 
-def wide_grads_kernel(with_qkv, place, normed, act_own, act_far, d_up_own, d_up_far, grad_rows, mixed, out_rows, *refs):
-    if with_qkv:
-        above, d_qkv, own, far = refs
-    else:
-        own, far = refs
-    units = act_own.shape[1]
-    piece = units // 2
+JOB_REFS = {"up": 3, "down": 3, "out": 2, "qkv": 2}
+
+
+def job_rows(job, units):
+    return {"up": D, "down": units, "out": LANES, "qkv": 3 * LANES}[job]
+
+
+def wide_grads_kernel(jobs, place, *refs):
+    refs, (own_a, send_a, keep_b, send_b, own, far) = refs[:-6], refs[-6:]
     side = lax.rem(place[2], 2)
-    own[:D] = dot_tn(normed[...], d_up_own[...]).astype(bf16)
-    own[D : D + units] = dot_tn(act_own[...], grad_rows[...]).astype(bf16)
-    d_up = dot_tn(normed[...], d_up_far[...]).astype(bf16)
-    d_down = dot_tn(act_far[...], grad_rows[...]).astype(bf16)
-    far[:D] = jnp.where(side == 0, d_up, jnp.concatenate([d_up[:, piece:], d_up[:, :piece]], axis=1))
-    far[D : D + units] = jnp.where(side == 0, d_down, jnp.concatenate([d_down[piece:], d_down[:piece]], axis=0))
-    d_out = dot_tn(mixed[...], out_rows[...]).astype(bf16)
-    at = D + units
-    own[at : at + LANES] = d_out[:LANES]
-    far[at : at + LANES] = d_out[LANES:]
-    if with_qkv:
-        at += LANES
-        for kind in range(3):
-            found = dot_tn(above[...], d_qkv[kind]).astype(bf16)
-            for block in range(D // LANES):
-                rows = slice(at + kind * LANES, at + (kind + 1) * LANES)
-                lanes = slice(block * LANES, (block + 1) * LANES)
-                own[rows, lanes] = found[lanes, :LANES]
-                far[rows, lanes] = found[lanes, LANES:]
-
-
-def halve_kernel(place, own, got, keep_out, send_out):
-    rows = own.shape[0] // 2
-    total = own[...].astype(f32) + got[...].astype(f32)
+    at = 0
+    for job in jobs:
+        mine, refs = refs[: JOB_REFS[job]], refs[JOB_REFS[job] :]
+        if job == "up":
+            normed, grad_own, grad_far = mine
+            units = grad_own.shape[1]
+            piece = units // 2
+            own[at : at + D] = dot_tn(normed[...], grad_own[...]).astype(bf16)
+            found = dot_tn(normed[...], grad_far[...]).astype(bf16)
+            turned = jnp.concatenate([found[:, piece:], found[:, :piece]], axis=1)
+            far[at : at + D] = jnp.where(side == 0, found, turned)
+            at += D
+        elif job == "down":
+            act_own, act_far, grad = mine
+            units = act_own.shape[1]
+            piece = units // 2
+            own[at : at + units] = dot_tn(act_own[...], grad[...]).astype(bf16)
+            found = dot_tn(act_far[...], grad[...]).astype(bf16)
+            turned = jnp.concatenate([found[piece:], found[:piece]], axis=0)
+            far[at : at + units] = jnp.where(side == 0, found, turned)
+            at += units
+        elif job == "out":
+            mixed, grad = mine
+            found = dot_tn(mixed[...], grad[...]).astype(bf16)
+            own[at : at + LANES] = found[:LANES]
+            far[at : at + LANES] = found[LANES:]
+            at += LANES
+        else:
+            normed, d_qkv = mine
+            for kind in range(3):
+                found = dot_tn(normed[...], d_qkv[kind]).astype(bf16)
+                for block in range(D // LANES):
+                    lanes = slice(block * LANES, (block + 1) * LANES)
+                    own[at : at + LANES, lanes] = found[lanes, :LANES]
+                    far[at : at + LANES, lanes] = found[lanes, LANES:]
+                at += LANES
+    part, piece = at // 2, at // 4
+    own_a[...] = own[:part]
+    send_a[...] = far[:part]
+    for k, ref in enumerate((own, far)):
+        first, second = ref[part : part + piece], ref[part + piece :]
+        keep_b[k * piece : (k + 1) * piece] = jnp.where(side == 0, first, second)
+        send_b[k * piece : (k + 1) * piece] = jnp.where(side == 0, second, first)
+
+
+def second_kernel(place, own_a, got_a, keep_b, got_b, keep_a_out, send_a_out, keep_b_out, send_b_out):
+    piece = keep_a_out.shape[0]
     side = lax.rem(place[2], 2)
-    keep_out[...] = jnp.where(side == 0, total[:rows], total[rows:])
-    send_out[...] = jnp.where(side == 0, total[rows:], total[:rows]).astype(bf16)
+    total = own_a[...].astype(f32) + got_a[...].astype(f32)
+    keep_a_out[...] = jnp.where(side == 0, total[:piece], total[piece:])
+    send_a_out[...] = jnp.where(side == 0, total[piece:], total[:piece]).astype(bf16)
+    total = keep_b[...].astype(f32) + got_b[...].astype(f32)
+    keep_b_out[...] = total[:piece]
+    send_b_out[...] = total[piece:].astype(bf16)
+
+
+def line_bit(place, step):
+    return lax.rem(lax.div(place[2], 2 * step), 2)
+
+
+def give_half(place, step, total, keep_out, send_out):
+    rows = total.shape[0] // 2
+    low = line_bit(place, step) == 0
+    keep_out[...] = jnp.where(low, total[:rows], total[rows:])
+    send_out[...] = jnp.where(low, total[rows:], total[:rows]).astype(bf16)
+
+
+def third_kernel(step, place, keep_a, got_a, keep_b, got_b, keep_out, send_out):
+    total = jnp.concatenate([keep_a[...] + got_a[...].astype(f32), keep_b[...] + got_b[...].astype(f32)], axis=0)
+    give_half(place, step, total, keep_out, send_out)
+
+
+def halve_kernel(step, place, keep, got, keep_out, send_out):
+    give_half(place, step, keep[...] + got[...].astype(f32), keep_out, send_out)
 
 
 def add_kernel(keep, got, out):
     out[...] = (keep[...] + got[...].astype(f32)).astype(bf16)
 
 
-def fold_kernel(ways, got, out):
-    rows = got.shape[0] // ways
-    whole = got[...].astype(f32)
-    total = sum(whole[k * rows : (k + 1) * rows] for k in range(ways)).astype(bf16)
-    for k in range(ways):
-        out[k * rows : (k + 1) * rows] = total
+def join_kernel(step, place, mine, got, out):
+    low = line_bit(place, step) == 0
+    rows = mine.shape[0]
+    out[:rows] = jnp.where(low, mine[...], got[...])
+    out[rows:] = jnp.where(low, got[...], mine[...])
 
 
 def last_qkv_kernel(normed, d_qkv, own_out, far_out):
@@ -679,18 +740,23 @@
 
 def in_order(place, mine, other):
     side = lax.rem(place[2], 2)
-    return jnp.where(side == 0, mine[...], other[...]), jnp.where(side == 0, other[...], mine[...])
-
-
-def finish_wide_kernel(place, low_mine, low_other, high_mine, high_other, up_out, down_out, out_out, above_out):
-    units = up_out.shape[2]
-    for layer, pair in ((0, (low_mine, low_other)), (1, (high_mine, high_other))):
-        whole = jnp.concatenate(in_order(place, *pair), axis=0)
-        up_out[layer] = whole[:D].astype(f32)
-        down_out[layer] = whole[D : D + units].astype(f32)
-        out_out[layer] = whole[D + units : D + units + LANES].astype(f32)
-        if layer == 0:
-            above_out[...] = whole[D + units + LANES :]
+    piece = mine.shape[0] // 2
+    first, second = jnp.where(side == 0, mine[...], other[...]), jnp.where(side == 0, other[...], mine[...])
+    return jnp.concatenate([first[:piece], second[:piece], first[piece:], second[piece:]], axis=0)
+
+
+def finish_wide_kernel(groups, place, *refs):
+    outs = dict(zip(("up", "down", "out"), refs[-4:-1]))
+    for group, (layers, jobs) in enumerate(groups):
+        whole = in_order(place, refs[2 * group], refs[2 * group + 1])
+        at = 0
+        for layer, job in zip(layers, jobs):
+            rows = whole[at : at + job_rows(job, outs["up"].shape[2])]
+            at += rows.shape[0]
+            if job == "qkv":
+                refs[-1][...] = rows
+            else:
+                outs[job][layer] = rows.astype(f32)
 
 
 def finish_qkv_kernel(last, above, out):
@@ -701,19 +767,25 @@
             out[1, kind, lanes] = above[kind * LANES : (kind + 1) * LANES, lanes].astype(f32)
 
 
-def call(body, outs, operands, scalars=0, scratch=(), scalar_outs=0):
+def call(body, outs, operands, scalars=0, scratch=(), scalar_outs=0, bulk=(), bulk_outs=()):
+    specs = [SM] * scalars + [VM] * (len(operands) - scalars)
+    out_specs = [VM] * (len(outs) - scalar_outs) + [SM] * scalar_outs
+    for index in bulk:
+        specs[index] = pl.BlockSpec()
+    for index in bulk_outs:
+        out_specs[index] = pl.BlockSpec()
     return pl.pallas_call(
         body,
         out_shape=tuple(jax.ShapeDtypeStruct(shape, kind) for shape, kind in outs),
-        in_specs=[SM] * scalars + [VM] * (len(operands) - scalars),
-        out_specs=tuple([VM] * (len(outs) - scalar_outs) + [SM] * scalar_outs),
+        in_specs=specs,
+        out_specs=tuple(out_specs),
         scratch_shapes=scratch,
         compiler_params=pltpu.CompilerParams(vmem_limit_bytes=24 * 2**20),
     )(*operands)
 
 
 def after(value, *others):
-    return lax.optimization_barrier((value, *others))[0]
+    return lax.optimization_barrier((value, *others))[0] if others else value
 
 
 def core_swap(value):
@@ -745,7 +817,7 @@
     return lax.ppermute(value, AXES, pairs)
 
 
-def scan(value, flags, chunks, reverse):
+def scan(value, flags, chunks, reverse, others=lambda: ()):
     places, _ = flag_places(chunks)
     found, arrived = None, None
     for stage, (size, ways, last) in enumerate(scan_plan(chunks)):
@@ -766,9 +838,9 @@
             got.append(chunk_move(value, target))
         at = places[reverse, stage]
         if last:
-            return (found, tuple(got), at), arrived
+            return (found, tuple(got), at), arrived, value
         arrived = arrived or tuple(got)
-        operands = (flags, value, *got) + (() if found is None else (found,))
+        operands = (flags, after(value, *others()), *got) + (() if found is None else (found,))
         value, found = call(
             functools.partial(combine_kernel, at, ways, found is not None),
             ((value.shape, bf16), (value.shape, f32)),
@@ -777,12 +849,9 @@
         )
 
 
-def line_exchange(value):
-    shards, parts = lax.axis_size("seq"), lax.axis_size("mlp")
-    groups = [
-        [shard * parts + part for shard in range(side, shards, 2)] for side in range(2) for part in range(parts)
-    ]
-    return lax.all_to_all(value, AXES, 0, 0, axis_index_groups=groups, tiled=True)
+def line_swap(value, step):
+    count = lax.axis_size("seq")
+    return lax.ppermute(value, "seq", [(i, i ^ (2 * step)) for i in range(count)])
 
 
 def by_place(flag, mine, other):
@@ -866,7 +935,8 @@
                 1,
             )
         halo = chunk_move(halo, lambda c: c + 1)
-        (found, parts_got, at), arrived = scan(state, flags, chunks, False)
+        one, two, sums = call(far_kernel, (heads_like,) * 3, (qkv, causal))
+        (found, parts_got, at), arrived, _ = scan(state, flags, chunks, False, lambda: (one, halo))
         if layer == 0:
             down_a[0] = far_swap(after(down_piece(0), *arrived))
             up_b[0] = side_swap(after(up_a[0], *arrived))
@@ -875,11 +945,11 @@
             far_out[1] = far_swap(after(w_out[1], *arrived))
             up_a[1] = far_swap(after(up_piece(1), *arrived))
             down_a[1] = far_swap(after(down_piece(1), *arrived))
-            up_b[1] = side_swap(after(up_a[1], *arrived))
-            down_b[1] = side_swap(after(down_a[1], *arrived))
-        near, one, two, sums = call(
-            local_kernel, (heads_like,) * 4, (place, qkv, halo, causal, band), 1
-        )
+            up_b[1] = side_swap(up_a[1])
+            down_b[1] = side_swap(down_a[1])
+        (near,) = call(near_kernel, (heads_like,), (place, qkv, halo, band), 1)
+        if layer == 0:
+            found = after(found, far_qkv[1])
         mixed, far_one, far_two, root, prefix, state, piece = call(
             functools.partial(mix_kernel, layer, at, len(parts_got)),
             (heads_low, heads_like, heads_like, heads_like, heads_like, state_like, low_like),
@@ -887,6 +957,8 @@
             2,
         )
         weights = (w_up, w_down, up_a[layer], down_a[layer], up_b[layer], down_b[layer])
+        if layer == 0:
+            hidden = after(hidden, far_out[1], up_a[1])
         middle, normed_ffn, pre_own, pre_far, act_own, act_far, piece_ffn = call(
             functools.partial(ffn_kernel, layer),
             (hidden_like, low_like, ffn_like, ffn_like, ffn_low, ffn_low, low_like),
@@ -897,6 +969,8 @@
              weights, pre_own, pre_far, act_own, act_far)
         )
         base, adds = middle, (piece_ffn, core_swap(piece_ffn))
+        if layer == 0:
+            base = after(base, down_a[1])
     out_mine, out_theirs = call(output_kernel, (shard_like, shard_like), (place, base, *adds), 1)
     output = jnp.concatenate(by_place(half, out_mine, far_swap(out_theirs)))
 
@@ -906,9 +980,63 @@
 
     base, adds = None, None
     d_gain_attn, d_gain_ffn, d_blends = [None] * LAYERS, [None] * LAYERS, [None] * LAYERS
-    wide_sums = [None] * LAYERS
     d_qkvs = [None] * LAYERS
-    arrived = None
+    first_steps = []
+
+    def first_step(jobs, operands):
+        height = sum(job_rows(job, units) for job in jobs)
+        outs = tuple(((height // 2, D), bf16) for _ in range(4))
+        scratch = (pltpu.VMEM((height, D), bf16), pltpu.VMEM((height, D), bf16))
+        return call(
+            functools.partial(wide_grads_kernel, jobs), outs, (place, *operands), 1, scratch=scratch, bulk_outs=(0, 2)
+        )
+
+    def second_step(layers, jobs, own_a, send_a, keep_b, send_b, *others):
+        height = own_a.shape[0] // 2
+        got_a, got_b = far_swap(send_a), side_swap(send_b)
+        return call(
+            second_kernel,
+            (((height, D), f32), ((height, D), bf16)) * 2,
+            (place, own_a, after(got_a, *others), keep_b, got_b),
+            1,
+            bulk=(1, 3),
+            bulk_outs=(0, 2),
+        )
+
+    line = [1 << k for k in range((shards // 2).bit_length() - 1)]
+
+    def third_step(keep_a, send_a, keep_b, send_b, *others):
+        height = keep_a.shape[0]
+        got_a, got_b = side_swap(send_a), far_swap(send_b)
+        keep, send = call(
+            functools.partial(third_kernel, line[0]),
+            (((height, D), f32), ((height, D), bf16)),
+            (place, keep_a, after(got_a, *others), keep_b, got_b),
+            1,
+            bulk=(1, 3),
+        )
+        for place_at, step in enumerate(line):
+            got = line_swap(send, step)
+            if place_at + 1 == len(line):
+                (value,) = call(add_kernel, (((height, D), bf16),), (keep, got))
+                break
+            height //= 2
+            keep, send = call(
+                functools.partial(halve_kernel, line[place_at + 1]),
+                (((height, D), f32), ((height, D), bf16)),
+                (place, keep, got),
+                1,
+            )
+        for step in reversed(line):
+            height *= 2
+            (value,) = call(
+                functools.partial(join_kernel, step),
+                (((height, D), bf16),),
+                (place, value, line_swap(value, step)),
+                1,
+            )
+        return value, side_swap(value)
+
     for layer in reversed(range(LAYERS)):
         (hidden, normed, qkv, state, halo, mixed, far_one, far_two, root, prefix, middle, normed_ffn,
          weights, pre_own, pre_far, act_own, act_far) = saved[layer]
@@ -934,38 +1062,46 @@
              root, carried, blends),
             1,
         )
-        (found, parts_got, at), arrived = scan(state_back, flags, chunks, True)
         ext = HALO + rows + HALO
-        dq, dk_one, dk_two, dk_near, dv, halo_back, blend_near = call(
-            functools.partial(local_back_kernel, layer),
-            (heads_low, heads_like, heads_like, heads_like, heads_like, halo_like, ((1, wide), f32)),
-            (place, qkv, halo, causal, causal_t, band, carried, state, prefix, d_mixed, num_one, num_two, d_zeta,
-             blends),
+        dq_near, dk_near, dv_near, halo_back, blend_near = call(
+            functools.partial(near_back_kernel, layer),
+            (heads_like, heads_like, heads_like, halo_like, ((1, wide), f32)),
+            (place, qkv, halo, band, d_mixed, blends),
             1,
             scratch=(pltpu.VMEM((ext, LANES), f32), pltpu.VMEM((ext, LANES), f32)),
         )
         halo_back = chunk_move(halo_back, lambda c: c - 1)
-        with_qkv = layer + 1 < LAYERS
-        height = D + units + LANES + (3 * LANES if with_qkv else 0)
-        own, far = call(
-            functools.partial(wide_grads_kernel, with_qkv),
-            (((height, D), bf16), ((height, D), bf16)),
-            (place, normed_ffn, act_own, act_far, d_up_own, d_up_far, grad_rows, mixed, out_rows)
-            + ((saved[layer + 1][1], d_qkvs[layer + 1]) if with_qkv else ()),
+        (found, parts_got, at), arrived, value = scan(state_back, flags, chunks, True, lambda: (dq_near,))
+        ready = [value]
+        if layer + 1 == LAYERS:
+            jobs = ("up", "down", "out")
+            operands = (after(normed_ffn, value), d_up_own, d_up_far, act_own, act_far, grad_rows, mixed, out_rows)
+            groups = [((layer,) * 3, jobs, operands)]
+        else:
+            second = second_step(*first_steps[0], value)
+            above = saved[layer + 1][1]
+            groups = [
+                (
+                    (layer + 1, layer),
+                    ("qkv", "up"),
+                    (after(above, second[1], value), d_qkvs[layer + 1], normed_ffn, d_up_own, d_up_far),
+                ),
+                (
+                    (layer, layer),
+                    ("down", "out"),
+                    (after(act_own, second[1], value), act_far, grad_rows, mixed, out_rows),
+                ),
+            ]
+        for layers, jobs, operands in groups:
+            first_steps.append((layers, jobs, *first_step(jobs, operands)))
+            ready.append(first_steps[-1][3])
+        dq, dk_one, dk_two, dv = call(
+            far_back_kernel,
+            (heads_low, heads_like, heads_like, heads_like),
+            (place, qkv, causal, causal_t, carried, state, prefix, after(num_one, *ready), num_two, d_zeta, dq_near,
+             dv_near),
             1,
         )
-        keep, send = call(
-            halve_kernel,
-            (((height // 2, D), f32), ((height // 2, D), bf16)),
-            (place, own, far_swap(after(far, *arrived))),
-            1,
-        )
-        (folded,) = call(add_kernel, (((height // 2, D), bf16),), (keep, side_swap(send)))
-        (folded,) = call(
-            functools.partial(fold_kernel, shards // 2), (((height // 2, D), bf16),), (line_exchange(folded),)
-        )
-        folded = line_exchange(folded)
-        wide_sums[layer] = (folded, side_swap(folded))
         d_qkvs[layer], piece = call(
             functools.partial(qkv_back_kernel, layer, at, len(parts_got)),
             (qkv_like, low_like),
@@ -997,14 +1133,18 @@
     last = lax.all_to_all(spread, "seq", 0, 0, tiled=True).reshape(3 * D, LANES)
     d_inputs = jnp.concatenate(by_place(half, mine, far_swap(theirs)))
 
+    wide_sums = [third_step(*second, d_qkvs[0])]
+    for step in first_steps[1:]:
+        wide_sums.append(third_step(*second_step(*step, d_qkvs[0])))
+    plan = [(step[0], step[1]) for step in first_steps]
     count = 2 * LAYERS + 3 * LAYERS
     d_norm_attn = rest[:LAYERS]
     d_norm_ffn = rest[LAYERS : 2 * LAYERS]
     d_blend = jnp.sum(rest[2 * LAYERS : count].reshape(LAYERS, 3, 2, HD), axis=3)
     d_up, d_down, d_out, above = call(
-        finish_wide_kernel,
+        functools.partial(finish_wide_kernel, plan),
         (((LAYERS, D, units), f32), ((LAYERS, units, D), f32), ((LAYERS, LANES, D), f32), ((3 * LANES, D), bf16)),
-        (place, *wide_sums[0], *wide_sums[1]),
+        (place, *[ref for pair in wide_sums for ref in pair]),
         1,
     )
     (d_qkv,) = call(finish_qkv_kernel, (((LAYERS, 3, D, LANES), f32),), (last, above))

time: 358 us -> 307 us (0.86)
  waiting for transfers between devices: 168 us -> 107 us
  starting transfers between devices: 106 us -> 113 us
    all_to_all x4 -> x0, waiting for transfers between devices: 43.7 us -> none  [line_exchange(): lax.all_to_all(value, AXES, 0, 0, axis_index_groups=groups, tiled=True)]
    ppermute x28, waiting for transfers between devices: 48 us -> 18.8 us  [chunk_move(): return lax.ppermute(value, AXES, pairs)]
    ppermute x0 -> x12, waiting for transfers between devices: none -> 23.1 us  [line_swap(): return lax.ppermute(value, 'seq', [(i, i ^ 2 * step) for i in range(count)])]
    ppermute x8 -> x13, waiting for transfers between devices: 54.8 us -> 34 us  [side_swap(): return lax.ppermute(value, 'seq', [(i, i ^ 1) for i in range(count)])]
    ppermute x0 -> x12, starting transfers between devices: none -> 16.2 us  [line_swap(): return lax.ppermute(value, 'seq', [(i, i ^ 2 * step) for i in range(count)])]
    all_to_all x4 -> x0, starting transfers between devices: 16.2 us -> none  [line_exchange(): lax.all_to_all(value, AXES, 0, 0, axis_index_groups=groups, tiled=True)]
    ppermute x14 -> x18, waiting for transfers between devices: 14.5 us -> 26.7 us  [far_swap(): return lax.ppermute(value, 'mlp', [(i, i ^ 2) for i in range(count)])]
    pallas_call x37 -> x54, Pallas kernels: 63.3 us -> 65.7 us  [call(): pl.pallas_call(body, out_shape=tuple((jax.ShapeDtypeStruct(shape, kind) f...]
  transfers between devices with their start and end apart: 69 -> 86, of which waited for: 27 -> 32; matrix products, arithmetic and copies ran while one was open for 2% -> 3% of each run, Pallas kernels for 15% -> 17%
where the time goes in v3:
time: 307 us; the launch traced here: 306 us
  starting transfers between devices  113 us (37%)
  waiting for transfers between devices  107 us (35%)
  Pallas kernels  65.7 us (21%)
  local copies, waits for them, and re-layouts  17.4 us (6%)
    pallas_call x54, Pallas kernels, call(): pl.pallas_call(body, out_shape=tuple((jax.ShapeDtypeStruct(shape, kind) f...  65.7 us
    ppermute x28, starting transfers between devices, chunk_move(): return lax.ppermute(value, AXES, pairs)  48 us
    ppermute x13, waiting for transfers between devices, side_swap(): return lax.ppermute(value, 'seq', [(i, i ^ 1) for i in range(count)])  34 us
    ppermute x18, waiting for transfers between devices, far_swap(): return lax.ppermute(value, 'mlp', [(i, i ^ 2) for i in range(count)])  26.7 us
    ppermute x12, waiting for transfers between devices, line_swap(): return lax.ppermute(value, 'seq', [(i, i ^ 2 * step) for i in range(count)])  23.1 us
    ppermute x28, waiting for transfers between devices, chunk_move(): return lax.ppermute(value, AXES, pairs)  18.8 us
    ppermute x18, starting transfers between devices, far_swap(): return lax.ppermute(value, 'mlp', [(i, i ^ 2) for i in range(count)])  18.1 us
    ppermute x12, starting transfers between devices, line_swap(): return lax.ppermute(value, 'seq', [(i, i ^ 2 * step) for i in range(count)])  16.2 us
  transfers between devices with their start and end apart: 86, of which 32 were waited for; matrix products, arithmetic and copies ran while one was open for 3% of the time, Pallas kernels for 17%

profile of v3, /device:TPU:0, one launch (start us, length us, event | category | flops | bytes accessed | tf_op | source)
XLA Modules:
  0.0 306.0 jit_solution(17241671980909465214)
XLA Ops:
  4.6 3.0 collective-permute-start
  10.4 3.9 %collective-permute-start.4 = (s32[1,128]{1,0:T(1,128)S(1)}, s32[1,128]{1,0:T(1,128)S(1)}, u32[]{:S(2)}, u32[]{:S(2)}) collective-permute-start(s32[1,128]{1,0:T(1,128)S(1)} %slice_bitcast_fusion.4), channel_id=1, source_target_pairs={{0,4},{4,8},{8,12},{12,16},{16,20},{20,24},{24,28},{1,5},{5,9},{9,... | collective-permute-start | bytes 1544 | tf_op jit(solution)/shard_map/ppermute | solution.py:900
  17.4 4.0 %collective-permute-done.3.refs_5_.other = bf16[3,512,128]{2,1,0:T(8,128)(2,1)S(1)} collective-permute-done((bf16[3,512,128]{2,1,0:T(8,128)(2,1)}, bf16[3,512,128]{2,1,0:T(8,128)(2,1)S(1)}, u32[]{:S(2)}, u32[]{:S(2)}) %collective-permute-start.3) | collective-permute-done | bytes 393248 | tf_op jit(solution)/shard_map/ppermute | solution.py:798
  28.2 2.5 collective-permute-done.7.refs_3_
  37.9 6.6 %collective-permute-done.10.halo = bf16[2,2,32,128]{3,2,1,0:T(8,128)(2,1)S(1)} collective-permute-done((bf16[2,2,32,128]{3,2,1,0:T(8,128)(2,1)S(1)}, bf16[2,2,32,128]{3,2,1,0:T(8,128)(2,1)S(1)}, u32[]{:S(2)}, u32[]{:S(2)}) %collective-permute-start.10) | collective-permute-done | bytes 32800 | tf_op jit(solution)/shard_map/ppermute | solution.py:817
  45.2 3.5 %collective-permute-start.13 = (bf16[2,144,128]{2,1,0:T(8,128)(2,1)S(1)}, bf16[2,144,128]{2,1,0:T(8,128)(2,1)S(1)}, u32[]{:S(2)}, u32[]{:S(2)}) collective-permute-start(bf16[2,144,128]{2,1,0:T(8,128)(2,1)S(1)} %get-tuple-element.223), channel_id=1, source_target_pairs={{0,8},{1,9},{2,10},{3,11},{4,12},{5,13},{6,14},{7,15},{8,16},{9,17... | collective-permute-start | bytes 221192 | tf_op jit(solution)/shard_map/ppermute | solution.py:817
  48.7 4.5 %collective-permute-start.14 = (bf16[2,144,128]{2,1,0:T(8,128)(2,1)S(1)}, bf16[2,144,128]{2,1,0:T(8,128)(2,1)S(1)}, u32[]{:S(2)}, u32[]{:S(2)}) collective-permute-start(bf16[2,144,128]{2,1,0:T(8,128)(2,1)S(1)} %get-tuple-element.223), channel_id=1, source_target_pairs={{0,16},{1,17},{2,18},{3,19},{4,20},{5,21},{6,22},{7,23},{8,24},{9,... | collective-permute-start | bytes 221192 | tf_op jit(solution)/shard_map/ppermute | solution.py:817
  54.6 2.9 shard_map.181.near
  57.5 2.5 collective-permute-start.9
  63.5 5.8 %collective-permute-done.8.other = bf16[128,512]{1,0:T(8,128)(2,1)S(1)} collective-permute-done((bf16[128,512]{1,0:T(8,128)(2,1)S(1)}, bf16[128,512]{1,0:T(8,128)(2,1)S(1)}, u32[]{:S(2)}, u32[]{:S(2)}) %collective-permute-start.8) | collective-permute-done | bytes 131104 | tf_op jit(solution)/shard_map/ppermute | solution.py:798
  72.2 4.9 %collective-permute-done.21.down_a.refs_8_ = bf16[256,512]{1,0:T(8,128)(2,1)S(1)} collective-permute-done((bf16[256,512]{1,0:T(8,128)(2,1)S(1)}, bf16[256,512]{1,0:T(8,128)(2,1)S(1)}, u32[]{:S(2)}, u32[]{:S(2)}) %collective-permute-start.21) | collective-permute-done | bytes 262176 | tf_op jit(solution)/shard_map/ppermute | solution.py:798
  86.7 4.3 %collective-permute-start.27 = (bf16[2,144,128]{2,1,0:T(8,128)(2,1)S(1)}, bf16[2,144,128]{2,1,0:T(8,128)(2,1)S(1)}, u32[]{:S(2)}, u32[]{:S(2)}) collective-permute-start(bf16[2,144,128]{2,1,0:T(8,128)(2,1)S(1)} %get-tuple-element.242), channel_id=1, source_target_pairs={{0,8},{1,9},{2,10},{3,11},{4,12},{5,13},{6,14},{7,15},{8,16},{9,17... | collective-permute-start | bytes 221192 | tf_op jit(solution)/shard_map/ppermute | solution.py:817
  91.0 3.1 %collective-permute-start.28 = (bf16[2,144,128]{2,1,0:T(8,128)(2,1)S(1)}, bf16[2,144,128]{2,1,0:T(8,128)(2,1)S(1)}, u32[]{:S(2)}, u32[]{:S(2)}) collective-permute-start(bf16[2,144,128]{2,1,0:T(8,128)(2,1)S(1)} %get-tuple-element.242), channel_id=1, source_target_pairs={{0,16},{1,17},{2,18},{3,19},{4,20},{5,21},{6,22},{7,23},{8,24},{9,... | collective-permute-start | bytes 221192 | tf_op jit(solution)/shard_map/ppermute | solution.py:817
  97.8 2.9 shard_map.187.near
  103.2 3.9 %collective-permute-done.35.refs_2_ = bf16[256,128]{1,0:T(8,128)(2,1)S(1)} collective-permute-done((bf16[256,128]{1,0:T(8,128)(2,1)S(1)}, bf16[256,128]{1,0:T(8,128)(2,1)S(1)}, u32[]{:S(2)}, u32[]{:S(2)}) %collective-permute-start.35) | collective-permute-done | bytes 65568 | tf_op jit(solution)/shard_map/ppermute | solution.py:798
  114.3 2.5 collective-permute-start.41
  116.8 4.2 %shard_map.196 = (f32[256,256]{1,0:T(8,128)S(1)}, f32[256,256]{1,0:T(8,128)S(1)}, f32[256,256]{1,0:T(8,128)S(1)}, bf16[2,2,32,128]{3,2,1,0:T(8,128)(2,1)S(1)}, f32[1,256]{1,0:T(1,128)S(1)}) custom-call(s32[3]{0:T(128)S(1)} %pad_add_fusion.place.refs_0_, bf16[3,256,256]{2,1,0:T(8,128)(2,1)S(1)} %get-tuple-element.234.qkv, ...), custom_call_target="tpu_custom_call" | custom-call | tf_op jit(solution)/shard_map/pallas_call | solution.py:777
  128.4 2.7 shard_map.199
  144.8 4.2 %shard_map.203 = (f32[256,256]{1,0:T(8,128)S(1)}, f32[256,256]{1,0:T(8,128)S(1)}, f32[256,256]{1,0:T(8,128)S(1)}, bf16[2,2,32,128]{3,2,1,0:T(8,128)(2,1)S(1)}, f32[1,256]{1,0:T(1,128)S(1)}) custom-call(s32[3]{0:T(128)S(1)} %pad_add_fusion.place.refs_0_, bf16[3,256,256]{2,1,0:T(8,128)(2,1)S(1)} %get-tuple-element.209.qkv, ...), custom_call_target="tpu_custom_call" | custom-call | tf_op jit(solution)/shard_map/pallas_call | solution.py:777
  149.0 3.6 %collective-permute-done.48.refs_1_ = bf16[2,144,128]{2,1,0:T(8,128)(2,1)S(1)} collective-permute-done((bf16[2,144,128]{2,1,0:T(8,128)(2,1)S(1)}, bf16[2,144,128]{2,1,0:T(8,128)(2,1)S(1)}, u32[]{:S(2)}, u32[]{:S(2)}) %collective-permute-start.48) | collective-permute-done | bytes 73760 | tf_op jit(solution)/shard_map/ppermute | solution.py:817
  170.8 2.7 shard_map.208
  179.2 9.1 %all-to-all-start = ((bf16[16,208,128]{2,1,0:T(8,128)(2,1)}), bf16[16,208,128]{2,1,0:T(8,128)(2,1)S(1)}, u32[]{:S(2)}, u32[]{:S(2)}) async-start(bf16[16,208,128]{2,1,0:T(8,128)(2,1)} %get-tuple-element.350), calls=%async_computation | async-start | bytes 1703936 | tf_op jit(solution)/shard_map/all_to_all | solution.py:1127
  192.4 13.6 %collective-permute-done.59.got_a = bf16[288,512]{1,0:T(8,128)(2,1)S(1)} collective-permute-done((bf16[288,512]{1,0:T(8,128)(2,1)}, bf16[288,512]{1,0:T(8,128)(2,1)S(1)}, u32[]{:S(2)}, u32[]{:S(2)}) %collective-permute-start.59) | collective-permute-done | bytes 294944 | tf_op jit(solution)/shard_map/ppermute | solution.py:803
  210.0 7.4 %collective-permute-done.66.got_a = bf16[448,512]{1,0:T(8,128)(2,1)S(1)} collective-permute-done((bf16[448,512]{1,0:T(8,128)(2,1)}, bf16[448,512]{1,0:T(8,128)(2,1)S(1)}, u32[]{:S(2)}, u32[]{:S(2)}) %collective-permute-start.66) | collective-permute-done | bytes 458784 | tf_op jit(solution)/shard_map/ppermute | solution.py:798
  235.5 5.0 %collective-permute-done.63.got = bf16[144,512]{1,0:T(8,128)(2,1)S(1)} collective-permute-done((bf16[144,512]{1,0:T(8,128)(2,1)S(1)}, bf16[144,512]{1,0:T(8,128)(2,1)S(1)}, u32[]{:S(2)}, u32[]{:S(2)}) %collective-permute-start.63) | collective-permute-done | bytes 147488 | tf_op jit(solution)/shard_map/ppermute | solution.py:854
  241.0 4.0 %collective-permute-start.64 = (bf16[288,512]{1,0:T(8,128)(2,1)S(1)}, bf16[288,512]{1,0:T(8,128)(2,1)S(1)}, u32[]{:S(2)}, u32[]{:S(2)}) collective-permute-start(bf16[288,512]{1,0:T(8,128)(2,1)S(1)} %shard_map.216.mine), channel_id=1, source_target_pairs={{0,8},{4,12},{8,0},{12,4},{16,24},{20,28},{24,16},{28,20},{1,9},{5... | collective-permute-start | bytes 884744 | tf_op jit(solution)/shard_map/ppermute | solution.py:854
  249.2 8.4 %collective-permute-done.71.got = bf16[112,512]{1,0:T(8,128)(2,1)S(1)} collective-permute-done((bf16[112,512]{1,0:T(8,128)(2,1)S(1)}, bf16[112,512]{1,0:T(8,128)(2,1)S(1)}, u32[]{:S(2)}, u32[]{:S(2)}) %collective-permute-start.71) | collective-permute-done | bytes 114720 | tf_op jit(solution)/shard_map/ppermute | solution.py:854
  257.7 2.9 collective-permute-done.80.got
  262.7 3.5 %collective-permute-done.81.got = bf16[80,512]{1,0:T(8,128)(2,1)S(1)} collective-permute-done((bf16[80,512]{1,0:T(8,128)(2,1)S(1)}, bf16[80,512]{1,0:T(8,128)(2,1)S(1)}, u32[]{:S(2)}, u32[]{:S(2)}) %collective-permute-start.81) | collective-permute-done | bytes 81952 | tf_op jit(solution)/shard_map/ppermute | solution.py:854
  271.0 3.5 %all-to-all-start.1 = ((bf16[8,192,128]{2,1,0:T(8,128)(2,1)}), bf16[8,192,128]{2,1,0:T(8,128)(2,1)S(1)}, u32[]{:S(2)}, u32[]{:S(2)}) async-start(bf16[8,192,128]{2,1,0:T(8,128)(2,1)} %get-tuple-element.352), calls=%async_computation.1 | async-start | bytes 786432 | tf_op jit(solution)/shard_map/all_to_all | solution.py:1133
  282.4 18.0 %collective-permute-done.83.refs_5_ = bf16[320,512]{1,0:T(8,128)(2,1)S(1)} collective-permute-done((bf16[320,512]{1,0:T(8,128)(2,1)S(1)}, bf16[320,512]{1,0:T(8,128)(2,1)S(1)}, u32[]{:S(2)}, u32[]{:S(2)}) %collective-permute-start.83) | collective-permute-done | bytes 327712 | tf_op jit(solution)/shard_map/ppermute | solution.py:803
  300.5 2.9 shard_map.230
  (277 shorter events, 147.7 us)
Async XLA Ops:
  27.8 20.9 %collective-permute-start.17 = (bf16[512,256]{1,0:T(8,128)(2,1)S(1)}, bf16[512,256]{1,0:T(8,128)(2,1)S(1)}, u32[]{:S(2)}, u32[]{:S(2)}) collective-permute-start(bf16[512,256]{1,0:T(8,128)(2,1)S(1)} %dynamic-slice_bitcast_fusion.2), channel_id=1, source_target_pairs={{0,2},{1,3},{2,0},{3,1},{4,6},{5,7},{6,4},{7,5},{8,10},{9,11},{10,... | collective-permute-start | bytes 786440 | tf_op jit(solution)/shard_map/ppermute | solution.py:798
  30.7 22.5 %collective-permute-start.12 = (bf16[3,512,128]{2,1,0:T(8,128)(2,1)}, bf16[3,512,128]{2,1,0:T(8,128)(2,1)S(1)}, u32[]{:S(2)}, u32[]{:S(2)}) collective-permute-start(bf16[3,512,128]{2,1,0:T(8,128)(2,1)} %get-tuple-element.221), channel_id=1, source_target_pairs={{0,2},{1,3},{2,0},{3,1},{4,6},{5,7},{6,4},{7,5},{8,10},{9,11},{10,... | collective-permute-start | bytes 1179656 | tf_op jit(solution)/shard_map/ppermute | solution.py:798
  34.8 26.5 %collective-permute-start.18 = (bf16[256,512]{1,0:T(8,128)(2,1)S(1)}, bf16[256,512]{1,0:T(8,128)(2,1)S(1)}, u32[]{:S(2)}, u32[]{:S(2)}) collective-permute-start(bf16[256,512]{1,0:T(8,128)(2,1)S(1)} %get-tuple-element.227), channel_id=1, source_target_pairs={{0,2},{1,3},{2,0},{3,1},{4,6},{5,7},{6,4},{7,5},{8,10},{9,11},{10,... | collective-permute-start | bytes 786440 | tf_op jit(solution)/shard_map/ppermute | solution.py:798
  36.4 21.1 %collective-permute-start.11 = (bf16[128,512]{1,0:T(8,128)(2,1)S(1)}, bf16[128,512]{1,0:T(8,128)(2,1)S(1)}, u32[]{:S(2)}, u32[]{:S(2)}) collective-permute-start(bf16[128,512]{1,0:T(8,128)(2,1)S(1)} %get-tuple-element.218), channel_id=1, source_target_pairs={{0,2},{1,3},{2,0},{3,1},{4,6},{5,7},{6,4},{7,5},{8,10},{9,11},{10,... | collective-permute-start | bytes 393224 | tf_op jit(solution)/shard_map/ppermute | solution.py:798
  45.2 14.9 %collective-permute-start.13 = (bf16[2,144,128]{2,1,0:T(8,128)(2,1)S(1)}, bf16[2,144,128]{2,1,0:T(8,128)(2,1)S(1)}, u32[]{:S(2)}, u32[]{:S(2)}) collective-permute-start(bf16[2,144,128]{2,1,0:T(8,128)(2,1)S(1)} %get-tuple-element.223), channel_id=1, source_target_pairs={{0,8},{1,9},{2,10},{3,11},{4,12},{5,13},{6,14},{7,15},{8,16},{9,17... | collective-permute-start | bytes 221192 | tf_op jit(solution)/shard_map/ppermute | solution.py:817
  48.7 13.4 %collective-permute-start.14 = (bf16[2,144,128]{2,1,0:T(8,128)(2,1)S(1)}, bf16[2,144,128]{2,1,0:T(8,128)(2,1)S(1)}, u32[]{:S(2)}, u32[]{:S(2)}) collective-permute-start(bf16[2,144,128]{2,1,0:T(8,128)(2,1)S(1)} %get-tuple-element.223), channel_id=1, source_target_pairs={{0,16},{1,17},{2,18},{3,19},{4,20},{5,21},{6,22},{7,23},{8,24},{9,... | collective-permute-start | bytes 221192 | tf_op jit(solution)/shard_map/ppermute | solution.py:817
  86.7 14.0 %collective-permute-start.27 = (bf16[2,144,128]{2,1,0:T(8,128)(2,1)S(1)}, bf16[2,144,128]{2,1,0:T(8,128)(2,1)S(1)}, u32[]{:S(2)}, u32[]{:S(2)}) collective-permute-start(bf16[2,144,128]{2,1,0:T(8,128)(2,1)S(1)} %get-tuple-element.242), channel_id=1, source_target_pairs={{0,8},{1,9},{2,10},{3,11},{4,12},{5,13},{6,14},{7,15},{8,16},{9,17... | collective-permute-start | bytes 221192 | tf_op jit(solution)/shard_map/ppermute | solution.py:817
  135.2 24.6 %collective-permute-start.51 = (bf16[576,512]{1,0:T(8,128)(2,1)S(1)}, bf16[576,512]{1,0:T(8,128)(2,1)S(1)}, u32[]{:S(2)}, u32[]{:S(2)}) collective-permute-start(bf16[576,512]{1,0:T(8,128)(2,1)S(1)} %get-tuple-element.277), channel_id=1, source_target_pairs={{0,2},{1,3},{2,0},{3,1},{4,6},{5,7},{6,4},{7,5},{8,10},{9,11},{10,... | collective-permute-start | bytes 1769480 | tf_op jit(solution)/shard_map/ppermute | solution.py:798
  135.3 26.1 %collective-permute-start.52 = (bf16[576,512]{1,0:T(8,128)(2,1)S(1)}, bf16[576,512]{1,0:T(8,128)(2,1)S(1)}, u32[]{:S(2)}, u32[]{:S(2)}) collective-permute-start(bf16[576,512]{1,0:T(8,128)(2,1)S(1)} %get-tuple-element.310), channel_id=1, source_target_pairs={{0,4},{4,0},{8,12},{12,8},{16,20},{20,16},{24,28},{28,24},{1,5},{5... | collective-permute-start | bytes 1769480 | tf_op jit(solution)/shard_map/ppermute | solution.py:803
  155.9 17.6 %collective-permute-start.54 = (bf16[2,144,128]{2,1,0:T(8,128)(2,1)S(1)}, bf16[2,144,128]{2,1,0:T(8,128)(2,1)S(1)}, u32[]{:S(2)}, u32[]{:S(2)}) collective-permute-start(bf16[2,144,128]{2,1,0:T(8,128)(2,1)S(1)} %get-tuple-element.305), channel_id=1, source_target_pairs={{8,0},{9,1},{10,2},{11,3},{12,4},{13,5},{14,6},{15,7},{16,8},{17,9... | collective-permute-start | bytes 221192 | tf_op jit(solution)/shard_map/ppermute | solution.py:817
  157.2 16.3 %collective-permute-start.55 = (bf16[2,144,128]{2,1,0:T(8,128)(2,1)S(1)}, bf16[2,144,128]{2,1,0:T(8,128)(2,1)S(1)}, u32[]{:S(2)}, u32[]{:S(2)}) collective-permute-start(bf16[2,144,128]{2,1,0:T(8,128)(2,1)S(1)} %get-tuple-element.305), channel_id=1, source_target_pairs={{16,0},{17,1},{18,2},{19,3},{20,4},{21,5},{22,6},{23,7},{24,8},{25... | collective-permute-start | bytes 221192 | tf_op jit(solution)/shard_map/ppermute | solution.py:817
  158.5 15.0 %collective-permute-start.56 = (bf16[2,144,128]{2,1,0:T(8,128)(2,1)S(1)}, bf16[2,144,128]{2,1,0:T(8,128)(2,1)S(1)}, u32[]{:S(2)}, u32[]{:S(2)}) collective-permute-start(bf16[2,144,128]{2,1,0:T(8,128)(2,1)S(1)} %get-tuple-element.305), channel_id=1, source_target_pairs={{24,0},{25,1},{26,2},{27,3},{28,4},{29,5},{30,6},{31,7}} | collective-permute-start | bytes 221192 | tf_op jit(solution)/shard_map/ppermute | solution.py:817
  159.8 13.6 %collective-permute-start.53 = (bf16[2,2,32,128]{3,2,1,0:T(8,128)(2,1)S(1)}, bf16[2,2,32,128]{3,2,1,0:T(8,128)(2,1)S(1)}, u32[]{:S(2)}, u32[]{:S(2)}) collective-permute-start(bf16[2,2,32,128]{3,2,1,0:T(8,128)(2,1)S(1)} %get-tuple-element.334), channel_id=1, source_target_pairs={{2,0},{3,1},{4,2},{5,3},{6,4},{7,5},{8,6},{9,7},{10,8},{11,9},{12,... | collective-permute-start | bytes 98312 | tf_op jit(solution)/shard_map/ppermute | solution.py:817
  179.2 91.0 %all-to-all-start = ((bf16[16,208,128]{2,1,0:T(8,128)(2,1)}), bf16[16,208,128]{2,1,0:T(8,128)(2,1)S(1)}, u32[]{:S(2)}, u32[]{:S(2)}) async-start(bf16[16,208,128]{2,1,0:T(8,128)(2,1)} %get-tuple-element.350), calls=%async_computation | async-start | bytes 1703936 | tf_op jit(solution)/shard_map/all_to_all | solution.py:1127
  188.2 17.7 %collective-permute-start.59 = (bf16[288,512]{1,0:T(8,128)(2,1)}, bf16[288,512]{1,0:T(8,128)(2,1)S(1)}, u32[]{:S(2)}, u32[]{:S(2)}) collective-permute-start(bf16[288,512]{1,0:T(8,128)(2,1)} %copy-done.28), channel_id=1, source_target_pairs={{0,4},{4,0},{8,12},{12,8},{16,20},{20,16},{24,28},{28,24},{1,5},{5... | collective-permute-start | bytes 884744 | tf_op jit(solution)/shard_map/ppermute | solution.py:803
  190.2 15.9 %collective-permute-start.60 = (bf16[288,512]{1,0:T(8,128)(2,1)S(1)}, bf16[288,512]{1,0:T(8,128)(2,1)S(1)}, u32[]{:S(2)}, u32[]{:S(2)}) collective-permute-start(bf16[288,512]{1,0:T(8,128)(2,1)S(1)} %copy-done.27), channel_id=1, source_target_pairs={{0,2},{1,3},{2,0},{3,1},{4,6},{5,7},{6,4},{7,5},{8,10},{9,11},{10,... | collective-permute-start | bytes 884744 | tf_op jit(solution)/shard_map/ppermute | solution.py:798
  191.6 25.7 %collective-permute-start.66 = (bf16[448,512]{1,0:T(8,128)(2,1)}, bf16[448,512]{1,0:T(8,128)(2,1)S(1)}, u32[]{:S(2)}, u32[]{:S(2)}) collective-permute-start(bf16[448,512]{1,0:T(8,128)(2,1)} %get-tuple-element.317), channel_id=1, source_target_pairs={{0,2},{1,3},{2,0},{3,1},{4,6},{5,7},{6,4},{7,5},{8,10},{9,11},{10,... | collective-permute-start | bytes 1376264 | tf_op jit(solution)/shard_map/ppermute | solution.py:798
  192.2 25.2 %collective-permute-start.67 = (bf16[448,512]{1,0:T(8,128)(2,1)}, bf16[448,512]{1,0:T(8,128)(2,1)S(1)}, u32[]{:S(2)}, u32[]{:S(2)}) collective-permute-start(bf16[448,512]{1,0:T(8,128)(2,1)} %get-tuple-element.364), channel_id=1, source_target_pairs={{0,4},{4,0},{8,12},{12,8},{16,20},{20,16},{24,28},{28,24},{1,5},{5... | collective-permute-start | bytes 1376264 | tf_op jit(solution)/shard_map/ppermute | solution.py:803
  206.8 15.3 %collective-permute-start.61 = (bf16[288,512]{1,0:T(8,128)(2,1)S(1)}, bf16[288,512]{1,0:T(8,128)(2,1)S(1)}, u32[]{:S(2)}, u32[]{:S(2)}) collective-permute-start(bf16[288,512]{1,0:T(8,128)(2,1)S(1)} %get-tuple-element.358), channel_id=1, source_target_pairs={{0,8},{4,12},{8,0},{12,4},{16,24},{20,28},{24,16},{28,20},{1,9},{5... | collective-permute-start | bytes 884744 | tf_op jit(solution)/shard_map/ppermute | solution.py:854
  208.5 16.3 %collective-permute-start.75 = (bf16[320,512]{1,0:T(8,128)(2,1)}, bf16[320,512]{1,0:T(8,128)(2,1)S(1)}, u32[]{:S(2)}, u32[]{:S(2)}) collective-permute-start(bf16[320,512]{1,0:T(8,128)(2,1)} %copy-done.25), channel_id=1, source_target_pairs={{0,2},{1,3},{2,0},{3,1},{4,6},{5,7},{6,4},{7,5},{8,10},{9,11},{10,... | collective-permute-start | bytes 983048 | tf_op jit(solution)/shard_map/ppermute | solution.py:798
  210.0 14.8 %collective-permute-start.76 = (bf16[320,512]{1,0:T(8,128)(2,1)}, bf16[320,512]{1,0:T(8,128)(2,1)S(1)}, u32[]{:S(2)}, u32[]{:S(2)}) collective-permute-start(bf16[320,512]{1,0:T(8,128)(2,1)} %copy-done.24), channel_id=1, source_target_pairs={{0,4},{4,0},{8,12},{12,8},{16,20},{20,16},{24,28},{28,24},{1,5},{5... | collective-permute-start | bytes 983048 | tf_op jit(solution)/shard_map/ppermute | solution.py:803
  230.2 14.8 %collective-permute-start.70 = (bf16[224,512]{1,0:T(8,128)(2,1)S(1)}, bf16[224,512]{1,0:T(8,128)(2,1)S(1)}, u32[]{:S(2)}, u32[]{:S(2)}) collective-permute-start(bf16[224,512]{1,0:T(8,128)(2,1)S(1)} %get-tuple-element.370), channel_id=1, source_target_pairs={{0,8},{4,12},{8,0},{12,4},{16,24},{20,28},{24,16},{28,20},{1,9},{5... | collective-permute-start | bytes 688136 | tf_op jit(solution)/shard_map/ppermute | solution.py:854
  234.8 12.2 %collective-permute-start.79 = (bf16[160,512]{1,0:T(8,128)(2,1)S(1)}, bf16[160,512]{1,0:T(8,128)(2,1)S(1)}, u32[]{:S(2)}, u32[]{:S(2)}) collective-permute-start(bf16[160,512]{1,0:T(8,128)(2,1)S(1)} %get-tuple-element.382), channel_id=1, source_target_pairs={{0,8},{4,12},{8,0},{12,4},{16,24},{20,28},{24,16},{28,20},{1,9},{5... | collective-permute-start | bytes 491528 | tf_op jit(solution)/shard_map/ppermute | solution.py:854
  235.5 25.3 %collective-permute-start.33 = (bf16[256,512]{1,0:T(8,128)(2,1)S(1)}, bf16[256,512]{1,0:T(8,128)(2,1)S(1)}, u32[]{:S(2)}, u32[]{:S(2)}) collective-permute-start(bf16[256,512]{1,0:T(8,128)(2,1)S(1)} %copy-done.17), channel_id=1, source_target_pairs={{0,1},{1,0},{2,3},{3,2},{4,5},{5,4},{6,7},{7,6},{8,9},{9,8},{10,11... | collective-permute-start | bytes 786440 | tf_op jit(solution)/shard_map/ppermute | solution.py:793
  241.0 28.5 %collective-permute-start.64 = (bf16[288,512]{1,0:T(8,128)(2,1)S(1)}, bf16[288,512]{1,0:T(8,128)(2,1)S(1)}, u32[]{:S(2)}, u32[]{:S(2)}) collective-permute-start(bf16[288,512]{1,0:T(8,128)(2,1)S(1)} %shard_map.216.mine), channel_id=1, source_target_pairs={{0,8},{4,12},{8,0},{12,4},{16,24},{20,28},{24,16},{28,20},{1,9},{5... | collective-permute-start | bytes 884744 | tf_op jit(solution)/shard_map/ppermute | solution.py:854
  247.7 13.0 %collective-permute-start.80 = (bf16[80,512]{1,0:T(8,128)(2,1)S(1)}, bf16[80,512]{1,0:T(8,128)(2,1)S(1)}, u32[]{:S(2)}, u32[]{:S(2)}) collective-permute-start(bf16[80,512]{1,0:T(8,128)(2,1)S(1)} %get-tuple-element.384), channel_id=1, source_target_pairs={{0,16},{4,20},{8,24},{12,28},{16,0},{20,4},{24,8},{28,12},{1,17},{... | collective-permute-start | bytes 245768 | tf_op jit(solution)/shard_map/ppermute | solution.py:854
  261.4 13.1 %collective-permute-start.34 = (bf16[256,128]{1,0:T(8,128)(2,1)S(1)}, bf16[256,128]{1,0:T(8,128)(2,1)S(1)}, u32[]{:S(2)}, u32[]{:S(2)}) collective-permute-start(bf16[256,128]{1,0:T(8,128)(2,1)S(1)} %get-tuple-element.247), channel_id=1, source_target_pairs={{0,2},{1,3},{2,0},{3,1},{4,6},{5,7},{6,4},{7,5},{8,10},{9,11},{10,... | collective-permute-start | bytes 196616 | tf_op jit(solution)/shard_map/ppermute | solution.py:798
  266.7 12.5 %collective-permute-start.82 = (bf16[160,512]{1,0:T(8,128)(2,1)S(1)}, bf16[160,512]{1,0:T(8,128)(2,1)S(1)}, u32[]{:S(2)}, u32[]{:S(2)}) collective-permute-start(bf16[160,512]{1,0:T(8,128)(2,1)S(1)} %shard_map.228.mine), channel_id=1, source_target_pairs={{0,8},{4,12},{8,0},{12,4},{16,24},{20,28},{24,16},{28,20},{1,9},{5... | collective-permute-start | bytes 491528 | tf_op jit(solution)/shard_map/ppermute | solution.py:854
  270.1 30.4 %collective-permute-start.65 = (bf16[576,512]{1,0:T(8,128)(2,1)S(1)}, bf16[576,512]{1,0:T(8,128)(2,1)S(1)}, u32[]{:S(2)}, u32[]{:S(2)}) collective-permute-start(bf16[576,512]{1,0:T(8,128)(2,1)S(1)} %shard_map.217.refs_0_), channel_id=1, source_target_pairs={{0,4},{4,0},{8,12},{12,8},{16,20},{20,16},{24,28},{28,24},{1,5},{5... | collective-permute-start | bytes 1769480 | tf_op jit(solution)/shard_map/ppermute | solution.py:803
  271.0 33.8 %all-to-all-start.1 = ((bf16[8,192,128]{2,1,0:T(8,128)(2,1)}), bf16[8,192,128]{2,1,0:T(8,128)(2,1)S(1)}, u32[]{:S(2)}, u32[]{:S(2)}) async-start(bf16[8,192,128]{2,1,0:T(8,128)(2,1)} %get-tuple-element.352), calls=%async_computation.1 | async-start | bytes 786432 | tf_op jit(solution)/shard_map/all_to_all | solution.py:1133
  278.3 22.1 %collective-permute-start.74 = (bf16[448,512]{1,0:T(8,128)(2,1)S(1)}, bf16[448,512]{1,0:T(8,128)(2,1)S(1)}, u32[]{:S(2)}, u32[]{:S(2)}) collective-permute-start(bf16[448,512]{1,0:T(8,128)(2,1)S(1)} %shard_map.223.refs_2_), channel_id=1, source_target_pairs={{0,4},{4,0},{8,12},{12,8},{16,20},{20,16},{24,28},{28,24},{1,5},{5... | collective-permute-start | bytes 1376264 | tf_op jit(solution)/shard_map/ppermute | solution.py:803
  279.8 20.7 %collective-permute-start.83 = (bf16[320,512]{1,0:T(8,128)(2,1)S(1)}, bf16[320,512]{1,0:T(8,128)(2,1)S(1)}, u32[]{:S(2)}, u32[]{:S(2)}) collective-permute-start(bf16[320,512]{1,0:T(8,128)(2,1)S(1)} %shard_map.229.refs_4_), channel_id=1, source_target_pairs={{0,4},{4,0},{8,12},{12,8},{16,20},{20,16},{24,28},{28,24},{1,5},{5... | collective-permute-start | bytes 983048 | tf_op jit(solution)/shard_map/ppermute | solution.py:803
  (86 other events, 689.7 us)

commit v4 on v3

--- a/solution.py
+++ b/solution.py
@@ -140,8 +140,8 @@
 
 
 def quarters(place):
-    half, core = place[0], place[1]
-    return 2 * half + core, 2 * (1 - half) + core, 2 * half + 1 - core, 2 * (1 - half) + 1 - core
+    half, part = place[0], place[1]
+    return 2 * part + half, 2 * part + 1 - half, 2 * (1 - part) + half, 2 * (1 - part) + 1 - half
 
 
 def quarter_lanes(quarter):
@@ -362,7 +362,7 @@
 
 
 def ffn_kernel(
-    layer, base, part_a, part_b, gains, up_own, down_own, up_a, down_a, up_b, down_b,
+    layer, base, part_a, part_b, gains, up_own, down_own, up_far, down_far,
     middle_out, normed_out, pre_own_out, pre_far_out, act_own_out, act_far_out, part_out,
 ):
     middle = base[...] + (part_a[...].astype(f32) + part_b[...].astype(f32))
@@ -372,12 +372,7 @@
     normed_out[...] = normed
     weights = (
         (up_own[layer], down_own[layer], pre_own_out, act_own_out),
-        (
-            jnp.concatenate([up_a[...], up_b[...]], axis=1),
-            jnp.concatenate([down_a[...], down_b[...]], axis=0),
-            pre_far_out,
-            act_far_out,
-        ),
+        (up_far[...], down_far[...], pre_far_out, act_far_out),
     )
     total = None
     for up, down, pre_out, act_out in weights:
@@ -393,7 +388,7 @@
 
 def shard_rows(whole, place, mine_out, theirs_out):
     first = [whole[:, m * LANES : (m + 1) * LANES] for m in range(4)]
-    even, odd = [jnp.where(place[1] == 0, first[2 * h], first[2 * h + 1]) for h in range(2)]
+    even, odd = [jnp.where(place[1] == 0, first[h], first[2 + h]) for h in range(2)]
     mine_out[...] = jnp.where(place[0] == 0, even, odd)
     theirs_out[...] = jnp.where(place[0] == 0, odd, even)
 
@@ -413,32 +408,27 @@
     if first:
         place, *refs = refs
         pieces, refs = refs[:4], refs[4:]
-        weights, outs = refs[:8], refs[8:]
+        weights, outs = refs[:6], refs[6:]
         resid_out, rows_out, d_up_own_out, d_up_far_out, part_out = outs
         for piece, quarter in zip(pieces, quarters(place)):
             resid_out[:, quarter_lanes(quarter)] = piece[...].astype(f32)
         resid = resid_out[...]
     else:
         base, part_a, part_b, hidden, gains, *refs = refs
-        weights, outs = refs[:8], refs[8:]
+        weights, outs = refs[:6], refs[6:]
         resid_out, rows_out, d_up_own_out, d_up_far_out, part_out, gain_out = outs
         back, gain_out[...] = norm_back(
             hidden[...], gains[layer + 1 : layer + 2], part_a[...].astype(f32) + part_b[...].astype(f32)
         )
         resid = base[...] + back
         resid_out[...] = resid
-    up_own, down_own, up_a, down_a, up_b, down_b, pre_own, pre_far = weights
+    up_own, down_own, up_far, down_far, pre_own, pre_far = weights
     rows = resid.astype(bf16)
     rows_out[...] = rows
     total = None
     for up, down, pre, out in (
         (up_own[layer], down_own[layer], pre_own, d_up_own_out),
-        (
-            jnp.concatenate([up_a[...], up_b[...]], axis=1),
-            jnp.concatenate([down_a[...], down_b[...]], axis=0),
-            pre_far,
-            d_up_far_out,
-        ),
+        (up_far[...], down_far[...], pre_far, d_up_far_out),
     ):
         d_up = (gelu_slope(pre[...]) * dot_nt(rows, down)).astype(bf16)
         out[...] = d_up
@@ -608,29 +598,20 @@
     return {"up": D, "down": units, "out": LANES, "qkv": 3 * LANES}[job]
 
 
-def wide_grads_kernel(jobs, place, *refs):
-    refs, (own_a, send_a, keep_b, send_b, own, far) = refs[:-6], refs[-6:]
-    side = lax.rem(place[2], 2)
+def fill_grads(jobs, refs, own, far):
     at = 0
     for job in jobs:
         mine, refs = refs[: JOB_REFS[job]], refs[JOB_REFS[job] :]
         if job == "up":
             normed, grad_own, grad_far = mine
-            units = grad_own.shape[1]
-            piece = units // 2
             own[at : at + D] = dot_tn(normed[...], grad_own[...]).astype(bf16)
-            found = dot_tn(normed[...], grad_far[...]).astype(bf16)
-            turned = jnp.concatenate([found[:, piece:], found[:, :piece]], axis=1)
-            far[at : at + D] = jnp.where(side == 0, found, turned)
+            far[at : at + D] = dot_tn(normed[...], grad_far[...]).astype(bf16)
             at += D
         elif job == "down":
             act_own, act_far, grad = mine
             units = act_own.shape[1]
-            piece = units // 2
             own[at : at + units] = dot_tn(act_own[...], grad[...]).astype(bf16)
-            found = dot_tn(act_far[...], grad[...]).astype(bf16)
-            turned = jnp.concatenate([found[piece:], found[:piece]], axis=0)
-            far[at : at + units] = jnp.where(side == 0, found, turned)
+            far[at : at + units] = dot_tn(act_far[...], grad[...]).astype(bf16)
             at += units
         elif job == "out":
             mixed, grad = mine
@@ -647,124 +628,100 @@
                     own[at : at + LANES, lanes] = found[lanes, :LANES]
                     far[at : at + LANES, lanes] = found[lanes, LANES:]
                 at += LANES
-    part, piece = at // 2, at // 4
-    own_a[...] = own[:part]
-    send_a[...] = far[:part]
-    for k, ref in enumerate((own, far)):
-        first, second = ref[part : part + piece], ref[part + piece :]
-        keep_b[k * piece : (k + 1) * piece] = jnp.where(side == 0, first, second)
-        send_b[k * piece : (k + 1) * piece] = jnp.where(side == 0, second, first)
-
-
-def second_kernel(place, own_a, got_a, keep_b, got_b, keep_a_out, send_a_out, keep_b_out, send_b_out):
-    piece = keep_a_out.shape[0]
-    side = lax.rem(place[2], 2)
-    total = own_a[...].astype(f32) + got_a[...].astype(f32)
-    keep_a_out[...] = jnp.where(side == 0, total[:piece], total[piece:])
-    send_a_out[...] = jnp.where(side == 0, total[piece:], total[:piece]).astype(bf16)
-    total = keep_b[...].astype(f32) + got_b[...].astype(f32)
-    keep_b_out[...] = total[:piece]
-    send_b_out[...] = total[piece:].astype(bf16)
-
-
-def line_bit(place, step):
-    return lax.rem(lax.div(place[2], 2 * step), 2)
-
-
-def give_half(place, step, total, keep_out, send_out):
+
+
+def grads_kernel(jobs, place, *refs):
+    fill_grads(jobs, refs[:-2], refs[-2], refs[-1])
+
+
+def shard_bit(place, bit):
+    return lax.rem(lax.div(place[2], 1 << bit), 2)
+
+
+def halve_kernel(bit, place, first, second, keep_out, send_out):
+    total = first[...].astype(f32) + second[...].astype(f32)
     rows = total.shape[0] // 2
-    low = line_bit(place, step) == 0
+    low = shard_bit(place, bit) == 0
     keep_out[...] = jnp.where(low, total[:rows], total[rows:])
     send_out[...] = jnp.where(low, total[rows:], total[:rows]).astype(bf16)
 
 
-def third_kernel(step, place, keep_a, got_a, keep_b, got_b, keep_out, send_out):
-    total = jnp.concatenate([keep_a[...] + got_a[...].astype(f32), keep_b[...] + got_b[...].astype(f32)], axis=0)
-    give_half(place, step, total, keep_out, send_out)
-
-
-def halve_kernel(step, place, keep, got, keep_out, send_out):
-    give_half(place, step, keep[...] + got[...].astype(f32), keep_out, send_out)
-
-
-def add_kernel(keep, got, out):
-    out[...] = (keep[...] + got[...].astype(f32)).astype(bf16)
-
-
-def join_kernel(step, place, mine, got, out):
-    low = line_bit(place, step) == 0
+def add_kernel(first, second, out):
+    out[...] = (first[...].astype(f32) + second[...].astype(f32)).astype(bf16)
+
+
+def join_kernel(bit, place, mine, got, out):
+    low = shard_bit(place, bit) == 0
     rows = mine.shape[0]
     out[:rows] = jnp.where(low, mine[...], got[...])
     out[rows:] = jnp.where(low, got[...], mine[...])
 
 
-def last_qkv_kernel(normed, d_qkv, own_out, far_out):
-    for kind in range(3):
-        found = dot_tn(normed[...], d_qkv[kind])
-        own_out[kind * D : (kind + 1) * D] = found[:, :LANES]
-        far_out[kind * D : (kind + 1) * D] = found[:, LANES:]
-
-
-def end_kernel(
-    shards, place, base, part_a, part_b, hidden, gains, own, far, *refs
-):
-    smalls, (mine_out, theirs_out, send_out) = refs[: 4 * LAYERS - 1], refs[4 * LAYERS - 1 :]
+def fold_kernel(ways, got, out, small_out):
+    rows = got.shape[0] // ways
+    total = sum(got[k * rows : (k + 1) * rows].astype(f32) for k in range(ways))
+    small_out[...] = total[rows - SMALL :, :LANES]
+    total = total[: rows - SMALL].astype(bf16)
+    for k in range(ways):
+        out[k * (rows - SMALL) : (k + 1) * (rows - SMALL)] = total
+
+
+def end_kernel(place, base, part_a, part_b, hidden, gains, *refs):
+    smalls, (mine_out, theirs_out, own_out, far_out) = refs[: 4 * LAYERS - 1], refs[4 * LAYERS - 1 :]
     gain_refs, blend_refs = smalls[: 2 * LAYERS - 1], smalls[2 * LAYERS - 1 :]
     back, gain = norm_back(hidden[...], gains[0:1], part_a[...].astype(f32) + part_b[...].astype(f32))
     shard_rows((base[...] + back).astype(bf16), place, mine_out, theirs_out)
-    block = own.shape[0] // shards
     gain_rows = jnp.concatenate([gain] + [ref[...] for ref in gain_refs], axis=0)
     blend_rows = jnp.concatenate([ref[...] for ref in blend_refs], axis=0)
+    extras = []
     for to in range(2):
         features = jnp.where(
             place[1] == 0,
-            gain_rows[:, 2 * to * LANES : (2 * to + 1) * LANES],
-            gain_rows[:, (2 * to + 1) * LANES : (2 * to + 2) * LANES],
+            gain_rows[:, to * LANES : (to + 1) * LANES],
+            gain_rows[:, (2 + to) * LANES : (3 + to) * LANES],
         )
         blends = jnp.where(place[0] == to, blend_rows[:, :LANES], blend_rows[:, LANES:])
-        empty = jnp.zeros((SMALL - 5 * LAYERS, LANES), f32)
-        extra = jnp.concatenate([features, blends, empty], axis=0).astype(bf16)
-        rows = jnp.where(place[0] == to, own[...], far[...])
-        for shard in range(shards):
-            send_out[2 * shard + to, :SMALL] = extra
-            send_out[2 * shard + to, SMALL:] = rows[shard * block : (shard + 1) * block].astype(bf16)
-
-
-def collect_kernel(shards, got, out, rest_out):
-    total = jnp.sum(got[...].astype(f32), axis=0)
-    rest_out[...] = total[:SMALL]
-    mine = total[SMALL:].astype(bf16)
-    for shard in range(shards):
-        out[shard] = mine
+        extras.append(jnp.concatenate([features, blends, jnp.zeros((SMALL - 5 * LAYERS, LANES), f32)], axis=0))
+    own_out[...] = jnp.where(place[0] == 0, extras[0], extras[1])
+    far_out[...] = jnp.where(place[0] == 0, extras[1], extras[0])
+
+
+def last_kernel(ways, own, far, small_own, small_far, out):
+    total = (own[...].astype(f32) + far[...].astype(f32)).astype(bf16)
+    small = small_own[...] + small_far[...]
+    small = jnp.concatenate([small, jnp.zeros((SMALL, D - LANES), f32)], axis=1).astype(bf16)
+    rows = total.shape[0] // ways
+    for k in range(ways):
+        at = k * (rows + SMALL)
+        out[at : at + rows] = total[k * rows : (k + 1) * rows]
+        out[at + rows : at + rows + SMALL] = small
 
 
 def in_order(place, mine, other):
-    side = lax.rem(place[2], 2)
-    piece = mine.shape[0] // 2
-    first, second = jnp.where(side == 0, mine[...], other[...]), jnp.where(side == 0, other[...], mine[...])
-    return jnp.concatenate([first[:piece], second[:piece], first[piece:], second[piece:]], axis=0)
-
-
-def finish_wide_kernel(groups, place, *refs):
-    outs = dict(zip(("up", "down", "out"), refs[-4:-1]))
+    low = shard_bit(place, 0) == 0
+    first, second = jnp.where(low, mine[...], other[...]), jnp.where(low, other[...], mine[...])
+    return jnp.concatenate([first, second], axis=0)
+
+
+def finish_kernel(groups, place, last, *refs):
+    refs, (up_out, down_out, out_out, qkv_out) = refs[:-4], refs[-4:]
+    outs = {"up": up_out, "down": down_out, "out": out_out}
+    qkv = {0: last[...]}
     for group, (layers, jobs) in enumerate(groups):
         whole = in_order(place, refs[2 * group], refs[2 * group + 1])
         at = 0
         for layer, job in zip(layers, jobs):
-            rows = whole[at : at + job_rows(job, outs["up"].shape[2])]
+            rows = whole[at : at + job_rows(job, up_out.shape[2])]
             at += rows.shape[0]
             if job == "qkv":
-                refs[-1][...] = rows
+                qkv[layer] = rows
             else:
                 outs[job][layer] = rows.astype(f32)
-
-
-def finish_qkv_kernel(last, above, out):
-    for kind in range(3):
-        out[0, kind] = last[kind * D : (kind + 1) * D].astype(f32)
-        for block in range(D // LANES):
-            lanes = slice(block * LANES, (block + 1) * LANES)
-            out[1, kind, lanes] = above[kind * LANES : (kind + 1) * LANES, lanes].astype(f32)
+    for layer in range(LAYERS):
+        for kind in range(3):
+            for block in range(D // LANES):
+                lanes = slice(block * LANES, (block + 1) * LANES)
+                qkv_out[layer, kind, lanes] = qkv[layer][kind * LANES : (kind + 1) * LANES, lanes].astype(f32)
 
 
 def call(body, outs, operands, scalars=0, scratch=(), scalar_outs=0, bulk=(), bulk_outs=()):
@@ -788,19 +745,14 @@
     return lax.optimization_barrier((value, *others))[0] if others else value
 
 
-def core_swap(value):
+def half_swap(value):
     count = lax.axis_size("mlp")
     return lax.ppermute(value, "mlp", [(i, i ^ 1) for i in range(count)])
 
 
-def far_swap(value):
+def part_swap(value):
     count = lax.axis_size("mlp")
     return lax.ppermute(value, "mlp", [(i, i ^ 2) for i in range(count)])
-
-
-def side_swap(value):
-    count = lax.axis_size("seq")
-    return lax.ppermute(value, "seq", [(i, i ^ 1) for i in range(count)])
 
 
 def chunk_move(value, target):
@@ -810,10 +762,8 @@
         goal = target(chunk)
         if goal is None or not 0 <= goal < 2 * shards:
             continue
-        for core in range(2):
-            pairs.append(
-                ((chunk // 2) * parts + (chunk % 2) * 2 + core, (goal // 2) * parts + (goal % 2) * 2 + core)
-            )
+        for part in range(2):
+            pairs.append(((chunk // 2) * parts + chunk % 2 + 2 * part, (goal // 2) * parts + goal % 2 + 2 * part))
     return lax.ppermute(value, AXES, pairs)
 
 
@@ -849,9 +799,9 @@
         )
 
 
-def line_swap(value, step):
+def shard_swap(value, bit):
     count = lax.axis_size("seq")
-    return lax.ppermute(value, "seq", [(i, i ^ (2 * step)) for i in range(count)])
+    return lax.ppermute(value, "seq", [(i, i ^ (1 << bit)) for i in range(count)])
 
 
 def by_place(flag, mine, other):
@@ -861,12 +811,12 @@
 def per_device(inputs, lengths, valid, norm_attn, w_qkv, blend, w_out, norm_ffn, w_up, w_down, grad_out):
     shards, parts = lax.axis_size("seq"), lax.axis_size("mlp")
     shard, part = lax.axis_index("seq"), lax.axis_index("mlp")
-    half, core = part // 2, part % 2
+    half = part % 2
     side = shard % 2
     rows = inputs.shape[0] // 2
     chunks = 2 * shards
     units = w_up.shape[2]
-    place = jnp.stack([half, core, shard]).astype(jnp.int32)
+    place = jnp.stack([half, part // 2, shard]).astype(jnp.int32)
 
     wide = 2 * LANES
     hidden_like = ((rows, D), f32)
@@ -882,23 +832,24 @@
     gain_like = ((1, D), f32)
 
     piece_like = ((rows + 3 * SMALL, LANES), bf16)
-    mine, theirs = call(pack_kernel, (piece_like, piece_like), (place, blend, inputs, norm_attn, norm_ffn), 2)
-    got = far_swap(theirs)
-    pieces = (mine, got, core_swap(mine), core_swap(got))
-    far_qkv = [far_swap(after(w_qkv[0], theirs)), None]
-    far_out = [far_swap(after(w_out[0], theirs)), None]
-
-    def up_piece(layer):
-        return lax.dynamic_slice_in_dim(w_up[layer], side * (units // 2), units // 2, 1)
-
-    def down_piece(layer):
-        return lax.dynamic_slice_in_dim(w_down[layer], side * (units // 2), units // 2, 0)
-
-    up_a, up_b, down_a, down_b = ([None] * LAYERS for _ in range(4))
-    up_a[0] = far_swap(after(up_piece(0), theirs))
+    mine, theirs = call(
+        pack_kernel,
+        (piece_like, piece_like),
+        (place, blend, inputs, norm_attn, norm_ffn),
+        2,
+        bulk=(2, 3, 4),
+    )
+    got = half_swap(theirs)
+    pieces = (mine, got, part_swap(mine), part_swap(got))
+    far_qkv, far_out, far_up, far_down = [
+        [half_swap(after(w[layer], theirs)) for layer in range(LAYERS)] for w in (w_qkv, w_out, w_up, w_down)
+    ]
+    grad_mine, grad_theirs = call(pack_grad_kernel, (shard_like, shard_like), (place, after(grad_out, theirs)), 1)
+    grad_got = half_swap(grad_theirs)
+    grad_pieces = (grad_mine, grad_got, part_swap(grad_mine), part_swap(grad_got))
 
     before = lax.ppermute(
-        valid[2 * rows - LANES :].reshape(1, LANES), "seq", [(source, source + 1) for source in range(shards - 1)]
+        after(valid, theirs)[2 * rows - LANES :].reshape(1, LANES), "seq", [(source, source + 1) for source in range(shards - 1)]
     )
     _, flag_count = flag_places(chunks)
     causal, causal_t, band, carried, tail, flags = call(
@@ -936,106 +887,82 @@
             )
         halo = chunk_move(halo, lambda c: c + 1)
         one, two, sums = call(far_kernel, (heads_like,) * 3, (qkv, causal))
-        (found, parts_got, at), arrived, _ = scan(state, flags, chunks, False, lambda: (one, halo))
-        if layer == 0:
-            down_a[0] = far_swap(after(down_piece(0), *arrived))
-            up_b[0] = side_swap(after(up_a[0], *arrived))
-            far_qkv[1] = far_swap(after(w_qkv[1], *arrived))
-            down_b[0] = side_swap(down_a[0])
-            far_out[1] = far_swap(after(w_out[1], *arrived))
-            up_a[1] = far_swap(after(up_piece(1), *arrived))
-            down_a[1] = far_swap(after(down_piece(1), *arrived))
-            up_b[1] = side_swap(up_a[1])
-            down_b[1] = side_swap(down_a[1])
+        (found, parts_got, at), arrived, _ = scan(state, flags, chunks, False, lambda: (one,))
         (near,) = call(near_kernel, (heads_like,), (place, qkv, halo, band), 1)
-        if layer == 0:
-            found = after(found, far_qkv[1])
         mixed, far_one, far_two, root, prefix, state, piece = call(
             functools.partial(mix_kernel, layer, at, len(parts_got)),
             (heads_low, heads_like, heads_like, heads_like, heads_like, state_like, low_like),
             (place, flags, qkv, near, one, two, sums, carried, blends, w_out, far_out[layer], found, *parts_got),
             2,
         )
-        weights = (w_up, w_down, up_a[layer], down_a[layer], up_b[layer], down_b[layer])
-        if layer == 0:
-            hidden = after(hidden, far_out[1], up_a[1])
+        weights = (w_up, w_down, far_up[layer], far_down[layer])
         middle, normed_ffn, pre_own, pre_far, act_own, act_far, piece_ffn = call(
             functools.partial(ffn_kernel, layer),
             (hidden_like, low_like, ffn_like, ffn_like, ffn_low, ffn_low, low_like),
-            (hidden, piece, core_swap(piece), gains, *weights),
+            (hidden, piece, part_swap(piece), gains, *weights),
         )
         saved.append(
             (hidden, normed, qkv, state, halo, mixed, far_one, far_two, root, prefix, middle, normed_ffn,
              weights, pre_own, pre_far, act_own, act_far)
         )
-        base, adds = middle, (piece_ffn, core_swap(piece_ffn))
-        if layer == 0:
-            base = after(base, down_a[1])
+        base, adds = middle, (piece_ffn, part_swap(piece_ffn))
     out_mine, out_theirs = call(output_kernel, (shard_like, shard_like), (place, base, *adds), 1)
-    output = jnp.concatenate(by_place(half, out_mine, far_swap(out_theirs)))
-
-    mine, theirs = call(pack_grad_kernel, (shard_like, shard_like), (place, after(grad_out, saved[0][2])), 1)
-    got = far_swap(theirs)
-    grad_pieces = (mine, got, core_swap(mine), core_swap(got))
+    output = jnp.concatenate(by_place(half, out_mine, half_swap(out_theirs)))
 
     base, adds = None, None
     d_gain_attn, d_gain_ffn, d_blends = [None] * LAYERS, [None] * LAYERS, [None] * LAYERS
     d_qkvs = [None] * LAYERS
-    first_steps = []
+    bits = (shards - 1).bit_length()
 
     def first_step(jobs, operands):
         height = sum(job_rows(job, units) for job in jobs)
-        outs = tuple(((height // 2, D), bf16) for _ in range(4))
-        scratch = (pltpu.VMEM((height, D), bf16), pltpu.VMEM((height, D), bf16))
-        return call(
-            functools.partial(wide_grads_kernel, jobs), outs, (place, *operands), 1, scratch=scratch, bulk_outs=(0, 2)
-        )
-
-    def second_step(layers, jobs, own_a, send_a, keep_b, send_b, *others):
-        height = own_a.shape[0] // 2
-        got_a, got_b = far_swap(send_a), side_swap(send_b)
-        return call(
-            second_kernel,
-            (((height, D), f32), ((height, D), bf16)) * 2,
-            (place, own_a, after(got_a, *others), keep_b, got_b),
-            1,
-            bulk=(1, 3),
-            bulk_outs=(0, 2),
-        )
-
-    line = [1 << k for k in range((shards // 2).bit_length() - 1)]
-
-    def third_step(keep_a, send_a, keep_b, send_b, *others):
-        height = keep_a.shape[0]
-        got_a, got_b = side_swap(send_a), far_swap(send_b)
-        keep, send = call(
-            functools.partial(third_kernel, line[0]),
-            (((height, D), f32), ((height, D), bf16)),
-            (place, keep_a, after(got_a, *others), keep_b, got_b),
-            1,
-            bulk=(1, 3),
-        )
-        for place_at, step in enumerate(line):
-            got = line_swap(send, step)
-            if place_at + 1 == len(line):
-                (value,) = call(add_kernel, (((height, D), bf16),), (keep, got))
-                break
+        like = ((height, D), bf16)
+        return call(functools.partial(grads_kernel, jobs), (like, like), (place, *operands), 1, bulk_outs=(0,))
+
+    def group_steps(own, far):
+        height = own.shape[0]
+        got = half_swap(far)
+        others = yield
+        if bits > 3:
+            (total,) = call(add_kernel, ((own.shape, bf16),), (own, after(got, *others)))
+            total = lax.psum(total, "seq").reshape(2, height // 2, D)
+            total = jnp.where(shard % 2 == 0, total, total[::-1])
+            for _ in range(2 * bits):
+                yield total
+            yield total[0], total[1]
+        keep = own
+        for bit in range(bits):
             height //= 2
             keep, send = call(
-                functools.partial(halve_kernel, line[place_at + 1]),
+                functools.partial(halve_kernel, bit),
                 (((height, D), f32), ((height, D), bf16)),
-                (place, keep, got),
+                (place, keep, after(got, *others)),
                 1,
+                bulk=(1,) if bit == 0 else (),
             )
-        for step in reversed(line):
+            got = shard_swap(send, bit)
+            others = yield send
+        (value,) = call(add_kernel, (((height, D), bf16),), (keep, after(got, *others)))
+        for bit in reversed(range(bits)):
+            got = shard_swap(value, bit)
+            if bit == 0:
+                break
+            others = yield value
             height *= 2
             (value,) = call(
-                functools.partial(join_kernel, step),
-                (((height, D), bf16),),
-                (place, value, line_swap(value, step)),
-                1,
+                functools.partial(join_kernel, bit), (((height, D), bf16),), (place, value, after(got, *others)), 1
             )
-        return value, side_swap(value)
+        yield value
+        yield (value, got)
+
+    groups = []
+
+    def start_group(layers, jobs, operands):
+        own, far = first_step(jobs, operands)
+        steps = group_steps(own, far)
+        next(steps)
+        groups.append((layers, jobs, steps))
+        return far
 
     for layer in reversed(range(LAYERS)):
         (hidden, normed, qkv, state, halo, mixed, far_one, far_two, root, prefix, middle, normed_ffn,
@@ -1058,43 +985,43 @@
             functools.partial(mix_back_kernel, layer),
             (hidden_like, low_like, heads_low, gain_like, heads_low, heads_low, heads_like, state_like,
              ((2, wide), f32)),
-            (place, resid, piece, core_swap(piece), middle, gains, w_out, far_out[layer], qkv, far_one, far_two,
+            (place, resid, piece, part_swap(piece), middle, gains, w_out, far_out[layer], qkv, far_one, far_two,
              root, carried, blends),
             1,
         )
+        before_near = ()
+        if layer == 0:
+            made = start_group(
+                (0, 1),
+                ("up", "qkv"),
+                (after(normed_ffn, state_back), d_up_own, d_up_far, saved[1][1], d_qkvs[1]),
+            )
+            made = start_group((0, 0), ("down", "out"), (after(act_own, made), act_far, grad_rows, mixed, out_rows))
+            before_near = (made,)
         ext = HALO + rows + HALO
         dq_near, dk_near, dv_near, halo_back, blend_near = call(
             functools.partial(near_back_kernel, layer),
             (heads_like, heads_like, heads_like, halo_like, ((1, wide), f32)),
-            (place, qkv, halo, band, d_mixed, blends),
+            (place, qkv, halo, band, after(d_mixed, *before_near), blends),
             1,
             scratch=(pltpu.VMEM((ext, LANES), f32), pltpu.VMEM((ext, LANES), f32)),
         )
         halo_back = chunk_move(halo_back, lambda c: c - 1)
-        (found, parts_got, at), arrived, value = scan(state_back, flags, chunks, True, lambda: (dq_near,))
+        before_scan = [dq_near]
+        if layer == 0:
+            before_scan.append(groups[0][2].send((dq_near,)))
+            before_scan.append(groups[1][2].send((before_scan[-1],)))
+        (found, parts_got, at), arrived, value = scan(state_back, flags, chunks, True, lambda: before_scan)
         ready = [value]
-        if layer + 1 == LAYERS:
-            jobs = ("up", "down", "out")
-            operands = (after(normed_ffn, value), d_up_own, d_up_far, act_own, act_far, grad_rows, mixed, out_rows)
-            groups = [((layer,) * 3, jobs, operands)]
+        if layer > 0:
+            made = start_group(
+                (layer,) * 3,
+                ("up", "down", "out"),
+                (after(normed_ffn, value), d_up_own, d_up_far, act_own, act_far, grad_rows, mixed, out_rows),
+            )
+            ready.append(made)
         else:
-            second = second_step(*first_steps[0], value)
-            above = saved[layer + 1][1]
-            groups = [
-                (
-                    (layer + 1, layer),
-                    ("qkv", "up"),
-                    (after(above, second[1], value), d_qkvs[layer + 1], normed_ffn, d_up_own, d_up_far),
-                ),
-                (
-                    (layer, layer),
-                    ("down", "out"),
-                    (after(act_own, second[1], value), act_far, grad_rows, mixed, out_rows),
-                ),
-            ]
-        for layers, jobs, operands in groups:
-            first_steps.append((layers, jobs, *first_step(jobs, operands)))
-            ready.append(first_steps[-1][3])
+            ready.append(groups[2][2].send((value,)))
         dq, dk_one, dk_two, dv = call(
             far_back_kernel,
             (heads_low, heads_like, heads_like, heads_like),
@@ -1102,6 +1029,11 @@
              dv_near),
             1,
         )
+        if layer > 0:
+            dq = after(dq, groups[0][2].send((dq,)))
+        else:
+            made = groups[0][2].send((dq,))
+            dq = after(dq, made)
         d_qkvs[layer], piece = call(
             functools.partial(qkv_back_kernel, layer, at, len(parts_got)),
             (qkv_like, low_like),
@@ -1110,44 +1042,56 @@
             2,
             scratch=(pltpu.VMEM((2, STATE, LANES), bf16),),
         )
-        base, adds = resid, (piece, core_swap(piece))
+        base, adds = resid, (piece, part_swap(piece))
         d_blends[layer] = (blend_near, blend_far)
 
-    last_like = ((3 * D, LANES), f32)
-    own, far = call(last_qkv_kernel, (last_like, last_like), (saved[0][1], d_qkvs[0]))
-    block = 3 * D // shards
+    last_like = ((3 * LANES, D), bf16)
+    own, far = call(functools.partial(grads_kernel, ("qkv",)), (last_like, last_like), (place, saved[0][1], d_qkvs[0]), 1)
     smalls = d_gain_attn[1:] + d_gain_ffn + [ref for pair in d_blends for ref in pair]
-    mine, theirs, send = call(
-        functools.partial(end_kernel, shards),
-        (shard_like, shard_like, ((chunks, SMALL + block, LANES), bf16)),
-        (place, base, *adds, saved[0][0], gains, own, far, *smalls),
+    small_like = ((SMALL, LANES), f32)
+    mine, theirs, small_own, small_far = call(
+        end_kernel,
+        (shard_like, shard_like, small_like, small_like),
+        (place, base, *adds, saved[0][0], gains, *smalls),
         1,
     )
-    groups = [[s * parts + h * 2 + c for s in range(shards) for h in range(2)] for c in range(2)]
-    got = lax.all_to_all(send, AXES, 0, 0, axis_index_groups=groups, tiled=True)
-    spread, rest = call(
-        functools.partial(collect_kernel, shards),
-        (((shards, block, LANES), bf16), ((SMALL, LANES), f32)),
-        (got,),
-    )
-    last = lax.all_to_all(spread, "seq", 0, 0, tiled=True).reshape(3 * D, LANES)
-    d_inputs = jnp.concatenate(by_place(half, mine, far_swap(theirs)))
-
-    wide_sums = [third_step(*second, d_qkvs[0])]
-    for step in first_steps[1:]:
-        wide_sums.append(third_step(*second_step(*step, d_qkvs[0])))
-    plan = [(step[0], step[1]) for step in first_steps]
-    count = 2 * LAYERS + 3 * LAYERS
-    d_norm_attn = rest[:LAYERS]
-    d_norm_ffn = rest[LAYERS : 2 * LAYERS]
-    d_blend = jnp.sum(rest[2 * LAYERS : count].reshape(LAYERS, 3, 2, HD), axis=3)
-    d_up, d_down, d_out, above = call(
-        functools.partial(finish_wide_kernel, plan),
-        (((LAYERS, D, units), f32), ((LAYERS, units, D), f32), ((LAYERS, LANES, D), f32), ((3 * LANES, D), bf16)),
-        (place, *[ref for pair in wide_sums for ref in pair]),
+    far, small_far = half_swap(far), half_swap(small_far)
+    if bits > 3:
+        last = lax.psum(own.astype(f32) + far.astype(f32), "seq").astype(bf16)
+        small = lax.psum(small_own + small_far, "seq")
+    else:
+        height = 3 * LANES + shards * SMALL
+        (made,) = call(
+            functools.partial(last_kernel, shards), (((height, D), bf16),), (own, far, small_own, small_far)
+        )
+        got = lax.all_to_all(made, "seq", 0, 0, tiled=True)
+    if bits > 3:
+        made = last
+    for turn in range(2 * bits - 1):
+        if turn == 2 and bits <= 3:
+            last, small = call(
+                functools.partial(fold_kernel, shards), (last_like, small_like), (after(got, made),)
+            )
+            last, made = lax.all_to_all(last, "seq", 0, 0, tiled=True), last
+        for _, _, steps in groups[(0 if turn < 2 * bits - 3 else 1) :]:
+            made = steps.send((made,))
+    d_inputs = jnp.concatenate(by_place(half, mine, half_swap(theirs)))
+    sums = [part for _, _, steps in groups for part in next(steps)]
+    d_up, d_down, d_out, d_qkv = call(
+        functools.partial(finish_kernel, [group[:2] for group in groups]),
+        (
+            ((LAYERS, D, units), f32),
+            ((LAYERS, units, D), f32),
+            ((LAYERS, LANES, D), f32),
+            ((LAYERS, 3, D, LANES), f32),
+        ),
+        (place, last, *sums),
         1,
     )
-    (d_qkv,) = call(finish_qkv_kernel, (((LAYERS, 3, D, LANES), f32),), (last, above))
+    count = 2 * LAYERS + 3 * LAYERS
+    d_norm_attn = small[:LAYERS]
+    d_norm_ffn = small[LAYERS : 2 * LAYERS]
+    d_blend = jnp.sum(small[2 * LAYERS : count].reshape(LAYERS, 3, 2, HD), axis=3)
     return (output, d_inputs, d_norm_attn, d_qkv, d_blend, d_out, d_norm_ffn, d_up, d_down)
 
 

time: 307 us -> 301 us (0.980)
  waiting for transfers between devices: 107 us -> 129 us
  starting transfers between devices: 113 us -> 97.7 us
  local copies, waits for them, and re-layouts: 17.4 us -> 5.85 us
    ppermute x56 -> x48, waiting for transfers between devices: 88 us -> 115 us  [the longest x18 63.2 us: shard_swap(): return lax.ppermute(value, 'seq', [(i, i ^ 1 << bit) for i in range(count)])]
    unnamed x66 -> x32, local copies, waits for them, and re-layouts: 11.8 us -> 3.87 us
    ppermute x56 -> x48, starting transfers between devices: 52.3 us -> 45.9 us  [the longest x18 27.1 us: shard_swap(): return lax.ppermute(value, 'seq', [(i, i ^ 1 << bit) for i in range(count)])]
    ppermute x28, starting transfers between devices: 48 us -> 42.3 us  [chunk_move(): return lax.ppermute(value, AXES, pairs)]
    ppermute x28, waiting for transfers between devices: 18.8 us -> 13.7 us  [chunk_move(): return lax.ppermute(value, AXES, pairs)]
    all_to_all x2, starting transfers between devices: 12.6 us -> 9.48 us  [the longest x1 5.28 us: per_device(): got = lax.all_to_all(made, 'seq', 0, 0, tiled=True)]
  transfers between devices with their start and end apart: 86 -> 78, of which waited for: 32 -> 27; matrix products, arithmetic and copies ran while one was open for 3% -> 1% of each run, Pallas kernels for 17% -> 16%
where the time goes in v4:
time: 301 us; the launch traced here: 300 us
  waiting for transfers between devices  129 us (43%)
  starting transfers between devices  97.7 us (32%)
  Pallas kernels  64.5 us (21%)
  local copies, waits for them, and re-layouts  5.85 us (2%)
    pallas_call x54, Pallas kernels, call(): pl.pallas_call(body, out_shape=tuple((jax.ShapeDtypeStruct(shape, kind) f...  64.5 us
    ppermute x18, waiting for transfers between devices, shard_swap(): return lax.ppermute(value, 'seq', [(i, i ^ 1 << bit) for i in range(count)])  63.2 us
    ppermute x12, waiting for transfers between devices, part_swap(): return lax.ppermute(value, 'mlp', [(i, i ^ 2) for i in range(count)])  50.2 us
    ppermute x28, starting transfers between devices, chunk_move(): return lax.ppermute(value, AXES, pairs)  42.3 us
    ppermute x18, starting transfers between devices, shard_swap(): return lax.ppermute(value, 'seq', [(i, i ^ 1 << bit) for i in range(count)])  27.1 us
    ppermute x28, waiting for transfers between devices, chunk_move(): return lax.ppermute(value, AXES, pairs)  13.7 us
    ppermute x12, starting transfers between devices, part_swap(): return lax.ppermute(value, 'mlp', [(i, i ^ 2) for i in range(count)])  10.2 us
  transfers between devices with their start and end apart: 78, of which 27 were waited for; matrix products, arithmetic and copies ran while one was open for 1% of the time, Pallas kernels for 16%

profile of v4, /device:TPU:0, one launch (start us, length us, event | category | flops | bytes accessed | tf_op | source)
XLA Modules:
  0.0 299.9 jit_solution(7491033682797380236)
XLA Ops:
  9.0 3.5 %collective-permute-start.4 = (s32[1,128]{1,0:T(1,128)S(1)}, s32[1,128]{1,0:T(1,128)S(1)}, u32[]{:S(2)}, u32[]{:S(2)}) collective-permute-start(s32[1,128]{1,0:T(1,128)S(1)} %slice_bitcast_fusion.8), channel_id=1, source_target_pairs={{0,4},{4,8},{8,12},{12,16},{16,20},{20,24},{24,28},{1,5},{5,9},{9,... | collective-permute-start | bytes 1544 | tf_op jit(solution)/shard_map/ppermute | solution.py:851
  26.8 4.2 %collective-permute-start.10 = (bf16[2,144,128]{2,1,0:T(8,128)(2,1)S(1)}, bf16[2,144,128]{2,1,0:T(8,128)(2,1)S(1)}, u32[]{:S(2)}, u32[]{:S(2)}) collective-permute-start(bf16[2,144,128]{2,1,0:T(8,128)(2,1)S(1)} %get-tuple-element.223), channel_id=1, source_target_pairs={{0,8},{2,10},{1,9},{3,11},{4,12},{6,14},{5,13},{7,15},{8,16},{10,1... | collective-permute-start | bytes 221192 | tf_op jit(solution)/shard_map/ppermute | solution.py:767
  31.0 5.2 %collective-permute-start.11 = (bf16[2,144,128]{2,1,0:T(8,128)(2,1)S(1)}, bf16[2,144,128]{2,1,0:T(8,128)(2,1)S(1)}, u32[]{:S(2)}, u32[]{:S(2)}) collective-permute-start(bf16[2,144,128]{2,1,0:T(8,128)(2,1)S(1)} %get-tuple-element.223), channel_id=1, source_target_pairs={{0,16},{2,18},{1,17},{3,19},{4,20},{6,22},{5,21},{7,23},{8,24},{10... | collective-permute-start | bytes 221192 | tf_op jit(solution)/shard_map/ppermute | solution.py:767
  37.5 2.9 shard_map.181.near
  42.3 7.4 %collective-permute-done.13.part_b = bf16[256,512]{1,0:T(8,128)(2,1)S(1)} collective-permute-done((bf16[256,512]{1,0:T(8,128)(2,1)S(1)}, bf16[256,512]{1,0:T(8,128)(2,1)S(1)}, u32[]{:S(2)}, u32[]{:S(2)}) %collective-permute-start.13) | collective-permute-done | bytes 262176 | tf_op jit(solution)/shard_map/ppermute | solution.py:755
  51.8 6.1 %collective-permute-done.16.refs_2_ = bf16[256,512]{1,0:T(8,128)(2,1)S(1)} collective-permute-done((bf16[256,512]{1,0:T(8,128)(2,1)S(1)}, bf16[256,512]{1,0:T(8,128)(2,1)S(1)}, u32[]{:S(2)}, u32[]{:S(2)}) %collective-permute-start.16) | collective-permute-done | bytes 262176 | tf_op jit(solution)/shard_map/ppermute | solution.py:755
  70.1 5.4 %collective-permute-start.24 = (bf16[2,144,128]{2,1,0:T(8,128)(2,1)S(1)}, bf16[2,144,128]{2,1,0:T(8,128)(2,1)S(1)}, u32[]{:S(2)}, u32[]{:S(2)}) collective-permute-start(bf16[2,144,128]{2,1,0:T(8,128)(2,1)S(1)} %get-tuple-element.241), channel_id=1, source_target_pairs={{0,16},{2,18},{1,17},{3,19},{4,20},{6,22},{5,21},{7,23},{8,24},{10... | collective-permute-start | bytes 221192 | tf_op jit(solution)/shard_map/ppermute | solution.py:767
  77.0 2.9 shard_map.187.near
  86.5 2.9 collective-permute-done.26.part_b
  94.6 8.6 %collective-permute-done.34.part_b = bf16[256,512]{1,0:T(8,128)(2,1)S(1)} collective-permute-done((bf16[256,512]{1,0:T(8,128)(2,1)S(1)}, bf16[256,512]{1,0:T(8,128)(2,1)S(1)}, u32[]{:S(2)}, u32[]{:S(2)}) %collective-permute-start.34) | collective-permute-done | bytes 262176 | tf_op jit(solution)/shard_map/ppermute | solution.py:755
  106.5 4.2 %shard_map.196 = (f32[256,256]{1,0:T(8,128)S(1)}, f32[256,256]{1,0:T(8,128)S(1)}, f32[256,256]{1,0:T(8,128)S(1)}, bf16[2,2,32,128]{3,2,1,0:T(8,128)(2,1)S(1)}, f32[1,256]{1,0:T(1,128)S(1)}) custom-call(s32[3]{0:T(128)S(1)} %pad_add_fusion.place.refs_0_, bf16[3,256,256]{2,1,0:T(8,128)(2,1)S(1)} %get-tuple-element.232.qkv, ...), custom_call_target="tpu_custom_call" | custom-call | tf_op jit(solution)/shard_map/pallas_call | solution.py:734
  118.5 2.7 shard_map.199
  122.2 3.1 %collective-permute-done.42.refs_2_ = bf16[2,144,128]{2,1,0:T(8,128)(2,1)S(1)} collective-permute-done((bf16[2,144,128]{2,1,0:T(8,128)(2,1)S(1)}, bf16[2,144,128]{2,1,0:T(8,128)(2,1)S(1)}, u32[]{:S(2)}, u32[]{:S(2)}) %collective-permute-start.42) | collective-permute-done | bytes 73760 | tf_op jit(solution)/shard_map/ppermute | solution.py:767
  127.2 7.1 %collective-permute-done.43.refs_2_ = bf16[256,512]{1,0:T(8,128)(2,1)S(1)} collective-permute-done((bf16[256,512]{1,0:T(8,128)(2,1)S(1)}, bf16[256,512]{1,0:T(8,128)(2,1)S(1)}, u32[]{:S(2)}, u32[]{:S(2)}) %collective-permute-start.43) | collective-permute-done | bytes 262176 | tf_op jit(solution)/shard_map/ppermute | solution.py:755
  136.3 6.2 %collective-permute-done.44.part_b = bf16[256,512]{1,0:T(8,128)(2,1)S(1)} collective-permute-done((bf16[256,512]{1,0:T(8,128)(2,1)S(1)}, bf16[256,512]{1,0:T(8,128)(2,1)S(1)}, u32[]{:S(2)}, u32[]{:S(2)}) %collective-permute-start.44) | collective-permute-done | bytes 262176 | tf_op jit(solution)/shard_map/ppermute | solution.py:755
  147.0 4.2 %shard_map.206 = (f32[256,256]{1,0:T(8,128)S(1)}, f32[256,256]{1,0:T(8,128)S(1)}, f32[256,256]{1,0:T(8,128)S(1)}, bf16[2,2,32,128]{3,2,1,0:T(8,128)(2,1)S(1)}, f32[1,256]{1,0:T(1,128)S(1)}) custom-call(s32[3]{0:T(128)S(1)} %pad_add_fusion.place.refs_0_, bf16[3,256,256]{2,1,0:T(8,128)(2,1)S(1)} %get-tuple-element.210.qkv, ...), custom_call_target="tpu_custom_call" | custom-call | tf_op jit(solution)/shard_map/pallas_call | solution.py:734
  151.2 9.8 %collective-permute-done.45.second = bf16[576,512]{1,0:T(8,128)(2,1)S(1)} collective-permute-done((bf16[576,512]{1,0:T(8,128)(2,1)S(1)}, bf16[576,512]{1,0:T(8,128)(2,1)S(1)}, u32[]{:S(2)}, u32[]{:S(2)}) %collective-permute-start.45) | collective-permute-done | bytes 589856 | tf_op jit(solution)/shard_map/ppermute | solution.py:804
  177.0 2.7 shard_map.211
  180.3 3.6 %collective-permute-done.54.refs_1_ = bf16[2,144,128]{2,1,0:T(8,128)(2,1)S(1)} collective-permute-done((bf16[2,144,128]{2,1,0:T(8,128)(2,1)S(1)}, bf16[2,144,128]{2,1,0:T(8,128)(2,1)S(1)}, u32[]{:S(2)}, u32[]{:S(2)}) %collective-permute-start.54) | collective-permute-done | bytes 73760 | tf_op jit(solution)/shard_map/ppermute | solution.py:767
  186.8 8.1 %collective-permute-done.56.part_b = bf16[256,512]{1,0:T(8,128)(2,1)S(1)} collective-permute-done((bf16[256,512]{1,0:T(8,128)(2,1)S(1)}, bf16[256,512]{1,0:T(8,128)(2,1)S(1)}, u32[]{:S(2)}, u32[]{:S(2)}) %collective-permute-start.56) | collective-permute-done | bytes 262176 | tf_op jit(solution)/shard_map/ppermute | solution.py:755
  198.0 5.3 %all-to-all-start = ((bf16[8,64,512]{2,1,0:T(8,128)(2,1)}), bf16[8,64,512]{2,1,0:T(8,128)(2,1)S(1)}, u32[]{:S(2)}, u32[]{:S(2)}) async-start(bf16[8,64,512]{2,1,0:T(8,128)(2,1)} %bitcast.13), calls=%async_computation | async-start | bytes 1048576 | tf_op jit(solution)/shard_map/all_to_all | solution.py:1067
  205.3 2.9 collective-permute-start.62
  208.2 16.2 %collective-permute-done.62.second = bf16[144,512]{1,0:T(8,128)(2,1)S(1)} collective-permute-done((bf16[144,512]{1,0:T(8,128)(2,1)S(1)}, bf16[144,512]{1,0:T(8,128)(2,1)S(1)}, u32[]{:S(2)}, u32[]{:S(2)}) %collective-permute-start.62) | collective-permute-done | bytes 147488 | tf_op jit(solution)/shard_map/ppermute | solution.py:804
  229.1 3.6 %collective-permute-done.65.got = bf16[144,512]{1,0:T(8,128)(2,1)S(1)} collective-permute-done((bf16[144,512]{1,0:T(8,128)(2,1)S(1)}, bf16[144,512]{1,0:T(8,128)(2,1)S(1)}, u32[]{:S(2)}, u32[]{:S(2)}) %collective-permute-start.65) | collective-permute-done | bytes 147488 | tf_op jit(solution)/shard_map/ppermute | solution.py:804
  237.1 11.1 %collective-permute-done.63.second = bf16[160,512]{1,0:T(8,128)(2,1)S(1)} collective-permute-done((bf16[160,512]{1,0:T(8,128)(2,1)S(1)}, bf16[160,512]{1,0:T(8,128)(2,1)S(1)}, u32[]{:S(2)}, u32[]{:S(2)}) %collective-permute-start.63) | collective-permute-done | bytes 163872 | tf_op jit(solution)/shard_map/ppermute | solution.py:804
  250.3 2.9 collective-permute-start.70
  254.0 4.2 %all-to-all-start.1 = ((bf16[8,48,512]{2,1,0:T(8,128)(2,1)}), bf16[8,48,512]{2,1,0:T(8,128)(2,1)S(1)}, u32[]{:S(2)}, u32[]{:S(2)}) async-start(bf16[8,48,512]{2,1,0:T(8,128)(2,1)} %bitcast.15), calls=%async_computation.1 | async-start | bytes 786432 | tf_op jit(solution)/shard_map/all_to_all | solution.py:1075
  263.3 2.7 collective-permute-start.72
  266.7 5.7 %collective-permute-done.72.got = bf16[80,512]{1,0:T(8,128)(2,1)S(1)} collective-permute-done((bf16[80,512]{1,0:T(8,128)(2,1)S(1)}, bf16[80,512]{1,0:T(8,128)(2,1)S(1)}, u32[]{:S(2)}, u32[]{:S(2)}) %collective-permute-start.72) | collective-permute-done | bytes 81952 | tf_op jit(solution)/shard_map/ppermute | solution.py:804
  272.9 4.2 %collective-permute-start.74 = (bf16[160,512]{1,0:T(8,128)(2,1)S(1)}, bf16[160,512]{1,0:T(8,128)(2,1)S(1)}, u32[]{:S(2)}, u32[]{:S(2)}) collective-permute-start(bf16[160,512]{1,0:T(8,128)(2,1)S(1)} %shard_map.228.mine), channel_id=1, source_target_pairs={{0,8},{4,12},{8,0},{12,4},{16,24},{20,28},{24,16},{28,20},{1,9},{5... | collective-permute-start | bytes 491528 | tf_op jit(solution)/shard_map/ppermute | solution.py:804
  285.1 11.3 %collective-permute-done.75.refs_5_ = bf16[320,512]{1,0:T(8,128)(2,1)S(1)} collective-permute-done((bf16[320,512]{1,0:T(8,128)(2,1)S(1)}, bf16[320,512]{1,0:T(8,128)(2,1)S(1)}, u32[]{:S(2)}, u32[]{:S(2)}) %collective-permute-start.75) | collective-permute-done | bytes 327712 | tf_op jit(solution)/shard_map/ppermute | solution.py:804
  296.4 3.5 %shard_map.231 = (f32[2,512,512]{2,1,0:T(8,128)}, f32[2,512,512]{2,1,0:T(8,128)}, f32[2,128,512]{2,1,0:T(8,128)}, f32[2,3,512,128]{3,2,1,0:T(8,128)}) custom-call(s32[3]{0:T(128)S(1)} %pad_add_fusion.place.refs_0_, bf16[384,512]{1,0:T(8,128)(2,1)S(1)} %bitcast.27, bf16[576,512]{1,0:T(8,128)(2,1)S(1)} %shard_map.224.refs_0_, ...), custom_call_target="tpu_custom_call" | custom-call | tf_op jit(solution)/shard_map/pallas_call | solution.py:734
  (224 shorter events, 123.7 us)
Async XLA Ops:
  5.0 10.6 %collective-permute-start.1 = (bf16[304,128]{1,0:T(8,128)(2,1)S(1)}, bf16[304,128]{1,0:T(8,128)(2,1)S(1)}, u32[]{:S(2)}, u32[]{:S(2)}) collective-permute-start(bf16[304,128]{1,0:T(8,128)(2,1)S(1)} %get-tuple-element.203.refs_0_), channel_id=1, source_target_pairs={{0,2},{1,3},{2,0},{3,1},{4,6},{5,7},{6,4},{7,5},{8,10},{9,11},{10,... | collective-permute-start | bytes 233480 | tf_op jit(solution)/shard_map/ppermute | solution.py:755
  12.7 29.6 %collective-permute-start.14 = (bf16[512,512]{1,0:T(8,128)(2,1)S(1)}, bf16[512,512]{1,0:T(8,128)(2,1)S(1)}, u32[]{:S(2)}, u32[]{:S(2)}) collective-permute-start(bf16[512,512]{1,0:T(8,128)(2,1)S(1)} %get-tuple-element.226), channel_id=1, source_target_pairs={{0,1},{1,0},{2,3},{3,2},{4,5},{5,4},{6,7},{7,6},{8,9},{9,8},{10,11... | collective-permute-start | bytes 1572872 | tf_op jit(solution)/shard_map/ppermute | solution.py:750
  13.8 28.4 %collective-permute-start.15 = (bf16[512,512]{1,0:T(8,128)(2,1)S(1)}, bf16[512,512]{1,0:T(8,128)(2,1)S(1)}, u32[]{:S(2)}, u32[]{:S(2)}) collective-permute-start(bf16[512,512]{1,0:T(8,128)(2,1)S(1)} %get-tuple-element.227), channel_id=1, source_target_pairs={{0,1},{1,0},{2,3},{3,2},{4,5},{5,4},{6,7},{7,6},{8,9},{9,8},{10,11... | collective-permute-start | bytes 1572872 | tf_op jit(solution)/shard_map/ppermute | solution.py:750
  19.0 12.0 %collective-permute-start.6 = (bf16[128,512]{1,0:T(8,128)(2,1)S(1)}, bf16[128,512]{1,0:T(8,128)(2,1)S(1)}, u32[]{:S(2)}, u32[]{:S(2)}) collective-permute-start(bf16[128,512]{1,0:T(8,128)(2,1)S(1)} %get-tuple-element.219), channel_id=1, source_target_pairs={{0,1},{1,0},{2,3},{3,2},{4,5},{5,4},{6,7},{7,6},{8,9},{9,8},{10,11... | collective-permute-start | bytes 393224 | tf_op jit(solution)/shard_map/ppermute | solution.py:750
  23.9 12.3 %collective-permute-start.5 = (bf16[2,2,32,128]{3,2,1,0:T(8,128)(2,1)S(1)}, bf16[2,2,32,128]{3,2,1,0:T(8,128)(2,1)S(1)}, u32[]{:S(2)}, u32[]{:S(2)}) collective-permute-start(bf16[2,2,32,128]{3,2,1,0:T(8,128)(2,1)S(1)} %get-tuple-element.211), channel_id=1, source_target_pairs={{0,1},{2,3},{1,4},{3,6},{4,5},{6,7},{5,8},{7,10},{8,9},{10,11},{9,... | collective-permute-start | bytes 98312 | tf_op jit(solution)/shard_map/ppermute | solution.py:767
  26.8 13.7 %collective-permute-start.10 = (bf16[2,144,128]{2,1,0:T(8,128)(2,1)S(1)}, bf16[2,144,128]{2,1,0:T(8,128)(2,1)S(1)}, u32[]{:S(2)}, u32[]{:S(2)}) collective-permute-start(bf16[2,144,128]{2,1,0:T(8,128)(2,1)S(1)} %get-tuple-element.223), channel_id=1, source_target_pairs={{0,8},{2,10},{1,9},{3,11},{4,12},{6,14},{5,13},{7,15},{8,16},{10,1... | collective-permute-start | bytes 221192 | tf_op jit(solution)/shard_map/ppermute | solution.py:767
  51.3 35.2 %collective-permute-start.27 = (bf16[512,512]{1,0:T(8,128)(2,1)S(1)}, bf16[512,512]{1,0:T(8,128)(2,1)S(1)}, u32[]{:S(2)}, u32[]{:S(2)}) collective-permute-start(bf16[512,512]{1,0:T(8,128)(2,1)S(1)} %get-tuple-element.243), channel_id=1, source_target_pairs={{0,1},{1,0},{2,3},{3,2},{4,5},{5,4},{6,7},{7,6},{8,9},{9,8},{10,11... | collective-permute-start | bytes 1572872 | tf_op jit(solution)/shard_map/ppermute | solution.py:750
  51.3 35.2 %collective-permute-start.28 = (bf16[512,512]{1,0:T(8,128)(2,1)S(1)}, bf16[512,512]{1,0:T(8,128)(2,1)S(1)}, u32[]{:S(2)}, u32[]{:S(2)}) collective-permute-start(bf16[512,512]{1,0:T(8,128)(2,1)S(1)} %get-tuple-element.244), channel_id=1, source_target_pairs={{0,1},{1,0},{2,3},{3,2},{4,5},{5,4},{6,7},{7,6},{8,9},{9,8},{10,11... | collective-permute-start | bytes 1572872 | tf_op jit(solution)/shard_map/ppermute | solution.py:750
  59.3 10.8 %collective-permute-start.19 = (bf16[128,512]{1,0:T(8,128)(2,1)S(1)}, bf16[128,512]{1,0:T(8,128)(2,1)S(1)}, u32[]{:S(2)}, u32[]{:S(2)}) collective-permute-start(bf16[128,512]{1,0:T(8,128)(2,1)S(1)} %get-tuple-element.237), channel_id=1, source_target_pairs={{0,1},{1,0},{2,3},{3,2},{4,5},{5,4},{6,7},{7,6},{8,9},{9,8},{10,11... | collective-permute-start | bytes 393224 | tf_op jit(solution)/shard_map/ppermute | solution.py:750
  64.4 11.1 %collective-permute-start.18 = (bf16[2,2,32,128]{3,2,1,0:T(8,128)(2,1)S(1)}, bf16[2,2,32,128]{3,2,1,0:T(8,128)(2,1)S(1)}, u32[]{:S(2)}, u32[]{:S(2)}) collective-permute-start(bf16[2,2,32,128]{3,2,1,0:T(8,128)(2,1)S(1)} %get-tuple-element.233), channel_id=1, source_target_pairs={{0,1},{2,3},{1,4},{3,6},{4,5},{6,7},{5,8},{7,10},{8,9},{10,11},{9,... | collective-permute-start | bytes 98312 | tf_op jit(solution)/shard_map/ppermute | solution.py:767
  67.5 12.5 %collective-permute-start.23 = (bf16[2,144,128]{2,1,0:T(8,128)(2,1)S(1)}, bf16[2,144,128]{2,1,0:T(8,128)(2,1)S(1)}, u32[]{:S(2)}, u32[]{:S(2)}) collective-permute-start(bf16[2,144,128]{2,1,0:T(8,128)(2,1)S(1)} %get-tuple-element.241), channel_id=1, source_target_pairs={{0,8},{2,10},{1,9},{3,11},{4,12},{6,14},{5,13},{7,15},{8,16},{10,1... | collective-permute-start | bytes 221192 | tf_op jit(solution)/shard_map/ppermute | solution.py:767
  145.2 20.6 %collective-permute-start.46 = (bf16[896,512]{1,0:T(8,128)(2,1)S(1)}, bf16[896,512]{1,0:T(8,128)(2,1)S(1)}, u32[]{:S(2)}, u32[]{:S(2)}) collective-permute-start(bf16[896,512]{1,0:T(8,128)(2,1)S(1)} %get-tuple-element.315), channel_id=1, source_target_pairs={{0,1},{1,0},{2,3},{3,2},{4,5},{5,4},{6,7},{7,6},{8,9},{9,8},{10,11... | collective-permute-start | bytes 2752520 | tf_op jit(solution)/shard_map/ppermute | solution.py:750
  145.3 15.7 %collective-permute-start.45 = (bf16[576,512]{1,0:T(8,128)(2,1)S(1)}, bf16[576,512]{1,0:T(8,128)(2,1)S(1)}, u32[]{:S(2)}, u32[]{:S(2)}) collective-permute-start(bf16[576,512]{1,0:T(8,128)(2,1)S(1)} %get-tuple-element.286), channel_id=1, source_target_pairs={{0,4},{4,0},{8,12},{12,8},{16,20},{20,16},{24,28},{28,24},{1,5},{5... | collective-permute-start | bytes 1769480 | tf_op jit(solution)/shard_map/ppermute | solution.py:804
  146.8 27.8 %collective-permute-start.50 = (bf16[640,512]{1,0:T(8,128)(2,1)S(1)}, bf16[640,512]{1,0:T(8,128)(2,1)S(1)}, u32[]{:S(2)}, u32[]{:S(2)}) collective-permute-start(bf16[640,512]{1,0:T(8,128)(2,1)S(1)} %get-tuple-element.321), channel_id=1, source_target_pairs={{0,1},{1,0},{2,3},{3,2},{4,5},{5,4},{6,7},{7,6},{8,9},{9,8},{10,11... | collective-permute-start | bytes 1966088 | tf_op jit(solution)/shard_map/ppermute | solution.py:750
  161.8 17.9 %collective-permute-start.51 = (bf16[288,512]{1,0:T(8,128)(2,1)S(1)}, bf16[288,512]{1,0:T(8,128)(2,1)S(1)}, u32[]{:S(2)}, u32[]{:S(2)}) collective-permute-start(bf16[288,512]{1,0:T(8,128)(2,1)S(1)} %get-tuple-element.326), channel_id=1, source_target_pairs={{0,8},{4,12},{8,0},{12,4},{16,24},{20,28},{24,16},{28,20},{1,9},{5... | collective-permute-start | bytes 884744 | tf_op jit(solution)/shard_map/ppermute | solution.py:804
  172.0 11.8 %collective-permute-start.54 = (bf16[2,144,128]{2,1,0:T(8,128)(2,1)S(1)}, bf16[2,144,128]{2,1,0:T(8,128)(2,1)S(1)}, u32[]{:S(2)}, u32[]{:S(2)}) collective-permute-start(bf16[2,144,128]{2,1,0:T(8,128)(2,1)S(1)} %get-tuple-element.331), channel_id=1, source_target_pairs={{16,0},{18,2},{17,1},{19,3},{20,4},{22,6},{21,5},{23,7},{24,8},{26... | collective-permute-start | bytes 221192 | tf_op jit(solution)/shard_map/ppermute | solution.py:767
  186.1 10.9 %collective-permute-start.58 = (bf16[384,512]{1,0:T(8,128)(2,1)S(1)}, bf16[384,512]{1,0:T(8,128)(2,1)S(1)}, u32[]{:S(2)}, u32[]{:S(2)}) collective-permute-start(bf16[384,512]{1,0:T(8,128)(2,1)S(1)} %get-tuple-element.363), channel_id=1, source_target_pairs={{0,1},{1,0},{2,3},{3,2},{4,5},{5,4},{6,7},{7,6},{8,9},{9,8},{10,11... | collective-permute-start | bytes 1179656 | tf_op jit(solution)/shard_map/ppermute | solution.py:750
  198.0 50.8 %all-to-all-start = ((bf16[8,64,512]{2,1,0:T(8,128)(2,1)}), bf16[8,64,512]{2,1,0:T(8,128)(2,1)S(1)}, u32[]{:S(2)}, u32[]{:S(2)}) async-start(bf16[8,64,512]{2,1,0:T(8,128)(2,1)} %bitcast.13), calls=%async_computation | async-start | bytes 1048576 | tf_op jit(solution)/shard_map/all_to_all | solution.py:1067
  203.3 21.3 %collective-permute-start.61 = (bf16[448,512]{1,0:T(8,128)(2,1)}, bf16[448,512]{1,0:T(8,128)(2,1)S(1)}, u32[]{:S(2)}, u32[]{:S(2)}) collective-permute-start(bf16[448,512]{1,0:T(8,128)(2,1)} %get-tuple-element.329), channel_id=1, source_target_pairs={{0,4},{4,0},{8,12},{12,8},{16,20},{20,16},{24,28},{28,24},{1,5},{5... | collective-permute-start | bytes 1376264 | tf_op jit(solution)/shard_map/ppermute | solution.py:804
  205.3 23.1 %collective-permute-start.60 = (bf16[320,512]{1,0:T(8,128)(2,1)}, bf16[320,512]{1,0:T(8,128)(2,1)S(1)}, u32[]{:S(2)}, u32[]{:S(2)}) collective-permute-start(bf16[320,512]{1,0:T(8,128)(2,1)} %copy-done.12), channel_id=1, source_target_pairs={{0,4},{4,0},{8,12},{12,8},{16,20},{20,16},{24,28},{28,24},{1,5},{5... | collective-permute-start | bytes 983048 | tf_op jit(solution)/shard_map/ppermute | solution.py:804
  205.3 19.1 %collective-permute-start.62 = (bf16[144,512]{1,0:T(8,128)(2,1)S(1)}, bf16[144,512]{1,0:T(8,128)(2,1)S(1)}, u32[]{:S(2)}, u32[]{:S(2)}) collective-permute-start(bf16[144,512]{1,0:T(8,128)(2,1)S(1)} %get-tuple-element.342), channel_id=1, source_target_pairs={{0,16},{4,20},{8,24},{12,28},{16,0},{20,4},{24,8},{28,12},{1,17},{... | collective-permute-start | bytes 442376 | tf_op jit(solution)/shard_map/ppermute | solution.py:804
  225.2 10.7 %collective-permute-start.64 = (bf16[224,512]{1,0:T(8,128)(2,1)S(1)}, bf16[224,512]{1,0:T(8,128)(2,1)S(1)}, u32[]{:S(2)}, u32[]{:S(2)}) collective-permute-start(bf16[224,512]{1,0:T(8,128)(2,1)S(1)} %get-tuple-element.371), channel_id=1, source_target_pairs={{0,8},{4,12},{8,0},{12,4},{16,24},{20,28},{24,16},{28,20},{1,9},{5... | collective-permute-start | bytes 688136 | tf_op jit(solution)/shard_map/ppermute | solution.py:804
  233.3 16.3 %collective-permute-start.66 = (bf16[288,512]{1,0:T(8,128)(2,1)S(1)}, bf16[288,512]{1,0:T(8,128)(2,1)S(1)}, u32[]{:S(2)}, u32[]{:S(2)}) collective-permute-start(bf16[288,512]{1,0:T(8,128)(2,1)S(1)} %shard_map.220.mine), channel_id=1, source_target_pairs={{0,8},{4,12},{8,0},{12,4},{16,24},{20,28},{24,16},{28,20},{1,9},{5... | collective-permute-start | bytes 884744 | tf_op jit(solution)/shard_map/ppermute | solution.py:804
  233.4 19.9 %collective-permute-start.29 = (bf16[256,512]{1,0:T(8,128)(2,1)S(1)}, bf16[256,512]{1,0:T(8,128)(2,1)S(1)}, u32[]{:S(2)}, u32[]{:S(2)}) collective-permute-start(bf16[256,512]{1,0:T(8,128)(2,1)S(1)} %copy-done.5), channel_id=1, source_target_pairs={{0,2},{1,3},{2,0},{3,1},{4,6},{5,7},{6,4},{7,5},{8,10},{9,11},{10,... | collective-permute-start | bytes 786440 | tf_op jit(solution)/shard_map/ppermute | solution.py:755
  234.0 14.2 %collective-permute-start.63 = (bf16[160,512]{1,0:T(8,128)(2,1)S(1)}, bf16[160,512]{1,0:T(8,128)(2,1)S(1)}, u32[]{:S(2)}, u32[]{:S(2)}) collective-permute-start(bf16[160,512]{1,0:T(8,128)(2,1)S(1)} %get-tuple-element.374), channel_id=1, source_target_pairs={{0,8},{4,12},{8,0},{12,4},{16,24},{20,28},{24,16},{28,20},{1,9},{5... | collective-permute-start | bytes 491528 | tf_op jit(solution)/shard_map/ppermute | solution.py:804
  236.5 13.7 %collective-permute-start.68 = (bf16[112,512]{1,0:T(8,128)(2,1)S(1)}, bf16[112,512]{1,0:T(8,128)(2,1)S(1)}, u32[]{:S(2)}, u32[]{:S(2)}) collective-permute-start(bf16[112,512]{1,0:T(8,128)(2,1)S(1)} %get-tuple-element.378), channel_id=1, source_target_pairs={{0,16},{4,20},{8,24},{12,28},{16,0},{20,4},{24,8},{28,12},{1,17},{... | collective-permute-start | bytes 344072 | tf_op jit(solution)/shard_map/ppermute | solution.py:804
  254.0 42.4 %all-to-all-start.1 = ((bf16[8,48,512]{2,1,0:T(8,128)(2,1)}), bf16[8,48,512]{2,1,0:T(8,128)(2,1)S(1)}, u32[]{:S(2)}, u32[]{:S(2)}) async-start(bf16[8,48,512]{2,1,0:T(8,128)(2,1)} %bitcast.15), calls=%async_computation.1 | async-start | bytes 786432 | tf_op jit(solution)/shard_map/all_to_all | solution.py:1075
  261.2 15.9 %collective-permute-start.71 = (bf16[224,512]{1,0:T(8,128)(2,1)S(1)}, bf16[224,512]{1,0:T(8,128)(2,1)S(1)}, u32[]{:S(2)}, u32[]{:S(2)}) collective-permute-start(bf16[224,512]{1,0:T(8,128)(2,1)S(1)} %shard_map.227.mine), channel_id=1, source_target_pairs={{0,8},{4,12},{8,0},{12,4},{16,24},{20,28},{24,16},{28,20},{1,9},{5... | collective-permute-start | bytes 688136 | tf_op jit(solution)/shard_map/ppermute | solution.py:804
  261.4 18.0 %collective-permute-start.57 = (bf16[256,128]{1,0:T(8,128)(2,1)S(1)}, bf16[256,128]{1,0:T(8,128)(2,1)S(1)}, u32[]{:S(2)}, u32[]{:S(2)}) collective-permute-start(bf16[256,128]{1,0:T(8,128)(2,1)S(1)} %copy-done.14), channel_id=1, source_target_pairs={{0,1},{1,0},{2,3},{3,2},{4,5},{5,4},{6,7},{7,6},{8,9},{9,8},{10,11... | collective-permute-start | bytes 196616 | tf_op jit(solution)/shard_map/ppermute | solution.py:750
  261.4 23.7 %collective-permute-start.67 = (bf16[576,512]{1,0:T(8,128)(2,1)S(1)}, bf16[576,512]{1,0:T(8,128)(2,1)S(1)}, u32[]{:S(2)}, u32[]{:S(2)}) collective-permute-start(bf16[576,512]{1,0:T(8,128)(2,1)S(1)} %shard_map.224.refs_0_), channel_id=1, source_target_pairs={{0,4},{4,0},{8,12},{12,8},{16,20},{20,16},{24,28},{28,24},{1,5},{5... | collective-permute-start | bytes 1769480 | tf_op jit(solution)/shard_map/ppermute | solution.py:804
  277.8 18.6 %collective-permute-start.73 = (bf16[448,512]{1,0:T(8,128)(2,1)S(1)}, bf16[448,512]{1,0:T(8,128)(2,1)S(1)}, u32[]{:S(2)}, u32[]{:S(2)}) collective-permute-start(bf16[448,512]{1,0:T(8,128)(2,1)S(1)} %shard_map.229.refs_2_), channel_id=1, source_target_pairs={{0,4},{4,0},{8,12},{12,8},{16,20},{20,16},{24,28},{28,24},{1,5},{5... | collective-permute-start | bytes 1376264 | tf_op jit(solution)/shard_map/ppermute | solution.py:804
  281.5 14.9 %collective-permute-start.75 = (bf16[320,512]{1,0:T(8,128)(2,1)S(1)}, bf16[320,512]{1,0:T(8,128)(2,1)S(1)}, u32[]{:S(2)}, u32[]{:S(2)}) collective-permute-start(bf16[320,512]{1,0:T(8,128)(2,1)S(1)} %shard_map.230.refs_4_), channel_id=1, source_target_pairs={{0,4},{4,0},{8,12},{12,8},{16,20},{20,16},{24,28},{28,24},{1,5},{5... | collective-permute-start | bytes 983048 | tf_op jit(solution)/shard_map/ppermute | solution.py:804
  (61 other events, 377.6 us)

commit v5 on v4

--- a/solution.py
+++ b/solution.py
@@ -180,7 +180,7 @@
     return places, at
 
 
-def setup_kernel(chunks, place, lengths, valid, before, causal_out, causal_t_out, band_out, carried_out, tail_out, flags_out):
+def setup_kernel(chunks, place, lengths, valid, causal_out, causal_t_out, carried_out, tail_out, flags_out):
     rows = causal_out.shape[0]
     chunk = place[2] * 2 + place[0]
     first_row = chunk * rows
@@ -195,7 +195,6 @@
     both = jnp.concatenate([starts, starts], axis=1)
     words = valid[...]
     own_words = jnp.where(place[0] == 0, words[:, :rows], words[:, rows:])
-    last_words = jnp.where(place[0] == 0, before[...], words[:, rows - LANES : rows])
     row_at = lax.broadcasted_iota(jnp.int32, (rows, rows), 0)
     lane_at = lax.broadcasted_iota(jnp.int32, (rows, rows), 1)
     own_column = jnp.sum(jnp.where(row_at == lane_at, own_words, 0), axis=1, keepdims=True)
@@ -205,18 +204,6 @@
     carried_out[...] = jnp.where(starts < first_row, 1.0, 0.0)
     last_start = start_of(first_row + rows - 1)
     tail_out[...] = jnp.where((starts == last_start) & (own_column == 1), 1.0, 0.0).astype(bf16)
-    all_words = jnp.concatenate([last_words, own_words, jnp.zeros((1, LANES), jnp.int32)], axis=1)
-    tile_row = lax.broadcasted_iota(jnp.int32, (TILE, LANES), 0)
-    tile_lane = lax.broadcasted_iota(jnp.int32, (TILE, LANES), 1)
-    gap = tile_row + HALO - tile_lane
-    for tile in range(rows // TILE):
-        key_starts = start_of(first_row + tile * TILE - HALO + lax.broadcasted_iota(jnp.int32, (1, LANES), 1))
-        offset = LANES - HALO + tile * TILE
-        key_words = all_words[:, offset : offset + LANES]
-        at = slice(tile * TILE, (tile + 1) * TILE)
-        allowed = (gap >= 0) & (gap <= BAND) & (starts[at] == key_starts) & ((key_words == 1) | (gap == 0))
-        band_out[at] = jnp.where(allowed, 0.0, masked_score)
-
     places, _ = flag_places(chunks)
     for reverse in (False, True):
         edge = start_of(first_row + (rows - 1 if reverse else 0))
@@ -237,6 +224,31 @@
                 at = places[reverse, stage] + 2 * step
                 flags_out[at] = jnp.where(ahead & (start == edge), 1.0, 0.0)
                 flags_out[at + 1] = jnp.where(start == group, 1.0, 0.0)
+
+
+def band_kernel(place, lengths, valid, before, band_out):
+    rows = band_out.shape[0]
+    first_row = (place[2] * 2 + place[0]) * rows
+    ends = item_ends(lengths)
+
+    def start_of(positions):
+        return item_start(lengths, ends, positions)
+
+    words = valid[...]
+    own_words = jnp.where(place[0] == 0, words[:, :rows], words[:, rows:])
+    last_words = jnp.where(place[0] == 0, before[...], words[:, rows - LANES : rows])
+    starts = start_of(first_row + lax.broadcasted_iota(jnp.int32, (rows, LANES), 0))
+    all_words = jnp.concatenate([last_words, own_words, jnp.zeros((1, LANES), jnp.int32)], axis=1)
+    tile_row = lax.broadcasted_iota(jnp.int32, (TILE, LANES), 0)
+    tile_lane = lax.broadcasted_iota(jnp.int32, (TILE, LANES), 1)
+    gap = tile_row + HALO - tile_lane
+    for tile in range(rows // TILE):
+        key_starts = start_of(first_row + tile * TILE - HALO + lax.broadcasted_iota(jnp.int32, (1, LANES), 1))
+        offset = LANES - HALO + tile * TILE
+        key_words = all_words[:, offset : offset + LANES]
+        at = slice(tile * TILE, (tile + 1) * TILE)
+        allowed = (gap >= 0) & (gap <= BAND) & (starts[at] == key_starts) & ((key_words == 1) | (gap == 0))
+        band_out[at] = jnp.where(allowed, 0.0, masked_score)
 
 
 def combine_kernel(at, ways, has_found, flags, *refs):
@@ -638,12 +650,16 @@
     return lax.rem(lax.div(place[2], 1 << bit), 2)
 
 
-def halve_kernel(bit, place, first, second, keep_out, send_out):
-    total = first[...].astype(f32) + second[...].astype(f32)
+def give_half(bit, place, total, keep_out, send_out):
     rows = total.shape[0] // 2
     low = shard_bit(place, bit) == 0
     keep_out[...] = jnp.where(low, total[:rows], total[rows:])
     send_out[...] = jnp.where(low, total[rows:], total[:rows]).astype(bf16)
+
+
+def halve_kernel(bit, rows, place, first, second, keep_out, send_out):
+    at = slice(*rows)
+    give_half(bit, place, first[at].astype(f32) + second[at].astype(f32), keep_out, send_out)
 
 
 def add_kernel(first, second, out):
@@ -655,15 +671,6 @@
     rows = mine.shape[0]
     out[:rows] = jnp.where(low, mine[...], got[...])
     out[rows:] = jnp.where(low, got[...], mine[...])
-
-
-def fold_kernel(ways, got, out, small_out):
-    rows = got.shape[0] // ways
-    total = sum(got[k * rows : (k + 1) * rows].astype(f32) for k in range(ways))
-    small_out[...] = total[rows - SMALL :, :LANES]
-    total = total[: rows - SMALL].astype(bf16)
-    for k in range(ways):
-        out[k * (rows - SMALL) : (k + 1) * (rows - SMALL)] = total
 
 
 def end_kernel(place, base, part_a, part_b, hidden, gains, *refs):
@@ -686,29 +693,25 @@
     far_out[...] = jnp.where(place[0] == 0, extras[1], extras[0])
 
 
-def last_kernel(ways, own, far, small_own, small_far, out):
-    total = (own[...].astype(f32) + far[...].astype(f32)).astype(bf16)
-    small = small_own[...] + small_far[...]
-    small = jnp.concatenate([small, jnp.zeros((SMALL, D - LANES), f32)], axis=1).astype(bf16)
-    rows = total.shape[0] // ways
-    for k in range(ways):
-        at = k * (rows + SMALL)
-        out[at : at + rows] = total[k * rows : (k + 1) * rows]
-        out[at + rows : at + rows + SMALL] = small
-
-
-def in_order(place, mine, other):
-    low = shard_bit(place, 0) == 0
+def last_kernel(bit, place, own, far, small_own, small_far, keep_out, send_out):
+    small = jnp.concatenate([small_own[...] + small_far[...], jnp.zeros((SMALL, D - LANES), f32)], axis=1)
+    small = jnp.concatenate([small, jnp.zeros((LANES - SMALL, D), f32)], axis=0)
+    total = jnp.concatenate([own[...].astype(f32) + far[...].astype(f32), small], axis=0)
+    give_half(bit, place, total, keep_out, send_out)
+
+
+def in_order(bit, place, mine, other):
+    low = shard_bit(place, bit) == 0
     first, second = jnp.where(low, mine[...], other[...]), jnp.where(low, other[...], mine[...])
     return jnp.concatenate([first, second], axis=0)
 
 
-def finish_kernel(groups, place, last, *refs):
-    refs, (up_out, down_out, out_out, qkv_out) = refs[:-4], refs[-4:]
+def finish_kernel(groups, place, *refs):
+    refs, (up_out, down_out, out_out, qkv_out, small_out) = refs[:-5], refs[-5:]
     outs = {"up": up_out, "down": down_out, "out": out_out}
-    qkv = {0: last[...]}
-    for group, (layers, jobs) in enumerate(groups):
-        whole = in_order(place, refs[2 * group], refs[2 * group + 1])
+    qkv = {}
+    for group, (layers, jobs, bit) in enumerate(groups):
+        whole = in_order(bit, place, refs[2 * group], refs[2 * group + 1])
         at = 0
         for layer, job in zip(layers, jobs):
             rows = whole[at : at + job_rows(job, up_out.shape[2])]
@@ -717,6 +720,7 @@
                 qkv[layer] = rows
             else:
                 outs[job][layer] = rows.astype(f32)
+    small_out[...] = whole[at : at + SMALL, :LANES].astype(f32)
     for layer in range(LAYERS):
         for kind in range(3):
             for block in range(D // LANES):
@@ -849,22 +853,24 @@
     grad_pieces = (grad_mine, grad_got, part_swap(grad_mine), part_swap(grad_got))
 
     before = lax.ppermute(
-        after(valid, theirs)[2 * rows - LANES :].reshape(1, LANES), "seq", [(source, source + 1) for source in range(shards - 1)]
+        after(valid, pieces[3])[2 * rows - LANES :].reshape(1, LANES), "seq", [(source, source + 1) for source in range(shards - 1)]
     )
     _, flag_count = flag_places(chunks)
-    causal, causal_t, band, carried, tail, flags = call(
+    causal, causal_t, carried, tail, flags = call(
         functools.partial(setup_kernel, chunks),
         (
             ((rows, rows), bf16),
             ((rows, rows), bf16),
             ((rows, LANES), f32),
-            ((rows, LANES), f32),
             ((rows, LANES), bf16),
             ((flag_count,), f32),
         ),
-        (place, lengths, valid.reshape(1, 2 * rows), before),
+        (place, lengths, valid.reshape(1, 2 * rows)),
         2,
         scalar_outs=1,
+    )
+    (band,) = call(
+        band_kernel, (((rows, LANES), f32),), (place, lengths, valid.reshape(1, 2 * rows), before), 2
     )
 
     saved = []
@@ -888,6 +894,8 @@
         halo = chunk_move(halo, lambda c: c + 1)
         one, two, sums = call(far_kernel, (heads_like,) * 3, (qkv, causal))
         (found, parts_got, at), arrived, _ = scan(state, flags, chunks, False, lambda: (one,))
+        if layer == 0:
+            found = after(found, *grad_pieces)
         (near,) = call(near_kernel, (heads_like,), (place, qkv, halo, band), 1)
         mixed, far_one, far_two, root, prefix, state, piece = call(
             functools.partial(mix_kernel, layer, at, len(parts_got)),
@@ -913,39 +921,48 @@
     d_gain_attn, d_gain_ffn, d_blends = [None] * LAYERS, [None] * LAYERS, [None] * LAYERS
     d_qkvs = [None] * LAYERS
     bits = (shards - 1).bit_length()
+    side_first, line_first = (0, 1, 2), (1, 2, 0)
 
     def first_step(jobs, operands):
         height = sum(job_rows(job, units) for job in jobs)
         like = ((height, D), bf16)
         return call(functools.partial(grads_kernel, jobs), (like, like), (place, *operands), 1, bulk_outs=(0,))
 
-    def group_steps(own, far):
-        height = own.shape[0]
-        got = half_swap(far)
+    def group_steps(order, rows, first, second):
+        height = rows[1] - rows[0]
         others = yield
-        if bits > 3:
-            (total,) = call(add_kernel, ((own.shape, bf16),), (own, after(got, *others)))
-            total = lax.psum(total, "seq").reshape(2, height // 2, D)
-            total = jnp.where(shard % 2 == 0, total, total[::-1])
-            for _ in range(2 * bits):
+        if bits != 3:
+            if len(first) > 1:
+                small = jnp.pad(first[1] + second[1], ((0, LANES - SMALL), (0, D - LANES)))
+                total = jnp.concatenate([first[0].astype(f32) + second[0].astype(f32), small])
+            else:
+                total = (first[0].astype(f32) + second[0].astype(f32))[slice(*rows)]
+            total = lax.psum(total, "seq").astype(bf16).reshape(2, height // 2, D)
+            total = jnp.where((shard >> order[0]) % 2 == 0, total, total[::-1])
+            for _ in range(6):
                 yield total
             yield total[0], total[1]
-        keep = own
-        for bit in range(bits):
+        for at, bit in enumerate(order):
             height //= 2
+            if at == 0 and len(first) > 1:
+                body, operands = functools.partial(last_kernel, bit), (first[0], second[0], first[1], second[1])
+            elif at == 0:
+                body, operands = functools.partial(halve_kernel, bit, rows), (first[0], second[0])
+            else:
+                body, operands = functools.partial(halve_kernel, bit, (0, 2 * height)), (keep, got)
             keep, send = call(
-                functools.partial(halve_kernel, bit),
+                body,
                 (((height, D), f32), ((height, D), bf16)),
-                (place, keep, after(got, *others)),
+                (place, operands[0], after(operands[1], *others), *operands[2:]),
                 1,
-                bulk=(1,) if bit == 0 else (),
+                bulk=(1,) if at == 0 else (),
             )
             got = shard_swap(send, bit)
             others = yield send
         (value,) = call(add_kernel, (((height, D), bf16),), (keep, after(got, *others)))
-        for bit in reversed(range(bits)):
+        for bit in reversed(order):
             got = shard_swap(value, bit)
-            if bit == 0:
+            if bit == order[0]:
                 break
             others = yield value
             height *= 2
@@ -957,12 +974,13 @@
 
     groups = []
 
-    def start_group(layers, jobs, operands):
-        own, far = first_step(jobs, operands)
-        steps = group_steps(own, far)
+    def start_group(layers, jobs, order, rows, first, second):
+        steps = group_steps(order, rows, first, second)
         next(steps)
-        groups.append((layers, jobs, steps))
-        return far
+        groups.append((layers, jobs, order[0], steps))
+
+    def step(index, *others):
+        return groups[index][3].send(others)
 
     for layer in reversed(range(LAYERS)):
         (hidden, normed, qkv, state, halo, mixed, far_one, far_two, root, prefix, middle, normed_ffn,
@@ -989,39 +1007,37 @@
              root, carried, blends),
             1,
         )
-        before_near = ()
-        if layer == 0:
-            made = start_group(
-                (0, 1),
-                ("up", "qkv"),
-                (after(normed_ffn, state_back), d_up_own, d_up_far, saved[1][1], d_qkvs[1]),
-            )
-            made = start_group((0, 0), ("down", "out"), (after(act_own, made), act_far, grad_rows, mixed, out_rows))
-            before_near = (made,)
         ext = HALO + rows + HALO
         dq_near, dk_near, dv_near, halo_back, blend_near = call(
             functools.partial(near_back_kernel, layer),
             (heads_like, heads_like, heads_like, halo_like, ((1, wide), f32)),
-            (place, qkv, halo, band, after(d_mixed, *before_near), blends),
+            (place, qkv, halo, band, d_mixed, blends),
             1,
             scratch=(pltpu.VMEM((ext, LANES), f32), pltpu.VMEM((ext, LANES), f32)),
         )
         halo_back = chunk_move(halo_back, lambda c: c - 1)
-        before_scan = [dq_near]
-        if layer == 0:
-            before_scan.append(groups[0][2].send((dq_near,)))
-            before_scan.append(groups[1][2].send((before_scan[-1],)))
-        (found, parts_got, at), arrived, value = scan(state_back, flags, chunks, True, lambda: before_scan)
-        ready = [value]
+        (found, parts_got, at), arrived, value = scan(state_back, flags, chunks, True, lambda: (dq_near,))
         if layer > 0:
-            made = start_group(
-                (layer,) * 3,
-                ("up", "down", "out"),
-                (after(normed_ffn, value), d_up_own, d_up_far, act_own, act_far, grad_rows, mixed, out_rows),
+            jobs = ("up", "down", "out")
+            own, far = first_step(
+                jobs, (after(normed_ffn, value), d_up_own, d_up_far, act_own, act_far, grad_rows, mixed, out_rows)
             )
-            ready.append(made)
+            start_group((layer,) * 3, jobs, side_first, (0, own.shape[0]), (own,), (half_swap(far),))
+            made = far
         else:
-            ready.append(groups[2][2].send((value,)))
+            made = step(0, value)
+            jobs = ("up", "qkv", "down", "out")
+            own, far = first_step(
+                jobs,
+                (after(normed_ffn, made), d_up_own, d_up_far, saved[1][1], d_qkvs[1], act_own, act_far, grad_rows,
+                 mixed, out_rows),
+            )
+            cut = job_rows("up", units) + job_rows("qkv", units)
+            got = half_swap(far)
+            start_group((0, 1), jobs[:2], side_first, (0, cut), (own,), (got,))
+            start_group((0, 0), jobs[2:], line_first, (cut, own.shape[0]), (own,), (got,))
+            made = far
+        ready = [made]
         dq, dk_one, dk_two, dv = call(
             far_back_kernel,
             (heads_low, heads_like, heads_like, heads_like),
@@ -1029,11 +1045,6 @@
              dv_near),
             1,
         )
-        if layer > 0:
-            dq = after(dq, groups[0][2].send((dq,)))
-        else:
-            made = groups[0][2].send((dq,))
-            dq = after(dq, made)
         d_qkvs[layer], piece = call(
             functools.partial(qkv_back_kernel, layer, at, len(parts_got)),
             (qkv_like, low_like),
@@ -1043,49 +1054,37 @@
             scratch=(pltpu.VMEM((2, STATE, LANES), bf16),),
         )
         base, adds = resid, (piece, part_swap(piece))
+        if layer > 0:
+            base = after(base, step(0, piece))
         d_blends[layer] = (blend_near, blend_far)
 
     last_like = ((3 * LANES, D), bf16)
-    own, far = call(functools.partial(grads_kernel, ("qkv",)), (last_like, last_like), (place, saved[0][1], d_qkvs[0]), 1)
+    made = step(0, step(2, step(1, piece)))
+    own, far = call(functools.partial(grads_kernel, ("qkv",)), (last_like, last_like), (place, after(saved[0][1], made), d_qkvs[0]), 1)
     smalls = d_gain_attn[1:] + d_gain_ffn + [ref for pair in d_blends for ref in pair]
     small_like = ((SMALL, LANES), f32)
     mine, theirs, small_own, small_far = call(
         end_kernel,
         (shard_like, shard_like, small_like, small_like),
-        (place, base, *adds, saved[0][0], gains, *smalls),
+        (place, after(base, far), *adds, saved[0][0], gains, *smalls),
         1,
     )
-    far, small_far = half_swap(far), half_swap(small_far)
-    if bits > 3:
-        last = lax.psum(own.astype(f32) + far.astype(f32), "seq").astype(bf16)
-        small = lax.psum(small_own + small_far, "seq")
-    else:
-        height = 3 * LANES + shards * SMALL
-        (made,) = call(
-            functools.partial(last_kernel, shards), (((height, D), bf16),), (own, far, small_own, small_far)
-        )
-        got = lax.all_to_all(made, "seq", 0, 0, tiled=True)
-    if bits > 3:
-        made = last
-    for turn in range(2 * bits - 1):
-        if turn == 2 and bits <= 3:
-            last, small = call(
-                functools.partial(fold_kernel, shards), (last_like, small_like), (after(got, made),)
-            )
-            last, made = lax.all_to_all(last, "seq", 0, 0, tiled=True), last
-        for _, _, steps in groups[(0 if turn < 2 * bits - 3 else 1) :]:
-            made = steps.send((made,))
+    start_group((0,), ("qkv",), line_first, (0, 4 * LANES), (own, small_own), (half_swap(far), half_swap(small_far)))
+    made = step(3, mine)
+    for index in (0, 1, 2, 3, 0, 1, 2, 3, 0, 1, 2, 3, 1, 2, 3, 1, 2, 3):
+        made = step(index, made)
     d_inputs = jnp.concatenate(by_place(half, mine, half_swap(theirs)))
-    sums = [part for _, _, steps in groups for part in next(steps)]
-    d_up, d_down, d_out, d_qkv = call(
-        functools.partial(finish_kernel, [group[:2] for group in groups]),
+    sums = [part for group in groups for part in next(group[3])]
+    d_up, d_down, d_out, d_qkv, small = call(
+        functools.partial(finish_kernel, [group[:3] for group in groups]),
         (
             ((LAYERS, D, units), f32),
             ((LAYERS, units, D), f32),
             ((LAYERS, LANES, D), f32),
             ((LAYERS, 3, D, LANES), f32),
+            small_like,
         ),
-        (place, last, *sums),
+        (place, *sums),
         1,
     )
     count = 2 * LAYERS + 3 * LAYERS

time: 301 us -> 261 us (0.87)
  waiting for transfers between devices: 129 us -> 105 us
  starting transfers between devices: 97.7 us -> 80.9 us
    ppermute x18 -> x24, waiting for transfers between devices: 63.2 us -> 40.3 us  [shard_swap(): return lax.ppermute(value, 'seq', [(i, i ^ 1 << bit) for i in range(count)])]
    all_to_all x2 -> x0, starting transfers between devices: 9.48 us -> none  [the longest x1 5.28 us: per_device(): got = lax.all_to_all(made, 'seq', 0, 0, tiled=True)]
    ppermute x18 -> x24, starting transfers between devices: 27.1 us -> 23.2 us  [shard_swap(): return lax.ppermute(value, 'seq', [(i, i ^ 1 << bit) for i in range(count)])]
    pallas_call x54 -> x58, Pallas kernels: 64.5 us -> 64.9 us  [call(): pl.pallas_call(body, out_shape=tuple((jax.ShapeDtypeStruct(shape, kind) f...]
  transfers between devices with their start and end apart: 78 -> 81, of which waited for: 27 -> 28; matrix products, arithmetic and copies ran while one was open for 1% -> 1% of each run, Pallas kernels for 16% -> 19%
where the time goes in v5:
time: 261 us; the launch traced here: 260 us
  waiting for transfers between devices  105 us (40%)
  starting transfers between devices  80.9 us (31%)
  Pallas kernels  64.9 us (25%)
  local copies, waits for them, and re-layouts  5.82 us (2%)
    pallas_call x58, Pallas kernels, call(): pl.pallas_call(body, out_shape=tuple((jax.ShapeDtypeStruct(shape, kind) f...  64.9 us
    ppermute x12, waiting for transfers between devices, part_swap(): return lax.ppermute(value, 'mlp', [(i, i ^ 2) for i in range(count)])  47.3 us
    ppermute x24, waiting for transfers between devices, shard_swap(): return lax.ppermute(value, 'seq', [(i, i ^ 1 << bit) for i in range(count)])  40.3 us
    ppermute x28, starting transfers between devices, chunk_move(): return lax.ppermute(value, AXES, pairs)  40.1 us
    ppermute x24, starting transfers between devices, shard_swap(): return lax.ppermute(value, 'seq', [(i, i ^ 1 << bit) for i in range(count)])  23.2 us
    ppermute x28, waiting for transfers between devices, chunk_move(): return lax.ppermute(value, AXES, pairs)  16.4 us
    ppermute x12, starting transfers between devices, part_swap(): return lax.ppermute(value, 'mlp', [(i, i ^ 2) for i in range(count)])  10.8 us
  transfers between devices with their start and end apart: 81, of which 28 were waited for; matrix products, arithmetic and copies ran while one was open for 1% of the time, Pallas kernels for 19%

profile of v5, /device:TPU:0, one launch (start us, length us, event | category | flops | bytes accessed | tf_op | source)
XLA Modules:
  0.0 260.1 jit_solution(10067711929130169558)
XLA Ops:
  5.1 2.6 collective-permute-start.1
  23.6 2.8 %collective-permute-start.5 = (s32[1,128]{1,0:T(1,128)S(1)}, s32[1,128]{1,0:T(1,128)S(1)}, u32[]{:S(2)}, u32[]{:S(2)}) collective-permute-start(s32[1,128]{1,0:T(1,128)S(1)} %slice_bitcast_fusion.8), channel_id=1, source_target_pairs={{0,4},{4,8},{8,12},{12,16},{16,20},{20,24},{24,28},{1,5},{5,9},{9,... | collective-permute-start | bytes 1544 | tf_op jit(solution)/shard_map/ppermute | solution.py:855
  28.0 3.5 %collective-permute-start.13 = (bf16[2,144,128]{2,1,0:T(8,128)(2,1)S(1)}, bf16[2,144,128]{2,1,0:T(8,128)(2,1)S(1)}, u32[]{:S(2)}, u32[]{:S(2)}) collective-permute-start(bf16[2,144,128]{2,1,0:T(8,128)(2,1)S(1)} %get-tuple-element.233), channel_id=1, source_target_pairs={{0,8},{2,10},{1,9},{3,11},{4,12},{6,14},{5,13},{7,15},{8,16},{10,1... | collective-permute-start | bytes 221192 | tf_op jit(solution)/shard_map/ppermute | solution.py:771
  31.6 4.5 %collective-permute-start.14 = (bf16[2,144,128]{2,1,0:T(8,128)(2,1)S(1)}, bf16[2,144,128]{2,1,0:T(8,128)(2,1)S(1)}, u32[]{:S(2)}, u32[]{:S(2)}) collective-permute-start(bf16[2,144,128]{2,1,0:T(8,128)(2,1)S(1)} %get-tuple-element.233), channel_id=1, source_target_pairs={{0,16},{2,18},{1,17},{3,19},{4,20},{6,22},{5,21},{7,23},{8,24},{10... | collective-permute-start | bytes 221192 | tf_op jit(solution)/shard_map/ppermute | solution.py:771
  38.2 2.9 %shard_map.182.near = f32[256,256]{1,0:T(8,128)S(1)} custom-call(s32[3]{0:T(128)S(1)} %pad_add_fusion.place.refs_0_, bf16[3,256,256]{2,1,0:T(8,128)(2,1)S(1)} %get-tuple-element.216.qkv, bf16[2,2,32,128]{3,2,1,0:T(8,128)(2,1)S(1)} %collective-permute-done.4.halo, f32[256,128]{1,0:T(8,128)S(1)} %shard_map.181.band), custom_call_target="tpu_custom_call" | custom-call | tf_op jit(solution)/shard_map/pallas_call | solution.py:738
  43.5 6.6 %collective-permute-done.16.part_b = bf16[256,512]{1,0:T(8,128)(2,1)S(1)} collective-permute-done((bf16[256,512]{1,0:T(8,128)(2,1)S(1)}, bf16[256,512]{1,0:T(8,128)(2,1)S(1)}, u32[]{:S(2)}, u32[]{:S(2)}) %collective-permute-start.16) | collective-permute-done | bytes 262176 | tf_op jit(solution)/shard_map/ppermute | solution.py:759
  52.6 5.5 %collective-permute-done.19.refs_2_ = bf16[256,512]{1,0:T(8,128)(2,1)S(1)} collective-permute-done((bf16[256,512]{1,0:T(8,128)(2,1)S(1)}, bf16[256,512]{1,0:T(8,128)(2,1)S(1)}, u32[]{:S(2)}, u32[]{:S(2)}) %collective-permute-start.19) | collective-permute-done | bytes 262176 | tf_op jit(solution)/shard_map/ppermute | solution.py:759
  60.0 2.5 collective-permute-start.24
  69.6 5.0 %collective-permute-start.27 = (bf16[2,144,128]{2,1,0:T(8,128)(2,1)S(1)}, bf16[2,144,128]{2,1,0:T(8,128)(2,1)S(1)}, u32[]{:S(2)}, u32[]{:S(2)}) collective-permute-start(bf16[2,144,128]{2,1,0:T(8,128)(2,1)S(1)} %get-tuple-element.251), channel_id=1, source_target_pairs={{0,16},{2,18},{1,17},{3,19},{4,20},{6,22},{5,21},{7,23},{8,24},{10... | collective-permute-start | bytes 221192 | tf_op jit(solution)/shard_map/ppermute | solution.py:771
  76.2 2.9 %shard_map.189.near = f32[256,256]{1,0:T(8,128)S(1)} custom-call(s32[3]{0:T(128)S(1)} %pad_add_fusion.place.refs_0_, bf16[3,256,256]{2,1,0:T(8,128)(2,1)S(1)} %get-tuple-element.242.qkv, bf16[2,2,32,128]{3,2,1,0:T(8,128)(2,1)S(1)} %collective-permute-done.21.halo, f32[256,128]{1,0:T(8,128)S(1)} %shard_map.181.band), custom_call_target="tpu_custom_call" | custom-call | tf_op jit(solution)/shard_map/pallas_call | solution.py:738
  80.6 8.0 %collective-permute-done.29.part_b = bf16[256,512]{1,0:T(8,128)(2,1)S(1)} collective-permute-done((bf16[256,512]{1,0:T(8,128)(2,1)S(1)}, bf16[256,512]{1,0:T(8,128)(2,1)S(1)}, u32[]{:S(2)}, u32[]{:S(2)}) %collective-permute-start.29) | collective-permute-done | bytes 262176 | tf_op jit(solution)/shard_map/ppermute | solution.py:759
  91.9 8.6 %collective-permute-done.34.part_b = bf16[256,512]{1,0:T(8,128)(2,1)S(1)} collective-permute-done((bf16[256,512]{1,0:T(8,128)(2,1)S(1)}, bf16[256,512]{1,0:T(8,128)(2,1)S(1)}, u32[]{:S(2)}, u32[]{:S(2)}) %collective-permute-start.34) | collective-permute-done | bytes 262176 | tf_op jit(solution)/shard_map/ppermute | solution.py:759
  103.9 4.1 %shard_map.197 = (f32[256,256]{1,0:T(8,128)S(1)}, f32[256,256]{1,0:T(8,128)S(1)}, f32[256,256]{1,0:T(8,128)S(1)}, bf16[2,2,32,128]{3,2,1,0:T(8,128)(2,1)S(1)}, f32[1,256]{1,0:T(1,128)S(1)}) custom-call(s32[3]{0:T(128)S(1)} %pad_add_fusion.place.refs_0_, bf16[3,256,256]{2,1,0:T(8,128)(2,1)S(1)} %get-tuple-element.242.qkv, ...), custom_call_target="tpu_custom_call" | custom-call | tf_op jit(solution)/shard_map/pallas_call | solution.py:738
  115.9 2.7 %shard_map.200 = (bf16[256,256]{1,0:T(8,128)(2,1)S(1)}, f32[256,256]{1,0:T(8,128)S(1)}, f32[256,256]{1,0:T(8,128)S(1)}, f32[256,256]{1,0:T(8,128)S(1)}) custom-call(s32[3]{0:T(128)S(1)} %pad_add_fusion.place.refs_0_, bf16[3,256,256]{2,1,0:T(8,128)(2,1)S(1)} %get-tuple-element.242.qkv, bf16[256,256]{1,0:T(8,128)(2,1)S(1)} %get-tuple-element.219.causal, ...), custom_call_target="tpu_custom_call" | custom-call | tf_op jit(solution)/shard_map/pallas_call | solution.py:738
  118.9 3.8 %collective-permute-done.42.refs_2_ = bf16[2,144,128]{2,1,0:T(8,128)(2,1)S(1)} collective-permute-done((bf16[2,144,128]{2,1,0:T(8,128)(2,1)S(1)}, bf16[2,144,128]{2,1,0:T(8,128)(2,1)S(1)}, u32[]{:S(2)}, u32[]{:S(2)}) %collective-permute-start.42) | collective-permute-done | bytes 73760 | tf_op jit(solution)/shard_map/ppermute | solution.py:771
  125.3 6.4 %collective-permute-done.43.refs_2_ = bf16[256,512]{1,0:T(8,128)(2,1)S(1)} collective-permute-done((bf16[256,512]{1,0:T(8,128)(2,1)S(1)}, bf16[256,512]{1,0:T(8,128)(2,1)S(1)}, u32[]{:S(2)}, u32[]{:S(2)}) %collective-permute-start.43) | collective-permute-done | bytes 262176 | tf_op jit(solution)/shard_map/ppermute | solution.py:759
  133.5 6.4 %collective-permute-done.44.part_b = bf16[256,512]{1,0:T(8,128)(2,1)S(1)} collective-permute-done((bf16[256,512]{1,0:T(8,128)(2,1)S(1)}, bf16[256,512]{1,0:T(8,128)(2,1)S(1)}, u32[]{:S(2)}, u32[]{:S(2)}) %collective-permute-start.44) | collective-permute-done | bytes 262176 | tf_op jit(solution)/shard_map/ppermute | solution.py:759
  143.3 4.2 %shard_map.205 = (f32[256,256]{1,0:T(8,128)S(1)}, f32[256,256]{1,0:T(8,128)S(1)}, f32[256,256]{1,0:T(8,128)S(1)}, bf16[2,2,32,128]{3,2,1,0:T(8,128)(2,1)S(1)}, f32[1,256]{1,0:T(1,128)S(1)}) custom-call(s32[3]{0:T(128)S(1)} %pad_add_fusion.place.refs_0_, bf16[3,256,256]{2,1,0:T(8,128)(2,1)S(1)} %get-tuple-element.216.qkv, ...), custom_call_target="tpu_custom_call" | custom-call | tf_op jit(solution)/shard_map/pallas_call | solution.py:738
  157.2 2.7 %shard_map.209 = (bf16[256,256]{1,0:T(8,128)(2,1)S(1)}, f32[256,256]{1,0:T(8,128)S(1)}, f32[256,256]{1,0:T(8,128)S(1)}, f32[256,256]{1,0:T(8,128)S(1)}) custom-call(s32[3]{0:T(128)S(1)} %pad_add_fusion.place.refs_0_, bf16[3,256,256]{2,1,0:T(8,128)(2,1)S(1)} %get-tuple-element.216.qkv, bf16[256,256]{1,0:T(8,128)(2,1)S(1)} %get-tuple-element.219.causal, ...), custom_call_target="tpu_custom_call" | custom-call | tf_op jit(solution)/shard_map/pallas_call | solution.py:738
  161.8 2.7 %collective-permute-done.53.refs_1_ = bf16[2,144,128]{2,1,0:T(8,128)(2,1)S(1)} collective-permute-done((bf16[2,144,128]{2,1,0:T(8,128)(2,1)S(1)}, bf16[2,144,128]{2,1,0:T(8,128)(2,1)S(1)}, u32[]{:S(2)}, u32[]{:S(2)}) %collective-permute-start.53) | collective-permute-done | bytes 73760 | tf_op jit(solution)/shard_map/ppermute | solution.py:771
  164.5 3.2 %collective-permute-done.54.refs_2_ = bf16[2,144,128]{2,1,0:T(8,128)(2,1)S(1)} collective-permute-done((bf16[2,144,128]{2,1,0:T(8,128)(2,1)S(1)}, bf16[2,144,128]{2,1,0:T(8,128)(2,1)S(1)}, u32[]{:S(2)}, u32[]{:S(2)}) %collective-permute-start.54) | collective-permute-done | bytes 73760 | tf_op jit(solution)/shard_map/ppermute | solution.py:771
  174.1 2.1 collective-permute-start.57
  176.2 4.8 %collective-permute-done.55.part_b = bf16[256,512]{1,0:T(8,128)(2,1)S(1)} collective-permute-done((bf16[256,512]{1,0:T(8,128)(2,1)S(1)}, bf16[256,512]{1,0:T(8,128)(2,1)S(1)}, u32[]{:S(2)}, u32[]{:S(2)}) %collective-permute-start.55) | collective-permute-done | bytes 262176 | tf_op jit(solution)/shard_map/ppermute | solution.py:759
  184.3 3.4 %collective-permute-start.60 = (bf16[144,512]{1,0:T(8,128)(2,1)S(1)}, bf16[144,512]{1,0:T(8,128)(2,1)S(1)}, u32[]{:S(2)}, u32[]{:S(2)}) collective-permute-start(bf16[144,512]{1,0:T(8,128)(2,1)S(1)} %shard_map.217.mine), channel_id=1, source_target_pairs={{0,16},{4,20},{8,24},{12,28},{16,0},{20,4},{24,8},{28,12},{1,17},{... | collective-permute-start | bytes 442376 | tf_op jit(solution)/shard_map/ppermute | solution.py:808
  189.5 6.7 %collective-permute-done.61.second = bf16[256,512]{1,0:T(8,128)(2,1)S(1)} collective-permute-done((bf16[256,512]{1,0:T(8,128)(2,1)S(1)}, bf16[256,512]{1,0:T(8,128)(2,1)S(1)}, u32[]{:S(2)}, u32[]{:S(2)}) %collective-permute-start.61) | collective-permute-done | bytes 262176 | tf_op jit(solution)/shard_map/ppermute | solution.py:808
  197.5 2.2 collective-permute-start.66
  202.2 4.8 %collective-permute-done.67.second = bf16[224,512]{1,0:T(8,128)(2,1)S(1)} collective-permute-done((bf16[224,512]{1,0:T(8,128)(2,1)S(1)}, bf16[224,512]{1,0:T(8,128)(2,1)S(1)}, u32[]{:S(2)}, u32[]{:S(2)}) %collective-permute-start.67) | collective-permute-done | bytes 229408 | tf_op jit(solution)/shard_map/ppermute | solution.py:808
  210.2 6.4 %collective-permute-done.65.second = bf16[128,512]{1,0:T(8,128)(2,1)S(1)} collective-permute-done((bf16[128,512]{1,0:T(8,128)(2,1)S(1)}, bf16[128,512]{1,0:T(8,128)(2,1)S(1)}, u32[]{:S(2)}, u32[]{:S(2)}) %collective-permute-start.65) | collective-permute-done | bytes 131104 | tf_op jit(solution)/shard_map/ppermute | solution.py:808
  230.2 6.5 %collective-permute-done.73.got = bf16[224,512]{1,0:T(8,128)(2,1)S(1)} collective-permute-done((bf16[224,512]{1,0:T(8,128)(2,1)S(1)}, bf16[224,512]{1,0:T(8,128)(2,1)S(1)}, u32[]{:S(2)}, u32[]{:S(2)}) %collective-permute-start.73) | collective-permute-done | bytes 229408 | tf_op jit(solution)/shard_map/ppermute | solution.py:808
  238.7 2.1 collective-permute-done.77.got
  244.8 10.4 %collective-permute-done.80.refs_7_ = bf16[256,512]{1,0:T(8,128)(2,1)S(1)} collective-permute-done((bf16[256,512]{1,0:T(8,128)(2,1)S(1)}, bf16[256,512]{1,0:T(8,128)(2,1)S(1)}, u32[]{:S(2)}, u32[]{:S(2)}) %collective-permute-start.80) | collective-permute-done | bytes 262176 | tf_op jit(solution)/shard_map/ppermute | solution.py:808
  255.2 3.5 %shard_map.235 = (f32[2,512,512]{2,1,0:T(8,128)}, f32[2,512,512]{2,1,0:T(8,128)}, f32[2,128,512]{2,1,0:T(8,128)}, f32[2,3,512,128]{3,2,1,0:T(8,128)}, f32[16,128]{1,0:T(8,128)S(1)}) custom-call(s32[3]{0:T(128)S(1)} %pad_add_fusion.place.refs_0_, bf16[576,512]{1,0:T(8,128)(2,1)S(1)} %shard_map.225.refs_0_, ...), custom_call_target="tpu_custom_call" | custom-call | tf_op jit(solution)/shard_map/pallas_call | solution.py:738
  (224 shorter events, 113.9 us)
Async XLA Ops:
  18.1 25.5 %collective-permute-start.17 = (bf16[512,512]{1,0:T(8,128)(2,1)S(1)}, bf16[512,512]{1,0:T(8,128)(2,1)S(1)}, u32[]{:S(2)}, u32[]{:S(2)}) collective-permute-start(bf16[512,512]{1,0:T(8,128)(2,1)S(1)} %get-tuple-element.236), channel_id=1, source_target_pairs={{0,1},{1,0},{2,3},{3,2},{4,5},{5,4},{6,7},{7,6},{8,9},{9,8},{10,11... | collective-permute-start | bytes 1572872 | tf_op jit(solution)/shard_map/ppermute | solution.py:754
  18.3 25.3 %collective-permute-start.18 = (bf16[512,512]{1,0:T(8,128)(2,1)S(1)}, bf16[512,512]{1,0:T(8,128)(2,1)S(1)}, u32[]{:S(2)}, u32[]{:S(2)}) collective-permute-start(bf16[512,512]{1,0:T(8,128)(2,1)S(1)} %get-tuple-element.237), channel_id=1, source_target_pairs={{0,1},{1,0},{2,3},{3,2},{4,5},{5,4},{6,7},{7,6},{8,9},{9,8},{10,11... | collective-permute-start | bytes 1572872 | tf_op jit(solution)/shard_map/ppermute | solution.py:754
  21.1 14.9 %collective-permute-start.4 = (bf16[2,2,32,128]{3,2,1,0:T(8,128)(2,1)S(1)}, bf16[2,2,32,128]{3,2,1,0:T(8,128)(2,1)S(1)}, u32[]{:S(2)}, u32[]{:S(2)}) collective-permute-start(bf16[2,2,32,128]{3,2,1,0:T(8,128)(2,1)S(1)} %get-tuple-element.217), channel_id=1, source_target_pairs={{0,1},{2,3},{1,4},{3,6},{4,5},{6,7},{5,8},{7,10},{8,9},{10,11},{9,... | collective-permute-start | bytes 98312 | tf_op jit(solution)/shard_map/ppermute | solution.py:771
  28.0 13.1 %collective-permute-start.13 = (bf16[2,144,128]{2,1,0:T(8,128)(2,1)S(1)}, bf16[2,144,128]{2,1,0:T(8,128)(2,1)S(1)}, u32[]{:S(2)}, u32[]{:S(2)}) collective-permute-start(bf16[2,144,128]{2,1,0:T(8,128)(2,1)S(1)} %get-tuple-element.233), channel_id=1, source_target_pairs={{0,8},{2,10},{1,9},{3,11},{4,12},{6,14},{5,13},{7,15},{8,16},{10,1... | collective-permute-start | bytes 221192 | tf_op jit(solution)/shard_map/ppermute | solution.py:771
  52.1 28.5 %collective-permute-start.30 = (bf16[512,512]{1,0:T(8,128)(2,1)S(1)}, bf16[512,512]{1,0:T(8,128)(2,1)S(1)}, u32[]{:S(2)}, u32[]{:S(2)}) collective-permute-start(bf16[512,512]{1,0:T(8,128)(2,1)S(1)} %get-tuple-element.253), channel_id=1, source_target_pairs={{0,1},{1,0},{2,3},{3,2},{4,5},{5,4},{6,7},{7,6},{8,9},{9,8},{10,11... | collective-permute-start | bytes 1572872 | tf_op jit(solution)/shard_map/ppermute | solution.py:754
  52.1 28.5 %collective-permute-start.31 = (bf16[512,512]{1,0:T(8,128)(2,1)S(1)}, bf16[512,512]{1,0:T(8,128)(2,1)S(1)}, u32[]{:S(2)}, u32[]{:S(2)}) collective-permute-start(bf16[512,512]{1,0:T(8,128)(2,1)S(1)} %get-tuple-element.254), channel_id=1, source_target_pairs={{0,1},{1,0},{2,3},{3,2},{4,5},{5,4},{6,7},{7,6},{8,9},{9,8},{10,11... | collective-permute-start | bytes 1572872 | tf_op jit(solution)/shard_map/ppermute | solution.py:754
  68.1 11.1 %collective-permute-start.26 = (bf16[2,144,128]{2,1,0:T(8,128)(2,1)S(1)}, bf16[2,144,128]{2,1,0:T(8,128)(2,1)S(1)}, u32[]{:S(2)}, u32[]{:S(2)}) collective-permute-start(bf16[2,144,128]{2,1,0:T(8,128)(2,1)S(1)} %get-tuple-element.251), channel_id=1, source_target_pairs={{0,8},{2,10},{1,9},{3,11},{4,12},{6,14},{5,13},{7,15},{8,16},{10,1... | collective-permute-start | bytes 221192 | tf_op jit(solution)/shard_map/ppermute | solution.py:771
  110.0 14.2 %collective-permute-start.38 = (bf16[1152,512]{1,0:T(8,128)(2,1)S(1)}, bf16[1152,512]{1,0:T(8,128)(2,1)S(1)}, u32[]{:S(2)}, u32[]{:S(2)}) collective-permute-start(bf16[1152,512]{1,0:T(8,128)(2,1)S(1)} %get-tuple-element.282), channel_id=1, source_target_pairs={{0,1},{1,0},{2,3},{3,2},{4,5},{5,4},{6,7},{7,6},{8,9},{9,8},{10,11... | collective-permute-start | bytes 3538952 | tf_op jit(solution)/shard_map/ppermute | solution.py:754
  125.2 22.9 %collective-permute-start.45 = (bf16[576,512]{1,0:T(8,128)(2,1)S(1)}, bf16[576,512]{1,0:T(8,128)(2,1)S(1)}, u32[]{:S(2)}, u32[]{:S(2)}) collective-permute-start(bf16[576,512]{1,0:T(8,128)(2,1)S(1)} %get-tuple-element.300), channel_id=1, source_target_pairs={{0,4},{4,0},{8,12},{12,8},{16,20},{20,16},{24,28},{28,24},{1,5},{5... | collective-permute-start | bytes 1769480 | tf_op jit(solution)/shard_map/ppermute | solution.py:808
  150.4 18.6 %collective-permute-start.50 = (bf16[1536,512]{1,0:T(8,128)(2,1)S(1)}, bf16[1536,512]{1,0:T(8,128)(2,1)S(1)}, u32[]{:S(2)}, u32[]{:S(2)}) collective-permute-start(bf16[1536,512]{1,0:T(8,128)(2,1)S(1)} %get-tuple-element.332), channel_id=1, source_target_pairs={{0,1},{1,0},{2,3},{3,2},{4,5},{5,4},{6,7},{7,6},{8,9},{9,8},{10,11... | collective-permute-start | bytes 4718600 | tf_op jit(solution)/shard_map/ppermute | solution.py:754
  150.8 19.8 %collective-permute-start.49 = (bf16[288,512]{1,0:T(8,128)(2,1)S(1)}, bf16[288,512]{1,0:T(8,128)(2,1)S(1)}, u32[]{:S(2)}, u32[]{:S(2)}) collective-permute-start(bf16[288,512]{1,0:T(8,128)(2,1)S(1)} %get-tuple-element.319), channel_id=1, source_target_pairs={{0,8},{4,12},{8,0},{12,4},{16,24},{20,28},{24,16},{28,20},{1,9},{5... | collective-permute-start | bytes 884744 | tf_op jit(solution)/shard_map/ppermute | solution.py:808
  154.3 10.2 %collective-permute-start.53 = (bf16[2,144,128]{2,1,0:T(8,128)(2,1)S(1)}, bf16[2,144,128]{2,1,0:T(8,128)(2,1)S(1)}, u32[]{:S(2)}, u32[]{:S(2)}) collective-permute-start(bf16[2,144,128]{2,1,0:T(8,128)(2,1)S(1)} %get-tuple-element.316), channel_id=1, source_target_pairs={{16,0},{18,2},{17,1},{19,3},{20,4},{22,6},{21,5},{23,7},{24,8},{26... | collective-permute-start | bytes 221192 | tf_op jit(solution)/shard_map/ppermute | solution.py:771
  155.6 12.1 %collective-permute-start.54 = (bf16[2,144,128]{2,1,0:T(8,128)(2,1)S(1)}, bf16[2,144,128]{2,1,0:T(8,128)(2,1)S(1)}, u32[]{:S(2)}, u32[]{:S(2)}) collective-permute-start(bf16[2,144,128]{2,1,0:T(8,128)(2,1)S(1)} %get-tuple-element.316), channel_id=1, source_target_pairs={{24,0},{26,2},{25,1},{27,3},{28,4},{30,6},{29,5},{31,7}} | collective-permute-start | bytes 221192 | tf_op jit(solution)/shard_map/ppermute | solution.py:771
  172.7 15.0 %collective-permute-start.63 = (bf16[448,512]{1,0:T(8,128)(2,1)S(1)}, bf16[448,512]{1,0:T(8,128)(2,1)S(1)}, u32[]{:S(2)}, u32[]{:S(2)}) collective-permute-start(bf16[448,512]{1,0:T(8,128)(2,1)S(1)} %get-tuple-element.349), channel_id=1, source_target_pairs={{0,4},{4,0},{8,12},{12,8},{16,20},{20,16},{24,28},{28,24},{1,5},{5... | collective-permute-start | bytes 1376264 | tf_op jit(solution)/shard_map/ppermute | solution.py:808
  174.1 14.7 %collective-permute-start.62 = (bf16[320,512]{1,0:T(8,128)(2,1)S(1)}, bf16[320,512]{1,0:T(8,128)(2,1)S(1)}, u32[]{:S(2)}, u32[]{:S(2)}) collective-permute-start(bf16[320,512]{1,0:T(8,128)(2,1)S(1)} %get-tuple-element.351), channel_id=1, source_target_pairs={{0,8},{4,12},{8,0},{12,4},{16,24},{20,28},{24,16},{28,20},{1,9},{5... | collective-permute-start | bytes 983048 | tf_op jit(solution)/shard_map/ppermute | solution.py:808
  174.1 10.1 %collective-permute-start.57 = (bf16[144,512]{1,0:T(8,128)(2,1)S(1)}, bf16[144,512]{1,0:T(8,128)(2,1)S(1)}, u32[]{:S(2)}, u32[]{:S(2)}) collective-permute-start(bf16[144,512]{1,0:T(8,128)(2,1)S(1)} %get-tuple-element.353), channel_id=1, source_target_pairs={{0,16},{4,20},{8,24},{12,28},{16,0},{20,4},{24,8},{28,12},{1,17},{... | collective-permute-start | bytes 442376 | tf_op jit(solution)/shard_map/ppermute | solution.py:808
  183.8 12.4 %collective-permute-start.61 = (bf16[256,512]{1,0:T(8,128)(2,1)S(1)}, bf16[256,512]{1,0:T(8,128)(2,1)S(1)}, u32[]{:S(2)}, u32[]{:S(2)}) collective-permute-start(bf16[256,512]{1,0:T(8,128)(2,1)S(1)} %get-tuple-element.372), channel_id=1, source_target_pairs={{0,8},{4,12},{8,0},{12,4},{16,24},{20,28},{24,16},{28,20},{1,9},{5... | collective-permute-start | bytes 786440 | tf_op jit(solution)/shard_map/ppermute | solution.py:808
  184.3 12.6 %collective-permute-start.60 = (bf16[144,512]{1,0:T(8,128)(2,1)S(1)}, bf16[144,512]{1,0:T(8,128)(2,1)S(1)}, u32[]{:S(2)}, u32[]{:S(2)}) collective-permute-start(bf16[144,512]{1,0:T(8,128)(2,1)S(1)} %shard_map.217.mine), channel_id=1, source_target_pairs={{0,16},{4,20},{8,24},{12,28},{16,0},{20,4},{24,8},{28,12},{1,17},{... | collective-permute-start | bytes 442376 | tf_op jit(solution)/shard_map/ppermute | solution.py:808
  188.4 18.6 %collective-permute-start.67 = (bf16[224,512]{1,0:T(8,128)(2,1)S(1)}, bf16[224,512]{1,0:T(8,128)(2,1)S(1)}, u32[]{:S(2)}, u32[]{:S(2)}) collective-permute-start(bf16[224,512]{1,0:T(8,128)(2,1)S(1)} %get-tuple-element.378), channel_id=1, source_target_pairs={{0,8},{4,12},{8,0},{12,4},{16,24},{20,28},{24,16},{28,20},{1,9},{5... | collective-permute-start | bytes 688136 | tf_op jit(solution)/shard_map/ppermute | solution.py:808
  197.4 20.7 %collective-permute-start.64 = (bf16[288,512]{1,0:T(8,128)(2,1)S(1)}, bf16[288,512]{1,0:T(8,128)(2,1)S(1)}, u32[]{:S(2)}, u32[]{:S(2)}) collective-permute-start(bf16[288,512]{1,0:T(8,128)(2,1)S(1)} %shard_map.221.mine), channel_id=1, source_target_pairs={{0,8},{4,12},{8,0},{12,4},{16,24},{20,28},{24,16},{28,20},{1,9},{5... | collective-permute-start | bytes 884744 | tf_op jit(solution)/shard_map/ppermute | solution.py:808
  197.5 11.0 %collective-permute-start.66 = (bf16[160,512]{1,0:T(8,128)(2,1)S(1)}, bf16[160,512]{1,0:T(8,128)(2,1)S(1)}, u32[]{:S(2)}, u32[]{:S(2)}) collective-permute-start(bf16[160,512]{1,0:T(8,128)(2,1)S(1)} %get-tuple-element.380), channel_id=1, source_target_pairs={{0,16},{4,20},{8,24},{12,28},{16,0},{20,4},{24,8},{28,12},{1,17},{... | collective-permute-start | bytes 491528 | tf_op jit(solution)/shard_map/ppermute | solution.py:808
  199.7 22.8 %collective-permute-start.32 = (bf16[256,512]{1,0:T(8,128)(2,1)S(1)}, bf16[256,512]{1,0:T(8,128)(2,1)S(1)}, u32[]{:S(2)}, u32[]{:S(2)}) collective-permute-start(bf16[256,512]{1,0:T(8,128)(2,1)S(1)} %get-tuple-element.256.part_a), channel_id=1, source_target_pairs={{0,2},{1,3},{2,0},{3,1},{4,6},{5,7},{6,4},{7,5},{8,10},{9,11},{10,... | collective-permute-start | bytes 786440 | tf_op jit(solution)/shard_map/ppermute | solution.py:759
  201.4 15.3 %collective-permute-start.65 = (bf16[128,512]{1,0:T(8,128)(2,1)S(1)}, bf16[128,512]{1,0:T(8,128)(2,1)S(1)}, u32[]{:S(2)}, u32[]{:S(2)}) collective-permute-start(bf16[128,512]{1,0:T(8,128)(2,1)S(1)} %get-tuple-element.382), channel_id=1, source_target_pairs={{0,16},{4,20},{8,24},{12,28},{16,0},{20,4},{24,8},{28,12},{1,17},{... | collective-permute-start | bytes 393224 | tf_op jit(solution)/shard_map/ppermute | solution.py:808
  207.6 11.1 %collective-permute-start.69 = (bf16[112,512]{1,0:T(8,128)(2,1)S(1)}, bf16[112,512]{1,0:T(8,128)(2,1)S(1)}, u32[]{:S(2)}, u32[]{:S(2)}) collective-permute-start(bf16[112,512]{1,0:T(8,128)(2,1)S(1)} %get-tuple-element.388), channel_id=1, source_target_pairs={{0,16},{4,20},{8,24},{12,28},{16,0},{20,4},{24,8},{28,12},{1,17},{... | collective-permute-start | bytes 344072 | tf_op jit(solution)/shard_map/ppermute | solution.py:808
  223.2 21.6 %collective-permute-start.68 = (bf16[576,512]{1,0:T(8,128)(2,1)S(1)}, bf16[576,512]{1,0:T(8,128)(2,1)S(1)}, u32[]{:S(2)}, u32[]{:S(2)}) collective-permute-start(bf16[576,512]{1,0:T(8,128)(2,1)S(1)} %shard_map.225.refs_0_), channel_id=1, source_target_pairs={{0,4},{4,0},{8,12},{12,8},{16,20},{20,16},{24,28},{28,24},{1,5},{5... | collective-permute-start | bytes 1769480 | tf_op jit(solution)/shard_map/ppermute | solution.py:808
  225.3 11.4 %collective-permute-start.73 = (bf16[224,512]{1,0:T(8,128)(2,1)S(1)}, bf16[224,512]{1,0:T(8,128)(2,1)S(1)}, u32[]{:S(2)}, u32[]{:S(2)}) collective-permute-start(bf16[224,512]{1,0:T(8,128)(2,1)S(1)} %shard_map.229.mine), channel_id=1, source_target_pairs={{0,8},{4,12},{8,0},{12,4},{16,24},{20,28},{24,16},{28,20},{1,9},{5... | collective-permute-start | bytes 688136 | tf_op jit(solution)/shard_map/ppermute | solution.py:808
  226.4 14.4 %collective-permute-start.77 = (bf16[160,512]{1,0:T(8,128)(2,1)S(1)}, bf16[160,512]{1,0:T(8,128)(2,1)S(1)}, u32[]{:S(2)}, u32[]{:S(2)}) collective-permute-start(bf16[160,512]{1,0:T(8,128)(2,1)S(1)} %shard_map.230.mine), channel_id=1, source_target_pairs={{0,16},{4,20},{8,24},{12,28},{16,0},{20,4},{24,8},{28,12},{1,17},{... | collective-permute-start | bytes 491528 | tf_op jit(solution)/shard_map/ppermute | solution.py:808
  229.1 13.5 %collective-permute-start.79 = (bf16[128,512]{1,0:T(8,128)(2,1)S(1)}, bf16[128,512]{1,0:T(8,128)(2,1)S(1)}, u32[]{:S(2)}, u32[]{:S(2)}) collective-permute-start(bf16[128,512]{1,0:T(8,128)(2,1)S(1)} %shard_map.231.mine), channel_id=1, source_target_pairs={{0,16},{4,20},{8,24},{12,28},{16,0},{20,4},{24,8},{28,12},{1,17},{... | collective-permute-start | bytes 393224 | tf_op jit(solution)/shard_map/ppermute | solution.py:808
  230.1 14.1 %collective-permute-start.56 = (bf16[256,128]{1,0:T(8,128)(2,1)S(1)}, bf16[256,128]{1,0:T(8,128)(2,1)S(1)}, u32[]{:S(2)}, u32[]{:S(2)}) collective-permute-start(bf16[256,128]{1,0:T(8,128)(2,1)S(1)} %get-tuple-element.366), channel_id=1, source_target_pairs={{0,1},{1,0},{2,3},{3,2},{4,5},{5,4},{6,7},{7,6},{8,9},{9,8},{10,11... | collective-permute-start | bytes 196616 | tf_op jit(solution)/shard_map/ppermute | solution.py:754
  237.2 18.0 %collective-permute-start.76 = (bf16[448,512]{1,0:T(8,128)(2,1)S(1)}, bf16[448,512]{1,0:T(8,128)(2,1)S(1)}, u32[]{:S(2)}, u32[]{:S(2)}) collective-permute-start(bf16[448,512]{1,0:T(8,128)(2,1)S(1)} %shard_map.232.refs_2_), channel_id=1, source_target_pairs={{0,4},{4,0},{8,12},{12,8},{16,20},{20,16},{24,28},{28,24},{1,5},{5... | collective-permute-start | bytes 1376264 | tf_op jit(solution)/shard_map/ppermute | solution.py:808
  241.4 13.8 %collective-permute-start.78 = (bf16[320,512]{1,0:T(8,128)(2,1)S(1)}, bf16[320,512]{1,0:T(8,128)(2,1)S(1)}, u32[]{:S(2)}, u32[]{:S(2)}) collective-permute-start(bf16[320,512]{1,0:T(8,128)(2,1)S(1)} %shard_map.233.refs_4_), channel_id=1, source_target_pairs={{0,8},{4,12},{8,0},{12,4},{16,24},{20,28},{24,16},{28,20},{1,9},{5... | collective-permute-start | bytes 983048 | tf_op jit(solution)/shard_map/ppermute | solution.py:808
  243.2 12.0 %collective-permute-start.80 = (bf16[256,512]{1,0:T(8,128)(2,1)S(1)}, bf16[256,512]{1,0:T(8,128)(2,1)S(1)}, u32[]{:S(2)}, u32[]{:S(2)}) collective-permute-start(bf16[256,512]{1,0:T(8,128)(2,1)S(1)} %shard_map.234.refs_6_), channel_id=1, source_target_pairs={{0,8},{4,12},{8,0},{12,4},{16,24},{20,28},{24,16},{28,20},{1,9},{5... | collective-permute-start | bytes 786440 | tf_op jit(solution)/shard_map/ppermute | solution.py:808
  (59 other events, 375.9 us)

commit v6 on v5

--- a/solution.py
+++ b/solution.py
@@ -104,6 +104,13 @@
     return back, jnp.sum(grad * hidden * scale, axis=0, keepdims=True)
 
 
+def halo_bias(halo):
+    ones = jnp.ones((LANES - HALO, LANES), bf16)
+    flags = jnp.concatenate([halo[4], ones], axis=0)
+    flags = dot_nt(jnp.ones((2 * TILE, LANES), bf16), flags)
+    return jnp.where(flags > 0.5 * LANES, 0.0, masked_score)
+
+
 def extend(halo, rows):
     return jnp.concatenate([halo, rows, jnp.zeros((HALO, LANES), bf16)], axis=0)
 
@@ -116,20 +123,33 @@
     return jnp.concatenate([high, middle, low], axis=0)
 
 
-def pack_kernel(place, blend, inputs, norm_attn, norm_ffn, mine_out, theirs_out):
-    rows = inputs.shape[0] // 2
-    low = low_lanes(1)
-    small = [norm_attn[...], norm_ffn[...]]
-    for layer in range(LAYERS):
-        for kind in range(3):
-            small.append(jnp.where(low, blend[layer, kind, 0], blend[layer, kind, 1]))
-    small.append(jnp.zeros((SMALL - 5 * LAYERS, LANES), f32))
+def pack_kernel(place, inputs, norm_attn, norm_ffn, mine_out, theirs_out, rows_in, attn_in, ffn_in, sems):
+    copies = [
+        pltpu.make_async_copy(source, target, sems.at[k])
+        for k, (source, target) in enumerate(((inputs, rows_in), (norm_attn, attn_in), (norm_ffn, ffn_in)))
+    ]
+    for copy in copies:
+        copy.start()
+    for copy in copies:
+        copy.wait()
+    rows = rows_in.shape[0] // 2
+    small = [attn_in[...], ffn_in[...], jnp.zeros((SMALL - 2 * LAYERS, LANES), f32)]
     small = three_parts(jnp.concatenate(small, axis=0))
-    first, second = inputs[:rows], inputs[rows:]
+    first, second = rows_in[:rows], rows_in[rows:]
     mine_out[:rows] = jnp.where(place[0] == 0, first, second)
     theirs_out[:rows] = jnp.where(place[0] == 0, second, first)
     mine_out[rows:] = small
     theirs_out[rows:] = small
+
+
+def pack_blend_kernel(blend, out):
+    low = low_lanes(1)
+    rows = []
+    for layer in range(LAYERS):
+        for kind in range(3):
+            rows.append(jnp.where(low, blend[layer, kind, 0], blend[layer, kind, 1]))
+    rows.append(jnp.zeros((SMALL - 3 * LAYERS, LANES), f32))
+    out[...] = jnp.concatenate(rows, axis=0)
 
 
 def pack_grad_kernel(place, grads, mine_out, theirs_out):
@@ -180,7 +200,9 @@
     return places, at
 
 
-def setup_kernel(chunks, place, lengths, valid, causal_out, causal_t_out, carried_out, tail_out, flags_out):
+def setup_kernel(
+    chunks, place, lengths, valid, causal_out, causal_t_out, band_out, carried_out, tail_out, edge_out, flags_out
+):
     rows = causal_out.shape[0]
     chunk = place[2] * 2 + place[0]
     first_row = chunk * rows
@@ -203,7 +225,20 @@
     causal_t_out[...] = jnp.where((row_at <= lane_at) & same & (own_column == 1), 1.0, 0.0).astype(bf16)
     carried_out[...] = jnp.where(starts < first_row, 1.0, 0.0)
     last_start = start_of(first_row + rows - 1)
+    edge_out[...] = jnp.where(jnp.broadcast_to(own_column, (rows, LANES))[rows - HALO :] == 1, 1.0, 0.0).astype(bf16)
     tail_out[...] = jnp.where((starts == last_start) & (own_column == 1), 1.0, 0.0).astype(bf16)
+    all_words = jnp.concatenate([jnp.ones((1, LANES), jnp.int32), own_words, jnp.zeros((1, LANES), jnp.int32)], axis=1)
+    tile_row = lax.broadcasted_iota(jnp.int32, (TILE, LANES), 0)
+    tile_lane = lax.broadcasted_iota(jnp.int32, (TILE, LANES), 1)
+    gap = tile_row + HALO - tile_lane
+    for tile in range(rows // TILE):
+        key_starts = start_of(first_row + tile * TILE - HALO + lax.broadcasted_iota(jnp.int32, (1, LANES), 1))
+        offset = LANES - HALO + tile * TILE
+        key_words = all_words[:, offset : offset + LANES]
+        at = slice(tile * TILE, (tile + 1) * TILE)
+        allowed = (gap >= 0) & (gap <= BAND) & (starts[at] == key_starts) & ((key_words == 1) | (gap == 0))
+        band_out[at] = jnp.where(allowed, 0.0, masked_score)
+
     places, _ = flag_places(chunks)
     for reverse in (False, True):
         edge = start_of(first_row + (rows - 1 if reverse else 0))
@@ -226,31 +261,6 @@
                 flags_out[at + 1] = jnp.where(start == group, 1.0, 0.0)
 
 
-def band_kernel(place, lengths, valid, before, band_out):
-    rows = band_out.shape[0]
-    first_row = (place[2] * 2 + place[0]) * rows
-    ends = item_ends(lengths)
-
-    def start_of(positions):
-        return item_start(lengths, ends, positions)
-
-    words = valid[...]
-    own_words = jnp.where(place[0] == 0, words[:, :rows], words[:, rows:])
-    last_words = jnp.where(place[0] == 0, before[...], words[:, rows - LANES : rows])
-    starts = start_of(first_row + lax.broadcasted_iota(jnp.int32, (rows, LANES), 0))
-    all_words = jnp.concatenate([last_words, own_words, jnp.zeros((1, LANES), jnp.int32)], axis=1)
-    tile_row = lax.broadcasted_iota(jnp.int32, (TILE, LANES), 0)
-    tile_lane = lax.broadcasted_iota(jnp.int32, (TILE, LANES), 1)
-    gap = tile_row + HALO - tile_lane
-    for tile in range(rows // TILE):
-        key_starts = start_of(first_row + tile * TILE - HALO + lax.broadcasted_iota(jnp.int32, (1, LANES), 1))
-        offset = LANES - HALO + tile * TILE
-        key_words = all_words[:, offset : offset + LANES]
-        at = slice(tile * TILE, (tile + 1) * TILE)
-        allowed = (gap >= 0) & (gap <= BAND) & (starts[at] == key_starts) & ((key_words == 1) | (gap == 0))
-        band_out[at] = jnp.where(allowed, 0.0, masked_score)
-
-
 def combine_kernel(at, ways, has_found, flags, *refs):
     got, refs = refs[:ways], refs[ways:]
     total = sum(flags[at + 2 * step + 1] * got[step][...].astype(f32) for step in range(ways))
@@ -268,20 +278,19 @@
 
 def qkv_kernel(first, layer, place, *refs):
     if first:
-        refs, outs = refs[:7], refs[7:]
-        pieces, (own, other, tail) = refs[:4], refs[4:]
-        hidden_out, normed_out, qkv_out, state_out, halo_out, gains, blends_out = outs
+        refs, outs = refs[:8], refs[8:]
+        pieces, (own, other, tail, edge) = refs[:4], refs[4:]
+        hidden_out, normed_out, qkv_out, state_out, halo_out, gains = outs
         rows = hidden_out.shape[0]
-        for index, (piece, quarter) in enumerate(zip(pieces, quarters(place))):
+        for piece, quarter in zip(pieces, quarters(place)):
             hidden_out[:, quarter_lanes(quarter)] = piece[:rows].astype(f32)
             parts = piece[rows:].astype(f32)
             small = parts[:SMALL] + parts[SMALL : 2 * SMALL] + parts[2 * SMALL :]
             gains[:, quarter_lanes(quarter)] = small
-            if index < 2:
-                blends_out[:, index * LANES : (index + 1) * LANES] = small
         hidden = hidden_out[...]
     else:
-        base, part_a, part_b, gains, own, other, tail, hidden_out, normed_out, qkv_out, state_out, halo_out = refs
+        base, part_a, part_b, gains, own, other, tail, edge, *outs = refs
+        hidden_out, normed_out, qkv_out, state_out, halo_out = outs
         hidden = base[...] + (part_a[...].astype(f32) + part_b[...].astype(f32))
         hidden_out[...] = hidden
     rows = hidden.shape[0]
@@ -305,8 +314,9 @@
             dot_tn(two, values),
             jnp.sum(one.astype(f32), axis=0, keepdims=True),
         )
-        halo_out[quarter, 0] = keys[rows - HALO :]
-        halo_out[quarter, 1] = values[rows - HALO :]
+        halo_out[2 * quarter] = keys[rows - HALO :]
+        halo_out[2 * quarter + 1] = values[rows - HALO :]
+    halo_out[4] = edge[...]
 
 
 def far_kernel(qkv, causal, one_out, two_out, sums_out):
@@ -323,16 +333,18 @@
 
 def near_kernel(place, qkv, halo, band, near_out):
     rows = qkv.shape[1]
+    bias = halo_bias(halo)
     for pair in range(2):
         quarter = place[0] if pair == 0 else 1 - place[0]
         lanes = slice(pair * LANES, (pair + 1) * LANES)
         queries, keys, values = qkv[0, :, lanes], qkv[1, :, lanes], qkv[2, :, lanes]
-        ext_keys = extend(halo[quarter, 0], keys)
-        ext_values = extend(halo[quarter, 1], values)
+        ext_keys = extend(halo[2 * quarter], keys)
+        ext_values = extend(halo[2 * quarter + 1], values)
         for tile in range(rows // TILE):
             at = slice(tile * TILE, (tile + 1) * TILE)
             window = slice(tile * TILE, tile * TILE + LANES)
             allowed = jnp.concatenate([band[at], band[at]], axis=0)
+            allowed = allowed + bias if tile == 0 else allowed
             scores = dot_nt(split_heads(queries[at]), ext_keys[window]) * score_scale + allowed
             weights = jnp.exp(scores - jnp.max(scores, axis=1, keepdims=True))
             weights = weights / jnp.sum(weights, axis=1, keepdims=True)
@@ -344,7 +356,7 @@
     mixed_out, far_one_out, far_two_out, root_out, prefix_out, state, part_out = refs[count:]
     last_combine(at, flags, found, got, state)
     mixed = []
-    row = 2 * LAYERS + 3 * layer
+    row = 3 * layer
     for pair in range(2):
         quarter = place[0] if pair == 0 else 1 - place[0]
         lanes = slice(pair * LANES, (pair + 1) * LANES)
@@ -460,7 +472,7 @@
     )
     resid = base[...] + back
     resid_out[...] = resid
-    blend = blends[2 * LAYERS + 3 * layer : 2 * LAYERS + 3 * layer + 3]
+    blend = blends[3 * layer : 3 * layer + 3]
     rows = resid.astype(bf16)
     rows_out[...] = rows
     weight = jnp.concatenate([own[layer], other[...]], axis=0)
@@ -498,15 +510,16 @@
 ):
     rows = qkv.shape[1]
     row_low = lax.broadcasted_iota(jnp.int32, (2 * TILE, 1), 0) < TILE
-    row = 2 * LAYERS + 3 * layer
+    bias = halo_bias(halo)
+    row = 3 * layer
     for pair in range(2):
         quarter = place[0] if pair == 0 else 1 - place[0]
         lanes = slice(pair * LANES, (pair + 1) * LANES)
         queries, keys, values = qkv[0, :, lanes], qkv[1, :, lanes], qkv[2, :, lanes]
         grads = d_mixed[:, lanes]
         blend = blends[row : row + 1, lanes]
-        ext_keys = extend(halo[quarter, 0], keys)
-        ext_values = extend(halo[quarter, 1], values)
+        ext_keys = extend(halo[2 * quarter], keys)
+        ext_values = extend(halo[2 * quarter + 1], values)
         near_k[...] = jnp.zeros_like(near_k)
         near_v[...] = jnp.zeros_like(near_v)
         blend_rows = jnp.where(row_low, blend[:, :1], blend[:, HD : HD + 1])
@@ -515,6 +528,7 @@
             at = slice(tile * TILE, (tile + 1) * TILE)
             window = slice(tile * TILE, tile * TILE + LANES)
             allowed = jnp.concatenate([band[at], band[at]], axis=0)
+            allowed = allowed + bias if tile == 0 else allowed
             query_split, grad_split = split_heads(queries[at]), split_heads(grads[at])
             scores = dot_nt(query_split, ext_keys[window]) * score_scale + allowed
             probs = jnp.exp(scores - jnp.max(scores, axis=1, keepdims=True))
@@ -706,10 +720,9 @@
     return jnp.concatenate([first, second], axis=0)
 
 
-def finish_kernel(groups, place, *refs):
-    refs, (up_out, down_out, out_out, qkv_out, small_out) = refs[:-5], refs[-5:]
+def finish_wide_kernel(groups, place, *refs):
+    refs, (up_out, down_out, out_out, above_out) = refs[:-4], refs[-4:]
     outs = {"up": up_out, "down": down_out, "out": out_out}
-    qkv = {}
     for group, (layers, jobs, bit) in enumerate(groups):
         whole = in_order(bit, place, refs[2 * group], refs[2 * group + 1])
         at = 0
@@ -717,15 +730,28 @@
             rows = whole[at : at + job_rows(job, up_out.shape[2])]
             at += rows.shape[0]
             if job == "qkv":
-                qkv[layer] = rows
+                above_out[...] = rows
             else:
                 outs[job][layer] = rows.astype(f32)
-    small_out[...] = whole[at : at + SMALL, :LANES].astype(f32)
-    for layer in range(LAYERS):
+
+
+def finish_qkv_kernel(bit, place, mine, other, above, qkv_out, attn_out, ffn_out, blend_out):
+    whole = in_order(bit, place, mine, other)
+    at = 3 * LANES
+    for layer, rows in enumerate((whole, above)):
         for kind in range(3):
             for block in range(D // LANES):
                 lanes = slice(block * LANES, (block + 1) * LANES)
-                qkv_out[layer, kind, lanes] = qkv[layer][kind * LANES : (kind + 1) * LANES, lanes].astype(f32)
+                qkv_out[layer, kind, lanes] = rows[kind * LANES : (kind + 1) * LANES, lanes].astype(f32)
+    small = whole[at : at + SMALL, :LANES].astype(f32)
+    attn_out[...] = small[:LAYERS]
+    ffn_out[...] = small[LAYERS : 2 * LAYERS]
+    blends = small[2 * LAYERS : 5 * LAYERS]
+    low = low_lanes(3 * LAYERS)
+    lane = lax.broadcasted_iota(jnp.int32, (3 * LAYERS, LANES), 1)
+    first = jnp.sum(jnp.where(low, blends, 0.0), axis=1, keepdims=True)
+    second = jnp.sum(jnp.where(low, 0.0, blends), axis=1, keepdims=True)
+    blend_out[...] = jnp.where(lane == 0, first, second)
 
 
 def call(body, outs, operands, scalars=0, scratch=(), scalar_outs=0, bulk=(), bulk_outs=()):
@@ -759,6 +785,11 @@
     return lax.ppermute(value, "mlp", [(i, i ^ 2) for i in range(count)])
 
 
+def both_swap(value):
+    count = lax.axis_size("mlp")
+    return lax.ppermute(value, "mlp", [(i, i ^ 3) for i in range(count)])
+
+
 def chunk_move(value, target):
     shards, parts = lax.axis_size("seq"), lax.axis_size("mlp")
     pairs = []
@@ -836,59 +867,65 @@
     gain_like = ((1, D), f32)
 
     piece_like = ((rows + 3 * SMALL, LANES), bf16)
-    mine, theirs = call(
+    (blend_rows,) = call(pack_blend_kernel, (((SMALL, LANES), f32),), (blend,), 1)
+    mine, theirs = pl.pallas_call(
         pack_kernel,
-        (piece_like, piece_like),
-        (place, blend, inputs, norm_attn, norm_ffn),
-        2,
-        bulk=(2, 3, 4),
-    )
+        out_shape=tuple(jax.ShapeDtypeStruct(*piece_like) for _ in range(2)),
+        in_specs=[SM] + [pl.BlockSpec(memory_space=pl.ANY)] * 3,
+        out_specs=(VM, VM),
+        scratch_shapes=(
+            pltpu.VMEM(inputs.shape, bf16),
+            pltpu.VMEM(norm_attn.shape, f32),
+            pltpu.VMEM(norm_ffn.shape, f32),
+            pltpu.SemaphoreType.DMA((3,)),
+        ),
+        compiler_params=pltpu.CompilerParams(vmem_limit_bytes=24 * 2**20),
+    )(place, inputs, norm_attn, norm_ffn)
     got = half_swap(theirs)
-    pieces = (mine, got, part_swap(mine), part_swap(got))
+    pieces = (mine, got, part_swap(mine), both_swap(theirs))
     far_qkv, far_out, far_up, far_down = [
-        [half_swap(after(w[layer], theirs)) for layer in range(LAYERS)] for w in (w_qkv, w_out, w_up, w_down)
+        [
+            half_swap(after(w[layer], theirs)) for layer in range(LAYERS)
+        ]
+        for w in (w_qkv, w_out, w_up, w_down)
     ]
     grad_mine, grad_theirs = call(pack_grad_kernel, (shard_like, shard_like), (place, after(grad_out, theirs)), 1)
-    grad_got = half_swap(grad_theirs)
-    grad_pieces = (grad_mine, grad_got, part_swap(grad_mine), part_swap(grad_got))
-
-    before = lax.ppermute(
-        after(valid, pieces[3])[2 * rows - LANES :].reshape(1, LANES), "seq", [(source, source + 1) for source in range(shards - 1)]
-    )
+    grad_pieces = (grad_mine, half_swap(grad_theirs), part_swap(grad_mine), both_swap(grad_theirs))
+
     _, flag_count = flag_places(chunks)
-    causal, causal_t, carried, tail, flags = call(
+    causal, causal_t, band, carried, tail, edge, flags = call(
         functools.partial(setup_kernel, chunks),
         (
             ((rows, rows), bf16),
             ((rows, rows), bf16),
             ((rows, LANES), f32),
+            ((rows, LANES), f32),
             ((rows, LANES), bf16),
+            ((HALO, LANES), bf16),
             ((flag_count,), f32),
         ),
         (place, lengths, valid.reshape(1, 2 * rows)),
         2,
         scalar_outs=1,
     )
-    (band,) = call(
-        band_kernel, (((rows, LANES), f32),), (place, lengths, valid.reshape(1, 2 * rows), before), 2
-    )
+    blends = jnp.concatenate([blend_rows, half_swap(blend_rows)], axis=1)
 
     saved = []
     base, adds = None, None
     for layer in range(LAYERS):
-        outs = (hidden_like, low_like, qkv_like, state_like, halo_like)
+        outs = (hidden_like, low_like, qkv_like, state_like, ((5, HALO, LANES), bf16))
         if layer == 0:
-            hidden, normed, qkv, state, halo, gains, blends = call(
+            hidden, normed, qkv, state, halo, gains = call(
                 functools.partial(qkv_kernel, True, layer),
-                outs + (((SMALL, D), f32), ((SMALL, wide), f32)),
-                (place, *pieces, w_qkv, far_qkv[layer], tail),
+                outs + (((SMALL, D), f32),),
+                (place, *pieces, w_qkv, far_qkv[layer], tail, edge),
                 1,
             )
         else:
             hidden, normed, qkv, state, halo = call(
                 functools.partial(qkv_kernel, False, layer),
                 outs,
-                (place, base, *adds, gains, w_qkv, far_qkv[layer], tail),
+                (place, base, *adds, gains, w_qkv, far_qkv[layer], tail, edge),
                 1,
             )
         halo = chunk_move(halo, lambda c: c + 1)
@@ -913,10 +950,8 @@
             (hidden, normed, qkv, state, halo, mixed, far_one, far_two, root, prefix, middle, normed_ffn,
              weights, pre_own, pre_far, act_own, act_far)
         )
-        base, adds = middle, (piece_ffn, part_swap(piece_ffn))
-    out_mine, out_theirs = call(output_kernel, (shard_like, shard_like), (place, base, *adds), 1)
-    output = jnp.concatenate(by_place(half, out_mine, half_swap(out_theirs)))
-
+        base, adds = middle, (piece_ffn, part_swap(piece_ffn) if layer + 1 < LAYERS else None)
+    last_base, last_piece = base, adds[0]
     base, adds = None, None
     d_gain_attn, d_gain_ffn, d_blends = [None] * LAYERS, [None] * LAYERS, [None] * LAYERS
     d_qkvs = [None] * LAYERS
@@ -972,7 +1007,7 @@
         yield value
         yield (value, got)
 
-    groups = []
+    groups, taken = [], {}
 
     def start_group(layers, jobs, order, rows, first, second):
         steps = group_steps(order, rows, first, second)
@@ -980,6 +1015,7 @@
         groups.append((layers, jobs, order[0], steps))
 
     def step(index, *others):
+        taken[index] = taken.get(index, 0) + 1
         return groups[index][3].send(others)
 
     for layer in reversed(range(LAYERS)):
@@ -999,6 +1035,27 @@
                 outs + (gain_like,),
                 (base, *adds, saved[layer + 1][0], gains, *weights, pre_own, pre_far),
             )
+        def upper_grads(*others):
+            jobs = ("up", "down", "out")
+            own, far = first_step(
+                jobs, (after(normed_ffn, *others), d_up_own, d_up_far, act_own, act_far, grad_rows, mixed, out_rows)
+            )
+            start_group((layer,) * 3, jobs, side_first, (0, own.shape[0]), (own,), (half_swap(far),))
+            return far
+
+        def lower_grads(*others):
+            jobs = ("up", "qkv", "down", "out")
+            operands = (
+                after(normed_ffn, *others), d_up_own, d_up_far, saved[1][1], d_qkvs[1], act_own, act_far, grad_rows,
+                mixed, out_rows,
+            )
+            own, far = first_step(jobs, operands)
+            cut = job_rows("up", units) + job_rows("qkv", units)
+            got = half_swap(far)
+            start_group((0, 1), jobs[:2], side_first, (0, cut), (own,), (got,))
+            start_group((0,) * len(jobs[2:]), jobs[2:], line_first, (cut, own.shape[0]), (own,), (got,))
+            return far
+
         (resid, out_rows, d_mixed, d_gain_ffn[layer], num_one, num_two, d_zeta, state_back, blend_far) = call(
             functools.partial(mix_back_kernel, layer),
             (hidden_like, low_like, heads_low, gain_like, heads_low, heads_low, heads_like, state_like,
@@ -1017,27 +1074,12 @@
         )
         halo_back = chunk_move(halo_back, lambda c: c - 1)
         (found, parts_got, at), arrived, value = scan(state_back, flags, chunks, True, lambda: (dq_near,))
+        ready = [value]
         if layer > 0:
-            jobs = ("up", "down", "out")
-            own, far = first_step(
-                jobs, (after(normed_ffn, value), d_up_own, d_up_far, act_own, act_far, grad_rows, mixed, out_rows)
-            )
-            start_group((layer,) * 3, jobs, side_first, (0, own.shape[0]), (own,), (half_swap(far),))
-            made = far
+            ready.append(upper_grads(value))
         else:
-            made = step(0, value)
-            jobs = ("up", "qkv", "down", "out")
-            own, far = first_step(
-                jobs,
-                (after(normed_ffn, made), d_up_own, d_up_far, saved[1][1], d_qkvs[1], act_own, act_far, grad_rows,
-                 mixed, out_rows),
-            )
-            cut = job_rows("up", units) + job_rows("qkv", units)
-            got = half_swap(far)
-            start_group((0, 1), jobs[:2], side_first, (0, cut), (own,), (got,))
-            start_group((0, 0), jobs[2:], line_first, (cut, own.shape[0]), (own,), (got,))
-            made = far
-        ready = [made]
+            ready.append(step(0, *ready))
+            ready.append(lower_grads(*ready))
         dq, dk_one, dk_two, dv = call(
             far_back_kernel,
             (heads_low, heads_like, heads_like, heads_like),
@@ -1058,9 +1100,16 @@
             base = after(base, step(0, piece))
         d_blends[layer] = (blend_near, blend_far)
 
-    last_like = ((3 * LANES, D), bf16)
     made = step(0, step(2, step(1, piece)))
-    own, far = call(functools.partial(grads_kernel, ("qkv",)), (last_like, last_like), (place, after(saved[0][1], made), d_qkvs[0]), 1)
+    jobs = ("qkv",)
+    height = job_rows("qkv", units)
+    last_like = ((height, D), bf16)
+    own, far = call(
+        functools.partial(grads_kernel, jobs),
+        (last_like, last_like),
+        (place, after(saved[0][1], made), d_qkvs[0]),
+        1,
+    )
     smalls = d_gain_attn[1:] + d_gain_ffn + [ref for pair in d_blends for ref in pair]
     small_like = ((SMALL, LANES), f32)
     mine, theirs, small_own, small_far = call(
@@ -1069,28 +1118,43 @@
         (place, after(base, far), *adds, saved[0][0], gains, *smalls),
         1,
     )
-    start_group((0,), ("qkv",), line_first, (0, 4 * LANES), (own, small_own), (half_swap(far), half_swap(small_far)))
+    start_group((0,), jobs, line_first, (0, height + LANES), (own, small_own), (half_swap(far), half_swap(small_far)))
     made = step(3, mine)
-    for index in (0, 1, 2, 3, 0, 1, 2, 3, 0, 1, 2, 3, 1, 2, 3, 1, 2, 3):
-        made = step(index, made)
+    for turn in range(6):
+        for index in range(4):
+            if taken[index] < 6:
+                made = step(index, made)
+        if turn == 1:
+            last_piece = after(last_piece, made)
+            out_mine, out_theirs = call(
+                output_kernel, (shard_like, shard_like), (place, last_base, last_piece, part_swap(last_piece)), 1
+            )
+            output = jnp.concatenate(by_place(half, out_mine, half_swap(out_theirs)))
     d_inputs = jnp.concatenate(by_place(half, mine, half_swap(theirs)))
     sums = [part for group in groups for part in next(group[3])]
-    d_up, d_down, d_out, d_qkv, small = call(
-        functools.partial(finish_kernel, [group[:3] for group in groups]),
+    d_up, d_down, d_out, above = call(
+        functools.partial(finish_wide_kernel, [group[:3] for group in groups[:3]]),
         (
             ((LAYERS, D, units), f32),
             ((LAYERS, units, D), f32),
             ((LAYERS, LANES, D), f32),
-            ((LAYERS, 3, D, LANES), f32),
-            small_like,
+            ((3 * LANES, D), bf16),
         ),
-        (place, *sums),
+        (place, *sums[:6]),
         1,
     )
-    count = 2 * LAYERS + 3 * LAYERS
-    d_norm_attn = small[:LAYERS]
-    d_norm_ffn = small[LAYERS : 2 * LAYERS]
-    d_blend = jnp.sum(small[2 * LAYERS : count].reshape(LAYERS, 3, 2, HD), axis=3)
+    d_qkv, d_norm_attn, d_norm_ffn, d_blend = call(
+        functools.partial(finish_qkv_kernel, line_first[0]),
+        (
+            ((LAYERS, 3, D, LANES), f32),
+            ((LAYERS, LANES), f32),
+            ((LAYERS, LANES), f32),
+            ((3 * LAYERS, LANES), f32),
+        ),
+        (place, *sums[6:], above),
+        1,
+    )
+    d_blend = d_blend[:, :2].reshape(LAYERS, 3, 2)
     return (output, d_inputs, d_norm_attn, d_qkv, d_blend, d_out, d_norm_ffn, d_up, d_down)
 
 

time: 261 us -> 257 us (0.985)
  waiting for transfers between devices: 105 us -> 99 us
    ppermute x12 -> x10, waiting for transfers between devices: 47.3 us -> 42 us  [part_swap(): return lax.ppermute(value, 'mlp', [(i, i ^ 2) for i in range(count)])]
    ppermute x24, waiting for transfers between devices: 40.3 us -> 37 us  [shard_swap(): return lax.ppermute(value, 'seq', [(i, i ^ 1 << bit) for i in range(count)])]
    ppermute x24, starting transfers between devices: 23.2 us -> 25.9 us  [shard_swap(): return lax.ppermute(value, 'seq', [(i, i ^ 1 << bit) for i in range(count)])]
    ppermute x12 -> x10, starting transfers between devices: 10.8 us -> 8.59 us  [part_swap(): return lax.ppermute(value, 'mlp', [(i, i ^ 2) for i in range(count)])]
  transfers between devices with their start and end apart: 81 -> 81, of which waited for: 28 -> 27; matrix products, arithmetic and copies ran while one was open for 1% -> 1% of each run, Pallas kernels for 19% -> 21%
where the time goes in v6:
time: 257 us; the launch traced here: 256 us
  waiting for transfers between devices  99 us (39%)
  starting transfers between devices  82.7 us (32%)
  Pallas kernels  65.9 us (26%)
  local copies, waits for them, and re-layouts  5.38 us (2%)
    pallas_call x58, Pallas kernels, call(): pl.pallas_call(body, out_shape=tuple((jax.ShapeDtypeStruct(shape, kind) f...  65.1 us
    ppermute x10, waiting for transfers between devices, part_swap(): return lax.ppermute(value, 'mlp', [(i, i ^ 2) for i in range(count)])  42 us
    ppermute x28, starting transfers between devices, chunk_move(): return lax.ppermute(value, AXES, pairs)  41.8 us
    ppermute x24, waiting for transfers between devices, shard_swap(): return lax.ppermute(value, 'seq', [(i, i ^ 1 << bit) for i in range(count)])  37 us
    ppermute x24, starting transfers between devices, shard_swap(): return lax.ppermute(value, 'seq', [(i, i ^ 1 << bit) for i in range(count)])  25.9 us
    ppermute x28, waiting for transfers between devices, chunk_move(): return lax.ppermute(value, AXES, pairs)  18.8 us
    ppermute x10, starting transfers between devices, part_swap(): return lax.ppermute(value, 'mlp', [(i, i ^ 2) for i in range(count)])  8.59 us
  transfers between devices with their start and end apart: 81, of which 27 were waited for; matrix products, arithmetic and copies ran while one was open for 1% of the time, Pallas kernels for 21%

profile of v6, /device:TPU:0, one launch (start us, length us, event | category | flops | bytes accessed | tf_op | source)
XLA Modules:
  0.0 256.1 jit_solution(16107579866462504231)
XLA Ops:
  4.4 2.6 %collective-permute-start.2 = (bf16[304,128]{1,0:T(8,128)(2,1)S(1)}, bf16[304,128]{1,0:T(8,128)(2,1)S(1)}, u32[]{:S(2)}, u32[]{:S(2)}) collective-permute-start(bf16[304,128]{1,0:T(8,128)(2,1)S(1)} %get-tuple-element.215), channel_id=1, source_target_pairs={{0,3},{1,2},{2,1},{3,0},{4,7},{5,6},{6,5},{7,4},{8,11},{9,10},{10,... | collective-permute-start | bytes 233480 | tf_op jit(solution)/shard_map/ppermute | solution.py:790
  22.9 2.3 collective-permute-start.4
  26.8 3.5 %collective-permute-start.13 = (bf16[2,144,128]{2,1,0:T(8,128)(2,1)S(1)}, bf16[2,144,128]{2,1,0:T(8,128)(2,1)S(1)}, u32[]{:S(2)}, u32[]{:S(2)}) collective-permute-start(bf16[2,144,128]{2,1,0:T(8,128)(2,1)S(1)} %get-tuple-element.237), channel_id=1, source_target_pairs={{0,8},{2,10},{1,9},{3,11},{4,12},{6,14},{5,13},{7,15},{8,16},{10,1... | collective-permute-start | bytes 221192 | tf_op jit(solution)/shard_map/ppermute | solution.py:802
  30.3 4.5 %collective-permute-start.14 = (bf16[2,144,128]{2,1,0:T(8,128)(2,1)S(1)}, bf16[2,144,128]{2,1,0:T(8,128)(2,1)S(1)}, u32[]{:S(2)}, u32[]{:S(2)}) collective-permute-start(bf16[2,144,128]{2,1,0:T(8,128)(2,1)S(1)} %get-tuple-element.237), channel_id=1, source_target_pairs={{0,16},{2,18},{1,17},{3,19},{4,20},{6,22},{5,21},{7,23},{8,24},{10... | collective-permute-start | bytes 221192 | tf_op jit(solution)/shard_map/ppermute | solution.py:802
  36.1 2.7 %shard_map.181.near = f32[256,256]{1,0:T(8,128)S(1)} custom-call(s32[3]{0:T(128)S(1)} %pad_add_fusion.place.refs_0_, bf16[3,256,256]{2,1,0:T(8,128)(2,1)S(1)} %get-tuple-element.221.qkv, bf16[5,32,128]{2,1,0:T(8,128)(2,1)S(1)} %collective-permute-done.4.halo, f32[256,128]{1,0:T(8,128)S(1)} %get-tuple-element.223.band), custom_call_target="tpu_custom_call" | custom-call | tf_op jit(solution)/shard_map/pallas_call | solution.py:764
  41.0 7.8 %collective-permute-done.16.part_b = bf16[256,512]{1,0:T(8,128)(2,1)S(1)} collective-permute-done((bf16[256,512]{1,0:T(8,128)(2,1)S(1)}, bf16[256,512]{1,0:T(8,128)(2,1)S(1)}, u32[]{:S(2)}, u32[]{:S(2)}) %collective-permute-start.16) | collective-permute-done | bytes 262176 | tf_op jit(solution)/shard_map/ppermute | solution.py:785
  51.1 6.8 %collective-permute-done.19.refs_2_ = bf16[256,512]{1,0:T(8,128)(2,1)S(1)} collective-permute-done((bf16[256,512]{1,0:T(8,128)(2,1)S(1)}, bf16[256,512]{1,0:T(8,128)(2,1)S(1)}, u32[]{:S(2)}, u32[]{:S(2)}) %collective-permute-start.19) | collective-permute-done | bytes 262176 | tf_op jit(solution)/shard_map/ppermute | solution.py:785
  61.2 3.5 %collective-permute-done.24.refs_2_ = bf16[2,144,128]{2,1,0:T(8,128)(2,1)S(1)} collective-permute-done((bf16[2,144,128]{2,1,0:T(8,128)(2,1)S(1)}, bf16[2,144,128]{2,1,0:T(8,128)(2,1)S(1)}, u32[]{:S(2)}, u32[]{:S(2)}) %collective-permute-start.24) | collective-permute-done | bytes 73760 | tf_op jit(solution)/shard_map/ppermute | solution.py:802
  69.4 6.3 %collective-permute-start.27 = (bf16[2,144,128]{2,1,0:T(8,128)(2,1)S(1)}, bf16[2,144,128]{2,1,0:T(8,128)(2,1)S(1)}, u32[]{:S(2)}, u32[]{:S(2)}) collective-permute-start(bf16[2,144,128]{2,1,0:T(8,128)(2,1)S(1)} %get-tuple-element.255), channel_id=1, source_target_pairs={{0,16},{2,18},{1,17},{3,19},{4,20},{6,22},{5,21},{7,23},{8,24},{10... | collective-permute-start | bytes 221192 | tf_op jit(solution)/shard_map/ppermute | solution.py:802
  77.2 2.7 %shard_map.189.near = f32[256,256]{1,0:T(8,128)S(1)} custom-call(s32[3]{0:T(128)S(1)} %pad_add_fusion.place.refs_0_, bf16[3,256,256]{2,1,0:T(8,128)(2,1)S(1)} %get-tuple-element.246.qkv, bf16[5,32,128]{2,1,0:T(8,128)(2,1)S(1)} %collective-permute-done.21.halo, f32[256,128]{1,0:T(8,128)S(1)} %get-tuple-element.223.band), custom_call_target="tpu_custom_call" | custom-call | tf_op jit(solution)/shard_map/pallas_call | solution.py:764
  81.9 6.6 %collective-permute-done.29.part_b = bf16[256,512]{1,0:T(8,128)(2,1)S(1)} collective-permute-done((bf16[256,512]{1,0:T(8,128)(2,1)S(1)}, bf16[256,512]{1,0:T(8,128)(2,1)S(1)}, u32[]{:S(2)}, u32[]{:S(2)}) %collective-permute-start.29) | collective-permute-done | bytes 262176 | tf_op jit(solution)/shard_map/ppermute | solution.py:785
  92.1 5.7 %collective-permute-done.32.part_b = bf16[256,512]{1,0:T(8,128)(2,1)S(1)} collective-permute-done((bf16[256,512]{1,0:T(8,128)(2,1)S(1)}, bf16[256,512]{1,0:T(8,128)(2,1)S(1)}, u32[]{:S(2)}, u32[]{:S(2)}) %collective-permute-start.32) | collective-permute-done | bytes 262176 | tf_op jit(solution)/shard_map/ppermute | solution.py:785
  99.3 3.1 %collective-permute-start.34 = (bf16[2,144,128]{2,1,0:T(8,128)(2,1)S(1)}, bf16[2,144,128]{2,1,0:T(8,128)(2,1)S(1)}, u32[]{:S(2)}, u32[]{:S(2)}) collective-permute-start(bf16[2,144,128]{2,1,0:T(8,128)(2,1)S(1)} %get-tuple-element.273.refs_0_), channel_id=1, source_target_pairs={{0,4},{2,6},{1,5},{3,7},{4,0},{6,2},{5,1},{7,3},{8,12},{10,14},{9,... | collective-permute-start | bytes 221192 | tf_op jit(solution)/shard_map/ppermute | solution.py:802
  102.5 4.2 %shard_map.196 = (f32[256,256]{1,0:T(8,128)S(1)}, f32[256,256]{1,0:T(8,128)S(1)}, f32[256,256]{1,0:T(8,128)S(1)}, bf16[2,2,32,128]{3,2,1,0:T(8,128)(2,1)S(1)}, f32[1,256]{1,0:T(1,128)S(1)}) custom-call(s32[3]{0:T(128)S(1)} %pad_add_fusion.place.refs_0_, bf16[3,256,256]{2,1,0:T(8,128)(2,1)S(1)} %get-tuple-element.246.qkv, ...), custom_call_target="tpu_custom_call" | custom-call | tf_op jit(solution)/shard_map/pallas_call | solution.py:764
  114.3 2.7 %shard_map.199 = (bf16[256,256]{1,0:T(8,128)(2,1)S(1)}, f32[256,256]{1,0:T(8,128)S(1)}, f32[256,256]{1,0:T(8,128)S(1)}, f32[256,256]{1,0:T(8,128)S(1)}) custom-call(s32[3]{0:T(128)S(1)} %pad_add_fusion.place.refs_0_, bf16[3,256,256]{2,1,0:T(8,128)(2,1)S(1)} %get-tuple-element.246.qkv, bf16[256,256]{1,0:T(8,128)(2,1)S(1)} %get-tuple-element.224.causal, ...), custom_call_target="tpu_custom_call" | custom-call | tf_op jit(solution)/shard_map/pallas_call | solution.py:764
  117.5 3.6 %collective-permute-done.40.refs_2_ = bf16[2,144,128]{2,1,0:T(8,128)(2,1)S(1)} collective-permute-done((bf16[2,144,128]{2,1,0:T(8,128)(2,1)S(1)}, bf16[2,144,128]{2,1,0:T(8,128)(2,1)S(1)}, u32[]{:S(2)}, u32[]{:S(2)}) %collective-permute-start.40) | collective-permute-done | bytes 73760 | tf_op jit(solution)/shard_map/ppermute | solution.py:802
  126.0 4.2 %collective-permute-done.42.refs_2_ = bf16[256,512]{1,0:T(8,128)(2,1)S(1)} collective-permute-done((bf16[256,512]{1,0:T(8,128)(2,1)S(1)}, bf16[256,512]{1,0:T(8,128)(2,1)S(1)}, u32[]{:S(2)}, u32[]{:S(2)}) %collective-permute-start.42) | collective-permute-done | bytes 262176 | tf_op jit(solution)/shard_map/ppermute | solution.py:785
  132.4 6.1 %collective-permute-done.43.part_b = bf16[256,512]{1,0:T(8,128)(2,1)S(1)} collective-permute-done((bf16[256,512]{1,0:T(8,128)(2,1)S(1)}, bf16[256,512]{1,0:T(8,128)(2,1)S(1)}, u32[]{:S(2)}, u32[]{:S(2)}) %collective-permute-start.43) | collective-permute-done | bytes 262176 | tf_op jit(solution)/shard_map/ppermute | solution.py:785
  142.0 4.2 %shard_map.204 = (f32[256,256]{1,0:T(8,128)S(1)}, f32[256,256]{1,0:T(8,128)S(1)}, f32[256,256]{1,0:T(8,128)S(1)}, bf16[2,2,32,128]{3,2,1,0:T(8,128)(2,1)S(1)}, f32[1,256]{1,0:T(1,128)S(1)}) custom-call(s32[3]{0:T(128)S(1)} %pad_add_fusion.place.refs_0_, bf16[3,256,256]{2,1,0:T(8,128)(2,1)S(1)} %get-tuple-element.221.qkv, ...), custom_call_target="tpu_custom_call" | custom-call | tf_op jit(solution)/shard_map/pallas_call | solution.py:764
  156.9 2.7 %shard_map.208 = (bf16[256,256]{1,0:T(8,128)(2,1)S(1)}, f32[256,256]{1,0:T(8,128)S(1)}, f32[256,256]{1,0:T(8,128)S(1)}, f32[256,256]{1,0:T(8,128)S(1)}) custom-call(s32[3]{0:T(128)S(1)} %pad_add_fusion.place.refs_0_, bf16[3,256,256]{2,1,0:T(8,128)(2,1)S(1)} %get-tuple-element.221.qkv, bf16[256,256]{1,0:T(8,128)(2,1)S(1)} %get-tuple-element.224.causal, ...), custom_call_target="tpu_custom_call" | custom-call | tf_op jit(solution)/shard_map/pallas_call | solution.py:764
  160.9 5.7 %collective-permute-done.51.refs_1_ = bf16[2,144,128]{2,1,0:T(8,128)(2,1)S(1)} collective-permute-done((bf16[2,144,128]{2,1,0:T(8,128)(2,1)S(1)}, bf16[2,144,128]{2,1,0:T(8,128)(2,1)S(1)}, u32[]{:S(2)}, u32[]{:S(2)}) %collective-permute-start.51) | collective-permute-done | bytes 73760 | tf_op jit(solution)/shard_map/ppermute | solution.py:802
  175.5 4.4 %collective-permute-done.54.part_b = bf16[256,512]{1,0:T(8,128)(2,1)S(1)} collective-permute-done((bf16[256,512]{1,0:T(8,128)(2,1)S(1)}, bf16[256,512]{1,0:T(8,128)(2,1)S(1)}, u32[]{:S(2)}, u32[]{:S(2)}) %collective-permute-start.54) | collective-permute-done | bytes 262176 | tf_op jit(solution)/shard_map/ppermute | solution.py:785
  183.6 3.4 %collective-permute-start.63 = (bf16[144,512]{1,0:T(8,128)(2,1)S(1)}, bf16[144,512]{1,0:T(8,128)(2,1)S(1)}, u32[]{:S(2)}, u32[]{:S(2)}) collective-permute-start(bf16[144,512]{1,0:T(8,128)(2,1)S(1)} %shard_map.216.mine), channel_id=1, source_target_pairs={{0,16},{4,20},{8,24},{12,28},{16,0},{20,4},{24,8},{28,12},{1,17},{... | collective-permute-start | bytes 442376 | tf_op jit(solution)/shard_map/ppermute | solution.py:839
  188.8 6.3 %collective-permute-done.56.second = bf16[256,512]{1,0:T(8,128)(2,1)S(1)} collective-permute-done((bf16[256,512]{1,0:T(8,128)(2,1)S(1)}, bf16[256,512]{1,0:T(8,128)(2,1)S(1)}, u32[]{:S(2)}, u32[]{:S(2)}) %collective-permute-start.56) | collective-permute-done | bytes 262176 | tf_op jit(solution)/shard_map/ppermute | solution.py:839
  196.7 2.2 collective-permute-start.61
  199.6 7.1 %collective-permute-done.62.second = bf16[224,512]{1,0:T(8,128)(2,1)S(1)} collective-permute-done((bf16[224,512]{1,0:T(8,128)(2,1)S(1)}, bf16[224,512]{1,0:T(8,128)(2,1)S(1)}, u32[]{:S(2)}, u32[]{:S(2)}) %collective-permute-start.62) | collective-permute-done | bytes 229408 | tf_op jit(solution)/shard_map/ppermute | solution.py:839
  209.1 6.1 %collective-permute-done.60.second = bf16[128,512]{1,0:T(8,128)(2,1)S(1)} collective-permute-done((bf16[128,512]{1,0:T(8,128)(2,1)S(1)}, bf16[128,512]{1,0:T(8,128)(2,1)S(1)}, u32[]{:S(2)}, u32[]{:S(2)}) %collective-permute-start.60) | collective-permute-done | bytes 131104 | tf_op jit(solution)/shard_map/ppermute | solution.py:839
  225.8 2.5 collective-permute-start.75
  230.8 4.3 %collective-permute-done.76.got = bf16[224,512]{1,0:T(8,128)(2,1)S(1)} collective-permute-done((bf16[224,512]{1,0:T(8,128)(2,1)S(1)}, bf16[224,512]{1,0:T(8,128)(2,1)S(1)}, u32[]{:S(2)}, u32[]{:S(2)}) %collective-permute-start.76) | collective-permute-done | bytes 229408 | tf_op jit(solution)/shard_map/ppermute | solution.py:839
  237.5 2.8 %collective-permute-done.75.got = bf16[160,512]{1,0:T(8,128)(2,1)S(1)} collective-permute-done((bf16[160,512]{1,0:T(8,128)(2,1)S(1)}, bf16[160,512]{1,0:T(8,128)(2,1)S(1)}, u32[]{:S(2)}, u32[]{:S(2)}) %collective-permute-start.75) | collective-permute-done | bytes 163872 | tf_op jit(solution)/shard_map/ppermute | solution.py:839
  244.4 6.1 %collective-permute-done.80.refs_5_ = bf16[320,512]{1,0:T(8,128)(2,1)S(1)} collective-permute-done((bf16[320,512]{1,0:T(8,128)(2,1)S(1)}, bf16[320,512]{1,0:T(8,128)(2,1)S(1)}, u32[]{:S(2)}, u32[]{:S(2)}) %collective-permute-start.80) | collective-permute-done | bytes 327712 | tf_op jit(solution)/shard_map/ppermute | solution.py:839
  250.5 2.9 %shard_map.235 = (f32[2,512,512]{2,1,0:T(8,128)}, f32[2,512,512]{2,1,0:T(8,128)}, f32[2,128,512]{2,1,0:T(8,128)}, bf16[384,512]{1,0:T(8,128)(2,1)S(1)}) custom-call(s32[3]{0:T(128)S(1)} %pad_add_fusion.place.refs_0_, bf16[576,512]{1,0:T(8,128)(2,1)S(1)} %shard_map.225.refs_0_, bf16[576,512]{1,0:T(8,128)(2,1)S(1)} %collective-permute-done.78.refs_1_, ...), custom_call_target="tpu_custom_call" | custom-call | tf_op jit(solution)/shard_map/pallas_call | solution.py:764
  (225 shorter events, 114.9 us)
Async XLA Ops:
  4.4 10.6 %collective-permute-start.2 = (bf16[304,128]{1,0:T(8,128)(2,1)S(1)}, bf16[304,128]{1,0:T(8,128)(2,1)S(1)}, u32[]{:S(2)}, u32[]{:S(2)}) collective-permute-start(bf16[304,128]{1,0:T(8,128)(2,1)S(1)} %get-tuple-element.215), channel_id=1, source_target_pairs={{0,3},{1,2},{2,1},{3,0},{4,7},{5,6},{6,5},{7,4},{8,11},{9,10},{10,... | collective-permute-start | bytes 233480 | tf_op jit(solution)/shard_map/ppermute | solution.py:790
  15.0 26.0 %collective-permute-start.17 = (bf16[512,512]{1,0:T(8,128)(2,1)S(1)}, bf16[512,512]{1,0:T(8,128)(2,1)S(1)}, u32[]{:S(2)}, u32[]{:S(2)}) collective-permute-start(bf16[512,512]{1,0:T(8,128)(2,1)S(1)} %get-tuple-element.240), channel_id=1, source_target_pairs={{0,1},{1,0},{2,3},{3,2},{4,5},{5,4},{6,7},{7,6},{8,9},{9,8},{10,11... | collective-permute-start | bytes 1572872 | tf_op jit(solution)/shard_map/ppermute | solution.py:780
  15.2 25.8 %collective-permute-start.18 = (bf16[512,512]{1,0:T(8,128)(2,1)S(1)}, bf16[512,512]{1,0:T(8,128)(2,1)S(1)}, u32[]{:S(2)}, u32[]{:S(2)}) collective-permute-start(bf16[512,512]{1,0:T(8,128)(2,1)S(1)} %get-tuple-element.241), channel_id=1, source_target_pairs={{0,1},{1,0},{2,3},{3,2},{4,5},{5,4},{6,7},{7,6},{8,9},{9,8},{10,11... | collective-permute-start | bytes 1572872 | tf_op jit(solution)/shard_map/ppermute | solution.py:780
  18.7 11.6 %collective-permute-start.6 = (bf16[128,512]{1,0:T(8,128)(2,1)S(1)}, bf16[128,512]{1,0:T(8,128)(2,1)S(1)}, u32[]{:S(2)}, u32[]{:S(2)}) collective-permute-start(bf16[128,512]{1,0:T(8,128)(2,1)S(1)} %get-tuple-element.229), channel_id=1, source_target_pairs={{0,1},{1,0},{2,3},{3,2},{4,5},{5,4},{6,7},{7,6},{8,9},{9,8},{10,11... | collective-permute-start | bytes 393224 | tf_op jit(solution)/shard_map/ppermute | solution.py:780
  22.9 11.9 %collective-permute-start.4 = (bf16[5,32,128]{2,1,0:T(8,128)(2,1)S(1)}, bf16[5,32,128]{2,1,0:T(8,128)(2,1)S(1)}, u32[]{:S(2)}, u32[]{:S(2)}) collective-permute-start(bf16[5,32,128]{2,1,0:T(8,128)(2,1)S(1)} %get-tuple-element.222), channel_id=1, source_target_pairs={{0,1},{2,3},{1,4},{3,6},{4,5},{6,7},{5,8},{7,10},{8,9},{10,11},{9,... | collective-permute-start | bytes 122888 | tf_op jit(solution)/shard_map/ppermute | solution.py:802
  26.8 12.0 %collective-permute-start.13 = (bf16[2,144,128]{2,1,0:T(8,128)(2,1)S(1)}, bf16[2,144,128]{2,1,0:T(8,128)(2,1)S(1)}, u32[]{:S(2)}, u32[]{:S(2)}) collective-permute-start(bf16[2,144,128]{2,1,0:T(8,128)(2,1)S(1)} %get-tuple-element.237), channel_id=1, source_target_pairs={{0,8},{2,10},{1,9},{3,11},{4,12},{6,14},{5,13},{7,15},{8,16},{10,1... | collective-permute-start | bytes 221192 | tf_op jit(solution)/shard_map/ppermute | solution.py:802
  40.7 10.4 %collective-permute-start.20 = (bf16[3,512,128]{2,1,0:T(8,128)(2,1)S(1)}, bf16[3,512,128]{2,1,0:T(8,128)(2,1)S(1)}, u32[]{:S(2)}, u32[]{:S(2)}) collective-permute-start(bf16[3,512,128]{2,1,0:T(8,128)(2,1)S(1)} %get-tuple-element.244), channel_id=1, source_target_pairs={{0,1},{1,0},{2,3},{3,2},{4,5},{5,4},{6,7},{7,6},{8,9},{9,8},{10,11... | collective-permute-start | bytes 1179656 | tf_op jit(solution)/shard_map/ppermute | solution.py:780
  50.5 31.4 %collective-permute-start.30 = (bf16[512,512]{1,0:T(8,128)(2,1)S(1)}, bf16[512,512]{1,0:T(8,128)(2,1)S(1)}, u32[]{:S(2)}, u32[]{:S(2)}) collective-permute-start(bf16[512,512]{1,0:T(8,128)(2,1)S(1)} %get-tuple-element.257), channel_id=1, source_target_pairs={{0,1},{1,0},{2,3},{3,2},{4,5},{5,4},{6,7},{7,6},{8,9},{9,8},{10,11... | collective-permute-start | bytes 1572872 | tf_op jit(solution)/shard_map/ppermute | solution.py:780
  50.5 31.4 %collective-permute-start.31 = (bf16[512,512]{1,0:T(8,128)(2,1)S(1)}, bf16[512,512]{1,0:T(8,128)(2,1)S(1)}, u32[]{:S(2)}, u32[]{:S(2)}) collective-permute-start(bf16[512,512]{1,0:T(8,128)(2,1)S(1)} %get-tuple-element.258), channel_id=1, source_target_pairs={{0,1},{1,0},{2,3},{3,2},{4,5},{5,4},{6,7},{7,6},{8,9},{9,8},{10,11... | collective-permute-start | bytes 1572872 | tf_op jit(solution)/shard_map/ppermute | solution.py:780
  64.7 11.0 %collective-permute-start.21 = (bf16[5,32,128]{2,1,0:T(8,128)(2,1)S(1)}, bf16[5,32,128]{2,1,0:T(8,128)(2,1)S(1)}, u32[]{:S(2)}, u32[]{:S(2)}) collective-permute-start(bf16[5,32,128]{2,1,0:T(8,128)(2,1)S(1)} %get-tuple-element.247), channel_id=1, source_target_pairs={{0,1},{2,3},{1,4},{3,6},{4,5},{6,7},{5,8},{7,10},{8,9},{10,11},{9,... | collective-permute-start | bytes 122888 | tf_op jit(solution)/shard_map/ppermute | solution.py:802
  67.6 12.3 %collective-permute-start.26 = (bf16[2,144,128]{2,1,0:T(8,128)(2,1)S(1)}, bf16[2,144,128]{2,1,0:T(8,128)(2,1)S(1)}, u32[]{:S(2)}, u32[]{:S(2)}) collective-permute-start(bf16[2,144,128]{2,1,0:T(8,128)(2,1)S(1)} %get-tuple-element.255), channel_id=1, source_target_pairs={{0,8},{2,10},{1,9},{3,11},{4,12},{6,14},{5,13},{7,15},{8,16},{10,1... | collective-permute-start | bytes 221192 | tf_op jit(solution)/shard_map/ppermute | solution.py:802
  69.4 10.5 %collective-permute-start.27 = (bf16[2,144,128]{2,1,0:T(8,128)(2,1)S(1)}, bf16[2,144,128]{2,1,0:T(8,128)(2,1)S(1)}, u32[]{:S(2)}, u32[]{:S(2)}) collective-permute-start(bf16[2,144,128]{2,1,0:T(8,128)(2,1)S(1)} %get-tuple-element.255), channel_id=1, source_target_pairs={{0,16},{2,18},{1,17},{3,19},{4,20},{6,22},{5,21},{7,23},{8,24},{10... | collective-permute-start | bytes 221192 | tf_op jit(solution)/shard_map/ppermute | solution.py:802
  108.7 14.5 %collective-permute-start.36 = (bf16[1152,512]{1,0:T(8,128)(2,1)S(1)}, bf16[1152,512]{1,0:T(8,128)(2,1)S(1)}, u32[]{:S(2)}, u32[]{:S(2)}) collective-permute-start(bf16[1152,512]{1,0:T(8,128)(2,1)S(1)} %get-tuple-element.284), channel_id=1, source_target_pairs={{0,1},{1,0},{2,3},{3,2},{4,5},{5,4},{6,7},{7,6},{8,9},{9,8},{10,11... | collective-permute-start | bytes 3538952 | tf_op jit(solution)/shard_map/ppermute | solution.py:780
  124.1 22.8 %collective-permute-start.41 = (bf16[576,512]{1,0:T(8,128)(2,1)S(1)}, bf16[576,512]{1,0:T(8,128)(2,1)S(1)}, u32[]{:S(2)}, u32[]{:S(2)}) collective-permute-start(bf16[576,512]{1,0:T(8,128)(2,1)S(1)} %get-tuple-element.303), channel_id=1, source_target_pairs={{0,4},{4,0},{8,12},{12,8},{16,20},{20,16},{24,28},{28,24},{1,5},{5... | collective-permute-start | bytes 1769480 | tf_op jit(solution)/shard_map/ppermute | solution.py:839
  149.2 18.7 %collective-permute-start.48 = (bf16[1536,512]{1,0:T(8,128)(2,1)S(1)}, bf16[1536,512]{1,0:T(8,128)(2,1)S(1)}, u32[]{:S(2)}, u32[]{:S(2)}) collective-permute-start(bf16[1536,512]{1,0:T(8,128)(2,1)S(1)} %get-tuple-element.333), channel_id=1, source_target_pairs={{0,1},{1,0},{2,3},{3,2},{4,5},{5,4},{6,7},{7,6},{8,9},{9,8},{10,11... | collective-permute-start | bytes 4718600 | tf_op jit(solution)/shard_map/ppermute | solution.py:780
  149.4 20.1 %collective-permute-start.47 = (bf16[288,512]{1,0:T(8,128)(2,1)S(1)}, bf16[288,512]{1,0:T(8,128)(2,1)S(1)}, u32[]{:S(2)}, u32[]{:S(2)}) collective-permute-start(bf16[288,512]{1,0:T(8,128)(2,1)S(1)} %get-tuple-element.320), channel_id=1, source_target_pairs={{0,8},{4,12},{8,0},{12,4},{16,24},{20,28},{24,16},{28,20},{1,9},{5... | collective-permute-start | bytes 884744 | tf_op jit(solution)/shard_map/ppermute | solution.py:839
  154.0 12.6 %collective-permute-start.51 = (bf16[2,144,128]{2,1,0:T(8,128)(2,1)S(1)}, bf16[2,144,128]{2,1,0:T(8,128)(2,1)S(1)}, u32[]{:S(2)}, u32[]{:S(2)}) collective-permute-start(bf16[2,144,128]{2,1,0:T(8,128)(2,1)S(1)} %get-tuple-element.317), channel_id=1, source_target_pairs={{16,0},{18,2},{17,1},{19,3},{20,4},{22,6},{21,5},{23,7},{24,8},{26... | collective-permute-start | bytes 221192 | tf_op jit(solution)/shard_map/ppermute | solution.py:802
  155.3 11.3 %collective-permute-start.52 = (bf16[2,144,128]{2,1,0:T(8,128)(2,1)S(1)}, bf16[2,144,128]{2,1,0:T(8,128)(2,1)S(1)}, u32[]{:S(2)}, u32[]{:S(2)}) collective-permute-start(bf16[2,144,128]{2,1,0:T(8,128)(2,1)S(1)} %get-tuple-element.317), channel_id=1, source_target_pairs={{24,0},{26,2},{25,1},{27,3},{28,4},{30,6},{29,5},{31,7}} | collective-permute-start | bytes 221192 | tf_op jit(solution)/shard_map/ppermute | solution.py:802
  172.0 15.1 %collective-permute-start.58 = (bf16[448,512]{1,0:T(8,128)(2,1)S(1)}, bf16[448,512]{1,0:T(8,128)(2,1)S(1)}, u32[]{:S(2)}, u32[]{:S(2)}) collective-permute-start(bf16[448,512]{1,0:T(8,128)(2,1)S(1)} %get-tuple-element.350), channel_id=1, source_target_pairs={{0,4},{4,0},{8,12},{12,8},{16,20},{20,16},{24,28},{28,24},{1,5},{5... | collective-permute-start | bytes 1376264 | tf_op jit(solution)/shard_map/ppermute | solution.py:839
  173.4 14.7 %collective-permute-start.57 = (bf16[320,512]{1,0:T(8,128)(2,1)S(1)}, bf16[320,512]{1,0:T(8,128)(2,1)S(1)}, u32[]{:S(2)}, u32[]{:S(2)}) collective-permute-start(bf16[320,512]{1,0:T(8,128)(2,1)S(1)} %get-tuple-element.352), channel_id=1, source_target_pairs={{0,8},{4,12},{8,0},{12,4},{16,24},{20,28},{24,16},{28,20},{1,9},{5... | collective-permute-start | bytes 983048 | tf_op jit(solution)/shard_map/ppermute | solution.py:839
  182.7 12.4 %collective-permute-start.56 = (bf16[256,512]{1,0:T(8,128)(2,1)S(1)}, bf16[256,512]{1,0:T(8,128)(2,1)S(1)}, u32[]{:S(2)}, u32[]{:S(2)}) collective-permute-start(bf16[256,512]{1,0:T(8,128)(2,1)S(1)} %get-tuple-element.373), channel_id=1, source_target_pairs={{0,8},{4,12},{8,0},{12,4},{16,24},{20,28},{24,16},{28,20},{1,9},{5... | collective-permute-start | bytes 786440 | tf_op jit(solution)/shard_map/ppermute | solution.py:839
  183.6 12.0 %collective-permute-start.63 = (bf16[144,512]{1,0:T(8,128)(2,1)S(1)}, bf16[144,512]{1,0:T(8,128)(2,1)S(1)}, u32[]{:S(2)}, u32[]{:S(2)}) collective-permute-start(bf16[144,512]{1,0:T(8,128)(2,1)S(1)} %shard_map.216.mine), channel_id=1, source_target_pairs={{0,16},{4,20},{8,24},{12,28},{16,0},{20,4},{24,8},{28,12},{1,17},{... | collective-permute-start | bytes 442376 | tf_op jit(solution)/shard_map/ppermute | solution.py:839
  187.8 18.9 %collective-permute-start.62 = (bf16[224,512]{1,0:T(8,128)(2,1)S(1)}, bf16[224,512]{1,0:T(8,128)(2,1)S(1)}, u32[]{:S(2)}, u32[]{:S(2)}) collective-permute-start(bf16[224,512]{1,0:T(8,128)(2,1)S(1)} %get-tuple-element.379), channel_id=1, source_target_pairs={{0,8},{4,12},{8,0},{12,4},{16,24},{20,28},{24,16},{28,20},{1,9},{5... | collective-permute-start | bytes 688136 | tf_op jit(solution)/shard_map/ppermute | solution.py:839
  196.2 20.5 %collective-permute-start.70 = (bf16[288,512]{1,0:T(8,128)(2,1)S(1)}, bf16[288,512]{1,0:T(8,128)(2,1)S(1)}, u32[]{:S(2)}, u32[]{:S(2)}) collective-permute-start(bf16[288,512]{1,0:T(8,128)(2,1)S(1)} %shard_map.220.mine), channel_id=1, source_target_pairs={{0,8},{4,12},{8,0},{12,4},{16,24},{20,28},{24,16},{28,20},{1,9},{5... | collective-permute-start | bytes 884744 | tf_op jit(solution)/shard_map/ppermute | solution.py:839
  196.7 11.0 %collective-permute-start.61 = (bf16[160,512]{1,0:T(8,128)(2,1)S(1)}, bf16[160,512]{1,0:T(8,128)(2,1)S(1)}, u32[]{:S(2)}, u32[]{:S(2)}) collective-permute-start(bf16[160,512]{1,0:T(8,128)(2,1)S(1)} %get-tuple-element.381), channel_id=1, source_target_pairs={{0,16},{4,20},{8,24},{12,28},{16,0},{20,4},{24,8},{28,12},{1,17},{... | collective-permute-start | bytes 491528 | tf_op jit(solution)/shard_map/ppermute | solution.py:839
  198.9 16.3 %collective-permute-start.60 = (bf16[128,512]{1,0:T(8,128)(2,1)S(1)}, bf16[128,512]{1,0:T(8,128)(2,1)S(1)}, u32[]{:S(2)}, u32[]{:S(2)}) collective-permute-start(bf16[128,512]{1,0:T(8,128)(2,1)S(1)} %get-tuple-element.384), channel_id=1, source_target_pairs={{0,16},{4,20},{8,24},{12,28},{16,0},{20,4},{24,8},{28,12},{1,17},{... | collective-permute-start | bytes 393224 | tf_op jit(solution)/shard_map/ppermute | solution.py:839
  223.5 20.9 %collective-permute-start.78 = (bf16[576,512]{1,0:T(8,128)(2,1)S(1)}, bf16[576,512]{1,0:T(8,128)(2,1)S(1)}, u32[]{:S(2)}, u32[]{:S(2)}) collective-permute-start(bf16[576,512]{1,0:T(8,128)(2,1)S(1)} %shard_map.225.refs_0_), channel_id=1, source_target_pairs={{0,4},{4,0},{8,12},{12,8},{16,20},{20,16},{24,28},{28,24},{1,5},{5... | collective-permute-start | bytes 1769480 | tf_op jit(solution)/shard_map/ppermute | solution.py:839
  225.8 14.5 %collective-permute-start.75 = (bf16[160,512]{1,0:T(8,128)(2,1)S(1)}, bf16[160,512]{1,0:T(8,128)(2,1)S(1)}, u32[]{:S(2)}, u32[]{:S(2)}) collective-permute-start(bf16[160,512]{1,0:T(8,128)(2,1)S(1)} %shard_map.230.mine), channel_id=1, source_target_pairs={{0,16},{4,20},{8,24},{12,28},{16,0},{20,4},{24,8},{28,12},{1,17},{... | collective-permute-start | bytes 491528 | tf_op jit(solution)/shard_map/ppermute | solution.py:839
  228.9 13.0 %collective-permute-start.74 = (bf16[128,512]{1,0:T(8,128)(2,1)S(1)}, bf16[128,512]{1,0:T(8,128)(2,1)S(1)}, u32[]{:S(2)}, u32[]{:S(2)}) collective-permute-start(bf16[128,512]{1,0:T(8,128)(2,1)S(1)} %shard_map.231.mine), channel_id=1, source_target_pairs={{0,16},{4,20},{8,24},{12,28},{16,0},{20,4},{24,8},{28,12},{1,17},{... | collective-permute-start | bytes 393224 | tf_op jit(solution)/shard_map/ppermute | solution.py:839
  230.7 13.0 %collective-permute-start.65 = (bf16[256,128]{1,0:T(8,128)(2,1)S(1)}, bf16[256,128]{1,0:T(8,128)(2,1)S(1)}, u32[]{:S(2)}, u32[]{:S(2)}) collective-permute-start(bf16[256,128]{1,0:T(8,128)(2,1)S(1)} %get-tuple-element.396), channel_id=1, source_target_pairs={{0,1},{1,0},{2,3},{3,2},{4,5},{5,4},{6,7},{7,6},{8,9},{9,8},{10,11... | collective-permute-start | bytes 196616 | tf_op jit(solution)/shard_map/ppermute | solution.py:780
  235.6 14.9 %collective-permute-start.79 = (bf16[448,512]{1,0:T(8,128)(2,1)S(1)}, bf16[448,512]{1,0:T(8,128)(2,1)S(1)}, u32[]{:S(2)}, u32[]{:S(2)}) collective-permute-start(bf16[448,512]{1,0:T(8,128)(2,1)S(1)} %shard_map.232.refs_2_), channel_id=1, source_target_pairs={{0,4},{4,0},{8,12},{12,8},{16,20},{20,16},{24,28},{28,24},{1,5},{5... | collective-permute-start | bytes 1376264 | tf_op jit(solution)/shard_map/ppermute | solution.py:839
  242.4 11.0 %collective-permute-start.77 = (bf16[256,512]{1,0:T(8,128)(2,1)S(1)}, bf16[256,512]{1,0:T(8,128)(2,1)S(1)}, u32[]{:S(2)}, u32[]{:S(2)}) collective-permute-start(bf16[256,512]{1,0:T(8,128)(2,1)S(1)} %shard_map.234.mine), channel_id=1, source_target_pairs={{0,8},{4,12},{8,0},{12,4},{16,24},{20,28},{24,16},{28,20},{1,9},{5... | collective-permute-start | bytes 786440 | tf_op jit(solution)/shard_map/ppermute | solution.py:839
  (60 other events, 364.5 us)

commit v7 on v6

--- a/solution.py
+++ b/solution.py
@@ -754,19 +754,21 @@
     blend_out[...] = jnp.where(lane == 0, first, second)
 
 
-def call(body, outs, operands, scalars=0, scratch=(), scalar_outs=0, bulk=(), bulk_outs=()):
+def call(body, outs, operands, scalars=0, scratch=(), scalar_outs=0, bulk=(), bulk_outs=(), flops=None):
     specs = [SM] * scalars + [VM] * (len(operands) - scalars)
     out_specs = [VM] * (len(outs) - scalar_outs) + [SM] * scalar_outs
     for index in bulk:
         specs[index] = pl.BlockSpec()
     for index in bulk_outs:
         out_specs[index] = pl.BlockSpec()
+    cost = flops and pl.CostEstimate(flops=flops, bytes_accessed=0, transcendentals=0)
     return pl.pallas_call(
         body,
         out_shape=tuple(jax.ShapeDtypeStruct(shape, kind) for shape, kind in outs),
         in_specs=specs,
         out_specs=tuple(out_specs),
         scratch_shapes=scratch,
+        cost_estimate=cost,
         compiler_params=pltpu.CompilerParams(vmem_limit_bytes=24 * 2**20),
     )(*operands)
 
@@ -889,8 +891,6 @@
         ]
         for w in (w_qkv, w_out, w_up, w_down)
     ]
-    grad_mine, grad_theirs = call(pack_grad_kernel, (shard_like, shard_like), (place, after(grad_out, theirs)), 1)
-    grad_pieces = (grad_mine, half_swap(grad_theirs), part_swap(grad_mine), both_swap(grad_theirs))
 
     _, flag_count = flag_places(chunks)
     causal, causal_t, band, carried, tail, edge, flags = call(
@@ -929,9 +929,11 @@
                 1,
             )
         halo = chunk_move(halo, lambda c: c + 1)
-        one, two, sums = call(far_kernel, (heads_like,) * 3, (qkv, causal))
+        one, two, sums = call(far_kernel, (heads_like,) * 3, (qkv, causal), flops=10**9)
         (found, parts_got, at), arrived, _ = scan(state, flags, chunks, False, lambda: (one,))
         if layer == 0:
+            grad_mine, grad_theirs = call(pack_grad_kernel, (shard_like, shard_like), (place, after(grad_out, normed)), 1)
+            grad_pieces = (grad_mine, half_swap(grad_theirs), part_swap(grad_mine), both_swap(grad_theirs))
             found = after(found, *grad_pieces)
         (near,) = call(near_kernel, (heads_like,), (place, qkv, halo, band), 1)
         mixed, far_one, far_two, root, prefix, state, piece = call(

time: 257 us -> 255 us (level)
  waiting for transfers between devices: 99 us -> 89.3 us
  starting transfers between devices: 82.7 us -> 90.6 us
    ppermute x10, waiting for transfers between devices: 42 us -> 35.1 us  [part_swap(): return lax.ppermute(value, 'mlp', [(i, i ^ 2) for i in range(count)])]
    ppermute x10, starting transfers between devices: 8.59 us -> 13.3 us  [part_swap(): return lax.ppermute(value, 'mlp', [(i, i ^ 2) for i in range(count)])]
    ppermute x28, waiting for transfers between devices: 18.8 us -> 14.6 us  [chunk_move(): return lax.ppermute(value, AXES, pairs)]
  transfers between devices with their start and end apart: 81 -> 81, of which waited for: 27 -> 24; matrix products, arithmetic and copies ran while one was open for 1% -> 1% of each run, Pallas kernels for 21% -> 21%
where the time goes in v7:
time: 255 us; the launch traced here: 254 us
  starting transfers between devices  90.6 us (36%)
  waiting for transfers between devices  89.3 us (35%)
  Pallas kernels  65.9 us (26%)
  local copies, waits for them, and re-layouts  5.32 us (2%)
    pallas_call x58, Pallas kernels, call(): pl.pallas_call(body, out_shape=tuple((jax.ShapeDtypeStruct(shape, kind) f...  65.1 us
    ppermute x28, starting transfers between devices, chunk_move(): return lax.ppermute(value, AXES, pairs)  43.7 us
    ppermute x24, waiting for transfers between devices, shard_swap(): return lax.ppermute(value, 'seq', [(i, i ^ 1 << bit) for i in range(count)])  38.3 us
    ppermute x10, waiting for transfers between devices, part_swap(): return lax.ppermute(value, 'mlp', [(i, i ^ 2) for i in range(count)])  35.1 us
    ppermute x24, starting transfers between devices, shard_swap(): return lax.ppermute(value, 'seq', [(i, i ^ 1 << bit) for i in range(count)])  24.3 us
    ppermute x28, waiting for transfers between devices, chunk_move(): return lax.ppermute(value, AXES, pairs)  14.6 us
    ppermute x10, starting transfers between devices, part_swap(): return lax.ppermute(value, 'mlp', [(i, i ^ 2) for i in range(count)])  13.3 us
  transfers between devices with their start and end apart: 81, of which 24 were waited for; matrix products, arithmetic and copies ran while one was open for 1% of the time, Pallas kernels for 21%

profile of v7, /device:TPU:0, one launch (start us, length us, event | category | flops | bytes accessed | tf_op | source)
XLA Modules:
  0.0 254.2 jit_solution(4587714914233270457)
XLA Ops:
  4.4 2.6 %collective-permute-start.2 = (bf16[304,128]{1,0:T(8,128)(2,1)S(1)}, bf16[304,128]{1,0:T(8,128)(2,1)S(1)}, u32[]{:S(2)}, u32[]{:S(2)}) collective-permute-start(bf16[304,128]{1,0:T(8,128)(2,1)S(1)} %get-tuple-element.215), channel_id=1, source_target_pairs={{0,3},{1,2},{2,1},{3,0},{4,7},{5,6},{6,5},{7,4},{8,11},{9,10},{10,... | collective-permute-start | bytes 233480 | tf_op jit(solution)/shard_map/ppermute | solution.py:792
  25.2 5.2 %collective-permute-start.13 = (bf16[2,144,128]{2,1,0:T(8,128)(2,1)S(1)}, bf16[2,144,128]{2,1,0:T(8,128)(2,1)S(1)}, u32[]{:S(2)}, u32[]{:S(2)}) collective-permute-start(bf16[2,144,128]{2,1,0:T(8,128)(2,1)S(1)} %get-tuple-element.238), channel_id=1, source_target_pairs={{0,8},{2,10},{1,9},{3,11},{4,12},{6,14},{5,13},{7,15},{8,16},{10,1... | collective-permute-start | bytes 221192 | tf_op jit(solution)/shard_map/ppermute | solution.py:804
  30.4 4.5 %collective-permute-start.14 = (bf16[2,144,128]{2,1,0:T(8,128)(2,1)S(1)}, bf16[2,144,128]{2,1,0:T(8,128)(2,1)S(1)}, u32[]{:S(2)}, u32[]{:S(2)}) collective-permute-start(bf16[2,144,128]{2,1,0:T(8,128)(2,1)S(1)} %get-tuple-element.238), channel_id=1, source_target_pairs={{0,16},{2,18},{1,17},{3,19},{4,20},{6,22},{5,21},{7,23},{8,24},{10... | collective-permute-start | bytes 221192 | tf_op jit(solution)/shard_map/ppermute | solution.py:804
  36.2 2.7 %shard_map.181.near = f32[256,256]{1,0:T(8,128)S(1)} custom-call(s32[3]{0:T(128)S(1)} %pad_add_fusion.place.refs_0_, bf16[3,256,256]{2,1,0:T(8,128)(2,1)S(1)} %get-tuple-element.221.qkv, bf16[5,32,128]{2,1,0:T(8,128)(2,1)S(1)} %collective-permute-done.4.halo, f32[256,128]{1,0:T(8,128)S(1)} %get-tuple-element.223.band), custom_call_target="tpu_custom_call" | custom-call | tf_op jit(solution)/shard_map/pallas_call | solution.py:765
  41.7 6.3 %collective-permute-done.16.part_b = bf16[256,512]{1,0:T(8,128)(2,1)S(1)} collective-permute-done((bf16[256,512]{1,0:T(8,128)(2,1)S(1)}, bf16[256,512]{1,0:T(8,128)(2,1)S(1)}, u32[]{:S(2)}, u32[]{:S(2)}) %collective-permute-start.16) | collective-permute-done | bytes 262176 | tf_op jit(solution)/shard_map/ppermute | solution.py:787
  51.1 4.9 %collective-permute-done.19.refs_2_ = bf16[256,512]{1,0:T(8,128)(2,1)S(1)} collective-permute-done((bf16[256,512]{1,0:T(8,128)(2,1)S(1)}, bf16[256,512]{1,0:T(8,128)(2,1)S(1)}, u32[]{:S(2)}, u32[]{:S(2)}) %collective-permute-start.19) | collective-permute-done | bytes 262176 | tf_op jit(solution)/shard_map/ppermute | solution.py:787
  59.6 3.0 %collective-permute-done.24.refs_2_ = bf16[2,144,128]{2,1,0:T(8,128)(2,1)S(1)} collective-permute-done((bf16[2,144,128]{2,1,0:T(8,128)(2,1)S(1)}, bf16[2,144,128]{2,1,0:T(8,128)(2,1)S(1)}, u32[]{:S(2)}, u32[]{:S(2)}) %collective-permute-start.24) | collective-permute-done | bytes 73760 | tf_op jit(solution)/shard_map/ppermute | solution.py:804
  67.4 6.2 %collective-permute-start.27 = (bf16[2,144,128]{2,1,0:T(8,128)(2,1)S(1)}, bf16[2,144,128]{2,1,0:T(8,128)(2,1)S(1)}, u32[]{:S(2)}, u32[]{:S(2)}) collective-permute-start(bf16[2,144,128]{2,1,0:T(8,128)(2,1)S(1)} %get-tuple-element.256), channel_id=1, source_target_pairs={{0,16},{2,18},{1,17},{3,19},{4,20},{6,22},{5,21},{7,23},{8,24},{10... | collective-permute-start | bytes 221192 | tf_op jit(solution)/shard_map/ppermute | solution.py:804
  75.1 2.7 %shard_map.189.near = f32[256,256]{1,0:T(8,128)S(1)} custom-call(s32[3]{0:T(128)S(1)} %pad_add_fusion.place.refs_0_, bf16[3,256,256]{2,1,0:T(8,128)(2,1)S(1)} %get-tuple-element.247.qkv, bf16[5,32,128]{2,1,0:T(8,128)(2,1)S(1)} %collective-permute-done.21.halo, f32[256,128]{1,0:T(8,128)S(1)} %get-tuple-element.223.band), custom_call_target="tpu_custom_call" | custom-call | tf_op jit(solution)/shard_map/pallas_call | solution.py:765
  80.5 6.3 %collective-permute-done.29.part_b = bf16[256,512]{1,0:T(8,128)(2,1)S(1)} collective-permute-done((bf16[256,512]{1,0:T(8,128)(2,1)S(1)}, bf16[256,512]{1,0:T(8,128)(2,1)S(1)}, u32[]{:S(2)}, u32[]{:S(2)}) %collective-permute-start.29) | collective-permute-done | bytes 262176 | tf_op jit(solution)/shard_map/ppermute | solution.py:787
  91.2 5.4 %collective-permute-done.32.part_b = bf16[256,512]{1,0:T(8,128)(2,1)S(1)} collective-permute-done((bf16[256,512]{1,0:T(8,128)(2,1)S(1)}, bf16[256,512]{1,0:T(8,128)(2,1)S(1)}, u32[]{:S(2)}, u32[]{:S(2)}) %collective-permute-start.32) | collective-permute-done | bytes 262176 | tf_op jit(solution)/shard_map/ppermute | solution.py:787
  98.1 2.7 %collective-permute-start.34 = (bf16[2,144,128]{2,1,0:T(8,128)(2,1)S(1)}, bf16[2,144,128]{2,1,0:T(8,128)(2,1)S(1)}, u32[]{:S(2)}, u32[]{:S(2)}) collective-permute-start(bf16[2,144,128]{2,1,0:T(8,128)(2,1)S(1)} %get-tuple-element.273.refs_0_), channel_id=1, source_target_pairs={{0,4},{2,6},{1,5},{3,7},{4,0},{6,2},{5,1},{7,3},{8,12},{10,14},{9,... | collective-permute-start | bytes 221192 | tf_op jit(solution)/shard_map/ppermute | solution.py:804
  100.8 4.2 %shard_map.196 = (f32[256,256]{1,0:T(8,128)S(1)}, f32[256,256]{1,0:T(8,128)S(1)}, f32[256,256]{1,0:T(8,128)S(1)}, bf16[2,2,32,128]{3,2,1,0:T(8,128)(2,1)S(1)}, f32[1,256]{1,0:T(1,128)S(1)}) custom-call(s32[3]{0:T(128)S(1)} %pad_add_fusion.place.refs_0_, bf16[3,256,256]{2,1,0:T(8,128)(2,1)S(1)} %get-tuple-element.247.qkv, ...), custom_call_target="tpu_custom_call" | custom-call | tf_op jit(solution)/shard_map/pallas_call | solution.py:765
  112.6 2.7 %shard_map.199 = (bf16[256,256]{1,0:T(8,128)(2,1)S(1)}, f32[256,256]{1,0:T(8,128)S(1)}, f32[256,256]{1,0:T(8,128)S(1)}, f32[256,256]{1,0:T(8,128)S(1)}) custom-call(s32[3]{0:T(128)S(1)} %pad_add_fusion.place.refs_0_, bf16[3,256,256]{2,1,0:T(8,128)(2,1)S(1)} %get-tuple-element.247.qkv, bf16[256,256]{1,0:T(8,128)(2,1)S(1)} %get-tuple-element.224.causal, ...), custom_call_target="tpu_custom_call" | custom-call | tf_op jit(solution)/shard_map/pallas_call | solution.py:765
  115.8 3.6 %collective-permute-done.40.refs_2_ = bf16[2,144,128]{2,1,0:T(8,128)(2,1)S(1)} collective-permute-done((bf16[2,144,128]{2,1,0:T(8,128)(2,1)S(1)}, bf16[2,144,128]{2,1,0:T(8,128)(2,1)S(1)}, u32[]{:S(2)}, u32[]{:S(2)}) %collective-permute-start.40) | collective-permute-done | bytes 73760 | tf_op jit(solution)/shard_map/ppermute | solution.py:804
  125.1 3.4 %collective-permute-done.42.refs_2_ = bf16[256,512]{1,0:T(8,128)(2,1)S(1)} collective-permute-done((bf16[256,512]{1,0:T(8,128)(2,1)S(1)}, bf16[256,512]{1,0:T(8,128)(2,1)S(1)}, u32[]{:S(2)}, u32[]{:S(2)}) %collective-permute-start.42) | collective-permute-done | bytes 262176 | tf_op jit(solution)/shard_map/ppermute | solution.py:787
  131.5 5.3 %collective-permute-done.43.part_b = bf16[256,512]{1,0:T(8,128)(2,1)S(1)} collective-permute-done((bf16[256,512]{1,0:T(8,128)(2,1)S(1)}, bf16[256,512]{1,0:T(8,128)(2,1)S(1)}, u32[]{:S(2)}, u32[]{:S(2)}) %collective-permute-start.43) | collective-permute-done | bytes 262176 | tf_op jit(solution)/shard_map/ppermute | solution.py:787
  140.4 4.2 %shard_map.204 = (f32[256,256]{1,0:T(8,128)S(1)}, f32[256,256]{1,0:T(8,128)S(1)}, f32[256,256]{1,0:T(8,128)S(1)}, bf16[2,2,32,128]{3,2,1,0:T(8,128)(2,1)S(1)}, f32[1,256]{1,0:T(1,128)S(1)}) custom-call(s32[3]{0:T(128)S(1)} %pad_add_fusion.place.refs_0_, bf16[3,256,256]{2,1,0:T(8,128)(2,1)S(1)} %get-tuple-element.221.qkv, ...), custom_call_target="tpu_custom_call" | custom-call | tf_op jit(solution)/shard_map/pallas_call | solution.py:765
  155.2 2.7 %shard_map.208 = (bf16[256,256]{1,0:T(8,128)(2,1)S(1)}, f32[256,256]{1,0:T(8,128)S(1)}, f32[256,256]{1,0:T(8,128)S(1)}, f32[256,256]{1,0:T(8,128)S(1)}) custom-call(s32[3]{0:T(128)S(1)} %pad_add_fusion.place.refs_0_, bf16[3,256,256]{2,1,0:T(8,128)(2,1)S(1)} %get-tuple-element.221.qkv, bf16[256,256]{1,0:T(8,128)(2,1)S(1)} %get-tuple-element.224.causal, ...), custom_call_target="tpu_custom_call" | custom-call | tf_op jit(solution)/shard_map/pallas_call | solution.py:765
  159.2 5.7 %collective-permute-done.51.refs_1_ = bf16[2,144,128]{2,1,0:T(8,128)(2,1)S(1)} collective-permute-done((bf16[2,144,128]{2,1,0:T(8,128)(2,1)S(1)}, bf16[2,144,128]{2,1,0:T(8,128)(2,1)S(1)}, u32[]{:S(2)}, u32[]{:S(2)}) %collective-permute-start.51) | collective-permute-done | bytes 73760 | tf_op jit(solution)/shard_map/ppermute | solution.py:804
  174.6 3.6 %collective-permute-done.54.part_b = bf16[256,512]{1,0:T(8,128)(2,1)S(1)} collective-permute-done((bf16[256,512]{1,0:T(8,128)(2,1)S(1)}, bf16[256,512]{1,0:T(8,128)(2,1)S(1)}, u32[]{:S(2)}, u32[]{:S(2)}) %collective-permute-start.54) | collective-permute-done | bytes 262176 | tf_op jit(solution)/shard_map/ppermute | solution.py:787
  181.1 2.4 collective-permute-done.59.second
  183.5 3.4 %collective-permute-start.63 = (bf16[144,512]{1,0:T(8,128)(2,1)S(1)}, bf16[144,512]{1,0:T(8,128)(2,1)S(1)}, u32[]{:S(2)}, u32[]{:S(2)}) collective-permute-start(bf16[144,512]{1,0:T(8,128)(2,1)S(1)} %shard_map.216.mine), channel_id=1, source_target_pairs={{0,16},{4,20},{8,24},{12,28},{16,0},{20,4},{24,8},{28,12},{1,17},{... | collective-permute-start | bytes 442376 | tf_op jit(solution)/shard_map/ppermute | solution.py:841
  188.4 6.1 %collective-permute-done.56.second = bf16[256,512]{1,0:T(8,128)(2,1)S(1)} collective-permute-done((bf16[256,512]{1,0:T(8,128)(2,1)S(1)}, bf16[256,512]{1,0:T(8,128)(2,1)S(1)}, u32[]{:S(2)}, u32[]{:S(2)}) %collective-permute-start.56) | collective-permute-done | bytes 262176 | tf_op jit(solution)/shard_map/ppermute | solution.py:841
  195.8 2.2 collective-permute-start.61
  198.7 7.7 %collective-permute-done.62.second = bf16[224,512]{1,0:T(8,128)(2,1)S(1)} collective-permute-done((bf16[224,512]{1,0:T(8,128)(2,1)S(1)}, bf16[224,512]{1,0:T(8,128)(2,1)S(1)}, u32[]{:S(2)}, u32[]{:S(2)}) %collective-permute-start.62) | collective-permute-done | bytes 229408 | tf_op jit(solution)/shard_map/ppermute | solution.py:841
  208.5 5.5 %collective-permute-done.60.second = bf16[128,512]{1,0:T(8,128)(2,1)S(1)} collective-permute-done((bf16[128,512]{1,0:T(8,128)(2,1)S(1)}, bf16[128,512]{1,0:T(8,128)(2,1)S(1)}, u32[]{:S(2)}, u32[]{:S(2)}) %collective-permute-start.60) | collective-permute-done | bytes 131104 | tf_op jit(solution)/shard_map/ppermute | solution.py:841
  224.7 2.3 collective-permute-start.75
  229.1 4.4 %collective-permute-done.76.got = bf16[224,512]{1,0:T(8,128)(2,1)S(1)} collective-permute-done((bf16[224,512]{1,0:T(8,128)(2,1)S(1)}, bf16[224,512]{1,0:T(8,128)(2,1)S(1)}, u32[]{:S(2)}, u32[]{:S(2)}) %collective-permute-start.76) | collective-permute-done | bytes 229408 | tf_op jit(solution)/shard_map/ppermute | solution.py:841
  235.9 2.7 %collective-permute-done.75.got = bf16[160,512]{1,0:T(8,128)(2,1)S(1)} collective-permute-done((bf16[160,512]{1,0:T(8,128)(2,1)S(1)}, bf16[160,512]{1,0:T(8,128)(2,1)S(1)}, u32[]{:S(2)}, u32[]{:S(2)}) %collective-permute-start.75) | collective-permute-done | bytes 163872 | tf_op jit(solution)/shard_map/ppermute | solution.py:841
  242.6 6.1 %collective-permute-done.80.refs_5_ = bf16[320,512]{1,0:T(8,128)(2,1)S(1)} collective-permute-done((bf16[320,512]{1,0:T(8,128)(2,1)S(1)}, bf16[320,512]{1,0:T(8,128)(2,1)S(1)}, u32[]{:S(2)}, u32[]{:S(2)}) %collective-permute-start.80) | collective-permute-done | bytes 327712 | tf_op jit(solution)/shard_map/ppermute | solution.py:841
  248.7 2.9 %shard_map.235 = (f32[2,512,512]{2,1,0:T(8,128)}, f32[2,512,512]{2,1,0:T(8,128)}, f32[2,128,512]{2,1,0:T(8,128)}, bf16[384,512]{1,0:T(8,128)(2,1)S(1)}) custom-call(s32[3]{0:T(128)S(1)} %pad_add_fusion.place.refs_0_, bf16[576,512]{1,0:T(8,128)(2,1)S(1)} %shard_map.225.refs_0_, bf16[576,512]{1,0:T(8,128)(2,1)S(1)} %collective-permute-done.78.refs_1_, ...), custom_call_target="tpu_custom_call" | custom-call | tf_op jit(solution)/shard_map/pallas_call | solution.py:765
  (225 shorter events, 119.0 us)
Async XLA Ops:
  18.4 23.3 %collective-permute-start.17 = (bf16[512,512]{1,0:T(8,128)(2,1)S(1)}, bf16[512,512]{1,0:T(8,128)(2,1)S(1)}, u32[]{:S(2)}, u32[]{:S(2)}) collective-permute-start(bf16[512,512]{1,0:T(8,128)(2,1)S(1)} %get-tuple-element.241), channel_id=1, source_target_pairs={{0,1},{1,0},{2,3},{3,2},{4,5},{5,4},{6,7},{7,6},{8,9},{9,8},{10,11... | collective-permute-start | bytes 1572872 | tf_op jit(solution)/shard_map/ppermute | solution.py:782
  19.8 21.9 %collective-permute-start.18 = (bf16[512,512]{1,0:T(8,128)(2,1)S(1)}, bf16[512,512]{1,0:T(8,128)(2,1)S(1)}, u32[]{:S(2)}, u32[]{:S(2)}) collective-permute-start(bf16[512,512]{1,0:T(8,128)(2,1)S(1)} %get-tuple-element.242), channel_id=1, source_target_pairs={{0,1},{1,0},{2,3},{3,2},{4,5},{5,4},{6,7},{7,6},{8,9},{9,8},{10,11... | collective-permute-start | bytes 1572872 | tf_op jit(solution)/shard_map/ppermute | solution.py:782
  21.4 13.5 %collective-permute-start.12 = (bf16[256,128]{1,0:T(8,128)(2,1)S(1)}, bf16[256,128]{1,0:T(8,128)(2,1)S(1)}, u32[]{:S(2)}, u32[]{:S(2)}) collective-permute-start(bf16[256,128]{1,0:T(8,128)(2,1)S(1)} %get-tuple-element.236), channel_id=1, source_target_pairs={{0,3},{1,2},{2,1},{3,0},{4,7},{5,6},{6,5},{7,4},{8,11},{9,10},{10,... | collective-permute-start | bytes 196616 | tf_op jit(solution)/shard_map/ppermute | solution.py:792
  25.2 13.8 %collective-permute-start.13 = (bf16[2,144,128]{2,1,0:T(8,128)(2,1)S(1)}, bf16[2,144,128]{2,1,0:T(8,128)(2,1)S(1)}, u32[]{:S(2)}, u32[]{:S(2)}) collective-permute-start(bf16[2,144,128]{2,1,0:T(8,128)(2,1)S(1)} %get-tuple-element.238), channel_id=1, source_target_pairs={{0,8},{2,10},{1,9},{3,11},{4,12},{6,14},{5,13},{7,15},{8,16},{10,1... | collective-permute-start | bytes 221192 | tf_op jit(solution)/shard_map/ppermute | solution.py:804
  50.6 29.9 %collective-permute-start.30 = (bf16[512,512]{1,0:T(8,128)(2,1)S(1)}, bf16[512,512]{1,0:T(8,128)(2,1)S(1)}, u32[]{:S(2)}, u32[]{:S(2)}) collective-permute-start(bf16[512,512]{1,0:T(8,128)(2,1)S(1)} %get-tuple-element.258), channel_id=1, source_target_pairs={{0,1},{1,0},{2,3},{3,2},{4,5},{5,4},{6,7},{7,6},{8,9},{9,8},{10,11... | collective-permute-start | bytes 1572872 | tf_op jit(solution)/shard_map/ppermute | solution.py:782
  50.6 29.9 %collective-permute-start.31 = (bf16[512,512]{1,0:T(8,128)(2,1)S(1)}, bf16[512,512]{1,0:T(8,128)(2,1)S(1)}, u32[]{:S(2)}, u32[]{:S(2)}) collective-permute-start(bf16[512,512]{1,0:T(8,128)(2,1)S(1)} %get-tuple-element.259), channel_id=1, source_target_pairs={{0,1},{1,0},{2,3},{3,2},{4,5},{5,4},{6,7},{7,6},{8,9},{9,8},{10,11... | collective-permute-start | bytes 1572872 | tf_op jit(solution)/shard_map/ppermute | solution.py:782
  62.6 11.0 %collective-permute-start.21 = (bf16[5,32,128]{2,1,0:T(8,128)(2,1)S(1)}, bf16[5,32,128]{2,1,0:T(8,128)(2,1)S(1)}, u32[]{:S(2)}, u32[]{:S(2)}) collective-permute-start(bf16[5,32,128]{2,1,0:T(8,128)(2,1)S(1)} %get-tuple-element.248), channel_id=1, source_target_pairs={{0,1},{2,3},{1,4},{3,6},{4,5},{6,7},{5,8},{7,10},{8,9},{10,11},{9,... | collective-permute-start | bytes 122888 | tf_op jit(solution)/shard_map/ppermute | solution.py:804
  65.5 12.3 %collective-permute-start.26 = (bf16[2,144,128]{2,1,0:T(8,128)(2,1)S(1)}, bf16[2,144,128]{2,1,0:T(8,128)(2,1)S(1)}, u32[]{:S(2)}, u32[]{:S(2)}) collective-permute-start(bf16[2,144,128]{2,1,0:T(8,128)(2,1)S(1)} %get-tuple-element.256), channel_id=1, source_target_pairs={{0,8},{2,10},{1,9},{3,11},{4,12},{6,14},{5,13},{7,15},{8,16},{10,1... | collective-permute-start | bytes 221192 | tf_op jit(solution)/shard_map/ppermute | solution.py:804
  67.4 10.4 %collective-permute-start.27 = (bf16[2,144,128]{2,1,0:T(8,128)(2,1)S(1)}, bf16[2,144,128]{2,1,0:T(8,128)(2,1)S(1)}, u32[]{:S(2)}, u32[]{:S(2)}) collective-permute-start(bf16[2,144,128]{2,1,0:T(8,128)(2,1)S(1)} %get-tuple-element.256), channel_id=1, source_target_pairs={{0,16},{2,18},{1,17},{3,19},{4,20},{6,22},{5,21},{7,23},{8,24},{10... | collective-permute-start | bytes 221192 | tf_op jit(solution)/shard_map/ppermute | solution.py:804
  107.0 15.3 %collective-permute-start.36 = (bf16[1152,512]{1,0:T(8,128)(2,1)S(1)}, bf16[1152,512]{1,0:T(8,128)(2,1)S(1)}, u32[]{:S(2)}, u32[]{:S(2)}) collective-permute-start(bf16[1152,512]{1,0:T(8,128)(2,1)S(1)} %get-tuple-element.284), channel_id=1, source_target_pairs={{0,1},{1,0},{2,3},{3,2},{4,5},{5,4},{6,7},{7,6},{8,9},{9,8},{10,11... | collective-permute-start | bytes 3538952 | tf_op jit(solution)/shard_map/ppermute | solution.py:782
  109.8 9.6 %collective-permute-start.40 = (bf16[2,144,128]{2,1,0:T(8,128)(2,1)S(1)}, bf16[2,144,128]{2,1,0:T(8,128)(2,1)S(1)}, u32[]{:S(2)}, u32[]{:S(2)}) collective-permute-start(bf16[2,144,128]{2,1,0:T(8,128)(2,1)S(1)} %get-tuple-element.274), channel_id=1, source_target_pairs={{24,0},{26,2},{25,1},{27,3},{28,4},{30,6},{29,5},{31,7}} | collective-permute-start | bytes 221192 | tf_op jit(solution)/shard_map/ppermute | solution.py:804
  123.2 22.0 %collective-permute-start.41 = (bf16[576,512]{1,0:T(8,128)(2,1)S(1)}, bf16[576,512]{1,0:T(8,128)(2,1)S(1)}, u32[]{:S(2)}, u32[]{:S(2)}) collective-permute-start(bf16[576,512]{1,0:T(8,128)(2,1)S(1)} %get-tuple-element.303), channel_id=1, source_target_pairs={{0,4},{4,0},{8,12},{12,8},{16,20},{20,16},{24,28},{28,24},{1,5},{5... | collective-permute-start | bytes 1769480 | tf_op jit(solution)/shard_map/ppermute | solution.py:841
  147.5 18.7 %collective-permute-start.48 = (bf16[1536,512]{1,0:T(8,128)(2,1)S(1)}, bf16[1536,512]{1,0:T(8,128)(2,1)S(1)}, u32[]{:S(2)}, u32[]{:S(2)}) collective-permute-start(bf16[1536,512]{1,0:T(8,128)(2,1)S(1)} %get-tuple-element.333), channel_id=1, source_target_pairs={{0,1},{1,0},{2,3},{3,2},{4,5},{5,4},{6,7},{7,6},{8,9},{9,8},{10,11... | collective-permute-start | bytes 4718600 | tf_op jit(solution)/shard_map/ppermute | solution.py:782
  147.8 20.0 %collective-permute-start.47 = (bf16[288,512]{1,0:T(8,128)(2,1)S(1)}, bf16[288,512]{1,0:T(8,128)(2,1)S(1)}, u32[]{:S(2)}, u32[]{:S(2)}) collective-permute-start(bf16[288,512]{1,0:T(8,128)(2,1)S(1)} %get-tuple-element.320), channel_id=1, source_target_pairs={{0,8},{4,12},{8,0},{12,4},{16,24},{20,28},{24,16},{28,20},{1,9},{5... | collective-permute-start | bytes 884744 | tf_op jit(solution)/shard_map/ppermute | solution.py:841
  152.3 12.6 %collective-permute-start.51 = (bf16[2,144,128]{2,1,0:T(8,128)(2,1)S(1)}, bf16[2,144,128]{2,1,0:T(8,128)(2,1)S(1)}, u32[]{:S(2)}, u32[]{:S(2)}) collective-permute-start(bf16[2,144,128]{2,1,0:T(8,128)(2,1)S(1)} %get-tuple-element.317), channel_id=1, source_target_pairs={{16,0},{18,2},{17,1},{19,3},{20,4},{22,6},{21,5},{23,7},{24,8},{26... | collective-permute-start | bytes 221192 | tf_op jit(solution)/shard_map/ppermute | solution.py:804
  153.6 11.3 %collective-permute-start.52 = (bf16[2,144,128]{2,1,0:T(8,128)(2,1)S(1)}, bf16[2,144,128]{2,1,0:T(8,128)(2,1)S(1)}, u32[]{:S(2)}, u32[]{:S(2)}) collective-permute-start(bf16[2,144,128]{2,1,0:T(8,128)(2,1)S(1)} %get-tuple-element.317), channel_id=1, source_target_pairs={{24,0},{26,2},{25,1},{27,3},{28,4},{30,6},{29,5},{31,7}} | collective-permute-start | bytes 221192 | tf_op jit(solution)/shard_map/ppermute | solution.py:804
  169.4 9.8 %collective-permute-start.53 = (bf16[384,512]{1,0:T(8,128)(2,1)S(1)}, bf16[384,512]{1,0:T(8,128)(2,1)S(1)}, u32[]{:S(2)}, u32[]{:S(2)}) collective-permute-start(bf16[384,512]{1,0:T(8,128)(2,1)S(1)} %get-tuple-element.358), channel_id=1, source_target_pairs={{0,1},{1,0},{2,3},{3,2},{4,5},{5,4},{6,7},{7,6},{8,9},{9,8},{10,11... | collective-permute-start | bytes 1179656 | tf_op jit(solution)/shard_map/ppermute | solution.py:782
  171.0 15.9 %collective-permute-start.58 = (bf16[448,512]{1,0:T(8,128)(2,1)S(1)}, bf16[448,512]{1,0:T(8,128)(2,1)S(1)}, u32[]{:S(2)}, u32[]{:S(2)}) collective-permute-start(bf16[448,512]{1,0:T(8,128)(2,1)S(1)} %get-tuple-element.350), channel_id=1, source_target_pairs={{0,4},{4,0},{8,12},{12,8},{16,20},{20,16},{24,28},{28,24},{1,5},{5... | collective-permute-start | bytes 1376264 | tf_op jit(solution)/shard_map/ppermute | solution.py:841
  172.5 15.2 %collective-permute-start.57 = (bf16[320,512]{1,0:T(8,128)(2,1)S(1)}, bf16[320,512]{1,0:T(8,128)(2,1)S(1)}, u32[]{:S(2)}, u32[]{:S(2)}) collective-permute-start(bf16[320,512]{1,0:T(8,128)(2,1)S(1)} %get-tuple-element.352), channel_id=1, source_target_pairs={{0,8},{4,12},{8,0},{12,4},{16,24},{20,28},{24,16},{28,20},{1,9},{5... | collective-permute-start | bytes 983048 | tf_op jit(solution)/shard_map/ppermute | solution.py:841
  172.5 11.0 %collective-permute-start.59 = (bf16[144,512]{1,0:T(8,128)(2,1)S(1)}, bf16[144,512]{1,0:T(8,128)(2,1)S(1)}, u32[]{:S(2)}, u32[]{:S(2)}) collective-permute-start(bf16[144,512]{1,0:T(8,128)(2,1)S(1)} %get-tuple-element.354), channel_id=1, source_target_pairs={{0,16},{4,20},{8,24},{12,28},{16,0},{20,4},{24,8},{28,12},{1,17},{... | collective-permute-start | bytes 442376 | tf_op jit(solution)/shard_map/ppermute | solution.py:841
  181.0 13.5 %collective-permute-start.56 = (bf16[256,512]{1,0:T(8,128)(2,1)S(1)}, bf16[256,512]{1,0:T(8,128)(2,1)S(1)}, u32[]{:S(2)}, u32[]{:S(2)}) collective-permute-start(bf16[256,512]{1,0:T(8,128)(2,1)S(1)} %get-tuple-element.373), channel_id=1, source_target_pairs={{0,8},{4,12},{8,0},{12,4},{16,24},{20,28},{24,16},{28,20},{1,9},{5... | collective-permute-start | bytes 786440 | tf_op jit(solution)/shard_map/ppermute | solution.py:841
  183.5 11.6 %collective-permute-start.63 = (bf16[144,512]{1,0:T(8,128)(2,1)S(1)}, bf16[144,512]{1,0:T(8,128)(2,1)S(1)}, u32[]{:S(2)}, u32[]{:S(2)}) collective-permute-start(bf16[144,512]{1,0:T(8,128)(2,1)S(1)} %shard_map.216.mine), channel_id=1, source_target_pairs={{0,16},{4,20},{8,24},{12,28},{16,0},{20,4},{24,8},{28,12},{1,17},{... | collective-permute-start | bytes 442376 | tf_op jit(solution)/shard_map/ppermute | solution.py:841
  187.6 18.8 %collective-permute-start.62 = (bf16[224,512]{1,0:T(8,128)(2,1)S(1)}, bf16[224,512]{1,0:T(8,128)(2,1)S(1)}, u32[]{:S(2)}, u32[]{:S(2)}) collective-permute-start(bf16[224,512]{1,0:T(8,128)(2,1)S(1)} %get-tuple-element.379), channel_id=1, source_target_pairs={{0,8},{4,12},{8,0},{12,4},{16,24},{20,28},{24,16},{28,20},{1,9},{5... | collective-permute-start | bytes 688136 | tf_op jit(solution)/shard_map/ppermute | solution.py:841
  195.7 19.0 %collective-permute-start.70 = (bf16[288,512]{1,0:T(8,128)(2,1)S(1)}, bf16[288,512]{1,0:T(8,128)(2,1)S(1)}, u32[]{:S(2)}, u32[]{:S(2)}) collective-permute-start(bf16[288,512]{1,0:T(8,128)(2,1)S(1)} %shard_map.220.mine), channel_id=1, source_target_pairs={{0,8},{4,12},{8,0},{12,4},{16,24},{20,28},{24,16},{28,20},{1,9},{5... | collective-permute-start | bytes 884744 | tf_op jit(solution)/shard_map/ppermute | solution.py:841
  195.8 11.4 %collective-permute-start.61 = (bf16[160,512]{1,0:T(8,128)(2,1)S(1)}, bf16[160,512]{1,0:T(8,128)(2,1)S(1)}, u32[]{:S(2)}, u32[]{:S(2)}) collective-permute-start(bf16[160,512]{1,0:T(8,128)(2,1)S(1)} %get-tuple-element.381), channel_id=1, source_target_pairs={{0,16},{4,20},{8,24},{12,28},{16,0},{20,4},{24,8},{28,12},{1,17},{... | collective-permute-start | bytes 491528 | tf_op jit(solution)/shard_map/ppermute | solution.py:841
  198.0 16.0 %collective-permute-start.60 = (bf16[128,512]{1,0:T(8,128)(2,1)S(1)}, bf16[128,512]{1,0:T(8,128)(2,1)S(1)}, u32[]{:S(2)}, u32[]{:S(2)}) collective-permute-start(bf16[128,512]{1,0:T(8,128)(2,1)S(1)} %get-tuple-element.384), channel_id=1, source_target_pairs={{0,16},{4,20},{8,24},{12,28},{16,0},{20,4},{24,8},{28,12},{1,17},{... | collective-permute-start | bytes 393224 | tf_op jit(solution)/shard_map/ppermute | solution.py:841
  222.1 20.6 %collective-permute-start.78 = (bf16[576,512]{1,0:T(8,128)(2,1)S(1)}, bf16[576,512]{1,0:T(8,128)(2,1)S(1)}, u32[]{:S(2)}, u32[]{:S(2)}) collective-permute-start(bf16[576,512]{1,0:T(8,128)(2,1)S(1)} %shard_map.225.refs_0_), channel_id=1, source_target_pairs={{0,4},{4,0},{8,12},{12,8},{16,20},{20,16},{24,28},{28,24},{1,5},{5... | collective-permute-start | bytes 1769480 | tf_op jit(solution)/shard_map/ppermute | solution.py:841
  224.7 13.9 %collective-permute-start.75 = (bf16[160,512]{1,0:T(8,128)(2,1)S(1)}, bf16[160,512]{1,0:T(8,128)(2,1)S(1)}, u32[]{:S(2)}, u32[]{:S(2)}) collective-permute-start(bf16[160,512]{1,0:T(8,128)(2,1)S(1)} %shard_map.230.mine), channel_id=1, source_target_pairs={{0,16},{4,20},{8,24},{12,28},{16,0},{20,4},{24,8},{28,12},{1,17},{... | collective-permute-start | bytes 491528 | tf_op jit(solution)/shard_map/ppermute | solution.py:841
  227.6 12.4 %collective-permute-start.74 = (bf16[128,512]{1,0:T(8,128)(2,1)S(1)}, bf16[128,512]{1,0:T(8,128)(2,1)S(1)}, u32[]{:S(2)}, u32[]{:S(2)}) collective-permute-start(bf16[128,512]{1,0:T(8,128)(2,1)S(1)} %shard_map.231.mine), channel_id=1, source_target_pairs={{0,16},{4,20},{8,24},{12,28},{16,0},{20,4},{24,8},{28,12},{1,17},{... | collective-permute-start | bytes 393224 | tf_op jit(solution)/shard_map/ppermute | solution.py:841
  229.0 12.9 %collective-permute-start.65 = (bf16[256,128]{1,0:T(8,128)(2,1)S(1)}, bf16[256,128]{1,0:T(8,128)(2,1)S(1)}, u32[]{:S(2)}, u32[]{:S(2)}) collective-permute-start(bf16[256,128]{1,0:T(8,128)(2,1)S(1)} %get-tuple-element.396), channel_id=1, source_target_pairs={{0,1},{1,0},{2,3},{3,2},{4,5},{5,4},{6,7},{7,6},{8,9},{9,8},{10,11... | collective-permute-start | bytes 196616 | tf_op jit(solution)/shard_map/ppermute | solution.py:782
  234.1 14.6 %collective-permute-start.79 = (bf16[448,512]{1,0:T(8,128)(2,1)S(1)}, bf16[448,512]{1,0:T(8,128)(2,1)S(1)}, u32[]{:S(2)}, u32[]{:S(2)}) collective-permute-start(bf16[448,512]{1,0:T(8,128)(2,1)S(1)} %shard_map.232.refs_2_), channel_id=1, source_target_pairs={{0,4},{4,0},{8,12},{12,8},{16,20},{20,16},{24,28},{28,24},{1,5},{5... | collective-permute-start | bytes 1376264 | tf_op jit(solution)/shard_map/ppermute | solution.py:841
  240.6 11.0 %collective-permute-start.77 = (bf16[256,512]{1,0:T(8,128)(2,1)S(1)}, bf16[256,512]{1,0:T(8,128)(2,1)S(1)}, u32[]{:S(2)}, u32[]{:S(2)}) collective-permute-start(bf16[256,512]{1,0:T(8,128)(2,1)S(1)} %shard_map.234.mine), channel_id=1, source_target_pairs={{0,8},{4,12},{8,0},{12,4},{16,24},{20,28},{24,16},{28,20},{1,9},{5... | collective-permute-start | bytes 786440 | tf_op jit(solution)/shard_map/ppermute | solution.py:841
  (60 other events, 364.9 us)

commit v8 on v7

--- a/solution.py
+++ b/solution.py
@@ -958,7 +958,7 @@
     d_gain_attn, d_gain_ffn, d_blends = [None] * LAYERS, [None] * LAYERS, [None] * LAYERS
     d_qkvs = [None] * LAYERS
     bits = (shards - 1).bit_length()
-    side_first, line_first = (0, 1, 2), (1, 2, 0)
+    side_first, line_first, last_order = (0, 1, 2), (1, 2, 0), (1, 0, 2)
 
     def first_step(jobs, operands):
         height = sum(job_rows(job, units) for job in jobs)
@@ -1120,7 +1120,7 @@
         (place, after(base, far), *adds, saved[0][0], gains, *smalls),
         1,
     )
-    start_group((0,), jobs, line_first, (0, height + LANES), (own, small_own), (half_swap(far), half_swap(small_far)))
+    start_group((0,), jobs, last_order, (0, height + LANES), (own, small_own), (half_swap(far), half_swap(small_far)))
     made = step(3, mine)
     for turn in range(6):
         for index in range(4):

time: 255 us -> 254 us (level)
  waiting for transfers between devices: 89.3 us -> 81.9 us
  starting transfers between devices: 90.6 us -> 97.2 us
    ppermute x24, waiting for transfers between devices: 38.3 us -> 30.9 us  [shard_swap(): return lax.ppermute(value, 'seq', [(i, i ^ 1 << bit) for i in range(count)])]
    ppermute x24, starting transfers between devices: 24.3 us -> 30.9 us  [shard_swap(): return lax.ppermute(value, 'seq', [(i, i ^ 1 << bit) for i in range(count)])]
where the time goes in v8:
time: 254 us; the launch traced here: 253 us
  starting transfers between devices  97.2 us (38%)
  waiting for transfers between devices  81.9 us (32%)
  Pallas kernels  65.9 us (26%)
  local copies, waits for them, and re-layouts  5.32 us (2%)
    pallas_call x58, Pallas kernels, call(): pl.pallas_call(body, out_shape=tuple((jax.ShapeDtypeStruct(shape, kind) f...  65.1 us
    ppermute x28, starting transfers between devices, chunk_move(): return lax.ppermute(value, AXES, pairs)  43.7 us
    ppermute x10, waiting for transfers between devices, part_swap(): return lax.ppermute(value, 'mlp', [(i, i ^ 2) for i in range(count)])  35.1 us
    ppermute x24, waiting for transfers between devices, shard_swap(): return lax.ppermute(value, 'seq', [(i, i ^ 1 << bit) for i in range(count)])  30.9 us
    ppermute x24, starting transfers between devices, shard_swap(): return lax.ppermute(value, 'seq', [(i, i ^ 1 << bit) for i in range(count)])  30.9 us
    ppermute x28, waiting for transfers between devices, chunk_move(): return lax.ppermute(value, AXES, pairs)  14.6 us
    ppermute x10, starting transfers between devices, part_swap(): return lax.ppermute(value, 'mlp', [(i, i ^ 2) for i in range(count)])  13.5 us
  transfers between devices with their start and end apart: 81, of which 24 were waited for; matrix products, arithmetic and copies ran while one was open for 1% of the time, Pallas kernels for 21%

profile of v8, /device:TPU:0, one launch (start us, length us, event | category | flops | bytes accessed | tf_op | source)
XLA Modules:
  0.0 253.5 jit_solution(17933420317593370770)
XLA Ops:
  4.4 2.6 %collective-permute-start.2 = (bf16[304,128]{1,0:T(8,128)(2,1)S(1)}, bf16[304,128]{1,0:T(8,128)(2,1)S(1)}, u32[]{:S(2)}, u32[]{:S(2)}) collective-permute-start(bf16[304,128]{1,0:T(8,128)(2,1)S(1)} %get-tuple-element.215), channel_id=1, source_target_pairs={{0,3},{1,2},{2,1},{3,0},{4,7},{5,6},{6,5},{7,4},{8,11},{9,10},{10,... | collective-permute-start | bytes 233480 | tf_op jit(solution)/shard_map/ppermute | solution.py:792
  25.2 5.2 %collective-permute-start.13 = (bf16[2,144,128]{2,1,0:T(8,128)(2,1)S(1)}, bf16[2,144,128]{2,1,0:T(8,128)(2,1)S(1)}, u32[]{:S(2)}, u32[]{:S(2)}) collective-permute-start(bf16[2,144,128]{2,1,0:T(8,128)(2,1)S(1)} %get-tuple-element.238), channel_id=1, source_target_pairs={{0,8},{2,10},{1,9},{3,11},{4,12},{6,14},{5,13},{7,15},{8,16},{10,1... | collective-permute-start | bytes 221192 | tf_op jit(solution)/shard_map/ppermute | solution.py:804
  30.4 4.5 %collective-permute-start.14 = (bf16[2,144,128]{2,1,0:T(8,128)(2,1)S(1)}, bf16[2,144,128]{2,1,0:T(8,128)(2,1)S(1)}, u32[]{:S(2)}, u32[]{:S(2)}) collective-permute-start(bf16[2,144,128]{2,1,0:T(8,128)(2,1)S(1)} %get-tuple-element.238), channel_id=1, source_target_pairs={{0,16},{2,18},{1,17},{3,19},{4,20},{6,22},{5,21},{7,23},{8,24},{10... | collective-permute-start | bytes 221192 | tf_op jit(solution)/shard_map/ppermute | solution.py:804
  36.2 2.7 %shard_map.181.near = f32[256,256]{1,0:T(8,128)S(1)} custom-call(s32[3]{0:T(128)S(1)} %pad_add_fusion.place.refs_0_, bf16[3,256,256]{2,1,0:T(8,128)(2,1)S(1)} %get-tuple-element.221.qkv, bf16[5,32,128]{2,1,0:T(8,128)(2,1)S(1)} %collective-permute-done.4.halo, f32[256,128]{1,0:T(8,128)S(1)} %get-tuple-element.223.band), custom_call_target="tpu_custom_call" | custom-call | tf_op jit(solution)/shard_map/pallas_call | solution.py:765
  41.7 6.3 %collective-permute-done.16.part_b = bf16[256,512]{1,0:T(8,128)(2,1)S(1)} collective-permute-done((bf16[256,512]{1,0:T(8,128)(2,1)S(1)}, bf16[256,512]{1,0:T(8,128)(2,1)S(1)}, u32[]{:S(2)}, u32[]{:S(2)}) %collective-permute-start.16) | collective-permute-done | bytes 262176 | tf_op jit(solution)/shard_map/ppermute | solution.py:787
  51.1 4.9 %collective-permute-done.19.refs_2_ = bf16[256,512]{1,0:T(8,128)(2,1)S(1)} collective-permute-done((bf16[256,512]{1,0:T(8,128)(2,1)S(1)}, bf16[256,512]{1,0:T(8,128)(2,1)S(1)}, u32[]{:S(2)}, u32[]{:S(2)}) %collective-permute-start.19) | collective-permute-done | bytes 262176 | tf_op jit(solution)/shard_map/ppermute | solution.py:787
  59.6 3.0 %collective-permute-done.24.refs_2_ = bf16[2,144,128]{2,1,0:T(8,128)(2,1)S(1)} collective-permute-done((bf16[2,144,128]{2,1,0:T(8,128)(2,1)S(1)}, bf16[2,144,128]{2,1,0:T(8,128)(2,1)S(1)}, u32[]{:S(2)}, u32[]{:S(2)}) %collective-permute-start.24) | collective-permute-done | bytes 73760 | tf_op jit(solution)/shard_map/ppermute | solution.py:804
  67.4 6.2 %collective-permute-start.27 = (bf16[2,144,128]{2,1,0:T(8,128)(2,1)S(1)}, bf16[2,144,128]{2,1,0:T(8,128)(2,1)S(1)}, u32[]{:S(2)}, u32[]{:S(2)}) collective-permute-start(bf16[2,144,128]{2,1,0:T(8,128)(2,1)S(1)} %get-tuple-element.256), channel_id=1, source_target_pairs={{0,16},{2,18},{1,17},{3,19},{4,20},{6,22},{5,21},{7,23},{8,24},{10... | collective-permute-start | bytes 221192 | tf_op jit(solution)/shard_map/ppermute | solution.py:804
  75.1 2.7 %shard_map.189.near = f32[256,256]{1,0:T(8,128)S(1)} custom-call(s32[3]{0:T(128)S(1)} %pad_add_fusion.place.refs_0_, bf16[3,256,256]{2,1,0:T(8,128)(2,1)S(1)} %get-tuple-element.247.qkv, bf16[5,32,128]{2,1,0:T(8,128)(2,1)S(1)} %collective-permute-done.21.halo, f32[256,128]{1,0:T(8,128)S(1)} %get-tuple-element.223.band), custom_call_target="tpu_custom_call" | custom-call | tf_op jit(solution)/shard_map/pallas_call | solution.py:765
  80.5 6.3 %collective-permute-done.29.part_b = bf16[256,512]{1,0:T(8,128)(2,1)S(1)} collective-permute-done((bf16[256,512]{1,0:T(8,128)(2,1)S(1)}, bf16[256,512]{1,0:T(8,128)(2,1)S(1)}, u32[]{:S(2)}, u32[]{:S(2)}) %collective-permute-start.29) | collective-permute-done | bytes 262176 | tf_op jit(solution)/shard_map/ppermute | solution.py:787
  91.2 5.4 %collective-permute-done.32.part_b = bf16[256,512]{1,0:T(8,128)(2,1)S(1)} collective-permute-done((bf16[256,512]{1,0:T(8,128)(2,1)S(1)}, bf16[256,512]{1,0:T(8,128)(2,1)S(1)}, u32[]{:S(2)}, u32[]{:S(2)}) %collective-permute-start.32) | collective-permute-done | bytes 262176 | tf_op jit(solution)/shard_map/ppermute | solution.py:787
  98.1 2.7 %collective-permute-start.34 = (bf16[2,144,128]{2,1,0:T(8,128)(2,1)S(1)}, bf16[2,144,128]{2,1,0:T(8,128)(2,1)S(1)}, u32[]{:S(2)}, u32[]{:S(2)}) collective-permute-start(bf16[2,144,128]{2,1,0:T(8,128)(2,1)S(1)} %get-tuple-element.273.refs_0_), channel_id=1, source_target_pairs={{0,4},{2,6},{1,5},{3,7},{4,0},{6,2},{5,1},{7,3},{8,12},{10,14},{9,... | collective-permute-start | bytes 221192 | tf_op jit(solution)/shard_map/ppermute | solution.py:804
  100.8 4.2 %shard_map.196 = (f32[256,256]{1,0:T(8,128)S(1)}, f32[256,256]{1,0:T(8,128)S(1)}, f32[256,256]{1,0:T(8,128)S(1)}, bf16[2,2,32,128]{3,2,1,0:T(8,128)(2,1)S(1)}, f32[1,256]{1,0:T(1,128)S(1)}) custom-call(s32[3]{0:T(128)S(1)} %pad_add_fusion.place.refs_0_, bf16[3,256,256]{2,1,0:T(8,128)(2,1)S(1)} %get-tuple-element.247.qkv, ...), custom_call_target="tpu_custom_call" | custom-call | tf_op jit(solution)/shard_map/pallas_call | solution.py:765
  112.6 2.7 %shard_map.199 = (bf16[256,256]{1,0:T(8,128)(2,1)S(1)}, f32[256,256]{1,0:T(8,128)S(1)}, f32[256,256]{1,0:T(8,128)S(1)}, f32[256,256]{1,0:T(8,128)S(1)}) custom-call(s32[3]{0:T(128)S(1)} %pad_add_fusion.place.refs_0_, bf16[3,256,256]{2,1,0:T(8,128)(2,1)S(1)} %get-tuple-element.247.qkv, bf16[256,256]{1,0:T(8,128)(2,1)S(1)} %get-tuple-element.224.causal, ...), custom_call_target="tpu_custom_call" | custom-call | tf_op jit(solution)/shard_map/pallas_call | solution.py:765
  115.8 3.6 %collective-permute-done.40.refs_2_ = bf16[2,144,128]{2,1,0:T(8,128)(2,1)S(1)} collective-permute-done((bf16[2,144,128]{2,1,0:T(8,128)(2,1)S(1)}, bf16[2,144,128]{2,1,0:T(8,128)(2,1)S(1)}, u32[]{:S(2)}, u32[]{:S(2)}) %collective-permute-start.40) | collective-permute-done | bytes 73760 | tf_op jit(solution)/shard_map/ppermute | solution.py:804
  125.1 3.4 %collective-permute-done.42.refs_2_ = bf16[256,512]{1,0:T(8,128)(2,1)S(1)} collective-permute-done((bf16[256,512]{1,0:T(8,128)(2,1)S(1)}, bf16[256,512]{1,0:T(8,128)(2,1)S(1)}, u32[]{:S(2)}, u32[]{:S(2)}) %collective-permute-start.42) | collective-permute-done | bytes 262176 | tf_op jit(solution)/shard_map/ppermute | solution.py:787
  131.5 5.3 %collective-permute-done.43.part_b = bf16[256,512]{1,0:T(8,128)(2,1)S(1)} collective-permute-done((bf16[256,512]{1,0:T(8,128)(2,1)S(1)}, bf16[256,512]{1,0:T(8,128)(2,1)S(1)}, u32[]{:S(2)}, u32[]{:S(2)}) %collective-permute-start.43) | collective-permute-done | bytes 262176 | tf_op jit(solution)/shard_map/ppermute | solution.py:787
  140.4 4.2 %shard_map.204 = (f32[256,256]{1,0:T(8,128)S(1)}, f32[256,256]{1,0:T(8,128)S(1)}, f32[256,256]{1,0:T(8,128)S(1)}, bf16[2,2,32,128]{3,2,1,0:T(8,128)(2,1)S(1)}, f32[1,256]{1,0:T(1,128)S(1)}) custom-call(s32[3]{0:T(128)S(1)} %pad_add_fusion.place.refs_0_, bf16[3,256,256]{2,1,0:T(8,128)(2,1)S(1)} %get-tuple-element.221.qkv, ...), custom_call_target="tpu_custom_call" | custom-call | tf_op jit(solution)/shard_map/pallas_call | solution.py:765
  155.2 2.7 %shard_map.208 = (bf16[256,256]{1,0:T(8,128)(2,1)S(1)}, f32[256,256]{1,0:T(8,128)S(1)}, f32[256,256]{1,0:T(8,128)S(1)}, f32[256,256]{1,0:T(8,128)S(1)}) custom-call(s32[3]{0:T(128)S(1)} %pad_add_fusion.place.refs_0_, bf16[3,256,256]{2,1,0:T(8,128)(2,1)S(1)} %get-tuple-element.221.qkv, bf16[256,256]{1,0:T(8,128)(2,1)S(1)} %get-tuple-element.224.causal, ...), custom_call_target="tpu_custom_call" | custom-call | tf_op jit(solution)/shard_map/pallas_call | solution.py:765
  159.2 5.7 %collective-permute-done.51.refs_1_ = bf16[2,144,128]{2,1,0:T(8,128)(2,1)S(1)} collective-permute-done((bf16[2,144,128]{2,1,0:T(8,128)(2,1)S(1)}, bf16[2,144,128]{2,1,0:T(8,128)(2,1)S(1)}, u32[]{:S(2)}, u32[]{:S(2)}) %collective-permute-start.51) | collective-permute-done | bytes 73760 | tf_op jit(solution)/shard_map/ppermute | solution.py:804
  174.6 3.6 %collective-permute-done.54.part_b = bf16[256,512]{1,0:T(8,128)(2,1)S(1)} collective-permute-done((bf16[256,512]{1,0:T(8,128)(2,1)S(1)}, bf16[256,512]{1,0:T(8,128)(2,1)S(1)}, u32[]{:S(2)}, u32[]{:S(2)}) %collective-permute-start.54) | collective-permute-done | bytes 262176 | tf_op jit(solution)/shard_map/ppermute | solution.py:787
  181.1 2.4 collective-permute-done.59.second
  183.5 3.4 %collective-permute-start.63 = (bf16[144,512]{1,0:T(8,128)(2,1)S(1)}, bf16[144,512]{1,0:T(8,128)(2,1)S(1)}, u32[]{:S(2)}, u32[]{:S(2)}) collective-permute-start(bf16[144,512]{1,0:T(8,128)(2,1)S(1)} %shard_map.216.mine), channel_id=1, source_target_pairs={{0,16},{4,20},{8,24},{12,28},{16,0},{20,4},{24,8},{28,12},{1,17},{... | collective-permute-start | bytes 442376 | tf_op jit(solution)/shard_map/ppermute | solution.py:841
  188.4 6.1 %collective-permute-done.56.second = bf16[256,512]{1,0:T(8,128)(2,1)S(1)} collective-permute-done((bf16[256,512]{1,0:T(8,128)(2,1)S(1)}, bf16[256,512]{1,0:T(8,128)(2,1)S(1)}, u32[]{:S(2)}, u32[]{:S(2)}) %collective-permute-start.56) | collective-permute-done | bytes 262176 | tf_op jit(solution)/shard_map/ppermute | solution.py:841
  198.0 6.1 %collective-permute-done.62.second = bf16[224,512]{1,0:T(8,128)(2,1)S(1)} collective-permute-done((bf16[224,512]{1,0:T(8,128)(2,1)S(1)}, bf16[224,512]{1,0:T(8,128)(2,1)S(1)}, u32[]{:S(2)}, u32[]{:S(2)}) %collective-permute-start.62) | collective-permute-done | bytes 229408 | tf_op jit(solution)/shard_map/ppermute | solution.py:841
  209.1 3.5 %collective-permute-start.67 = (bf16[64,512]{1,0:T(8,128)(2,1)S(1)}, bf16[64,512]{1,0:T(8,128)(2,1)S(1)}, u32[]{:S(2)}, u32[]{:S(2)}) collective-permute-start(bf16[64,512]{1,0:T(8,128)(2,1)S(1)} %get-tuple-element.393), channel_id=1, source_target_pairs={{0,16},{4,20},{8,24},{12,28},{16,0},{20,4},{24,8},{28,12},{1,17},{... | collective-permute-start | bytes 196616 | tf_op jit(solution)/shard_map/ppermute | solution.py:841
  215.5 2.4 collective-permute-start.71
  224.8 2.4 collective-permute-start.75
  229.6 3.3 %collective-permute-done.76.got = bf16[224,512]{1,0:T(8,128)(2,1)S(1)} collective-permute-done((bf16[224,512]{1,0:T(8,128)(2,1)S(1)}, bf16[224,512]{1,0:T(8,128)(2,1)S(1)}, u32[]{:S(2)}, u32[]{:S(2)}) %collective-permute-start.76) | collective-permute-done | bytes 229408 | tf_op jit(solution)/shard_map/ppermute | solution.py:841
  236.2 3.8 %collective-permute-done.74.got = bf16[128,512]{1,0:T(8,128)(2,1)S(1)} collective-permute-done((bf16[128,512]{1,0:T(8,128)(2,1)S(1)}, bf16[128,512]{1,0:T(8,128)(2,1)S(1)}, u32[]{:S(2)}, u32[]{:S(2)}) %collective-permute-start.74) | collective-permute-done | bytes 131104 | tf_op jit(solution)/shard_map/ppermute | solution.py:841
  242.9 3.2 %collective-permute-done.80.refs_5_ = bf16[320,512]{1,0:T(8,128)(2,1)S(1)} collective-permute-done((bf16[320,512]{1,0:T(8,128)(2,1)S(1)}, bf16[320,512]{1,0:T(8,128)(2,1)S(1)}, u32[]{:S(2)}, u32[]{:S(2)}) %collective-permute-start.80) | collective-permute-done | bytes 327712 | tf_op jit(solution)/shard_map/ppermute | solution.py:841
  247.9 2.9 %shard_map.235 = (f32[2,512,512]{2,1,0:T(8,128)}, f32[2,512,512]{2,1,0:T(8,128)}, f32[2,128,512]{2,1,0:T(8,128)}, bf16[384,512]{1,0:T(8,128)(2,1)S(1)}) custom-call(s32[3]{0:T(128)S(1)} %pad_add_fusion.place.refs_0_, bf16[576,512]{1,0:T(8,128)(2,1)S(1)} %shard_map.225.refs_0_, bf16[576,512]{1,0:T(8,128)(2,1)S(1)} %collective-permute-done.78.refs_1_, ...), custom_call_target="tpu_custom_call" | custom-call | tf_op jit(solution)/shard_map/pallas_call | solution.py:765
  (225 shorter events, 124.5 us)
Async XLA Ops:
  18.4 23.3 %collective-permute-start.17 = (bf16[512,512]{1,0:T(8,128)(2,1)S(1)}, bf16[512,512]{1,0:T(8,128)(2,1)S(1)}, u32[]{:S(2)}, u32[]{:S(2)}) collective-permute-start(bf16[512,512]{1,0:T(8,128)(2,1)S(1)} %get-tuple-element.241), channel_id=1, source_target_pairs={{0,1},{1,0},{2,3},{3,2},{4,5},{5,4},{6,7},{7,6},{8,9},{9,8},{10,11... | collective-permute-start | bytes 1572872 | tf_op jit(solution)/shard_map/ppermute | solution.py:782
  19.8 21.9 %collective-permute-start.18 = (bf16[512,512]{1,0:T(8,128)(2,1)S(1)}, bf16[512,512]{1,0:T(8,128)(2,1)S(1)}, u32[]{:S(2)}, u32[]{:S(2)}) collective-permute-start(bf16[512,512]{1,0:T(8,128)(2,1)S(1)} %get-tuple-element.242), channel_id=1, source_target_pairs={{0,1},{1,0},{2,3},{3,2},{4,5},{5,4},{6,7},{7,6},{8,9},{9,8},{10,11... | collective-permute-start | bytes 1572872 | tf_op jit(solution)/shard_map/ppermute | solution.py:782
  21.4 13.5 %collective-permute-start.12 = (bf16[256,128]{1,0:T(8,128)(2,1)S(1)}, bf16[256,128]{1,0:T(8,128)(2,1)S(1)}, u32[]{:S(2)}, u32[]{:S(2)}) collective-permute-start(bf16[256,128]{1,0:T(8,128)(2,1)S(1)} %get-tuple-element.236), channel_id=1, source_target_pairs={{0,3},{1,2},{2,1},{3,0},{4,7},{5,6},{6,5},{7,4},{8,11},{9,10},{10,... | collective-permute-start | bytes 196616 | tf_op jit(solution)/shard_map/ppermute | solution.py:792
  25.2 13.8 %collective-permute-start.13 = (bf16[2,144,128]{2,1,0:T(8,128)(2,1)S(1)}, bf16[2,144,128]{2,1,0:T(8,128)(2,1)S(1)}, u32[]{:S(2)}, u32[]{:S(2)}) collective-permute-start(bf16[2,144,128]{2,1,0:T(8,128)(2,1)S(1)} %get-tuple-element.238), channel_id=1, source_target_pairs={{0,8},{2,10},{1,9},{3,11},{4,12},{6,14},{5,13},{7,15},{8,16},{10,1... | collective-permute-start | bytes 221192 | tf_op jit(solution)/shard_map/ppermute | solution.py:804
  50.6 29.9 %collective-permute-start.30 = (bf16[512,512]{1,0:T(8,128)(2,1)S(1)}, bf16[512,512]{1,0:T(8,128)(2,1)S(1)}, u32[]{:S(2)}, u32[]{:S(2)}) collective-permute-start(bf16[512,512]{1,0:T(8,128)(2,1)S(1)} %get-tuple-element.258), channel_id=1, source_target_pairs={{0,1},{1,0},{2,3},{3,2},{4,5},{5,4},{6,7},{7,6},{8,9},{9,8},{10,11... | collective-permute-start | bytes 1572872 | tf_op jit(solution)/shard_map/ppermute | solution.py:782
  50.6 29.9 %collective-permute-start.31 = (bf16[512,512]{1,0:T(8,128)(2,1)S(1)}, bf16[512,512]{1,0:T(8,128)(2,1)S(1)}, u32[]{:S(2)}, u32[]{:S(2)}) collective-permute-start(bf16[512,512]{1,0:T(8,128)(2,1)S(1)} %get-tuple-element.259), channel_id=1, source_target_pairs={{0,1},{1,0},{2,3},{3,2},{4,5},{5,4},{6,7},{7,6},{8,9},{9,8},{10,11... | collective-permute-start | bytes 1572872 | tf_op jit(solution)/shard_map/ppermute | solution.py:782
  62.6 11.0 %collective-permute-start.21 = (bf16[5,32,128]{2,1,0:T(8,128)(2,1)S(1)}, bf16[5,32,128]{2,1,0:T(8,128)(2,1)S(1)}, u32[]{:S(2)}, u32[]{:S(2)}) collective-permute-start(bf16[5,32,128]{2,1,0:T(8,128)(2,1)S(1)} %get-tuple-element.248), channel_id=1, source_target_pairs={{0,1},{2,3},{1,4},{3,6},{4,5},{6,7},{5,8},{7,10},{8,9},{10,11},{9,... | collective-permute-start | bytes 122888 | tf_op jit(solution)/shard_map/ppermute | solution.py:804
  65.5 12.3 %collective-permute-start.26 = (bf16[2,144,128]{2,1,0:T(8,128)(2,1)S(1)}, bf16[2,144,128]{2,1,0:T(8,128)(2,1)S(1)}, u32[]{:S(2)}, u32[]{:S(2)}) collective-permute-start(bf16[2,144,128]{2,1,0:T(8,128)(2,1)S(1)} %get-tuple-element.256), channel_id=1, source_target_pairs={{0,8},{2,10},{1,9},{3,11},{4,12},{6,14},{5,13},{7,15},{8,16},{10,1... | collective-permute-start | bytes 221192 | tf_op jit(solution)/shard_map/ppermute | solution.py:804
  67.4 10.4 %collective-permute-start.27 = (bf16[2,144,128]{2,1,0:T(8,128)(2,1)S(1)}, bf16[2,144,128]{2,1,0:T(8,128)(2,1)S(1)}, u32[]{:S(2)}, u32[]{:S(2)}) collective-permute-start(bf16[2,144,128]{2,1,0:T(8,128)(2,1)S(1)} %get-tuple-element.256), channel_id=1, source_target_pairs={{0,16},{2,18},{1,17},{3,19},{4,20},{6,22},{5,21},{7,23},{8,24},{10... | collective-permute-start | bytes 221192 | tf_op jit(solution)/shard_map/ppermute | solution.py:804
  107.0 15.3 %collective-permute-start.36 = (bf16[1152,512]{1,0:T(8,128)(2,1)S(1)}, bf16[1152,512]{1,0:T(8,128)(2,1)S(1)}, u32[]{:S(2)}, u32[]{:S(2)}) collective-permute-start(bf16[1152,512]{1,0:T(8,128)(2,1)S(1)} %get-tuple-element.284), channel_id=1, source_target_pairs={{0,1},{1,0},{2,3},{3,2},{4,5},{5,4},{6,7},{7,6},{8,9},{9,8},{10,11... | collective-permute-start | bytes 3538952 | tf_op jit(solution)/shard_map/ppermute | solution.py:782
  123.2 22.0 %collective-permute-start.41 = (bf16[576,512]{1,0:T(8,128)(2,1)S(1)}, bf16[576,512]{1,0:T(8,128)(2,1)S(1)}, u32[]{:S(2)}, u32[]{:S(2)}) collective-permute-start(bf16[576,512]{1,0:T(8,128)(2,1)S(1)} %get-tuple-element.303), channel_id=1, source_target_pairs={{0,4},{4,0},{8,12},{12,8},{16,20},{20,16},{24,28},{28,24},{1,5},{5... | collective-permute-start | bytes 1769480 | tf_op jit(solution)/shard_map/ppermute | solution.py:841
  147.5 18.7 %collective-permute-start.48 = (bf16[1536,512]{1,0:T(8,128)(2,1)S(1)}, bf16[1536,512]{1,0:T(8,128)(2,1)S(1)}, u32[]{:S(2)}, u32[]{:S(2)}) collective-permute-start(bf16[1536,512]{1,0:T(8,128)(2,1)S(1)} %get-tuple-element.333), channel_id=1, source_target_pairs={{0,1},{1,0},{2,3},{3,2},{4,5},{5,4},{6,7},{7,6},{8,9},{9,8},{10,11... | collective-permute-start | bytes 4718600 | tf_op jit(solution)/shard_map/ppermute | solution.py:782
  147.8 20.0 %collective-permute-start.47 = (bf16[288,512]{1,0:T(8,128)(2,1)S(1)}, bf16[288,512]{1,0:T(8,128)(2,1)S(1)}, u32[]{:S(2)}, u32[]{:S(2)}) collective-permute-start(bf16[288,512]{1,0:T(8,128)(2,1)S(1)} %get-tuple-element.320), channel_id=1, source_target_pairs={{0,8},{4,12},{8,0},{12,4},{16,24},{20,28},{24,16},{28,20},{1,9},{5... | collective-permute-start | bytes 884744 | tf_op jit(solution)/shard_map/ppermute | solution.py:841
  152.3 12.6 %collective-permute-start.51 = (bf16[2,144,128]{2,1,0:T(8,128)(2,1)S(1)}, bf16[2,144,128]{2,1,0:T(8,128)(2,1)S(1)}, u32[]{:S(2)}, u32[]{:S(2)}) collective-permute-start(bf16[2,144,128]{2,1,0:T(8,128)(2,1)S(1)} %get-tuple-element.317), channel_id=1, source_target_pairs={{16,0},{18,2},{17,1},{19,3},{20,4},{22,6},{21,5},{23,7},{24,8},{26... | collective-permute-start | bytes 221192 | tf_op jit(solution)/shard_map/ppermute | solution.py:804
  153.6 11.3 %collective-permute-start.52 = (bf16[2,144,128]{2,1,0:T(8,128)(2,1)S(1)}, bf16[2,144,128]{2,1,0:T(8,128)(2,1)S(1)}, u32[]{:S(2)}, u32[]{:S(2)}) collective-permute-start(bf16[2,144,128]{2,1,0:T(8,128)(2,1)S(1)} %get-tuple-element.317), channel_id=1, source_target_pairs={{24,0},{26,2},{25,1},{27,3},{28,4},{30,6},{29,5},{31,7}} | collective-permute-start | bytes 221192 | tf_op jit(solution)/shard_map/ppermute | solution.py:804
  171.0 15.9 %collective-permute-start.58 = (bf16[448,512]{1,0:T(8,128)(2,1)S(1)}, bf16[448,512]{1,0:T(8,128)(2,1)S(1)}, u32[]{:S(2)}, u32[]{:S(2)}) collective-permute-start(bf16[448,512]{1,0:T(8,128)(2,1)S(1)} %get-tuple-element.350), channel_id=1, source_target_pairs={{0,4},{4,0},{8,12},{12,8},{16,20},{20,16},{24,28},{28,24},{1,5},{5... | collective-permute-start | bytes 1376264 | tf_op jit(solution)/shard_map/ppermute | solution.py:841
  172.5 15.2 %collective-permute-start.57 = (bf16[320,512]{1,0:T(8,128)(2,1)S(1)}, bf16[320,512]{1,0:T(8,128)(2,1)S(1)}, u32[]{:S(2)}, u32[]{:S(2)}) collective-permute-start(bf16[320,512]{1,0:T(8,128)(2,1)S(1)} %get-tuple-element.352), channel_id=1, source_target_pairs={{0,8},{4,12},{8,0},{12,4},{16,24},{20,28},{24,16},{28,20},{1,9},{5... | collective-permute-start | bytes 983048 | tf_op jit(solution)/shard_map/ppermute | solution.py:841
  172.5 11.0 %collective-permute-start.59 = (bf16[144,512]{1,0:T(8,128)(2,1)S(1)}, bf16[144,512]{1,0:T(8,128)(2,1)S(1)}, u32[]{:S(2)}, u32[]{:S(2)}) collective-permute-start(bf16[144,512]{1,0:T(8,128)(2,1)S(1)} %get-tuple-element.354), channel_id=1, source_target_pairs={{0,16},{4,20},{8,24},{12,28},{16,0},{20,4},{24,8},{28,12},{1,17},{... | collective-permute-start | bytes 442376 | tf_op jit(solution)/shard_map/ppermute | solution.py:841
  181.0 13.5 %collective-permute-start.56 = (bf16[256,512]{1,0:T(8,128)(2,1)S(1)}, bf16[256,512]{1,0:T(8,128)(2,1)S(1)}, u32[]{:S(2)}, u32[]{:S(2)}) collective-permute-start(bf16[256,512]{1,0:T(8,128)(2,1)S(1)} %get-tuple-element.373), channel_id=1, source_target_pairs={{0,8},{4,12},{8,0},{12,4},{16,24},{20,28},{24,16},{28,20},{1,9},{5... | collective-permute-start | bytes 786440 | tf_op jit(solution)/shard_map/ppermute | solution.py:841
  183.5 11.6 %collective-permute-start.63 = (bf16[144,512]{1,0:T(8,128)(2,1)S(1)}, bf16[144,512]{1,0:T(8,128)(2,1)S(1)}, u32[]{:S(2)}, u32[]{:S(2)}) collective-permute-start(bf16[144,512]{1,0:T(8,128)(2,1)S(1)} %shard_map.216.mine), channel_id=1, source_target_pairs={{0,16},{4,20},{8,24},{12,28},{16,0},{20,4},{24,8},{28,12},{1,17},{... | collective-permute-start | bytes 442376 | tf_op jit(solution)/shard_map/ppermute | solution.py:841
  187.6 16.5 %collective-permute-start.62 = (bf16[224,512]{1,0:T(8,128)(2,1)S(1)}, bf16[224,512]{1,0:T(8,128)(2,1)S(1)}, u32[]{:S(2)}, u32[]{:S(2)}) collective-permute-start(bf16[224,512]{1,0:T(8,128)(2,1)S(1)} %get-tuple-element.379), channel_id=1, source_target_pairs={{0,8},{4,12},{8,0},{12,4},{16,24},{20,28},{24,16},{28,20},{1,9},{5... | collective-permute-start | bytes 688136 | tf_op jit(solution)/shard_map/ppermute | solution.py:841
  195.7 16.9 %collective-permute-start.70 = (bf16[288,512]{1,0:T(8,128)(2,1)S(1)}, bf16[288,512]{1,0:T(8,128)(2,1)S(1)}, u32[]{:S(2)}, u32[]{:S(2)}) collective-permute-start(bf16[288,512]{1,0:T(8,128)(2,1)S(1)} %shard_map.220.mine), channel_id=1, source_target_pairs={{0,8},{4,12},{8,0},{12,4},{16,24},{20,28},{24,16},{28,20},{1,9},{5... | collective-permute-start | bytes 884744 | tf_op jit(solution)/shard_map/ppermute | solution.py:841
  195.8 11.2 %collective-permute-start.61 = (bf16[160,512]{1,0:T(8,128)(2,1)S(1)}, bf16[160,512]{1,0:T(8,128)(2,1)S(1)}, u32[]{:S(2)}, u32[]{:S(2)}) collective-permute-start(bf16[160,512]{1,0:T(8,128)(2,1)S(1)} %get-tuple-element.381), channel_id=1, source_target_pairs={{0,16},{4,20},{8,24},{12,28},{16,0},{20,4},{24,8},{28,12},{1,17},{... | collective-permute-start | bytes 491528 | tf_op jit(solution)/shard_map/ppermute | solution.py:841
  198.0 10.5 %collective-permute-start.60 = (bf16[128,512]{1,0:T(8,128)(2,1)S(1)}, bf16[128,512]{1,0:T(8,128)(2,1)S(1)}, u32[]{:S(2)}, u32[]{:S(2)}) collective-permute-start(bf16[128,512]{1,0:T(8,128)(2,1)S(1)} %get-tuple-element.384), channel_id=1, source_target_pairs={{0,4},{4,0},{8,12},{12,8},{16,20},{20,16},{24,28},{28,24},{1,5},{5... | collective-permute-start | bytes 393224 | tf_op jit(solution)/shard_map/ppermute | solution.py:841
  218.0 10.9 %collective-permute-start.64 = (bf16[256,512]{1,0:T(8,128)(2,1)S(1)}, bf16[256,512]{1,0:T(8,128)(2,1)S(1)}, u32[]{:S(2)}, u32[]{:S(2)}) collective-permute-start(bf16[256,512]{1,0:T(8,128)(2,1)S(1)} %get-tuple-element.394.part_a), channel_id=1, source_target_pairs={{0,2},{1,3},{2,0},{3,1},{4,6},{5,7},{6,4},{7,5},{8,10},{9,11},{10,... | collective-permute-start | bytes 786440 | tf_op jit(solution)/shard_map/ppermute | solution.py:787
  220.9 22.0 %collective-permute-start.78 = (bf16[576,512]{1,0:T(8,128)(2,1)S(1)}, bf16[576,512]{1,0:T(8,128)(2,1)S(1)}, u32[]{:S(2)}, u32[]{:S(2)}) collective-permute-start(bf16[576,512]{1,0:T(8,128)(2,1)S(1)} %shard_map.225.refs_0_), channel_id=1, source_target_pairs={{0,4},{4,0},{8,12},{12,8},{16,20},{20,16},{24,28},{28,24},{1,5},{5... | collective-permute-start | bytes 1769480 | tf_op jit(solution)/shard_map/ppermute | solution.py:841
  222.6 10.3 %collective-permute-start.76 = (bf16[224,512]{1,0:T(8,128)(2,1)S(1)}, bf16[224,512]{1,0:T(8,128)(2,1)S(1)}, u32[]{:S(2)}, u32[]{:S(2)}) collective-permute-start(bf16[224,512]{1,0:T(8,128)(2,1)S(1)} %shard_map.229.mine), channel_id=1, source_target_pairs={{0,8},{4,12},{8,0},{12,4},{16,24},{20,28},{24,16},{28,20},{1,9},{5... | collective-permute-start | bytes 688136 | tf_op jit(solution)/shard_map/ppermute | solution.py:841
  224.8 10.7 %collective-permute-start.75 = (bf16[160,512]{1,0:T(8,128)(2,1)S(1)}, bf16[160,512]{1,0:T(8,128)(2,1)S(1)}, u32[]{:S(2)}, u32[]{:S(2)}) collective-permute-start(bf16[160,512]{1,0:T(8,128)(2,1)S(1)} %shard_map.230.mine), channel_id=1, source_target_pairs={{0,16},{4,20},{8,24},{12,28},{16,0},{20,4},{24,8},{28,12},{1,17},{... | collective-permute-start | bytes 491528 | tf_op jit(solution)/shard_map/ppermute | solution.py:841
  227.7 12.2 %collective-permute-start.74 = (bf16[128,512]{1,0:T(8,128)(2,1)S(1)}, bf16[128,512]{1,0:T(8,128)(2,1)S(1)}, u32[]{:S(2)}, u32[]{:S(2)}) collective-permute-start(bf16[128,512]{1,0:T(8,128)(2,1)S(1)} %shard_map.231.mine), channel_id=1, source_target_pairs={{0,4},{4,0},{8,12},{12,8},{16,20},{20,16},{24,28},{28,24},{1,5},{5... | collective-permute-start | bytes 393224 | tf_op jit(solution)/shard_map/ppermute | solution.py:841
  229.5 12.6 %collective-permute-start.65 = (bf16[256,128]{1,0:T(8,128)(2,1)S(1)}, bf16[256,128]{1,0:T(8,128)(2,1)S(1)}, u32[]{:S(2)}, u32[]{:S(2)}) collective-permute-start(bf16[256,128]{1,0:T(8,128)(2,1)S(1)} %get-tuple-element.396), channel_id=1, source_target_pairs={{0,1},{1,0},{2,3},{3,2},{4,5},{5,4},{6,7},{7,6},{8,9},{9,8},{10,11... | collective-permute-start | bytes 196616 | tf_op jit(solution)/shard_map/ppermute | solution.py:782
  233.6 14.3 %collective-permute-start.79 = (bf16[448,512]{1,0:T(8,128)(2,1)S(1)}, bf16[448,512]{1,0:T(8,128)(2,1)S(1)}, u32[]{:S(2)}, u32[]{:S(2)}) collective-permute-start(bf16[448,512]{1,0:T(8,128)(2,1)S(1)} %shard_map.232.refs_2_), channel_id=1, source_target_pairs={{0,4},{4,0},{8,12},{12,8},{16,20},{20,16},{24,28},{28,24},{1,5},{5... | collective-permute-start | bytes 1376264 | tf_op jit(solution)/shard_map/ppermute | solution.py:841
  240.5 10.3 %collective-permute-start.77 = (bf16[256,512]{1,0:T(8,128)(2,1)S(1)}, bf16[256,512]{1,0:T(8,128)(2,1)S(1)}, u32[]{:S(2)}, u32[]{:S(2)}) collective-permute-start(bf16[256,512]{1,0:T(8,128)(2,1)S(1)} %shard_map.234.mine), channel_id=1, source_target_pairs={{0,8},{4,12},{8,0},{12,4},{16,24},{20,28},{24,16},{28,20},{1,9},{5... | collective-permute-start | bytes 786440 | tf_op jit(solution)/shard_map/ppermute | solution.py:841
  (60 other events, 372.8 us)
